TPU v7x, 32 devices: a whole 2x2x4 slice. The times are simulated.
32 devices in a mesh: section: 2 (over y), tensor: 2 (over core), dp: 8 (over z, x).
Axes of the slice: x: 2, y: 2, z: 4, core: 2. Of those that a mesh axis runs over, the one named last changes fastest.
Arguments:
- inputs: bfloat16 [2, 8, 768, 1024], P(None, 'dp', None, 'tensor'), may hold values from -6 to 6
- cotangent: bfloat16 [2, 8, 768, 1024], P(None, 'dp', None, 'tensor'), may hold values from -6 to 6
- ln1_gain: bfloat16 [2, 1024], P('section', 'tensor'), may hold values from 0.25 to 1.75
- ln1_bias: bfloat16 [2, 1024], P('section', 'tensor'), may hold values from -1.75 to 1.75
- qkv_weight: bfloat16 [2, 1024, 3, 1024], P('section', None, None, 'tensor'), may hold values from -0.1875 to 0.1875
- qv_bias: bfloat16 [2, 2, 1024], P('section', None, 'tensor'), may hold values from -0.625 to 0.625
- out_weight: bfloat16 [2, 1024, 1024], P('section', 'tensor'), may hold values from -3 to 3
- out_bias: bfloat16 [2, 1024], P('section', 'tensor'), may hold values from -1.75 to 1.75
- scale_attn: bfloat16 [2, 1024], P('section', 'tensor'), may hold values from 0.29882812 to 1
- ln2_gain: bfloat16 [2, 1024], P('section', 'tensor'), may hold values from 0.25 to 1.75
- ln2_bias: bfloat16 [2, 1024], P('section', 'tensor'), may hold values from -1.75 to 1.75
- fc1_weight: bfloat16 [2, 1024, 4096], P('section', None, 'tensor'), may hold values from -0.1875 to 0.1875
- fc1_bias: bfloat16 [2, 4096], P('section', 'tensor'), may hold values from -3 to 3
- fc2_weight: bfloat16 [2, 4096, 1024], P('section', 'tensor'), may hold values from -0.09375 to 0.09375
- fc2_bias: bfloat16 [2, 1024], P('section', 'tensor'), may hold values from -1.75 to 1.75
- scale_mlp: bfloat16 [2, 1024], P('section', 'tensor'), may hold values from 0.29882812 to 1
Outputs:
- block_outputs: bfloat16 [2, 2, 8, 768, 1024], P('section', None, 'dp', None, 'tensor')
- input_grads: bfloat16 [2, 2, 8, 768, 1024], P('section', None, 'dp', None, 'tensor')
- grad_ln1_gain: float32 [2, 1024], P('section', 'tensor')
- grad_ln1_bias: float32 [2, 1024], P('section', 'tensor')
- grad_qkv_weight: float32 [2, 1024, 3, 1024], P('section', None, None, 'tensor')
- grad_qv_bias: float32 [2, 2, 1024], P('section', None, 'tensor')
- grad_out_weight: float32 [2, 1024, 1024], P('section', 'tensor')
- grad_out_bias: float32 [2, 1024], P('section', 'tensor')
- grad_scale_attn: float32 [2, 1024], P('section', 'tensor')
- grad_ln2_gain: float32 [2, 1024], P('section', 'tensor')
- grad_ln2_bias: float32 [2, 1024], P('section', 'tensor')
- grad_fc1_weight: float32 [2, 1024, 4096], P('section', None, 'tensor')
- grad_fc1_bias: float32 [2, 4096], P('section', 'tensor')
- grad_fc2_weight: float32 [2, 4096, 1024], P('section', 'tensor')
- grad_fc2_bias: float32 [2, 1024], P('section', 'tensor')
- grad_scale_mlp: float32 [2, 1024], P('section', 'tensor')
All inputs are finite; a program needn't handle non-finite values.
Results may differ from a plain program's by a relative error of at most 0.017.
Values may be sent and summed in bfloat16 or wider, within the bound.
No kernel may reach another device: no remote copies, remote signals or barrier semaphores. Data moves between devices by JAX's collectives and lax.ppermute only.
A program may use at most 512 MiB of HBM per device.

v0:
```python
import jax
import jax.numpy as jnp
from jax import lax
from jax.sharding import PartitionSpec as P

HEAD_DIM = 64


EPSILON = 1e-06


def from_behind(block, axis, distance):
    devices = range(lax.axis_size(axis))
    route = [(i - distance, i) for i in devices if i - distance in devices]
    return lax.ppermute(block, axis, route)


def shortened(x):
    return jax.tree.map(lambda a: a.astype(jnp.bfloat16) if a.dtype == jnp.float32 else a, x)


def norm_stats(values):
    centre = jnp.mean(values, axis=-1, keepdims=True)
    centred = values - centre
    spread = jnp.mean(centred * centred, axis=-1, keepdims=True)
    return (centre, lax.rsqrt(spread + EPSILON))


def contract_rows(left, right):
    return lax.dot_general(
        left, right, (((0,), (0,)), ((), ())), preferred_element_type=jnp.float32
    )


def contract_cols(left, right):
    return lax.dot_general(
        left, right, (((1,), (1,)), ((), ())), preferred_element_type=jnp.float32
    )


def guarded(active_tick, compute, operands):

    def skipped(values):
        return jax.tree.map(jnp.zeros_like, compute(values))

    return lax.cond(active_tick, compute, skipped, operands)


def block_slices(queries, key_rows, value_rows, number, per_image, block_rows):
    image_index = number // per_image
    start_row = number % per_image * block_rows
    query_image = lax.dynamic_index_in_dim(queries, image_index, 0, keepdims=False)
    key_image = lax.dynamic_index_in_dim(key_rows, image_index, 0, keepdims=False)
    value_image = lax.dynamic_index_in_dim(value_rows, image_index, 0, keepdims=False)
    return (image_index, start_row, query_image, key_image, value_image)


def attend_forward(queries, key_rows, value_rows, block_rows):
    image_count, seq_len, head_count, head_size = queries.shape
    per_image = seq_len // block_rows
    score_scale = head_size ** (-0.5)

    def one_block(number):
        image_index, start_row, query_block, key_image, value_image = block_slices(
            queries, key_rows, value_rows, number, per_image, block_rows
        )
        scores = (
            jnp.einsum("qhd,khd->hqk", query_block, key_image, preferred_element_type=jnp.float32)
            * score_scale
        )
        row_top = jnp.max(scores, axis=-1, keepdims=True)
        log_total = jnp.log(jnp.sum(jnp.exp(scores - row_top), axis=-1, keepdims=True)) + row_top
        weights = jnp.exp(scores - log_total).astype(jnp.bfloat16)
        mixed_heads = jnp.einsum(
            "hqk,khd->qhd", weights, value_image, preferred_element_type=jnp.float32
        )
        return (mixed_heads.astype(jnp.bfloat16), log_total[..., 0])

    mixed_heads, log_totals = lax.map(one_block, jnp.arange(image_count * per_image))
    return (mixed_heads.reshape(image_count * seq_len, head_count * head_size), log_totals)


def attend_backward(queries, key_rows, value_rows, log_totals, grad_mixed, block_rows):
    image_count, seq_len, head_count, head_size = queries.shape
    per_image = seq_len // block_rows
    score_scale = head_size ** (-0.5)

    def one_block(number):
        image_index, start_row, query_block, key_image, value_image = block_slices(
            queries, key_rows, value_rows, number, per_image, block_rows
        )
        grad_image = lax.dynamic_index_in_dim(grad_mixed, image_index, 0, keepdims=False)
        scores = (
            jnp.einsum("qhd,khd->hqk", query_block, key_image, preferred_element_type=jnp.float32)
            * score_scale
        )
        log_total = lax.dynamic_index_in_dim(log_totals, number, 0, keepdims=False)
        weights_full = jnp.exp(scores - log_total[..., None])
        weights = weights_full.astype(jnp.bfloat16)
        grad_weights = jnp.einsum(
            "qhd,khd->hqk", grad_image, value_image, preferred_element_type=jnp.float32
        )
        centre = jnp.sum(grad_weights * weights_full, axis=-1, keepdims=True)
        grad_scores = (weights_full * (grad_weights - centre)).astype(jnp.bfloat16)
        grad_query = (
            jnp.einsum("hqk,khd->qhd", grad_scores, key_image, preferred_element_type=jnp.float32)
            * score_scale
        )
        grad_key = (
            jnp.einsum("hqk,qhd->khd", grad_scores, query_block, preferred_element_type=jnp.float32)
            * score_scale
        )
        grad_value = jnp.einsum(
            "hqk,qhd->khd", weights, grad_image, preferred_element_type=jnp.float32
        )
        return (grad_query, grad_key, grad_value)

    grad_query, grad_key, grad_value = lax.map(one_block, jnp.arange(image_count * per_image))
    row_count = image_count * seq_len
    flat_width = head_count * head_size
    grad_query = grad_query.reshape(row_count, flat_width)
    grad_key = (
        grad_key.reshape(image_count, per_image, seq_len, flat_width)
        .sum(axis=1)
        .reshape(row_count, flat_width)
    )
    grad_value = (
        grad_value.reshape(image_count, per_image, seq_len, flat_width)
        .sum(axis=1)
        .reshape(row_count, flat_width)
    )
    return (grad_query, grad_key, grad_value)


def shards(
    inputs,
    cotangent,
    ln1_gain,
    ln1_bias,
    qkv_weight,
    qv_bias,
    out_weight,
    out_bias,
    scale_attn,
    ln2_gain,
    ln2_bias,
    fc1_weight,
    fc1_bias,
    fc2_weight,
    fc2_bias,
    scale_mlp,
):
    section_rank = lax.axis_index("section")
    tensor_rank = lax.axis_index("tensor")
    tensor_count = lax.axis_size("tensor")
    micro_count, images, seq_len, half_width = inputs.shape
    row_count = images * seq_len
    full_width = qkv_weight.shape[1]
    heads_here = half_width // HEAD_DIM
    w_qkv = qkv_weight[0].reshape(full_width, 3 * half_width)
    w_out = out_weight[0]
    w_up = fc1_weight[0]
    w_down = fc2_weight[0]
    bias_row = jnp.concatenate(
        [qv_bias[0, 0], jnp.zeros_like(qv_bias[0, 0]), qv_bias[0, 1]]
    ).astype(jnp.float32)
    out_shift = out_bias[0].astype(jnp.float32)
    attn_scale = scale_attn[0].astype(jnp.float32)
    up_shift = fc1_bias[0].astype(jnp.float32)
    down_shift = fc2_bias[0].astype(jnp.float32)
    mlp_scale = scale_mlp[0].astype(jnp.float32)
    gain_two_half = ln2_gain.astype(jnp.float32)
    bias_two_half = ln2_bias.astype(jnp.float32)

    def own_half(full_values):
        return lax.dynamic_slice_in_dim(full_values, tensor_rank * half_width, half_width, 1)

    def heads_view(flat):
        return flat.reshape(images, seq_len, heads_here, HEAD_DIM)

    def split_packed(packed):
        return (
            heads_view(packed[:, :half_width]),
            heads_view(packed[:, half_width : 2 * half_width]),
            heads_view(packed[:, 2 * half_width :]),
        )

    def attention_branch(normed):
        packed = (jnp.dot(normed, w_qkv, preferred_element_type=jnp.float32) + bias_row).astype(
            jnp.bfloat16
        )
        queries, key_rows, value_rows = split_packed(packed)
        mixed_heads, log_totals = attend_forward(queries, key_rows, value_rows, seq_len)
        partial_value = jnp.dot(mixed_heads, w_out, preferred_element_type=jnp.float32)
        return (packed, mixed_heads, log_totals, partial_value)

    def mlp_branch(normed):
        before = jnp.dot(normed, w_up, preferred_element_type=jnp.float32) + up_shift
        active = jax.nn.gelu(before, approximate=False).astype(jnp.bfloat16)
        return (before, jnp.dot(active, w_down, preferred_element_type=jnp.float32))

    def mlp_backward(operands):
        grad_branch_whole, normed_two, before = operands
        active_values, gelu_pull = jax.vjp(
            lambda values: jax.nn.gelu(values, approximate=False), before
        )
        active = active_values.astype(jnp.bfloat16)
        grad_down = contract_rows(active, grad_branch_whole)
        grad_active = contract_cols(grad_branch_whole, w_down)
        grad_before = gelu_pull(grad_active)[0].astype(jnp.bfloat16)
        grad_up = contract_rows(normed_two, grad_before)
        grad_up_shift = jnp.sum(grad_before.astype(jnp.float32), axis=0)
        partial_value = contract_cols(grad_before, w_up)
        return (grad_down, grad_up, grad_up_shift, partial_value)

    def attention_backward(operands):
        grad_att_whole, normed_one, packed, mixed_heads, log_totals = operands
        grad_out_w = contract_rows(mixed_heads, grad_att_whole)
        grad_mixed = contract_cols(grad_att_whole, w_out).astype(jnp.bfloat16)
        queries, key_rows, value_rows = split_packed(packed)
        grad_query, grad_key, grad_value = attend_backward(
            queries, key_rows, value_rows, log_totals, heads_view(grad_mixed), seq_len
        )
        grad_packed = jnp.concatenate([grad_query, grad_key, grad_value], axis=1).astype(
            jnp.bfloat16
        )
        grad_qkv = contract_rows(normed_one, grad_packed)
        grad_bias = jnp.sum(grad_packed.astype(jnp.float32), axis=0)
        partial_value = contract_cols(grad_packed, w_qkv)
        return (grad_out_w, grad_qkv, grad_bias, partial_value)

    def stat_columns(full_values, centre, scale, gain_full, partial_value):
        normal = (full_values - centre) * scale
        weighted = partial_value * gain_full
        row_stats = jnp.stack(
            [jnp.sum(weighted, axis=-1), jnp.sum(weighted * normal, axis=-1)], axis=-1
        )
        return jnp.tile(row_stats, (1, tensor_count))

    def norm_backward(half_values, centre, scale, gain_half, grad_half, row_stats):
        normal = (half_values - centre) * scale
        grad_normal = grad_half * gain_half
        total_width = half_width * tensor_count
        grad_in = scale * (
            grad_normal - row_stats[:, 0:1] / total_width - normal * row_stats[:, 1:2] / total_width
        )
        return (grad_in, jnp.sum(grad_half * normal, axis=0), jnp.sum(grad_half, axis=0))

    received = jnp.zeros((row_count, half_width), jnp.bfloat16)
    outputs = jnp.zeros((micro_count, row_count, half_width), jnp.bfloat16)
    kept_all = []
    for tick_index in range(micro_count + 1):
        micro_index = tick_index - section_rank
        active_tick = (micro_index >= 0) & (micro_index < micro_count)
        own_input = inputs[min(tick_index, micro_count - 1)].reshape(row_count, half_width)
        x_half = jnp.where(section_rank == 0, own_input, received)
        whole = lax.all_gather(x_half, "tensor", axis=1, tiled=True)
        gain_one = lax.all_gather(ln1_gain, "tensor", axis=1, tiled=True)
        bias_one = lax.all_gather(ln1_bias, "tensor", axis=1, tiled=True)
        forward_whole_values = whole.astype(jnp.float32)
        centre_one, scale_one = norm_stats(forward_whole_values)
        forward_normed_one = (
            (forward_whole_values - centre_one) * scale_one * gain_one.astype(jnp.float32)
            + bias_one.astype(jnp.float32)
        ).astype(jnp.bfloat16)
        forward_packed, forward_mixed_heads, forward_log_totals, forward_partial_value = guarded(
            active_tick, attention_branch, forward_normed_one
        )
        attended = (
            lax.psum_scatter(
                forward_partial_value.astype(jnp.bfloat16),
                "tensor",
                scatter_dimension=1,
                tiled=True,
            ).astype(jnp.float32)
            + out_shift
        )
        residual_half = own_half(forward_whole_values) + attn_scale * attended
        residual = lax.all_gather(
            residual_half.astype(jnp.bfloat16), "tensor", axis=1, tiled=True
        ).astype(residual_half.dtype)
        gain_two = lax.all_gather(
            gain_two_half.astype(jnp.bfloat16), "tensor", axis=1, tiled=True
        ).astype(gain_two_half.dtype)
        bias_two = lax.all_gather(
            bias_two_half.astype(jnp.bfloat16), "tensor", axis=1, tiled=True
        ).astype(bias_two_half.dtype)
        centre_two, scale_two = norm_stats(residual)
        forward_normed_two = ((residual - centre_two) * scale_two * gain_two + bias_two).astype(
            jnp.bfloat16
        )
        forward_before, forward_partial_two = guarded(active_tick, mlp_branch, forward_normed_two)
        branch = (
            lax.psum_scatter(
                forward_partial_two.astype(jnp.bfloat16), "tensor", scatter_dimension=1, tiled=True
            ).astype(jnp.float32)
            + down_shift
        )
        output = (residual_half + mlp_scale * branch).astype(jnp.bfloat16)
        forward_kept_state = {
            "whole": whole,
            "normed_one": forward_normed_one,
            "centre_one": centre_one,
            "scale_one": scale_one,
            "packed": forward_packed,
            "mixed_heads": forward_mixed_heads,
            "log_totals": forward_log_totals,
            "attended": attended,
            "residual": residual,
            "centre_two": centre_two,
            "scale_two": scale_two,
            "normed_two": forward_normed_two,
            "before": forward_before,
            "branch": branch,
            "gain_one": gain_one.astype(jnp.float32),
            "gain_two": gain_two,
        }
        output, kept_state = (output, forward_kept_state)
        kept_all.append(kept_state)
        slot_index = jnp.clip(micro_index, 0, micro_count - 1)
        current = lax.dynamic_index_in_dim(outputs, slot_index, 0, keepdims=False)
        outputs = lax.dynamic_update_index_in_dim(
            outputs, jnp.where(active_tick, output, current), slot_index, 0
        )
        if tick_index < micro_count:
            received = from_behind(output, "section", 1)
    received_grad = jnp.zeros((row_count, half_width), jnp.bfloat16)
    in_grads = jnp.zeros((micro_count, row_count, half_width), jnp.bfloat16)
    summed = None
    for tick_index in range(micro_count + 1):
        micro_index = tick_index - 1 + section_rank
        active_tick = (micro_index >= 0) & (micro_index < micro_count)
        own_grad = cotangent[min(tick_index, micro_count - 1)].reshape(row_count, half_width)
        grad_half = jnp.where(section_rank == 1, own_grad, received_grad)
        early_state = kept_all[max(tick_index - 1, 0)]
        late_state = kept_all[min(tick_index + 1, micro_count)]
        kept_state = jax.tree.map(
            lambda early_leaf, late_leaf: jnp.where(section_rank == 0, early_leaf, late_leaf),
            early_state,
            late_state,
        )
        grad_y = grad_half.astype(jnp.float32)
        grad_mlp_scale = jnp.sum(grad_y * kept_state["branch"], axis=0)
        grad_branch = (mlp_scale * grad_y).astype(jnp.bfloat16)
        grad_down_shift = jnp.sum(grad_branch.astype(jnp.float32), axis=0)
        backward_grad_branch_whole = lax.all_gather(grad_branch, "tensor", axis=1, tiled=True)
        backward_grad_down, backward_grad_up, backward_grad_up_shift, partial_two = guarded(
            active_tick,
            mlp_backward,
            (backward_grad_branch_whole, kept_state["normed_two"], kept_state["before"]),
        )
        columns_two = stat_columns(
            kept_state["residual"],
            kept_state["centre_two"],
            kept_state["scale_two"],
            kept_state["gain_two"],
            partial_two,
        )
        grad_normed_two = lax.psum_scatter(
            partial_two.astype(jnp.bfloat16), "tensor", scatter_dimension=1, tiled=True
        ).astype(jnp.float32)
        stats_two = lax.psum_scatter(
            columns_two.astype(jnp.bfloat16), "tensor", scatter_dimension=1, tiled=True
        ).astype(jnp.float32)
        grad_norm_in, grad_gain_two, grad_bias_two = norm_backward(
            own_half(kept_state["residual"]),
            kept_state["centre_two"],
            kept_state["scale_two"],
            own_half(kept_state["gain_two"]),
            grad_normed_two,
            stats_two,
        )
        grad_residual = grad_y + grad_norm_in
        grad_attn_scale = jnp.sum(grad_residual * kept_state["attended"], axis=0)
        grad_att = (attn_scale * grad_residual).astype(jnp.bfloat16)
        grad_out_shift = jnp.sum(grad_att.astype(jnp.float32), axis=0)
        backward_grad_att_whole = lax.all_gather(grad_att, "tensor", axis=1, tiled=True)
        backward_grad_out_w, backward_grad_qkv, backward_grad_bias, partial_one = guarded(
            active_tick,
            attention_backward,
            (
                backward_grad_att_whole,
                kept_state["normed_one"],
                kept_state["packed"],
                kept_state["mixed_heads"],
                kept_state["log_totals"],
            ),
        )
        whole_values = kept_state["whole"].astype(jnp.float32)
        columns_one = stat_columns(
            whole_values,
            kept_state["centre_one"],
            kept_state["scale_one"],
            kept_state["gain_one"],
            partial_one,
        )
        grad_normed_one = lax.psum_scatter(
            partial_one.astype(jnp.bfloat16), "tensor", scatter_dimension=1, tiled=True
        ).astype(jnp.float32)
        stats_one = lax.psum_scatter(
            columns_one.astype(jnp.bfloat16), "tensor", scatter_dimension=1, tiled=True
        ).astype(jnp.float32)
        grad_in_norm, grad_gain_one, grad_bias_one = norm_backward(
            own_half(whole_values),
            kept_state["centre_one"],
            kept_state["scale_one"],
            own_half(kept_state["gain_one"]),
            grad_normed_one,
            stats_one,
        )
        grad_input = grad_residual + grad_in_norm
        tick_mask = active_tick.astype(jnp.float32)
        backward_small_grads = (
            jnp.stack(
                [
                    grad_gain_one,
                    grad_bias_one,
                    backward_grad_bias[:half_width],
                    backward_grad_bias[2 * half_width :],
                    grad_out_shift,
                    grad_attn_scale,
                    grad_gain_two,
                    grad_bias_two,
                    grad_down_shift,
                    grad_mlp_scale,
                ],
                axis=1,
            )
            * tick_mask
        )
        grad_input, layer_grads = (
            grad_input.astype(jnp.bfloat16),
            (
                backward_grad_qkv,
                backward_grad_out_w,
                backward_grad_up,
                backward_grad_up_shift,
                backward_grad_down,
                backward_small_grads,
            ),
        )
        slot_index = jnp.clip(micro_index, 0, micro_count - 1)
        current = lax.dynamic_index_in_dim(in_grads, slot_index, 0, keepdims=False)
        in_grads = lax.dynamic_update_index_in_dim(
            in_grads, jnp.where(active_tick, grad_input, current), slot_index, 0
        )
        if summed is None:
            summed = layer_grads
        else:
            summed = jax.tree.map(lambda total, extra: total + extra, summed, layer_grads)
        if tick_index < micro_count:
            received_grad = from_behind(grad_input, "section", -1)
    final_grads = jax.tree.map(
        lambda part: part.astype(jnp.float32), lax.psum(shortened(summed), "dp")
    )
    grad_qkv, grad_out_w, grad_up, grad_up_shift, grad_down, small_grads = final_grads

    def column(position):
        return small_grads[:, position][None]

    block_outputs = outputs.reshape(1, micro_count, images, seq_len, half_width)
    input_grads = in_grads.reshape(1, micro_count, images, seq_len, half_width)
    return (
        block_outputs,
        input_grads,
        column(0),
        column(1),
        grad_qkv.reshape(1, full_width, 3, half_width),
        jnp.stack([small_grads[:, 2], small_grads[:, 3]])[None],
        grad_out_w[None],
        column(4),
        column(5),
        column(6),
        column(7),
        grad_up[None],
        grad_up_shift[None],
        grad_down[None],
        column(8),
        column(9),
    )


def solution(mesh):
    placed = (
        P(None, "dp", None, "tensor"),
        P(None, "dp", None, "tensor"),
        P("section", "tensor"),
        P("section", "tensor"),
        P("section", None, None, "tensor"),
        P("section", None, "tensor"),
        P("section", "tensor", None),
        P("section", "tensor"),
        P("section", "tensor"),
        P("section", "tensor"),
        P("section", "tensor"),
        P("section", None, "tensor"),
        P("section", "tensor"),
        P("section", "tensor", None),
        P("section", "tensor"),
        P("section", "tensor"),
    )
    return jax.shard_map(
        shards,
        mesh=mesh,
        in_specs=placed,
        out_specs=(
            P("section", None, "dp", None, "tensor"),
            P("section", None, "dp", None, "tensor"),
            P("section", "tensor"),
            P("section", "tensor"),
            P("section", None, None, "tensor"),
            P("section", None, "tensor"),
            P("section", "tensor", None),
            P("section", "tensor"),
            P("section", "tensor"),
            P("section", "tensor"),
            P("section", "tensor"),
            P("section", None, "tensor"),
            P("section", "tensor"),
            P("section", "tensor", None),
            P("section", "tensor"),
            P("section", "tensor"),
        ),
        check_vma=False,
    )
```

profile of v0, /device:TPU:0, one launch (start us, length us, event | category | flops | bytes accessed | tf_op | source)
XLA Modules:
  0.0 1504.8 jit_solution(13878695857174198294)
XLA Ops:
  30.3 44.0 %conditional.12 = (bf16[768,1536]{1,0:T(8,128)(2,1)}, bf16[768,512]{0,1:T(8,128)(2,1)}, f32[1,8,768]{2,1,0:T(8,128)S(1)}, bf16[768,1024]{1,0:T(8,128)(2,1)S(1)}) conditional(s32[]{:T(128)} %convert_element_type.482, () %tuple.134, (bf16[768,1024]{1,0:T(8,128)(2,1)}, bf16[1024,1536]{0,1:T(8,128)(2,1)S(1)}, f32[1536]{0:T(1024)S(1)}, ...), branch_computations={%region_2.3_spmd, %region_3.6_spmd} | conditional | flops 4469680128 | bytes 84260984 | solution.py:46
  106.6 24.8 %conditional.13 = (f32[768,2048]{1,0:T(8,128)}, bf16[768,1024]{1,0:T(8,128)(2,1)S(1)}) conditional(s32[]{:T(128)} %convert_element_type.482, () %tuple.136, (bf16[768,1024]{1,0:T(8,128)(2,1)}, bf16[1024,2048]{1,0:T(8,128)(2,1)S(1)}, f32[2048]{0:T(1024)S(1)}, bf16[2048,1024]{1,0:T(8,128)(2,1)}) %tuple.396), branch_computations={%region_9.10_spmd, %region_10.11_spmd} | conditional | flops 6546259968 | bytes 40902700 | solution.py:46
  113.5 17.9 %fusion.13 = bf16[768,1024]{1,0:T(8,128)(2,1)S(1)} fusion(bf16[2048,1024]{1,0:T(8,128)(2,1)S(1)} %copy-done.172, f32[768,2048]{1,0:T(8,128)} %convolution_add_fusion), kind=kOutput, calls=%fused_computation.28 | convolution fusion | flops 3323461632 | bytes 12058624 | tf_op jit(solution)/shard_map/cond/branch_1_fun/dot_general | solution.py:200
  148.2 17.2 %collective-permute-done = bf16[768,512]{1,0:T(8,128)(2,1)S(1)} collective-permute-done((bf16[768,512]{1,0:T(8,128)(2,1)S(1)}, bf16[768,512]{1,0:T(8,128)(2,1)S(1)}, u32[]{:S(2)}, u32[]{:S(2)}) %collective-permute-start) | collective-permute-done | bytes 786464 | tf_op jit(solution)/shard_map/ppermute | solution.py:15
  166.4 11.8 all-gather.16.cloned.1.call-done
  185.3 50.1 %conditional.14 = (bf16[768,1536]{1,0:T(8,128)(2,1)}, bf16[768,512]{0,1:T(8,128)(2,1)}, f32[1,8,768]{2,1,0:T(8,128)S(1)}, bf16[768,1024]{1,0:T(8,128)(2,1)}) conditional(s32[]{:T(128)} %convert_element_type.498, () %tuple.138, (bf16[768,1024]{1,0:T(8,128)(2,1)}, bf16[1024,1536]{0,1:T(8,128)(2,1)S(1)}, f32[1536]{0:T(1024)S(1)}, ...), branch_computations={%region_14.15_spmd, %region_15.18_spmd} | conditional | flops 4469680128 | bytes 84260984 | solution.py:46
  267.3 25.5 %conditional.15 = (f32[768,2048]{1,0:T(8,128)}, bf16[768,1024]{1,0:T(8,128)(2,1)}) conditional(s32[]{:T(128)} %convert_element_type.498, () %tuple.140, (bf16[768,1024]{1,0:T(8,128)(2,1)}, bf16[1024,2048]{1,0:T(8,128)(2,1)S(1)}, f32[2048]{0:T(1024)S(1)}, bf16[2048,1024]{1,0:T(8,128)(2,1)}) %tuple.397), branch_computations={%region_21.22_spmd, %region_22.23_spmd} | conditional | flops 6546259968 | bytes 40902700 | solution.py:46
  274.2 18.6 %fusion.58 = bf16[768,1024]{1,0:T(8,128)(2,1)} fusion(bf16[2048,1024]{1,0:T(8,128)(2,1)S(1)} %copy-done.173, f32[768,2048]{1,0:T(8,128)} %convolution_add_fusion.1), kind=kOutput, calls=%fused_computation.87 | convolution fusion | flops 3323461632 | bytes 12058624 | tf_op jit(solution)/shard_map/cond/branch_1_fun/dot_general | solution.py:200
  309.3 17.2 %collective-permute-done.1 = bf16[768,512]{1,0:T(8,128)(2,1)S(1)} collective-permute-done((bf16[768,512]{1,0:T(8,128)(2,1)S(1)}, bf16[768,512]{1,0:T(8,128)(2,1)S(1)}, u32[]{:S(2)}, u32[]{:S(2)}) %collective-permute-start.1) | collective-permute-done | bytes 786464 | tf_op jit(solution)/shard_map/ppermute | solution.py:15
  327.6 11.8 all-gather.20.cloned.1.call-done
  355.6 47.5 %reduce-scatter.21.cloned.1.call-done = bf16[768,512]{1,0:T(8,128)(2,1)} async-done(((bf16[768,1024]{1,0:T(8,128)(2,1)}), bf16[768,512]{1,0:T(8,128)(2,1)}) %reduce-scatter.21.cloned.1.call-update) | async-done | bytes 786448 | tf_op jit(solution)/shard_map/reduce_scatter | solution.py:270
  418.0 11.7 conditional.18
  445.4 36.0 %reduce-scatter.25.cloned.1.call-done = bf16[768,512]{1,0:T(8,128)(2,1)} async-done(((bf16[768,1024]{1,0:T(8,128)(2,1)}), bf16[768,512]{1,0:T(8,128)(2,1)}) %reduce-scatter.25.cloned.1.call-update) | async-done | bytes 786448 | tf_op jit(solution)/shard_map/reduce_scatter | solution.py:359
  498.1 14.6 conditional.19
  524.5 79.3 %reduce-scatter.27.cloned.1.call-done = bf16[768,512]{1,0:T(8,128)(2,1)} async-done(((bf16[768,1024]{1,0:T(8,128)(2,1)}), bf16[768,512]{1,0:T(8,128)(2,1)}) %reduce-scatter.27.cloned.1.call-update) | async-done | bytes 786448 | tf_op jit(solution)/shard_map/reduce_scatter | solution.py:397
  609.8 20.3 %collective-permute-done.2 = bf16[768,512]{1,0:T(8,128)(2,1)S(1)} collective-permute-done((bf16[768,512]{1,0:T(8,128)(2,1)S(1)}, bf16[768,512]{1,0:T(8,128)(2,1)S(1)}, u32[]{:S(2)}, u32[]{:S(2)}) %collective-permute-start.2) | collective-permute-done | bytes 786464 | tf_op jit(solution)/shard_map/ppermute | solution.py:15
  632.2 16.1 %conditional.17 = (f32[768,2048]{1,0:T(8,128)}, bf16[768,1024]{1,0:T(8,128)(2,1)}) conditional(s32[]{:T(128)} %convert_element_type.509, () %tuple.144, (bf16[768,1024]{1,0:T(8,128)(2,1)S(1)}, bf16[1024,2048]{1,0:T(8,128)(2,1)}, f32[2048]{0:T(1024)}, bf16[2048,1024]{1,0:T(8,128)(2,1)}) %tuple.399), branch_computations={%region_33.34_spmd, %region_34.35_spmd} | conditional | flops 6546259968 | bytes 40902700 | solution.py:46
  648.4 38.2 %conditional.20 = (f32[2048,1024]{1,0:T(8,128)S(1)}, f32[1024,2048]{1,0:T(8,128)S(1)}, f32[2048]{0:T(1024)S(1)}, f32[768,1024]{1,0:T(8,128)S(1)}) conditional(s32[]{:T(128)} %convert_element_type.535, () %tuple.150, (pred[768,2048]{1,0:T(32,128)(4,1)}, f32[768,2048]{1,0:T(8,128)}, f32[768,2048]{1,0:T(8,128)}, bf16[768,1024]{1,0:T(8,128)(2,1)}, ...), branch_computations={%region_51.52_spmd, %region_52.54_spmd} | conditional | flops 13008369664 | bytes 106438744 | solution.py:46
  648.4 22.6 %convert_reduce_fusion.2 = (f32[2048]{0:T(1024)S(1)}, bf16[768,2048]{1,0:T(8,128)(2,1)S(1)}, f32[768,2048]{1,0:T(8,128)S(1)}, f32[768,2048]{1,0:T(8,128)}) fusion(pred[768,2048]{1,0:T(32,128)(4,1)} %get-tuple-element.486, f32[768,2048]{1,0:T(8,128)} %get-tuple-element.487, f32[768,2048]{1,0:T(8,128)} %get-tuple-element.488, ...), kind=kOutput, calls=%fused_computation.222 | convolution fusion | flops 3339188224 | bytes 35659776 | tf_op jit(solution)/shard_map/cond/branch_1_fun/dot_general | solution.py:36
  697.9 13.6 reduce-scatter.29.cloned.1.call-done
  727.0 88.3 %conditional.21 = (f32[512,1024]{1,0:T(8,128)}, f32[768,1024]{1,0:T(8,128)}, f32[512,1]{0,1:T(1,128)S(1)}, f32[512,1]{0,1:T(1,128)}, f32[1024,1536]{0,1:T(8,128)}) conditional(s32[]{:T(128)} %convert_element_type.535, () %tuple.152, (pred[768,512]{1,0:T(32,128)(4,1)S(1)}, bf16[768,512]{0,1:T(8,128)(2,1)}, bf16[768,512]{0,1:T(8,128)(2,1)}, ...), branch_computations={%region_58.59_spmd, %region_59.62_spmd} | conditional | flops 9546102784 | bytes 229175520 | solution.py:46
  770.6 12.3 multiply_reduce_fusion.4
  782.9 13.1 multiply_convert_fusion.7
  844.8 13.3 collective-permute-done.3
  874.5 39.2 %conditional.22 = (f32[2048,1024]{1,0:T(8,128)S(1)}, f32[1024,2048]{1,0:T(8,128)S(1)}, f32[2048]{0:T(1024)S(1)}, f32[768,1024]{1,0:T(8,128)S(1)}) conditional(s32[]{:T(128)} %convert_element_type.549, () %tuple.154, (pred[768,2048]{1,0:T(32,128)(4,1)}, f32[768,2048]{1,0:T(8,128)}, f32[768,2048]{1,0:T(8,128)}, bf16[768,1024]{1,0:T(8,128)(2,1)}, ...), branch_computations={%region_66.67_spmd, %region_67.69_spmd} | conditional | flops 13008369664 | bytes 106438744 | solution.py:46
  874.8 22.8 %convert_reduce_fusion.4 = (f32[2048]{0:T(1024)S(1)}, bf16[768,2048]{1,0:T(8,128)(2,1)S(1)}, f32[768,2048]{1,0:T(8,128)S(1)}, f32[768,2048]{1,0:T(8,128)}) fusion(pred[768,2048]{1,0:T(32,128)(4,1)} %get-tuple-element.510, f32[768,2048]{1,0:T(8,128)} %get-tuple-element.511, f32[768,2048]{1,0:T(8,128)} %get-tuple-element.512, ...), kind=kOutput, calls=%fused_computation.265 | convolution fusion | flops 3339188224 | bytes 35659776 | tf_op jit(solution)/shard_map/cond/branch_1_fun/dot_general | solution.py:36
  949.4 87.9 %conditional.23 = (f32[512,1024]{1,0:T(8,128)}, f32[768,1024]{1,0:T(8,128)}, f32[512,1]{0,1:T(1,128)S(1)}, f32[512,1]{0,1:T(1,128)S(1)}, f32[1024,1536]{0,1:T(8,128)}) conditional(s32[]{:T(128)} %convert_element_type.549, () %tuple.156, (pred[768,512]{1,0:T(32,128)(4,1)S(1)}, bf16[768,512]{0,1:T(8,128)(2,1)}, bf16[768,512]{0,1:T(8,128)(2,1)}, ...), branch_computations={%region_73.74_spmd, %region_74.77_spmd} | conditional | flops 9546102784 | bytes 229167296 | solution.py:46
  992.9 12.3 multiply_reduce_fusion.5
  1005.2 13.1 multiply_convert_fusion.12
  1043.6 12.3 fusion.211
  1092.9 39.9 %all-reduce.6 = (bf16[512,10]{0,1:T(8,128)(2,1)S(1)}, bf16[1,2048]{1,0:T(2,128)(2,1)S(1)}) all-reduce(bf16[512,10]{0,1:T(8,128)(2,1)S(1)} %add_convert_fusion.16, bf16[1,2048]{1,0:T(2,128)(2,1)S(1)} %broadcast_in_dim.148), channel_id=1, replica_groups=mesh['section'=2,'tensor'=2,'dp'=8] {'dp'}, use_global_device_ids=true, to_apply=%region_105.106 | all-reduce | flops 7168 | bytes 28672 | tf_op jit(solution)/shard_map/psum | solution.py:454
  1138.2 341.9 %all-reduce.10.cloned.1.call-done = (bf16[1,1024,3,512]{1,3,2,0:T(8,128)(2,1)}, bf16[1,512,1024]{2,1,0:T(8,128)(2,1)}, bf16[1,1024,2048]{2,1,0:T(8,128)(2,1)}, bf16[1,2048,1024]{2,1,0:T(8,128)(2,1)}) async-done(((bf16[1,1024,3,512]{1,3,2,0:T(8,128)(2,1)}, bf16[1,512,1024]{2,1,0:T(8,128)(2,1)}, bf16[1,1024,2048]{2,1,0:T(8,128)(2,1)}, bf16[1,2048,1024]{2,1,0:T(8,128)(2,1)}), ...) | async-done | bytes 12582928 | tf_op jit(solution)/shard_map/psum | solution.py:454
  (652 shorter events, 677.2 us)
Async XLA Ops:
  7.2 15.5 %all-gather.36.cloned.1.call-start = ((), (), s32[]{:S(2)}) async-start(), calls=%async_computation.35 | async-start | bytes 2359296 | tf_op jit(solution)/shard_map/all_gather | solution.py:257
  9.3 75.6 %reduce-scatter.13.cloned.1.call-start = ((), (), s32[]{:S(2)}) async-start(), calls=%async_computation.12 | async-start | bytes 2359296 | tf_op jit(solution)/shard_map/reduce_scatter | solution.py:270
  11.5 332.9 %copy-start.75 = (f32[1,1024]{1,0:T(1,128)}, f32[1,1024]{1,0:T(1,128)S(1)}, u32[]{:S(2)}) copy-start(f32[1,1024]{1,0:T(1,128)S(1)} %convert_element_type.483) | copy-start | bytes 12292
  75.5 23.4 %all-gather.14.cloned.1.call-start = ((), (), s32[]{:S(2)}) async-start(), calls=%async_computation.13 | async-start | bytes 2359296 | tf_op jit(solution)/shard_map/all_gather | solution.py:279
  75.6 327.5 %copy-start.86 = (f32[1,512]{1,0:T(1,128)}, f32[1,512]{1,0:T(1,128)S(1)}, u32[]{:S(2)}) copy-start(f32[1,512]{1,0:T(1,128)S(1)} %add.553) | copy-start | bytes 6148
  75.7 405.7 %copy-start.79 = (f32[1,512]{1,0:T(1,128)}, f32[1,512]{1,0:T(1,128)S(1)}, u32[]{:S(2)}) copy-start(f32[1,512]{1,0:T(1,128)S(1)} %mul.905) | copy-start | bytes 6148
  87.8 54.2 %reduce-scatter.15.cloned.1.call-start = ((), (), s32[]{:S(2)}) async-start(), calls=%async_computation.14 | async-start | bytes 2359296 | tf_op jit(solution)/shard_map/reduce_scatter | solution.py:294
  132.6 45.7 %all-gather.16.cloned.1.call-start = ((), (), s32[]{:S(2)}) async-start(), calls=%async_computation.15 | async-start | bytes 2359296 | tf_op jit(solution)/shard_map/all_gather | solution.py:257
  144.5 20.9 %collective-permute-start = (bf16[768,512]{1,0:T(8,128)(2,1)S(1)}, bf16[768,512]{1,0:T(8,128)(2,1)S(1)}, u32[]{:S(2)}, u32[]{:S(2)}) collective-permute-start(bf16[768,512]{1,0:T(8,128)(2,1)S(1)} %get-tuple-element.942), channel_id=1, source_target_pairs={{0,16},{1,17},{2,18},{3,19},{4,20},{5,21},{6,22},{7,23},{8,24},{9,... | collective-permute-start | bytes 2359304 | tf_op jit(solution)/shard_map/ppermute | solution.py:15
  166.4 79.2 %reduce-scatter.17.cloned.1.call-start = ((), (), s32[]{:S(2)}) async-start(), calls=%async_computation.16 | async-start | bytes 2359296 | tf_op jit(solution)/shard_map/reduce_scatter | solution.py:270
  235.4 24.2 %all-gather.18.cloned.1.call-start = ((), (), s32[]{:S(2)}) async-start(), calls=%async_computation.17 | async-start | bytes 2359296 | tf_op jit(solution)/shard_map/all_gather | solution.py:279
  248.4 54.8 %reduce-scatter.19.cloned.1.call-start = ((), (), s32[]{:S(2)}) async-start(), calls=%async_computation.18 | async-start | bytes 2359296 | tf_op jit(solution)/shard_map/reduce_scatter | solution.py:294
  292.8 46.6 %all-gather.20.cloned.1.call-start = ((), (), s32[]{:S(2)}) async-start(), calls=%async_computation.19 | async-start | bytes 2359296 | tf_op jit(solution)/shard_map/all_gather | solution.py:257
  305.6 20.9 %collective-permute-start.1 = (bf16[768,512]{1,0:T(8,128)(2,1)S(1)}, bf16[768,512]{1,0:T(8,128)(2,1)S(1)}, u32[]{:S(2)}, u32[]{:S(2)}) collective-permute-start(bf16[768,512]{1,0:T(8,128)(2,1)S(1)} %get-tuple-element.940), channel_id=1, source_target_pairs={{0,16},{1,17},{2,18},{3,19},{4,20},{5,21},{6,22},{7,23},{8,24},{9,... | collective-permute-start | bytes 2359304 | tf_op jit(solution)/shard_map/ppermute | solution.py:15
  327.5 75.6 %reduce-scatter.21.cloned.1.call-start = ((), (), s32[]{:S(2)}) async-start(), calls=%async_computation.20 | async-start | bytes 2359296 | tf_op jit(solution)/shard_map/reduce_scatter | solution.py:270
  351.7 64.7 %all-gather.24.cloned.1.call-start = ((), (), s32[]{:S(2)}) async-start(), calls=%async_computation.23 | async-start | bytes 2359296 | tf_op jit(solution)/shard_map/all_gather | solution.py:346
  353.5 76.3 %all-gather.22.cloned.1.call-start = ((), (), s32[]{:S(2)}) async-start(), calls=%async_computation.21 | async-start | bytes 2359296 | tf_op jit(solution)/shard_map/all_gather | solution.py:279
  406.0 75.4 %reduce-scatter.25.cloned.1.call-start = ((), (), s32[]{:S(2)}) async-start(), calls=%async_computation.24 | async-start | bytes 2359296 | tf_op jit(solution)/shard_map/reduce_scatter | solution.py:359
  441.4 55.2 %all-gather.26.cloned.1.call-start = ((), (), s32[]{:S(2)}) async-start(), calls=%async_computation.25 | async-start | bytes 2359296 | tf_op jit(solution)/shard_map/all_gather | solution.py:377
  485.4 118.4 %reduce-scatter.27.cloned.1.call-start = ((), (), s32[]{:S(2)}) async-start(), calls=%async_computation.26 | async-start | bytes 2359296 | tf_op jit(solution)/shard_map/reduce_scatter | solution.py:397
  519.4 129.0 %all-gather.28.cloned.1.call-start = ((), (), s32[]{:S(2)}) async-start(), calls=%async_computation.27 | async-start | bytes 2359296 | tf_op jit(solution)/shard_map/all_gather | solution.py:346
  608.5 21.6 %collective-permute-start.2 = (bf16[768,512]{1,0:T(8,128)(2,1)S(1)}, bf16[768,512]{1,0:T(8,128)(2,1)S(1)}, u32[]{:S(2)}, u32[]{:S(2)}) collective-permute-start(bf16[768,512]{1,0:T(8,128)(2,1)S(1)} %get-tuple-element.936), channel_id=1, source_target_pairs={{16,0},{17,1},{18,2},{19,3},{20,4},{21,5},{22,6},{23,7},{24,8},{25... | collective-permute-start | bytes 2359304 | tf_op jit(solution)/shard_map/ppermute | solution.py:15
  632.1 79.4 %reduce-scatter.29.cloned.1.call-start = ((), (), s32[]{:S(2)}) async-start(), calls=%async_computation.28 | async-start | bytes 2359296 | tf_op jit(solution)/shard_map/reduce_scatter | solution.py:359
  693.9 33.0 %all-gather.30.cloned.1.call-start = ((), (), s32[]{:S(2)}) async-start(), calls=%async_computation.29 | async-start | bytes 2359296 | tf_op jit(solution)/shard_map/all_gather | solution.py:377
  715.8 116.8 %reduce-scatter.31.cloned.1.call-start = ((), (), s32[]{:S(2)}) async-start(), calls=%async_computation.30 | async-start | bytes 2359296 | tf_op jit(solution)/shard_map/reduce_scatter | solution.py:397
  821.9 22.9 %reduce-scatter.23.cloned.1.call-start = ((), (), s32[]{:S(2)}) async-start(), calls=%async_computation.22 | async-start | bytes 2359296 | tf_op jit(solution)/shard_map/reduce_scatter | solution.py:294
  822.5 52.0 %all-gather.32.cloned.1.call-start = ((), (), s32[]{:S(2)}) async-start(), calls=%async_computation.31 | async-start | bytes 2359296 | tf_op jit(solution)/shard_map/all_gather | solution.py:346
  836.1 21.9 %collective-permute-start.3 = (bf16[768,512]{1,0:T(8,128)(2,1)}, bf16[768,512]{1,0:T(8,128)(2,1)S(1)}, u32[]{:S(2)}, u32[]{:S(2)}) collective-permute-start(bf16[768,512]{1,0:T(8,128)(2,1)} %get-tuple-element.932), channel_id=1, source_target_pairs={{16,0},{17,1},{18,2},{19,3},{20,4},{21,5},{22,6},{23,7},{24,8},{25... | collective-permute-start | bytes 2359304 | tf_op jit(solution)/shard_map/ppermute | solution.py:15
  864.2 66.2 %reduce-scatter.33.cloned.1.call-start = ((), (), s32[]{:S(2)}) async-start(), calls=%async_computation.32 | async-start | bytes 2359296 | tf_op jit(solution)/shard_map/reduce_scatter | solution.py:359
  920.9 28.5 %all-gather.34.cloned.1.call-start = ((), (), s32[]{:S(2)}) async-start(), calls=%async_computation.33 | async-start | bytes 2359296 | tf_op jit(solution)/shard_map/all_gather | solution.py:377
  938.2 152.5 %reduce-scatter.35.cloned.1.call-start = ((), (), s32[]{:S(2)}) async-start(), calls=%async_computation.34 | async-start | bytes 2359296 | tf_op jit(solution)/shard_map/reduce_scatter | solution.py:397
  1043.5 436.7 %all-reduce.10.cloned.1.call-start = ((), (), s32[]{:S(2)}) async-start(), calls=%async_computation.36 | async-start | bytes 25165824 | tf_op jit(solution)/shard_map/psum | solution.py:454
  (169 other events, 4085.3 us)
Sparse Core Ops, SparseCore 0:
  10.1 12.4 all-gather.35
  75.6 9.2 reduce-scatter.12
  87.9 10.9 all-gather.13
  132.7 9.3 reduce-scatter.14
  166.5 11.7 all-gather.15
  235.5 10.0 reduce-scatter.16
  248.6 11.0 all-gather.17
  292.9 10.2 reduce-scatter.18
  327.6 11.7 all-gather.19
  351.8 51.2 reduce-scatter.20
  405.3 11.0 all-gather.23
  418.4 10.9 all-gather.21
  441.5 39.7 reduce-scatter.24
  485.5 10.9 all-gather.25
  519.5 84.2 reduce-scatter.26
  632.3 10.1 all-gather.27
  694.1 17.4 reduce-scatter.28
  715.9 10.9 all-gather.29
  822.0 10.2 reduce-scatter.30
  834.5 10.2 reduce-scatter.22
  864.3 10.1 all-gather.31
  921.0 9.2 reduce-scatter.32
  938.3 11.0 all-gather.33
  1043.6 9.3 reduce-scatter.34
  1079.2 400.8 all-reduce.9
where the time goes:
time: 1510 us; the launch traced here: 1500 us
  waiting for transfers between devices  734 us (49%)
  matrix products  295 us (20%)
  other arithmetic  245 us (16%)
  local copies, waits for them, and re-layouts  118 us (8%)
  blocking collectives  63.3 us (4%)
  loops' own time  19.8 us (1%)
  between operations  17 us (1%)
    psum x1, waiting for transfers between devices, shards(): lax.psum(shortened(summed), 'dp')  342 us
    reduce_scatter x3, waiting for transfers between devices, shards(): lax.psum_scatter(partial_one.astype(jnp.bfloat16), 'tensor', scatter_dime...  79.4 us
    dot_general x8, matrix products, contract_cols(): lax.dot_general(left, right, (((1,), (1,)), ((), ())), preferred_element_...  68.2 us
    ppermute x4, waiting for transfers between devices, from_behind(): return lax.ppermute(block, axis, route)  67.9 us
    reduce_scatter x3, waiting for transfers between devices, shards(): lax.psum_scatter(forward_partial_value.astype(jnp.bfloat16), 'tensor', sc...  62.7 us
    reduce_scatter x3, waiting for transfers between devices, shards(): lax.psum_scatter(partial_two.astype(jnp.bfloat16), 'tensor', scatter_dime...  55.1 us
    another operation x23, local copies, waits for them, and re-layouts  54.9 us
    psum x1, blocking collectives, shards(): lax.psum(shortened(summed), 'dp')  39.9 us
  transfers between devices with their start and end apart: 29, of which 25 were waited for; matrix products, arithmetic and copies ran while one was open for 6% of the time, Pallas kernels for 0%

commit v1 on v0

v1 whole, which is shorter than its diff:
```python
import math

import jax
import jax.numpy as jnp
from jax import lax
from jax.experimental import pallas as pl
from jax.experimental.pallas import tpu as pltpu
from jax.sharding import PartitionSpec as P

HEAD_DIM = 64
EPSILON = 1e-06
F32 = jnp.float32
BF16 = jnp.bfloat16
MIB = 1 << 20
VMEM_MIB = 60
SLOTS = 3
LN1G, LN1B, OUTB, SATT, LN2G, LN2B, FC2B, SMLP = range(8)


def dot(left, right):
    return jnp.dot(left, right, preferred_element_type=F32)


def dot_nt(left, right):
    return lax.dot_general(left, right, (((1,), (1,)), ((), ())), preferred_element_type=F32)


def dot_tn(left, right):
    return lax.dot_general(left, right, (((0,), (0,)), ((), ())), preferred_element_type=F32)


def norm_stats(values):
    centre = jnp.mean(values, axis=-1, keepdims=True)
    centred = values - centre
    spread = jnp.mean(centred * centred, axis=-1, keepdims=True)
    scale = lax.rsqrt(spread + EPSILON)
    return centred * scale, scale


def norm_backward(hat, scale, gain, error):
    weighted = error * gain
    mean_one = jnp.mean(weighted, axis=-1, keepdims=True)
    mean_two = jnp.mean(weighted * hat, axis=-1, keepdims=True)
    return scale * (weighted - mean_one - hat * mean_two)


def col_sum(values):
    return jnp.sum(values, axis=0, keepdims=True)


def call(kernel, scalars, grid, ins, outs, scratch=(), flops=0, moved=0):
    arrays = [a for a, _, _ in ins]
    in_specs = [pl.BlockSpec(b, m) for _, b, m in ins]
    aliases = {}
    for number, out in enumerate(outs):
        if out[4] is not None:
            aliases[1 + len(arrays)] = number
            arrays.append(out[4])
            in_specs.append(pl.BlockSpec(memory_space=pl.ANY))
    extra = len(aliases)
    in_count = len(ins)

    def body(*refs):
        kernel(*refs[: 1 + in_count], *refs[1 + in_count + extra :])

    return pl.pallas_call(
        body,
        out_shape=[jax.ShapeDtypeStruct(s, d) for s, d, _, _, _ in outs],
        grid_spec=pltpu.PrefetchScalarGridSpec(
            num_scalar_prefetch=1,
            grid=grid,
            in_specs=in_specs,
            out_specs=[pl.BlockSpec(b, m) for _, _, b, m, _ in outs],
            scratch_shapes=list(scratch),
        ),
        input_output_aliases=aliases,
        compiler_params=pltpu.CompilerParams(
            dimension_semantics=("arbitrary",) * len(grid), vmem_limit_bytes=VMEM_MIB * MIB
        ),
        cost_estimate=pl.CostEstimate(
            flops=int(flops), bytes_accessed=int(moved), transcendentals=0
        ),
    )(scalars, *arrays)


def manual(kernel, scalars, ins, outs, scratch, flops=0, moved=0):
    any_space = pl.BlockSpec(memory_space=pl.ANY)
    vmem_space = pl.BlockSpec(memory_space=pltpu.VMEM)
    arrays = [a for a, _ in ins]
    in_specs = [vmem_space if inside else any_space for _, inside in ins]
    aliases = {}
    for number, out in enumerate(outs):
        if out[3] is not None:
            aliases[1 + len(arrays)] = number
            arrays.append(out[3])
            in_specs.append(any_space)
    extra = len(aliases)
    in_count = len(ins)

    def body(*refs):
        kernel(*refs[: 1 + in_count], *refs[1 + in_count + extra :])

    return pl.pallas_call(
        body,
        out_shape=[jax.ShapeDtypeStruct(s, d) for s, d, _, _ in outs],
        in_specs=[pl.BlockSpec(memory_space=pltpu.SMEM)] + in_specs,
        out_specs=[vmem_space if inside else any_space for _, _, inside, _ in outs],
        scratch_shapes=list(scratch),
        input_output_aliases=aliases,
        compiler_params=pltpu.CompilerParams(vmem_limit_bytes=VMEM_MIB * MIB),
        cost_estimate=pl.CostEstimate(
            flops=int(flops), bytes_accessed=int(moved), transcendentals=0
        ),
    )(scalars, *arrays)


def begin(src, dst, sem):
    copy = pltpu.make_async_copy(src, dst, sem)
    copy.start()
    return copy


def dma_sems(count):
    return pltpu.SemaphoreType.DMA((count,))


def whole2(i, s):
    return (0, 0)


def slot3(i, s):
    return (s[0], 0, 0)


def fill_tokens(s, sources, target, sems):
    whole, number, other, relay, section = sources
    rows, width = target.shape
    half = width // 2
    rank = s[3]

    @pl.when(s[1] == section)
    def _():
        first = pl.multiple_of(rank * half, half)
        second = pl.multiple_of((1 - rank) * half, half)
        begin(
            whole.at[number, 0, pl.ds(pl.multiple_of(rank * rows, rows), rows)],
            target.at[:, pl.ds(first, half)],
            sems.at[0],
        )
        begin(other, target.at[:, pl.ds(second, half)], sems.at[1])

    @pl.when(s[1] != section)
    def _():
        begin(relay.at[:, pl.ds(0, half)], target.at[:, pl.ds(0, half)], sems.at[0])
        begin(relay.at[:, pl.ds(half, half)], target.at[:, pl.ds(half, half)], sems.at[1])


def await_tokens(relay, target, sems):
    half = target.shape[1] // 2
    for number in range(2):
        columns = pl.ds(number * half, half)
        pltpu.make_async_copy(
            relay.at[:, columns], target.at[:, columns], sems.at[number]
        ).wait()


def norm_kv(scalars, inputs, number, other, relay, vec, w_own, w_oth, bias_v, kept):
    rows, width = relay.shape
    half = width // 2

    def kernel(s, whole, oth_ref, relay_ref, v, own, oth, bv, x_out, n_out, kv_out,
               x_v, n_v, w_v, kv_v, tok_sems, w_sems, out_sems):
        @pl.when(s[2] == 1)
        def _():
            fill_tokens(s, (whole, number, oth_ref, relay_ref, 0), x_v, tok_sems)
            loads = []
            for part in range(4):
                ref = own if part < 2 else oth
                loads.append(begin(ref.at[1 + part % 2], w_v.at[part], w_sems.at[part]))
            await_tokens(relay_ref, x_v, tok_sems)
            outs = [begin(x_v, x_out.at[s[0]], out_sems.at[0])]
            hat, _ = norm_stats(x_v[...].astype(F32))
            n_v[...] = (hat * v[LN1G : LN1G + 1] + v[LN1B : LN1B + 1]).astype(BF16)
            outs.append(begin(n_v, n_out.at[s[0]], out_sems.at[1]))
            for part in range(4):
                loads[part].wait()
                result = dot(n_v[...], w_v[part])
                kind, side = part % 2, part // 2
                columns = slice(side * half, (side + 1) * half)
                if kind == 1:
                    result = result + bv[:, columns]
                kv_v[part] = result.astype(BF16)
                outs.append(
                    begin(
                        kv_v.at[part],
                        kv_out.at[kind, :, pl.ds(side * half, half)],
                        out_sems.at[2 + part],
                    )
                )
            for copy in outs:
                copy.wait()

    stack = (SLOTS, rows, width)
    return manual(
        kernel,
        scalars,
        [
            (inputs, False),
            (other, False),
            (relay, False),
            (vec, True),
            (w_own, False),
            (w_oth, False),
            (bias_v, True),
        ],
        [
            (stack, BF16, False, kept.get("x")),
            (stack, BF16, False, kept.get("normed1")),
            ((2, rows, width), BF16, False, None),
        ],
        [
            pltpu.VMEM((rows, width), BF16),
            pltpu.VMEM((rows, width), BF16),
            pltpu.VMEM((4, width, half), BF16),
            pltpu.VMEM((4, rows, half), BF16),
            dma_sems(2),
            dma_sems(4),
            dma_sems(6),
        ],
        flops=2 * rows * width * 2 * width,
        moved=4 * width * width + 10 * rows * width,
    )


def project_q(scalars, normed, w_own, w_oth, bias_q, kept):
    _, rows, width = normed.shape
    half = width // 2

    def kernel(s, n, own, oth, bq, q_out, n_v, w_v, q_v, in_sems, out_sems):
        @pl.when(s[2] == 1)
        def _():
            load = begin(n.at[s[0]], n_v, in_sems.at[0])
            loads = [
                begin(own.at[0], w_v.at[0], in_sems.at[1]),
                begin(oth.at[0], w_v.at[1], in_sems.at[2]),
            ]
            load.wait()
            outs = []
            for side in range(2):
                loads[side].wait()
                columns = slice(side * half, (side + 1) * half)
                q_v[side] = (dot(n_v[...], w_v[side]) + bq[:, columns]).astype(BF16)
                outs.append(
                    begin(
                        q_v.at[side],
                        q_out.at[s[0], :, pl.ds(side * half, half)],
                        out_sems.at[side],
                    )
                )
            for copy in outs:
                copy.wait()

    return manual(
        kernel,
        scalars,
        [(normed, False), (w_own, False), (w_oth, False), (bias_q, True)],
        [((SLOTS, rows, width), BF16, False, kept.get("q"))],
        [
            pltpu.VMEM((rows, width), BF16),
            pltpu.VMEM((2, width, half), BF16),
            pltpu.VMEM((2, rows, half), BF16),
            dma_sems(3),
            dma_sems(2),
        ],
        flops=2 * rows * width * width,
        moved=2 * width * width + 4 * rows * width,
    )[0]


def attend(scalars, q, kv_here, kv_there, kept):
    _, rows, width = q.shape
    pairs = width // (2 * HEAD_DIM)
    factor = HEAD_DIM**-0.5 * math.log2(math.e)
    lanes = 2 * HEAD_DIM

    def kernel(s, *refs):
        @pl.when(s[2] == 1)
        def _():
            compute(*refs)

    def compute(q_ref, here, there, e_out, o_out, mixed_out, inv_out, kv_out):
        qs = q_ref[0]
        kv_out[0, :, :rows] = here[...]
        kv_out[0, :, rows:] = there[...]
        keys = jnp.concatenate([here[0], there[0]], axis=0)
        values = jnp.concatenate([here[1], there[1]], axis=0)
        first_q = lax.broadcasted_iota(jnp.int32, (rows, lanes), 1) < HEAD_DIM
        first_k = lax.broadcasted_iota(jnp.int32, (2 * rows, lanes), 1) < HEAD_DIM
        results = []
        for head in range(2):
            mine_q = first_q if head == 0 else ~first_q
            mine_k = first_k if head == 0 else ~first_k
            scores = dot_nt(jnp.where(mine_q, qs, 0), keys) * factor
            top = jnp.max(scores, axis=-1, keepdims=True)
            grown = jnp.exp2(scores - top).astype(BF16)
            e_out[0, head] = grown
            results.append(dot(grown, jnp.where(mine_k, values, 1)))
        total = jnp.where(
            first_q,
            pltpu.roll(results[0], HEAD_DIM, 1),
            pltpu.roll(results[1], HEAD_DIM, 1),
        )
        inverse = 1.0 / total
        mixed = jnp.where(first_q, results[0], results[1]) * inverse
        o_out[0] = mixed
        mixed_out[0] = mixed.astype(BF16)
        inv_out[0] = inverse

    heads = 2 * pairs
    column = lambda i, s: (s[0], 0, i)
    return call(
        kernel,
        scalars,
        (pairs,),
        [
            (q, (1, rows, lanes), column),
            (kv_here, (2, rows, lanes), lambda i, s: (0, 0, i)),
            (kv_there, (2, rows, lanes), lambda i, s: (0, 0, (i + pairs // 2) % pairs)),
        ],
        [
            (
                (SLOTS, heads, rows, 2 * rows),
                BF16,
                (1, 2, rows, 2 * rows),
                lambda i, s: (s[0], i, 0, 0),
                kept.get("grown"),
            ),
            ((SLOTS, rows, width), F32, (1, rows, lanes), column, kept.get("mixed_full")),
            ((SLOTS, rows, width), BF16, (1, rows, lanes), column, kept.get("mixed")),
            ((SLOTS, rows, width), F32, (1, rows, lanes), column, kept.get("inverse")),
            (
                (SLOTS, 2, 2 * rows, width),
                BF16,
                (1, 2, 2 * rows, lanes),
                lambda i, s: (s[0], 0, 0, i),
                kept.get("kv"),
            ),
        ],
        flops=8 * rows * rows * width,
        moved=4 * heads * rows * rows + 30 * rows * width,
    )


def gelu_parts(x):
    size = jnp.abs(x)
    base = 1.0 + (0.3275911 * math.sqrt(0.5)) * size
    t = pl.reciprocal(base, approx=True)
    t = t * (2.0 - base * t)
    grown = jnp.exp2(x * x * (-0.5 * math.log2(math.e)))
    poly = 0.5 * 1.061405429
    for factor in (-1.453152027, 1.421413741, -0.284496736, 0.254829592):
        poly = poly * t + 0.5 * factor
    tail = poly * t * grown
    below = jnp.where(x < 0.0, tail, 1.0 - tail)
    return x * below, below + x * grown * (1.0 / math.sqrt(2.0 * math.pi))


CHUNK = 512


def mlp_forward(scalars, mixed, x, vec, wo_own, wo_oth, wu_own, wu_oth, wd_own, wd_oth, b_up, kept):
    _, rows, width = x.shape
    side_hidden = wu_own.shape[1]
    hidden = 2 * side_hidden
    half = width // 2
    steps = hidden // CHUNK
    split = steps // 2

    def kernel(
        s, m, x_ref, v, woo, wot, wuo, wut, wdo, wdt, bu,
        att_out, res_out, n_out, act_out, slope_out, branch_out, y_out, relay_out,
        m_v, x_v, wo_v, wu_v, wd_v, att_v, res_v, n_v, h_v, act_v, slope_v, branch_v, y_v, acc,
        in_sems, wu_sems, wd_sems, out_sems, act_sems, slope_sems,
    ):
        @pl.when(s[2] == 1)
        def _():
            slot = s[0]
            first = [
                begin(m.at[slot], m_v, in_sems.at[0]),
                begin(woo, wo_v.at[0], in_sems.at[1]),
                begin(wot, wo_v.at[1], in_sems.at[2]),
                begin(x_ref.at[slot], x_v, in_sems.at[3]),
            ]
            ups, downs = [], []
            for i in range(steps):
                part = pl.ds((i % split) * CHUNK, CHUNK)
                up, down = (wuo, wdo) if i < split else (wut, wdt)
                ups.append(begin(up.at[:, part], wu_v.at[i], wu_sems.at[i]))
                downs.append(begin(down.at[part], wd_v.at[i], wd_sems.at[i]))
            for copy in first:
                copy.wait()
            attended = dot(m_v[:, :half], wo_v[0]) + dot(m_v[:, half:], wo_v[1])
            attended = attended + v[OUTB : OUTB + 1]
            att_v[...] = attended.astype(BF16)
            residual = x_v[...].astype(F32) + v[SATT : SATT + 1] * attended
            res_v[...] = residual
            hat, _ = norm_stats(residual)
            n_v[...] = (hat * v[LN2G : LN2G + 1] + v[LN2B : LN2B + 1]).astype(BF16)
            outs = [
                begin(att_v, att_out.at[slot], out_sems.at[0]),
                begin(res_v, res_out.at[slot], out_sems.at[1]),
                begin(n_v, n_out.at[slot], out_sems.at[2]),
            ]

            def up_product(i):
                ups[i].wait()
                h_v[i % 2] = dot(n_v[...], wu_v[i]) + bu[i : i + 1]

            up_product(0)
            for i in range(steps):
                downs[i].wait()
                if i + 1 < steps:
                    up_product(i + 1)
                active, slope = gelu_parts(h_v[i % 2])
                act_v[i] = active.astype(BF16)
                slope_v[i] = slope.astype(BF16)
                part = pl.ds(i * CHUNK, CHUNK)
                outs.append(begin(act_v.at[i], act_out.at[slot, :, part], act_sems.at[i]))
                outs.append(begin(slope_v.at[i], slope_out.at[slot, :, part], slope_sems.at[i]))
                product = dot(act_v[i], wd_v[i])
                acc[...] = product if i == 0 else acc[...] + product
            branch = acc[...] + v[FC2B : FC2B + 1]
            y_v[...] = (res_v[...] + v[SMLP : SMLP + 1] * branch).astype(BF16)
            branch_v[...] = branch.astype(BF16)
            outs.append(begin(y_v, relay_out, out_sems.at[3]))
            outs.append(begin(y_v, y_out.at[slot], out_sems.at[4]))
            outs.append(begin(branch_v, branch_out.at[slot], out_sems.at[5]))
            for copy in outs:
                copy.wait()

    stack = (SLOTS, rows, width)
    tall = (SLOTS, rows, hidden)
    plain = pltpu.VMEM((rows, width), BF16)
    full = pltpu.VMEM((rows, width), F32)
    chunks = pltpu.VMEM((steps, rows, CHUNK), BF16)
    return manual(
        kernel,
        scalars,
        [
            (mixed, False),
            (x, False),
            (vec, True),
            (wo_own, False),
            (wo_oth, False),
            (wu_own, False),
            (wu_oth, False),
            (wd_own, False),
            (wd_oth, False),
            (b_up, True),
        ],
        [
            (stack, BF16, False, kept.get("attended")),
            (stack, F32, False, kept.get("residual")),
            (stack, BF16, False, kept.get("normed2")),
            (tall, BF16, False, kept.get("active")),
            (tall, BF16, False, kept.get("slope")),
            (stack, BF16, False, kept.get("branch")),
            (stack, BF16, False, kept.get("output")),
            ((rows, width), BF16, False, None),
        ],
        [
            plain,
            plain,
            pltpu.VMEM((2, half, width), BF16),
            pltpu.VMEM((steps, width, CHUNK), BF16),
            pltpu.VMEM((steps, CHUNK, width), BF16),
            plain,
            full,
            plain,
            pltpu.VMEM((2, rows, CHUNK), F32),
            chunks,
            chunks,
            plain,
            plain,
            full,
            dma_sems(4),
            dma_sems(steps),
            dma_sems(steps),
            dma_sems(6),
            dma_sems(steps),
            dma_sems(steps),
        ],
        flops=4 * rows * width * hidden + 2 * rows * width * width,
        moved=4 * width * hidden + 2 * width * width + 8 * rows * hidden,
    )


def mlp_backward(scalars, cotangent, number, other, relay, vec, wo_own, wo_oth, wu_own, wu_oth, wd_own, wd_oth, kept, grads):
    _, rows, width = kept["x"].shape
    side_hidden = wu_own.shape[1]
    hidden = 2 * side_hidden
    half = width // 2
    steps = hidden // CHUNK
    split = steps // 2

    def kernel(
        s, whole, oth_ref, relay_ref, branch, slope, res, att, v, woo, wot, wuo, wut, wdo, wdt,
        gb_out, before_out, ga_out, gm_out, gr_out, small_out, shift_out,
        g_v, branch_v, slope_v, res_v, att_v, wo_v, wu_v, wd_v, gb_v, d_v, before_v, ga_v, gm_v,
        gr_v, acc, tok_sems, in_sems, slope_sems, wu_sems, wd_sems, out_sems, before_sems,
    ):
        @pl.when(s[2] == 0)
        def _():
            small_out[...] = jnp.zeros_like(small_out)
            shift_out[...] = jnp.zeros_like(shift_out)

        @pl.when(s[2] == 1)
        def _():
            slot = s[0]
            fill_tokens(s, (whole, number, oth_ref, relay_ref, 1), g_v, tok_sems)
            branch_in = begin(branch.at[slot], branch_v, in_sems.at[0])
            ups, downs, slopes = [], [], []
            for i in range(steps):
                part = pl.ds((i % split) * CHUNK, CHUNK)
                up, down = (wuo, wdo) if i < split else (wut, wdt)
                downs.append(begin(down.at[part], wd_v.at[i], wd_sems.at[i]))
                slopes.append(
                    begin(
                        slope.at[slot, :, pl.ds(i * CHUNK, CHUNK)], slope_v.at[i], slope_sems.at[i]
                    )
                )
                ups.append(begin(up.at[:, part], wu_v.at[i], wu_sems.at[i]))
            last = [
                begin(res.at[slot], res_v, in_sems.at[1]),
                begin(att.at[slot], att_v, in_sems.at[2]),
                begin(woo, wo_v.at[0], in_sems.at[3]),
                begin(wot, wo_v.at[1], in_sems.at[4]),
            ]
            await_tokens(relay_ref, g_v, tok_sems)
            g = g_v[...].astype(F32)
            gb = (v[SMLP : SMLP + 1] * g).astype(BF16)
            gb_v[...] = gb
            outs = [begin(gb_v, gb_out.at[slot], out_sems.at[0])]

            def down_product(i):
                downs[i].wait()
                d_v[i % 2] = dot_nt(gb_v[...], wd_v[i])

            down_product(0)
            branch_in.wait()
            small_out[...] = jnp.zeros_like(small_out)
            small_out[0:1] = col_sum(g * branch_v[...].astype(F32))
            small_out[1:2] = col_sum(gb.astype(F32))
            for i in range(steps):
                slopes[i].wait()
                ups[i].wait()
                if i + 1 < steps:
                    down_product(i + 1)
                grad_before = (d_v[i % 2] * slope_v[i].astype(F32)).astype(BF16)
                before_v[i] = grad_before
                part = pl.ds(i * CHUNK, CHUNK)
                outs.append(begin(before_v.at[i], before_out.at[slot, :, part], before_sems.at[i]))
                shift_out[i : i + 1] = col_sum(grad_before.astype(F32))
                product = dot_nt(before_v[i], wu_v[i])
                acc[...] = product if i == 0 else acc[...] + product
            for copy in last:
                copy.wait()
            hat, scale = norm_stats(res_v[...])
            error = acc[...]
            grad = g_v[...].astype(F32) + norm_backward(hat, scale, v[LN2G : LN2G + 1], error)
            ga = (v[SATT : SATT + 1] * grad).astype(BF16)
            ga_v[...] = ga
            outs.append(begin(ga_v, ga_out.at[slot], out_sems.at[1]))
            gm_v[:, :half] = dot_nt(ga, wo_v[0]).astype(BF16)
            gm_v[:, half:] = dot_nt(ga, wo_v[1]).astype(BF16)
            outs.append(begin(gm_v, gm_out, out_sems.at[2]))
            gr_v[...] = grad
            outs.append(begin(gr_v, gr_out, out_sems.at[3]))
            small_out[2:3] = col_sum(error * hat)
            small_out[3:4] = col_sum(error)
            small_out[4:5] = col_sum(grad * att_v[...].astype(F32))
            small_out[5:6] = col_sum(ga.astype(F32))
            for copy in outs:
                copy.wait()

    stack = (SLOTS, rows, width)
    plain = pltpu.VMEM((rows, width), BF16)
    full = pltpu.VMEM((rows, width), F32)
    chunks = pltpu.VMEM((steps, rows, CHUNK), BF16)
    return manual(
        kernel,
        scalars,
        [
            (cotangent, False),
            (other, False),
            (relay, False),
            (kept["branch"], False),
            (kept["slope"], False),
            (kept["residual"], False),
            (kept["attended"], False),
            (vec, True),
            (wo_own, False),
            (wo_oth, False),
            (wu_own, False),
            (wu_oth, False),
            (wd_own, False),
            (wd_oth, False),
        ],
        [
            (stack, BF16, False, grads.get("branch")),
            ((SLOTS, rows, hidden), BF16, False, grads.get("before")),
            (stack, BF16, False, grads.get("attended")),
            ((rows, width), BF16, False, None),
            ((rows, width), F32, False, None),
            ((8, width), F32, True, None),
            ((steps, CHUNK), F32, True, None),
        ],
        [
            plain,
            plain,
            chunks,
            full,
            plain,
            pltpu.VMEM((2, half, width), BF16),
            pltpu.VMEM((steps, width, CHUNK), BF16),
            pltpu.VMEM((steps, CHUNK, width), BF16),
            plain,
            pltpu.VMEM((2, rows, CHUNK), F32),
            chunks,
            plain,
            plain,
            full,
            full,
            dma_sems(2),
            dma_sems(5),
            dma_sems(steps),
            dma_sems(steps),
            dma_sems(steps),
            dma_sems(4),
            dma_sems(steps),
        ],
        flops=4 * rows * width * hidden + 2 * rows * width * width,
        moved=4 * width * hidden + 2 * width * width + 8 * rows * hidden,
    )


def attend_backward(scalars, grad_mixed, kept):
    _, rows, width = kept["q"].shape
    pairs = width // (2 * HEAD_DIM)
    lanes = 2 * HEAD_DIM
    score_scale = HEAD_DIM**-0.5

    def kernel(s, *refs):
        @pl.when(s[2] == 1)
        def _():
            compute(*refs)

    def compute(gm, q_ref, kv, grown, full, inv, dq_out, here_out, there_out):
        qs = q_ref[0]
        keys = kv[0, 0]
        values = kv[0, 1]
        first_q = lax.broadcasted_iota(jnp.int32, (rows, lanes), 1) < HEAD_DIM
        scaled = (gm[...].astype(F32) * inv[0]).astype(BF16)
        product = scaled.astype(F32) * full[0]
        grad_q = []
        grad_k = None
        grad_v = None
        for head in range(2):
            mine = first_q if head == 0 else ~first_q
            own = jnp.where(mine, scaled, 0)
            centre = jnp.sum(jnp.where(mine, product, 0.0), axis=-1, keepdims=True)
            grad_probs = dot_nt(own, values)
            weight = grown[0, head]
            grad_scores = (weight.astype(F32) * (grad_probs - centre)).astype(BF16)
            grad_q.append(dot(grad_scores, keys))
            k_part = dot_tn(grad_scores, jnp.where(mine, qs, 0))
            v_part = dot_tn(weight, own)
            grad_k = k_part if head == 0 else grad_k + k_part
            grad_v = v_part if head == 0 else grad_v + v_part
        dq_out[...] = (jnp.where(first_q, grad_q[0], grad_q[1]) * score_scale).astype(BF16)
        grad_k = (grad_k * score_scale).astype(BF16)
        grad_v = grad_v.astype(BF16)
        here_out[0] = grad_k[:rows]
        here_out[1] = grad_v[:rows]
        there_out[0] = grad_k[rows:]
        there_out[1] = grad_v[rows:]

    column = lambda i, s: (s[0], 0, i)
    plain = lambda i, s: (0, i)
    return call(
        kernel,
        scalars,
        (pairs,),
        [
            (grad_mixed, (rows, lanes), plain),
            (kept["q"], (1, rows, lanes), column),
            (kept["kv"], (1, 2, 2 * rows, lanes), lambda i, s: (s[0], 0, 0, i)),
            (kept["grown"], (1, 2, rows, 2 * rows), lambda i, s: (s[0], i, 0, 0)),
            (kept["mixed_full"], (1, rows, lanes), column),
            (kept["inverse"], (1, rows, lanes), column),
        ],
        [
            ((rows, width), BF16, (rows, lanes), plain, None),
            ((2, rows, width), BF16, (2, rows, lanes), lambda i, s: (0, 0, i), None),
            ((2, rows, width), BF16, (2, rows, lanes), lambda i, s: (0, 0, i), None),
        ],
        flops=16 * rows * rows * width,
        moved=4 * 2 * pairs * rows * rows + 30 * rows * width,
    )


def qkv_backward(scalars, dq, dkv_here, dkv_there, w_own, w_oth, grad_res, vec, kept, grads):
    _, rows, width = kept["x"].shape
    half = width // 2

    def kernel(s, dq_ref, here, there, own, oth, gr, x_ref, v, packed_out, gx_out, relay_out,
               small_out, shift_out, a_v, b_v, p_v, w_v, gr_v, x_v, gx_v, acc,
               a_sems, b_sems, w_sems, in_sems, packed_sems, out_sems):
        @pl.when(s[2] == 0)
        def _():
            small_out[...] = jnp.zeros_like(small_out)
            shift_out[...] = jnp.zeros_like(shift_out)

        @pl.when(s[2] == 1)
        def _():
            slot = s[0]
            loads = []
            for part in range(6):
                kind, side = part % 3, part // 3
                columns = pl.ds(side * half, half)
                if kind == 0:
                    copies = [begin(dq_ref.at[:, columns], a_v.at[part], a_sems.at[part])]
                else:
                    turned = pl.ds((1 - side) * half, half)
                    copies = [
                        begin(here.at[kind - 1, :, columns], a_v.at[part], a_sems.at[part]),
                        begin(there.at[kind - 1, :, turned], b_v.at[part], b_sems.at[part]),
                    ]
                weight = own if side == 0 else oth
                copies.append(begin(weight.at[kind], w_v.at[part], w_sems.at[part]))
                loads.append(copies)
            last = [
                begin(x_ref.at[slot], x_v, in_sems.at[0]),
                begin(gr, gr_v, in_sems.at[1]),
            ]
            outs = []
            for part in range(6):
                for copy in loads[part]:
                    copy.wait()
                if part % 3 == 0:
                    packed = a_v[part]
                else:
                    packed = (a_v[part].astype(F32) + b_v[part].astype(F32)).astype(BF16)
                p_v[part] = packed
                outs.append(
                    begin(
                        p_v.at[part],
                        packed_out.at[slot, :, pl.ds(part * half, half)],
                        packed_sems.at[part],
                    )
                )
                shift_out[part : part + 1] = col_sum(packed.astype(F32))
                product = dot_nt(packed, w_v[part])
                acc[...] = product if part == 0 else acc[...] + product
            for copy in last:
                copy.wait()
            hat, scale = norm_stats(x_v[...].astype(F32))
            error = acc[...]
            grad = gr_v[...] + norm_backward(hat, scale, v[LN1G : LN1G + 1], error)
            gx_v[...] = grad.astype(BF16)
            outs.append(begin(gx_v, relay_out, out_sems.at[0]))
            outs.append(begin(gx_v, gx_out.at[slot], out_sems.at[1]))
            small_out[...] = jnp.zeros_like(small_out)
            small_out[0:1] = col_sum(error * hat)
            small_out[1:2] = col_sum(error)
            for copy in outs:
                copy.wait()

    stack = (SLOTS, rows, width)
    parts = pltpu.VMEM((6, rows, half), BF16)
    return manual(
        kernel,
        scalars,
        [
            (dq, False),
            (dkv_here, False),
            (dkv_there, False),
            (w_own, False),
            (w_oth, False),
            (grad_res, False),
            (kept["x"], False),
            (vec, True),
        ],
        [
            ((SLOTS, rows, 3 * width), BF16, False, grads.get("packed")),
            (stack, BF16, False, grads.get("input")),
            ((rows, width), BF16, False, None),
            ((8, width), F32, True, None),
            ((8, half), F32, True, None),
        ],
        [
            parts,
            parts,
            parts,
            pltpu.VMEM((6, width, half), BF16),
            pltpu.VMEM((rows, width), F32),
            pltpu.VMEM((rows, width), BF16),
            pltpu.VMEM((rows, width), BF16),
            pltpu.VMEM((rows, width), F32),
            dma_sems(6),
            dma_sems(6),
            dma_sems(6),
            dma_sems(2),
            dma_sems(6),
            dma_sems(2),
        ],
        flops=6 * rows * width * width,
        moved=6 * width * width + 16 * rows * width,
    )


def swap(block):
    return lax.ppermute(block, "tensor", [(0, 1), (1, 0)])


def ring_order(count):
    return list(range(0, count, 2)) + list(range(count - 1, 0, -2))


def ring_sum(parts):
    count = lax.axis_size("dp")
    order = ring_order(count)
    place = jnp.asarray([order.index(i) for i in range(count)], jnp.int32)[lax.axis_index("dp")]
    chunks = [part.shape[0] // (2 * count) for part in parts]
    signs = (1, -1)
    routes = [[(order[i], order[(i + s) % count]) for i in range(count)] for s in signs]

    def start(way, owner, chunk):
        return (way * count + owner % count) * chunk

    def own(way, owner):
        blocks = [
            lax.dynamic_slice_in_dim(part, start(way, owner, chunk), chunk, 0)
            for part, chunk in zip(parts, chunks)
        ]
        return blocks[0] if len(blocks) == 1 else jnp.concatenate(blocks, axis=0)

    moving = [own(w, place) for w in range(2)]
    for step in range(count - 1):
        arrived = [lax.ppermute(moving[w], "dp", routes[w]) for w in range(2)]
        moving = [
            (
                arrived[w].astype(F32) + own(w, place - signs[w] * (step + 1)).astype(F32)
            ).astype(BF16)
            for w in range(2)
        ]
    totals = [jnp.zeros(part.shape, F32) for part in parts]

    def put(totals, way, owner, block):
        done = []
        base = 0
        for total, chunk in zip(totals, chunks):
            piece = block[base : base + chunk].astype(F32)
            done.append(
                lax.dynamic_update_slice_in_dim(total, piece, start(way, owner, chunk), 0)
            )
            base += chunk
        return done

    for w in range(2):
        totals = put(totals, w, place + signs[w], moving[w])
    for step in range(count - 1):
        moving = [lax.ppermute(moving[w], "dp", routes[w]) for w in range(2)]
        for w in range(2):
            totals = put(totals, w, place - signs[w] * step, moving[w])
    return totals


def shards(
    inputs,
    cotangent,
    ln1_gain,
    ln1_bias,
    qkv_weight,
    qv_bias,
    out_weight,
    out_bias,
    scale_attn,
    ln2_gain,
    ln2_bias,
    fc1_weight,
    fc1_bias,
    fc2_weight,
    fc2_bias,
    scale_mlp,
):
    section = lax.axis_index("section")
    rank = lax.axis_index("tensor")
    micro, images, seq_len, half = inputs.shape
    assert micro == 2 and images == 1
    width = 2 * half
    rows = seq_len // 2
    hidden_half = fc1_weight.shape[2]
    low = rank == 0

    def whole_width(own, oth):
        return jnp.where(
            low, jnp.concatenate([own, oth], axis=-1), jnp.concatenate([oth, own], axis=-1)
        )

    def partner_tokens(block):
        return lax.dynamic_slice_in_dim(block, (1 - rank) * rows, rows, block.ndim - 2)

    def by_features(block):
        def part(index):
            return lax.dynamic_slice_in_dim(block, index * half, half, 2)

        own, oth = part(rank), swap(part(1 - rank))
        return jnp.where(
            low, jnp.concatenate([own, oth], axis=1), jnp.concatenate([oth, own], axis=1)
        )

    vectors = jnp.concatenate(
        [
            ln1_gain,
            ln1_bias,
            out_bias,
            scale_attn,
            ln2_gain,
            ln2_bias,
            fc2_bias,
            scale_mlp,
            qv_bias[0],
            fc1_bias.reshape(hidden_half // half, half),
        ],
        axis=0,
    )
    first_oth = swap(partner_tokens(inputs[0, 0]))
    vectors_oth = swap(vectors)
    wq_own = jnp.transpose(qkv_weight[0], (1, 0, 2))
    wq_oth = swap(wq_own)
    wo_own, wu_own, wd_own = out_weight[0], fc1_weight[0], fc2_weight[0]
    wo_late, wu_late, wd_late, first_oth = lax.optimization_barrier(
        (wo_own, wu_own, wd_own, first_oth)
    )
    wo_oth = swap(wo_late)
    wu_oth = swap(wu_late)
    wd_oth = swap(wd_late)
    later = jnp.stack([inputs[1, 0], cotangent[0, 0], cotangent[1, 0]])
    later_oth = swap(partner_tokens(later))
    in_oth = [first_oth, later_oth[0], later_oth[0]]
    cot_oth = [later_oth[1], later_oth[2], later_oth[2]]
    vec = whole_width(vectors[:8], vectors_oth[:8]).astype(F32)
    bias_q = jnp.concatenate([vectors[8:9], vectors_oth[8:9]], axis=1).astype(F32)
    bias_v = jnp.concatenate([vectors[9:10], vectors_oth[9:10]], axis=1).astype(F32)
    b_up = jnp.concatenate([vectors[10:], vectors_oth[10:]], axis=0).astype(F32)
    b_up = b_up.reshape(2 * hidden_half // CHUNK, CHUNK)

    def tick_scalars(number):
        active = (number >= 0) & (number < micro)
        slot = jnp.where(active, number, micro)
        return jnp.stack([slot, section, active.astype(jnp.int32), rank]).astype(jnp.int32)

    kept = {}
    received = jnp.zeros((rows, width), BF16)
    for tick in range(micro + 1):
        scalars = tick_scalars(tick - section)
        number = min(tick, micro - 1)
        kept["x"], kept["normed1"], kv_here = norm_kv(
            scalars, inputs, number, in_oth[tick], received, vec, wq_own, wq_oth, bias_v, kept
        )
        kv_there = swap(kv_here)
        kept["q"] = project_q(scalars, kept["normed1"], wq_own, wq_oth, bias_q, kept)
        kept["grown"], kept["mixed_full"], kept["mixed"], kept["inverse"], kept["kv"] = attend(
            scalars, kept["q"], kv_here, kv_there, kept
        )
        (
            kept["attended"],
            kept["residual"],
            kept["normed2"],
            kept["active"],
            kept["slope"],
            kept["branch"],
            kept["output"],
            relayed,
        ) = mlp_forward(
            scalars, kept["mixed"], kept["x"], vec, wo_own, wo_oth, wu_own, wu_oth, wd_own,
            wd_oth, b_up, kept,
        )
        if tick < micro:
            received = lax.ppermute(relayed, "section", [(0, 1)])

    block_outputs = by_features(kept["output"][:micro])

    def weight_grad(left, right):
        return lax.dot_general(
            left, right, (((0, 1), (0, 1)), ((), ())), preferred_element_type=F32
        ).astype(BF16)

    def paired(own, oth):
        return (own.astype(F32) + swap(oth).astype(F32)).astype(BF16)

    def both(name, part):
        return part[name][:micro]

    grads = {}
    received = jnp.zeros((rows, width), BF16)
    small_two = small_one = shift_up = shift_qkv = None
    for tick in range(micro + 1):
        scalars = tick_scalars(tick - 1 + section)
        number = min(tick, micro - 1)
        (
            grads["branch"],
            grads["before"],
            grads["attended"],
            grad_mixed,
            grad_res,
            small_b,
            shift_b,
        ) = mlp_backward(
            scalars, cotangent, number, cot_oth[tick], received, vec, wo_own, wo_oth, wu_own,
            wu_oth, wd_own, wd_oth, kept, grads,
        )
        if tick == micro:
            active = both("active", kept)
            g_branch = both("branch", grads)
            grad_down = paired(
                weight_grad(active[:, :, :hidden_half], g_branch),
                weight_grad(active[:, :, hidden_half:], g_branch),
            )
            normed2 = both("normed2", kept)
            before = both("before", grads)
            grad_up = paired(
                weight_grad(normed2, before[:, :, :hidden_half]),
                weight_grad(normed2, before[:, :, hidden_half:]),
            )
            grad_down, grad_up, grad_mixed = lax.optimization_barrier(
                (grad_down, grad_up, grad_mixed)
            )
        dq, dkv_here, dkv_send = attend_backward(scalars, grad_mixed, kept)
        dkv_there = swap(dkv_send)
        grads["packed"], grads["input"], relayed, small_a, shift_a = qkv_backward(
            scalars, dq, dkv_here, dkv_there, wq_own, wq_oth, grad_res, vec, kept, grads
        )
        if tick == 0:
            small_two, small_one, shift_up, shift_qkv = small_b, small_a, shift_b, shift_a
        else:
            small_two += small_b
            small_one += small_a
            shift_up += shift_b
            shift_qkv += shift_a
        if tick < micro:
            received = lax.ppermute(relayed, "section", [(1, 0)])

    total_down = lax.psum(grad_down, "dp").astype(F32)
    (total_up,) = ring_sum([grad_up])
    mixed = both("mixed", kept)
    g_att = both("attended", grads)
    grad_out = paired(
        weight_grad(mixed[:, :, :half], g_att), weight_grad(mixed[:, :, half:], g_att)
    )
    normed1 = both("normed1", kept)
    packed = both("packed", grads)

    def qkv_grad(base):
        return jnp.concatenate(
            [
                weight_grad(normed1, packed[:, :, (base + j) * half : (base + j + 1) * half])
                for j in range(3)
            ],
            axis=0,
        )

    grad_qkv = paired(qkv_grad(0), qkv_grad(3))

    feature_sums = jnp.concatenate([small_one[:2], small_two[:6]], axis=0)

    def feature_part(index):
        return lax.dynamic_slice_in_dim(feature_sums, index * half, half, 1)

    up_rows = shift_up.reshape(2, hidden_half // half, half)
    small_own = jnp.concatenate([feature_part(rank), shift_qkv[0:3], up_rows[0]], axis=0)
    small_oth = jnp.concatenate([feature_part(1 - rank), shift_qkv[3:6], up_rows[1]], axis=0)
    small = paired(small_own.astype(BF16), small_oth.astype(BF16))
    unit = 16 * lax.axis_size("dp")
    small = jnp.concatenate([small, jnp.zeros((-small.shape[0] % unit, half), BF16)], axis=0)
    total_qkv, out_left, out_right, sums = ring_sum(
        [grad_qkv, grad_out[:, :half], grad_out[:, half:], small]
    )
    total_qkv = total_qkv.reshape(3, width, half)
    total_out = jnp.concatenate([out_left, out_right], axis=1)
    input_grads = by_features(grads["input"][:micro])

    def row(number):
        return sums[number][None]

    return (
        block_outputs.reshape(1, micro, images, seq_len, half),
        input_grads.reshape(1, micro, images, seq_len, half),
        row(0),
        row(1),
        jnp.transpose(total_qkv, (1, 0, 2))[None],
        jnp.stack([sums[8], sums[10]])[None],
        total_out[None],
        row(7),
        row(6),
        row(4),
        row(5),
        total_up[None],
        sums[11 : 11 + hidden_half // half].reshape(1, hidden_half),
        total_down[None],
        row(3),
        row(2),
    )


def solution(mesh):
    placed = (
        P(None, "dp", None, "tensor"),
        P(None, "dp", None, "tensor"),
        P("section", "tensor"),
        P("section", "tensor"),
        P("section", None, None, "tensor"),
        P("section", None, "tensor"),
        P("section", "tensor", None),
        P("section", "tensor"),
        P("section", "tensor"),
        P("section", "tensor"),
        P("section", "tensor"),
        P("section", None, "tensor"),
        P("section", "tensor"),
        P("section", "tensor", None),
        P("section", "tensor"),
        P("section", "tensor"),
    )
    return jax.shard_map(
        shards,
        mesh=mesh,
        in_specs=placed,
        out_specs=(
            P("section", None, "dp", None, "tensor"),
            P("section", None, "dp", None, "tensor"),
            P("section", "tensor"),
            P("section", "tensor"),
            P("section", None, None, "tensor"),
            P("section", None, "tensor"),
            P("section", "tensor", None),
            P("section", "tensor"),
            P("section", "tensor"),
            P("section", "tensor"),
            P("section", "tensor"),
            P("section", None, "tensor"),
            P("section", "tensor"),
            P("section", "tensor", None),
            P("section", "tensor"),
            P("section", "tensor"),
        ),
        check_vma=False,
    )
```

time: 1510 us -> 813 us (0.54)
  waiting for transfers between devices: 734 us -> 314 us
  matrix products: 295 us -> 39 us
  Pallas kernels: 0 us -> 216 us
  other arithmetic: 245 us -> 62.4 us
  starting transfers between devices: 12.1 us -> 104 us
  local copies, waits for them, and re-layouts: 118 us -> 41.6 us
  blocking collectives: 63.3 us -> 0 us
  loops' own time: 19.8 us -> 0 us
    psum x1, waiting for transfers between devices: 342 us -> 0.01 us  [shards(): total_down = lax.psum(grad_down, 'dp').astype(F32)]
    ppermute x4 -> x80, waiting for transfers between devices: 67.9 us -> 314 us  [the longest x2 105 us: shards(): received = lax.ppermute(relayed, 'section', [(1, 0)])]
    dot_general x36 -> x12, matrix products: 279 us -> 39 us  [weight_grad(): lax.dot_general(left, right, (((0, 1), (0, 1)), ((), ())), preferred_elem...]
    reduce_scatter x12 -> x0, waiting for transfers between devices: 224 us -> none  [the longest x3 79.4 us: shards(): lax.psum_scatter(partial_one.astype(jnp.bfloat16), 'tensor', scatter_dime...]
    pallas_call x0 -> x21, Pallas kernels: none -> 216 us  [the longest x15 135 us: manual(): pl.pallas_call(body, out_shape=[jax.ShapeDtypeStruct(s, d) for s, d, _, _...]
    reduce_sum x33 -> x0, other arithmetic: 104 us -> none  [the longest x6 35.4 us: stat_columns(): jnp.sum(weighted, axis=-1)]
    all_gather x12 -> x0, waiting for transfers between devices: 99.7 us -> none  [the longest x3 32.9 us: shards(): lax.all_gather(grad_att, 'tensor', axis=1, tiled=True)]
    ppermute x4 -> x80, starting transfers between devices: 10.1 us -> 104 us  [the longest x28 48.5 us: ring_sum(): moving = [lax.ppermute(moving[w], 'dp', routes[w]) for w in range(2)]]
  transfers between devices with their start and end apart: 29 -> 81, of which waited for: 25 -> 48; matrix products, arithmetic and copies ran while one was open for 6% -> 14% of each run, Pallas kernels for 0% -> 10%
where the time goes in v1:
time: 813 us; the launch traced here: 805 us
  waiting for transfers between devices  314 us (39%)
  Pallas kernels  216 us (27%)
  starting transfers between devices  104 us (13%)
  other arithmetic  62.4 us (8%)
  local copies, waits for them, and re-layouts  41.6 us (5%)
  matrix products  39 us (5%)
  between operations  27.6 us (3%)
    pallas_call x15, Pallas kernels, manual(): pl.pallas_call(body, out_shape=[jax.ShapeDtypeStruct(s, d) for s, d, _, _...  135 us
    ppermute x2, waiting for transfers between devices, shards(): received = lax.ppermute(relayed, 'section', [(1, 0)])  105 us
    ppermute x28, waiting for transfers between devices, ring_sum(): arrived = [lax.ppermute(moving[w], 'dp', routes[w]) for w in range(2)]  92.1 us
    pallas_call x6, Pallas kernels, call(): pl.pallas_call(body, out_shape=[jax.ShapeDtypeStruct(s, d) for s, d, _, _...  81.4 us
    ppermute x28, waiting for transfers between devices, ring_sum(): moving = [lax.ppermute(moving[w], 'dp', routes[w]) for w in range(2)]  62.8 us
    ppermute x28, starting transfers between devices, ring_sum(): moving = [lax.ppermute(moving[w], 'dp', routes[w]) for w in range(2)]  48.5 us
    ppermute x28, starting transfers between devices, ring_sum(): arrived = [lax.ppermute(moving[w], 'dp', routes[w]) for w in range(2)]  42.2 us
    dot_general x12, matrix products, weight_grad(): lax.dot_general(left, right, (((0, 1), (0, 1)), ((), ())), preferred_elem...  39 us
  transfers between devices with their start and end apart: 81, of which 48 were waited for; matrix products, arithmetic and copies ran while one was open for 14% of the time, Pallas kernels for 10%

profile of v1, /device:TPU:0, one launch (start us, length us, event | category | flops | bytes accessed | tf_op | source)
XLA Modules:
  0.0 805.2 jit_solution(8099246500119438577)
XLA Ops:
  20.7 6.4 collective-permute-done.2
  32.4 5.9 shard_map.297
  50.0 15.2 %shard_map.299 = (bf16[3,16,384,768]{3,2,1,0:T(8,128)(2,1)}, f32[3,384,1024]{2,1,0:T(8,128)}, bf16[3,384,1024]{2,1,0:T(8,128)(2,1)}, f32[3,384,1024]{2,1,0:T(8,128)}, bf16[3,2,768,1024]{3,2,1,0:T(8,128)(2,1)}) custom-call(s32[4]{0:T(128)} %add_add_fusion.2.refs_0_, bf16[3,384,1024]{2,1,0:T(8,128)(2,1)} %shard_map.298.refs_1_.refs_5_, ...), custom_call_target="tpu_custom_call" | custom-call | flops 1207959552 | bytes 21233664 | tf_op jit(solution)/shard_map/pallas_call | solution.py:66
  66.2 22.6 %shard_map.300 = (bf16[3,384,1024]{2,1,0:T(8,128)(2,1)}, f32[3,384,1024]{2,1,0:T(8,128)}, bf16[3,384,1024]{2,1,0:T(8,128)(2,1)}, bf16[3,384,4096]{2,1,0:T(8,128)...) custom-call(s32[4]{0:T(128)} %add_add_fusion.2.refs_0_, ...), custom_call_target="tpu_custom_call" | custom-call | flops 7247757312 | bytes 31457280 | tf_op jit(solution)/shard_map/pallas_call | solution.py:103
  93.0 14.7 %collective-permute-done.8.refs_3_ = bf16[384,1024]{1,0:T(8,128)(2,1)S(1)} collective-permute-done((bf16[384,1024]{1,0:T(8,128)(2,1)}, bf16[384,1024]{1,0:T(8,128)(2,1)S(1)}, u32[]{:S(2)}, u32[]{:S(2)}) %collective-permute-start.8) | collective-permute-done | bytes 786464 | tf_op jit(solution)/shard_map/ppermute | solution.py:991
  108.6 6.3 shard_map.301
  120.3 15.2 %shard_map.303 = (bf16[3,16,384,768]{3,2,1,0:T(8,128)(2,1)}, f32[3,384,1024]{2,1,0:T(8,128)}, bf16[3,384,1024]{2,1,0:T(8,128)(2,1)}, f32[3,384,1024]{2,1,0:T(8,128)}, bf16[3,2,768,1024]{3,2,1,0:T(8,128)(2,1)}) custom-call(s32[4]{0:T(128)} %add_add_fusion.1.refs_0_, ...), custom_call_target="tpu_custom_call", output_to_operand_aliasing={{0}: (4, {}), {1}: (5, {}), {2}: (6, {}), {3}: (7, {}), {4}... | custom-call | flops 1207959552 | bytes 21233664 | tf_op jit(solution)/shard_map/pallas_call | solution.py:66
  135.5 22.4 %shard_map.304 = (bf16[3,384,1024]{2,1,0:T(8,128)(2,1)}, f32[3,384,1024]{2,1,0:T(8,128)}, bf16[3,384,1024]{2,1,0:T(8,128)(2,1)}, bf16[3,384,4096]{2,1,0:T(8,128)...) custom-call(s32[4]{0:T(128)} %add_add_fusion.1.refs_0_, ...), custom_call_target="tpu_custom_call", output_to_operand_aliasing={{0}: (11, {}), {1}: (12, {}), {2}: (13, {}), {3}: (14, {}),... | custom-call | flops 7247757312 | bytes 31457280 | tf_op jit(solution)/shard_map/pallas_call | solution.py:103
  163.4 17.1 %collective-permute-done.10.refs_3_ = bf16[384,1024]{1,0:T(8,128)(2,1)S(1)} collective-permute-done((bf16[384,1024]{1,0:T(8,128)(2,1)}, bf16[384,1024]{1,0:T(8,128)(2,1)S(1)}, u32[]{:S(2)}, u32[]{:S(2)}) %collective-permute-start.10) | collective-permute-done | bytes 786464 | tf_op jit(solution)/shard_map/ppermute | solution.py:991
  187.3 9.8 %shard_map.307 = (bf16[3,16,384,768]{3,2,1,0:T(8,128)(2,1)}, f32[3,384,1024]{2,1,0:T(8,128)}, bf16[3,384,1024]{2,1,0:T(8,128)(2,1)}, f32[3,384,1024]{2,1,0:T(8,128)}, bf16[3,2,768,1024]{3,2,1,0:T(8,128)(2,1)}) custom-call(s32[4]{0:T(128)} %add_add_fusion.refs_0_, ...), custom_call_target="tpu_custom_call", output_to_operand_aliasing={{0}: (4, {}), {1}: (5, {}), {2}: (6, {}), {3}: (7, {}), {4}... | custom-call | flops 1207959552 | bytes 21233664 | tf_op jit(solution)/shard_map/pallas_call | solution.py:66
  200.6 9.9 %shard_map.310 = (bf16[384,1024]{1,0:T(8,128)(2,1)}, bf16[2,384,1024]{2,1,0:T(8,128)(2,1)}, bf16[2,384,1024]{2,1,0:T(8,128)(2,1)}) custom-call(s32[4]{0:T(128)} %add_add_fusion.5.refs_0_, bf16[384,1024]{1,0:T(8,128)(2,1)} %get-tuple-element.160.refs_1_, bf16[3,384,1024]{2,1,0:T(8,128)(2,1)} %shard_map.306.refs_1_.refs_2_, ...), custom_call_target="tpu_custom_call" | custom-call | flops 2415919104 | bytes 21233664 | tf_op jit(solution)/shard_map/pallas_call | solution.py:66
  219.0 84.8 %collective-permute-done.14.refs_3_ = bf16[384,1024]{1,0:T(8,128)(2,1)S(1)} collective-permute-done((bf16[384,1024]{1,0:T(8,128)(2,1)}, bf16[384,1024]{1,0:T(8,128)(2,1)S(1)}, u32[]{:S(2)}, u32[]{:S(2)}) %collective-permute-start.14) | collective-permute-done | bytes 786464 | tf_op jit(solution)/shard_map/ppermute | solution.py:1053
  304.7 21.5 %shard_map.312 = (bf16[3,384,1024]{2,1,0:T(8,128)(2,1)}, bf16[3,384,4096]{2,1,0:T(8,128)(2,1)}, bf16[3,384,1024]{2,1,0:T(8,128)(2,1)}, bf16[384,1024]{1,0:T(8,12...) custom-call(s32[4]{0:T(128)} %add_add_fusion.4.refs_0_, ...), custom_call_target="tpu_custom_call", output_to_operand_aliasing={{0}: (15, {}), {1}: (16, {}), {2}: (17, {})} | custom-call | flops 7247757312 | bytes 31457280 | tf_op jit(solution)/shard_map/pallas_call | solution.py:103
  326.2 15.5 %shard_map.313 = (bf16[384,1024]{1,0:T(8,128)(2,1)}, bf16[2,384,1024]{2,1,0:T(8,128)(2,1)}, bf16[2,384,1024]{2,1,0:T(8,128)(2,1)}) custom-call(s32[4]{0:T(128)} %add_add_fusion.4.refs_0_, bf16[384,1024]{1,0:T(8,128)(2,1)} %get-tuple-element.173.refs_1_, bf16[3,384,1024]{2,1,0:T(8,128)(2,1)} %shard_map.306.refs_1_.refs_2_, ...), custom_call_target="tpu_custom_call" | custom-call | flops 2415919104 | bytes 21233664 | tf_op jit(solution)/shard_map/pallas_call | solution.py:66
  346.5 9.3 %shard_map.314 = (bf16[3,384,3072]{2,1,0:T(8,128)(2,1)}, bf16[3,384,1024]{2,1,0:T(8,128)(2,1)}, bf16[384,1024]{1,0:T(8,128)(2,1)}, f32[8,1024]{1,0:T(8,128)}, f32[8,512]{1,0:T(8,128)}) custom-call(s32[4]{0:T(128)} %add_add_fusion.4.refs_0_, bf16[384,1024]{1,0:T(8,128)(2,1)} %get-tuple-element.174.refs_1_, ...), custom_call_target="tpu_custom_call", output_to_operand_aliasing={{0}: (9, {}), {1}: (10, {})} | custom-call | flops 2415919104 | bytes 12582912 | tf_op jit(solution)/shard_map/pallas_call | solution.py:103
  357.8 19.8 %collective-permute-done.16.refs_3_ = bf16[384,1024]{1,0:T(8,128)(2,1)S(1)} collective-permute-done((bf16[384,1024]{1,0:T(8,128)(2,1)}, bf16[384,1024]{1,0:T(8,128)(2,1)S(1)}, u32[]{:S(2)}, u32[]{:S(2)}) %collective-permute-start.16) | collective-permute-done | bytes 786464 | tf_op jit(solution)/shard_map/ppermute | solution.py:1053
  378.4 21.9 %shard_map.315 = (bf16[3,384,1024]{2,1,0:T(8,128)(2,1)}, bf16[3,384,4096]{2,1,0:T(8,128)(2,1)}, bf16[3,384,1024]{2,1,0:T(8,128)(2,1)}, bf16[384,1024]{1,0:T(8,12...) custom-call(s32[4]{0:T(128)} %add_add_fusion.3.refs_0_, ...), custom_call_target="tpu_custom_call", output_to_operand_aliasing={{0}: (15, {}), {1}: (16, {}), {2}: (17, {})} | custom-call | flops 7247757312 | bytes 31457280 | tf_op jit(solution)/shard_map/pallas_call | solution.py:103
  400.3 7.1 bitcast_convert_fusion
  407.4 7.2 bitcast_convert_fusion.2
  435.7 5.8 bitcast_convert_fusion.3
  441.6 5.8 bitcast_convert_fusion.1
  451.5 7.8 add_convert_fusion.1
  481.7 15.7 %shard_map.316 = (bf16[384,1024]{1,0:T(8,128)(2,1)}, bf16[2,384,1024]{2,1,0:T(8,128)(2,1)}, bf16[2,384,1024]{2,1,0:T(8,128)(2,1)}) custom-call(s32[4]{0:T(128)} %add_add_fusion.3.refs_0_, bf16[384,1024]{1,0:T(8,128)(2,1)} %get-tuple-element.188.refs_1_, bf16[3,384,1024]{2,1,0:T(8,128)(2,1)} %shard_map.306.refs_1_.refs_2_, ...), custom_call_target="tpu_custom_call" | custom-call | flops 2415919104 | bytes 21233664 | tf_op jit(solution)/shard_map/pallas_call | solution.py:66
  526.2 9.7 %shard_map.317 = (bf16[3,384,3072]{2,1,0:T(8,128)(2,1)}, bf16[3,384,1024]{2,1,0:T(8,128)(2,1)}, bf16[384,1024]{1,0:T(8,128)(2,1)}, f32[8,1024]{1,0:T(8,128)}, f32[8,512]{1,0:T(8,128)}) custom-call(s32[4]{0:T(128)} %add_add_fusion.3.refs_0_, bf16[384,1024]{1,0:T(8,128)(2,1)} %get-tuple-element.189.refs_1_, ...), custom_call_target="tpu_custom_call", output_to_operand_aliasing={{0}: (9, {}), {1}: (10, {})} | custom-call | flops 2415919104 | bytes 12582912 | tf_op jit(solution)/shard_map/pallas_call | solution.py:103
  563.1 6.4 collective-permute-start.66
  592.8 7.6 collective-permute-done.70
  640.3 5.9 collective-permute-done.25
  664.0 11.2 %collective-permute-done.27 = bf16[264,512]{1,0:T(8,128)(2,1)S(1)} collective-permute-done((bf16[264,512]{1,0:T(8,128)(2,1)S(1)}, bf16[264,512]{1,0:T(8,128)(2,1)S(1)}, u32[]{:S(2)}, u32[]{:S(2)}) %collective-permute-start.27) | collective-permute-done | bytes 270368 | tf_op jit(solution)/shard_map/ppermute | solution.py:850
  681.1 15.9 %collective-permute-done.34 = bf16[264,512]{1,0:T(8,128)(2,1)S(1)} collective-permute-done((bf16[264,512]{1,0:T(8,128)(2,1)S(1)}, bf16[264,512]{1,0:T(8,128)(2,1)S(1)}, u32[]{:S(2)}, u32[]{:S(2)}) %collective-permute-start.34) | collective-permute-done | bytes 270368 | tf_op jit(solution)/shard_map/ppermute | solution.py:850
  702.1 12.7 %collective-permute-done.35 = bf16[264,512]{1,0:T(8,128)(2,1)S(1)} collective-permute-done((bf16[264,512]{1,0:T(8,128)(2,1)S(1)}, bf16[264,512]{1,0:T(8,128)(2,1)S(1)}, u32[]{:S(2)}, u32[]{:S(2)}) %collective-permute-start.35) | collective-permute-done | bytes 270368 | tf_op jit(solution)/shard_map/ppermute | solution.py:850
  723.1 6.6 broadcast_in_dim.129
  755.9 6.1 collective-permute-done.43
  (443 shorter events, 327.6 us)
Async XLA Ops:
  7.2 715.9 %all-reduce.3.cloned.1.call-start = ((), (), s32[]{:S(2)}) async-start(), calls=%async_computation | async-start | bytes 8388608 | tf_op jit(solution)/shard_map/psum | solution.py:1055
  7.2 23.3 %collective-permute-start.3 = (bf16[3,1024,512]{2,1,0:T(8,128)(2,1)}, bf16[3,1024,512]{2,1,0:T(8,128)(2,1)S(1)}, u32[]{:S(2)}, u32[]{:S(2)}) collective-permute-start(bf16[3,1024,512]{2,1,0:T(8,128)(2,1)} %bitcast.144), channel_id=1, source_target_pairs={{0,8},{8,0},{1,9},{9,1},{2,10},{10,2},{3,11},{11,3},{4,12},{12,4},... | collective-permute-start | bytes 9437192 | tf_op jit(solution)/shard_map/ppermute | solution.py:823
  13.6 51.6 %collective-permute-start.6 = (bf16[1024,2048]{1,0:T(8,128)(2,1)}, bf16[1024,2048]{1,0:T(8,128)(2,1)}, u32[]{:S(2)}, u32[]{:S(2)}) collective-permute-start(bf16[1024,2048]{1,0:T(8,128)(2,1)} %bitcast.154), channel_id=1, source_target_pairs={{0,8},{8,0},{1,9},{9,1},{2,10},{10,2},{3,11},{11,3},{4,12},{12,4},... | collective-permute-start | bytes 12582920 | tf_op jit(solution)/shard_map/ppermute | solution.py:823
  14.0 51.2 %collective-permute-start.7 = (bf16[2048,1024]{1,0:T(8,128)(2,1)}, bf16[2048,1024]{1,0:T(8,128)(2,1)}, u32[]{:S(2)}, u32[]{:S(2)}) collective-permute-start(bf16[2048,1024]{1,0:T(8,128)(2,1)} %bitcast.161), channel_id=1, source_target_pairs={{0,8},{8,0},{1,9},{9,1},{2,10},{10,2},{3,11},{11,3},{4,12},{12,4},... | collective-permute-start | bytes 12582920 | tf_op jit(solution)/shard_map/ppermute | solution.py:823
  38.7 26.5 %collective-permute-start.5 = (bf16[512,1024]{1,0:T(8,128)(2,1)}, bf16[512,1024]{1,0:T(8,128)(2,1)S(1)}, u32[]{:S(2)}, u32[]{:S(2)}) collective-permute-start(bf16[512,1024]{1,0:T(8,128)(2,1)} %bitcast.168), channel_id=1, source_target_pairs={{0,8},{8,0},{1,9},{9,1},{2,10},{10,2},{3,11},{11,3},{4,12},{12,4},... | collective-permute-start | bytes 3145736 | tf_op jit(solution)/shard_map/ppermute | solution.py:823
  42.4 48.3 %collective-permute-start = (bf16[3,384,512]{2,1,0:T(8,128)(2,1)}, bf16[3,384,512]{2,1,0:T(8,128)(2,1)}, u32[]{:S(2)}, u32[]{:S(2)}) collective-permute-start(bf16[3,384,512]{2,1,0:T(8,128)(2,1)} %fusion.11), channel_id=1, source_target_pairs={{0,8},{8,0},{1,9},{9,1},{2,10},{10,2},{3,11},{11,3},{4,12},{12,4},... | collective-permute-start | bytes 3538952 | tf_op jit(solution)/shard_map/ppermute | solution.py:823
  88.8 19.0 %collective-permute-start.8 = (bf16[384,1024]{1,0:T(8,128)(2,1)}, bf16[384,1024]{1,0:T(8,128)(2,1)S(1)}, u32[]{:S(2)}, u32[]{:S(2)}) collective-permute-start(bf16[384,1024]{1,0:T(8,128)(2,1)} %get-tuple-element.122), channel_id=1, source_target_pairs={{0,16},{1,17},{2,18},{3,19},{4,20},{5,21},{6,22},{7,23},{8,24},{9,... | collective-permute-start | bytes 2359304 | tf_op jit(solution)/shard_map/ppermute | solution.py:991
  158.0 22.6 %collective-permute-start.10 = (bf16[384,1024]{1,0:T(8,128)(2,1)}, bf16[384,1024]{1,0:T(8,128)(2,1)S(1)}, u32[]{:S(2)}, u32[]{:S(2)}) collective-permute-start(bf16[384,1024]{1,0:T(8,128)(2,1)} %get-tuple-element.138), channel_id=1, source_target_pairs={{0,16},{1,17},{2,18},{3,19},{4,20},{5,21},{6,22},{7,23},{8,24},{9,... | collective-permute-start | bytes 2359304 | tf_op jit(solution)/shard_map/ppermute | solution.py:991
  217.1 86.7 %collective-permute-start.14 = (bf16[384,1024]{1,0:T(8,128)(2,1)}, bf16[384,1024]{1,0:T(8,128)(2,1)S(1)}, u32[]{:S(2)}, u32[]{:S(2)}) collective-permute-start(bf16[384,1024]{1,0:T(8,128)(2,1)} %get-tuple-element.169), channel_id=1, source_target_pairs={{16,0},{17,1},{18,2},{19,3},{20,4},{21,5},{22,6},{23,7},{24,8},{25... | collective-permute-start | bytes 2359304 | tf_op jit(solution)/shard_map/ppermute | solution.py:1053
  355.9 21.7 %collective-permute-start.16 = (bf16[384,1024]{1,0:T(8,128)(2,1)}, bf16[384,1024]{1,0:T(8,128)(2,1)S(1)}, u32[]{:S(2)}, u32[]{:S(2)}) collective-permute-start(bf16[384,1024]{1,0:T(8,128)(2,1)} %get-tuple-element.180), channel_id=1, source_target_pairs={{16,0},{17,1},{18,2},{19,3},{20,4},{21,5},{22,6},{23,7},{24,8},{25... | collective-permute-start | bytes 2359304 | tf_op jit(solution)/shard_map/ppermute | solution.py:1053
  407.4 40.0 %collective-permute-start.18 = (bf16[1024,2048]{1,0:T(8,128)(2,1)}, bf16[1024,2048]{1,0:T(8,128)(2,1)}, u32[]{:S(2)}, u32[]{:S(2)}) collective-permute-start(bf16[1024,2048]{1,0:T(8,128)(2,1)} %bitcast_convert_fusion), channel_id=1, source_target_pairs={{0,8},{8,0},{1,9},{9,1},{2,10},{10,2},{3,11},{11,3},{4,12},{12,4},... | collective-permute-start | bytes 12582920 | tf_op jit(solution)/shard_map/ppermute | solution.py:823
  414.6 36.9 %collective-permute-start.17 = (bf16[2048,1024]{1,0:T(8,128)(2,1)}, bf16[2048,1024]{1,0:T(8,128)(2,1)}, u32[]{:S(2)}, u32[]{:S(2)}) collective-permute-start(bf16[2048,1024]{1,0:T(8,128)(2,1)} %bitcast_convert_fusion.2), channel_id=1, source_target_pairs={{0,8},{8,0},{1,9},{9,1},{2,10},{10,2},{3,11},{11,3},{4,12},{12,4},... | collective-permute-start | bytes 12582920 | tf_op jit(solution)/shard_map/ppermute | solution.py:823
  435.2 65.4 %collective-permute-start.22 = (bf16[512,1024]{1,0:T(8,128)(2,1)}, bf16[512,1024]{1,0:T(8,128)(2,1)}, u32[]{:S(2)}, u32[]{:S(2)}) collective-permute-start(bf16[512,1024]{1,0:T(8,128)(2,1)} %bitcast_convert_fusion.4), channel_id=1, source_target_pairs={{0,8},{8,0},{1,9},{9,1},{2,10},{10,2},{3,11},{11,3},{4,12},{12,4},... | collective-permute-start | bytes 3145736 | tf_op jit(solution)/shard_map/ppermute | solution.py:823
  479.0 18.4 %collective-permute-start.54 = (bf16[64,2048]{1,0:T(8,128)(2,1)S(1)}, bf16[64,2048]{1,0:T(8,128)(2,1)S(1)}, u32[]{:S(2)}, u32[]{:S(2)}) collective-permute-start(bf16[64,2048]{1,0:T(8,128)(2,1)S(1)} %get-tuple-element.241), channel_id=1, source_target_pairs={{0,2},{2,4},{4,6},{6,7},{7,5},{5,3},{3,1},{1,0},{8,10},{10,12},{12... | collective-permute-start | bytes 786440 | tf_op jit(solution)/shard_map/ppermute | solution.py:850
  480.6 16.8 %collective-permute-start.61 = (bf16[64,2048]{1,0:T(8,128)(2,1)S(1)}, bf16[64,2048]{1,0:T(8,128)(2,1)S(1)}, u32[]{:S(2)}, u32[]{:S(2)}) collective-permute-start(bf16[64,2048]{1,0:T(8,128)(2,1)S(1)} %get-tuple-element.240), channel_id=1, source_target_pairs={{0,1},{2,0},{4,2},{6,4},{7,6},{5,7},{3,5},{1,3},{8,9},{10,8},{12,1... | collective-permute-start | bytes 786440 | tf_op jit(solution)/shard_map/ppermute | solution.py:850
  497.4 27.6 %collective-permute-start.19 = (bf16[2,384,1024]{2,1,0:T(8,128)(2,1)}, bf16[2,384,1024]{2,1,0:T(8,128)(2,1)S(1)}, u32[]{:S(2)}, u32[]{:S(2)}) collective-permute-start(bf16[2,384,1024]{2,1,0:T(8,128)(2,1)} %get-tuple-element.191), channel_id=1, source_target_pairs={{0,8},{8,0},{1,9},{9,1},{2,10},{10,2},{3,11},{11,3},{4,12},{12,4},... | collective-permute-start | bytes 4718600 | tf_op jit(solution)/shard_map/ppermute | solution.py:823
  523.0 21.4 %collective-permute-start.57 = (bf16[64,2048]{1,0:T(8,128)(2,1)}, bf16[64,2048]{1,0:T(8,128)(2,1)}, u32[]{:S(2)}, u32[]{:S(2)}) collective-permute-start(bf16[64,2048]{1,0:T(8,128)(2,1)} %get-tuple-element.235), channel_id=1, source_target_pairs={{0,2},{2,4},{4,6},{6,7},{7,5},{5,3},{3,1},{1,0},{8,10},{10,12},{12... | collective-permute-start | bytes 786440 | tf_op jit(solution)/shard_map/ppermute | solution.py:850
  523.0 21.4 %collective-permute-start.64 = (bf16[64,2048]{1,0:T(8,128)(2,1)}, bf16[64,2048]{1,0:T(8,128)(2,1)}, u32[]{:S(2)}, u32[]{:S(2)}) collective-permute-start(bf16[64,2048]{1,0:T(8,128)(2,1)} %get-tuple-element.234), channel_id=1, source_target_pairs={{0,1},{2,0},{4,2},{6,4},{7,6},{5,7},{3,5},{1,3},{8,9},{10,8},{12,1... | collective-permute-start | bytes 786440 | tf_op jit(solution)/shard_map/ppermute | solution.py:850
  546.0 23.5 %collective-permute-start.65 = (bf16[64,2048]{1,0:T(8,128)(2,1)S(1)}, bf16[64,2048]{1,0:T(8,128)(2,1)S(1)}, u32[]{:S(2)}, u32[]{:S(2)}) collective-permute-start(bf16[64,2048]{1,0:T(8,128)(2,1)S(1)} %get-tuple-element.232), channel_id=1, source_target_pairs={{0,1},{2,0},{4,2},{6,4},{7,6},{5,7},{3,5},{1,3},{8,9},{10,8},{12,1... | collective-permute-start | bytes 786440 | tf_op jit(solution)/shard_map/ppermute | solution.py:850
  548.2 68.7 %collective-permute-start.21 = (bf16[3072,512]{1,0:T(8,128)(2,1)S(1)}, bf16[3072,512]{1,0:T(8,128)(2,1)S(1)}, u32[]{:S(2)}, u32[]{:S(2)}) collective-permute-start(bf16[3072,512]{1,0:T(8,128)(2,1)S(1)} %pad_maximum_fusion), channel_id=1, source_target_pairs={{0,8},{8,0},{1,9},{9,1},{2,10},{10,2},{3,11},{11,3},{4,12},{12,4},... | collective-permute-start | bytes 9437192 | tf_op jit(solution)/shard_map/ppermute | solution.py:823
  550.1 41.0 %collective-permute-start.20 = (bf16[2,384,512]{2,1,0:T(8,128)(2,1)S(1)}, bf16[2,384,512]{2,1,0:T(8,128)(2,1)S(1)}, u32[]{:S(2)}, u32[]{:S(2)}) collective-permute-start(bf16[2,384,512]{2,1,0:T(8,128)(2,1)S(1)} %get-tuple-element.263), channel_id=1, source_target_pairs={{0,8},{8,0},{1,9},{9,1},{2,10},{10,2},{3,11},{11,3},{4,12},{12,4},... | collective-permute-start | bytes 2359304 | tf_op jit(solution)/shard_map/ppermute | solution.py:823
  613.4 18.1 %collective-permute-start.75 = (bf16[64,2048]{1,0:T(8,128)(2,1)S(1)}, bf16[64,2048]{1,0:T(8,128)(2,1)S(1)}, u32[]{:S(2)}, u32[]{:S(2)}) collective-permute-start(bf16[64,2048]{1,0:T(8,128)(2,1)S(1)} %collective-permute-done.73), channel_id=1, source_target_pairs={{0,1},{2,0},{4,2},{6,4},{7,6},{5,7},{3,5},{1,3},{8,9},{10,8},{12,1... | collective-permute-start | bytes 786440 | tf_op jit(solution)/shard_map/ppermute | solution.py:873
  623.2 26.5 %collective-permute-start.76 = (bf16[64,2048]{1,0:T(8,128)(2,1)S(1)}, bf16[64,2048]{1,0:T(8,128)(2,1)S(1)}, u32[]{:S(2)}, u32[]{:S(2)}) collective-permute-start(bf16[64,2048]{1,0:T(8,128)(2,1)S(1)} %collective-permute-done.74), channel_id=1, source_target_pairs={{0,2},{2,4},{4,6},{6,7},{7,5},{5,3},{3,1},{1,0},{8,10},{10,12},{12... | collective-permute-start | bytes 786440 | tf_op jit(solution)/shard_map/ppermute | solution.py:873
  623.3 16.5 %collective-permute-start.31 = (bf16[264,512]{1,0:T(8,128)(2,1)S(1)}, bf16[264,512]{1,0:T(8,128)(2,1)S(1)}, u32[]{:S(2)}, u32[]{:S(2)}) collective-permute-start(bf16[264,512]{1,0:T(8,128)(2,1)S(1)} %pad_maximum_fusion.2), channel_id=1, source_target_pairs={{0,1},{2,0},{4,2},{6,4},{7,6},{5,7},{3,5},{1,3},{8,9},{10,8},{12,1... | collective-permute-start | bytes 811016 | tf_op jit(solution)/shard_map/ppermute | solution.py:850
  631.5 27.6 %collective-permute-start.77 = (bf16[64,2048]{1,0:T(8,128)(2,1)S(1)}, bf16[64,2048]{1,0:T(8,128)(2,1)S(1)}, u32[]{:S(2)}, u32[]{:S(2)}) collective-permute-start(bf16[64,2048]{1,0:T(8,128)(2,1)S(1)} %collective-permute-done.75), channel_id=1, source_target_pairs={{0,1},{2,0},{4,2},{6,4},{7,6},{5,7},{3,5},{1,3},{8,9},{10,8},{12,1... | collective-permute-start | bytes 786440 | tf_op jit(solution)/shard_map/ppermute | solution.py:873
  649.8 51.5 %collective-permute-start.78 = (bf16[64,2048]{1,0:T(8,128)(2,1)S(1)}, bf16[64,2048]{1,0:T(8,128)(2,1)S(1)}, u32[]{:S(2)}, u32[]{:S(2)}) collective-permute-start(bf16[64,2048]{1,0:T(8,128)(2,1)S(1)} %collective-permute-done.76), channel_id=1, source_target_pairs={{0,2},{2,4},{4,6},{6,7},{7,5},{5,3},{3,1},{1,0},{8,10},{10,12},{12... | collective-permute-start | bytes 786440 | tf_op jit(solution)/shard_map/ppermute | solution.py:873
  657.8 17.4 %collective-permute-start.27 = (bf16[264,512]{1,0:T(8,128)(2,1)S(1)}, bf16[264,512]{1,0:T(8,128)(2,1)S(1)}, u32[]{:S(2)}, u32[]{:S(2)}) collective-permute-start(bf16[264,512]{1,0:T(8,128)(2,1)S(1)} %add_convert_fusion.15), channel_id=1, source_target_pairs={{0,2},{2,4},{4,6},{6,7},{7,5},{5,3},{3,1},{1,0},{8,10},{10,12},{12... | collective-permute-start | bytes 811016 | tf_op jit(solution)/shard_map/ppermute | solution.py:850
  659.1 63.1 %collective-permute-start.79 = (bf16[64,2048]{1,0:T(8,128)(2,1)S(1)}, bf16[64,2048]{1,0:T(8,128)(2,1)S(1)}, u32[]{:S(2)}, u32[]{:S(2)}) collective-permute-start(bf16[64,2048]{1,0:T(8,128)(2,1)S(1)} %collective-permute-done.77), channel_id=1, source_target_pairs={{0,1},{2,0},{4,2},{6,4},{7,6},{5,7},{3,5},{1,3},{8,9},{10,8},{12,1... | collective-permute-start | bytes 786440 | tf_op jit(solution)/shard_map/ppermute | solution.py:873
  661.8 35.2 %collective-permute-start.34 = (bf16[264,512]{1,0:T(8,128)(2,1)S(1)}, bf16[264,512]{1,0:T(8,128)(2,1)S(1)}, u32[]{:S(2)}, u32[]{:S(2)}) collective-permute-start(bf16[264,512]{1,0:T(8,128)(2,1)S(1)} %add_convert_fusion.8), channel_id=1, source_target_pairs={{0,1},{2,0},{4,2},{6,4},{7,6},{5,7},{3,5},{1,3},{8,9},{10,8},{12,1... | collective-permute-start | bytes 811016 | tf_op jit(solution)/shard_map/ppermute | solution.py:850
  675.3 22.0 %collective-permute-start.28 = (bf16[264,512]{1,0:T(8,128)(2,1)S(1)}, bf16[264,512]{1,0:T(8,128)(2,1)S(1)}, u32[]{:S(2)}, u32[]{:S(2)}) collective-permute-start(bf16[264,512]{1,0:T(8,128)(2,1)S(1)} %add_convert_fusion.14), channel_id=1, source_target_pairs={{0,2},{2,4},{4,6},{6,7},{7,5},{5,3},{3,1},{1,0},{8,10},{10,12},{12... | collective-permute-start | bytes 811016 | tf_op jit(solution)/shard_map/ppermute | solution.py:850
  697.1 17.7 %collective-permute-start.35 = (bf16[264,512]{1,0:T(8,128)(2,1)S(1)}, bf16[264,512]{1,0:T(8,128)(2,1)S(1)}, u32[]{:S(2)}, u32[]{:S(2)}) collective-permute-start(bf16[264,512]{1,0:T(8,128)(2,1)S(1)} %add_convert_fusion.7), channel_id=1, source_target_pairs={{0,1},{2,0},{4,2},{6,4},{7,6},{5,7},{3,5},{1,3},{8,9},{10,8},{12,1... | collective-permute-start | bytes 811016 | tf_op jit(solution)/shard_map/ppermute | solution.py:850
  697.5 19.4 %collective-permute-start.29 = (bf16[264,512]{1,0:T(8,128)(2,1)S(1)}, bf16[264,512]{1,0:T(8,128)(2,1)S(1)}, u32[]{:S(2)}, u32[]{:S(2)}) collective-permute-start(bf16[264,512]{1,0:T(8,128)(2,1)S(1)} %add_convert_fusion.13), channel_id=1, source_target_pairs={{0,2},{2,4},{4,6},{6,7},{7,5},{5,3},{3,1},{1,0},{8,10},{10,12},{12... | collective-permute-start | bytes 811016 | tf_op jit(solution)/shard_map/ppermute | solution.py:850
  (114 other events, 1726.1 us)
Sparse Core Ops, SparseCore 0:
  513.1 208.5 all-reduce.2

commit v2 on v1

v2 whole, which is shorter than its diff:
```python
import math

import jax
import jax.numpy as jnp
from jax import lax
from jax.experimental import pallas as pl
from jax.experimental.pallas import tpu as pltpu
from jax.sharding import PartitionSpec as P

HEAD_DIM = 64
EPSILON = 1e-06
F32 = jnp.float32
BF16 = jnp.bfloat16
MIB = 1 << 20
VMEM_MIB = 62
TILE = 16
MICRO = 2
SPARE = MICRO
RANK, ACTIVE, UNITS = 0, 1, 3
LN1G, LN1B, OUTB, SATT, LN2G, LN2B, FC2B, SMLP = range(8)


def dot(left, right):
    return jnp.dot(left, right, preferred_element_type=F32)


def dot_nt(left, right):
    return lax.dot_general(left, right, (((1,), (1,)), ((), ())), preferred_element_type=F32)


def dot_tn(left, right):
    return lax.dot_general(left, right, (((0,), (0,)), ((), ())), preferred_element_type=F32)


def norm_stats(values):
    centre = jnp.mean(values, axis=-1, keepdims=True)
    centred = values - centre
    spread = jnp.mean(centred * centred, axis=-1, keepdims=True)
    scale = lax.rsqrt(spread + EPSILON)
    return centred * scale, scale


def tiles(rows):
    return [slice(r, r + TILE) for r in range(0, rows, TILE)]


def eights(values):
    total = values[:8]
    for r in range(8, values.shape[0], 8):
        total = total + values[r : r + 8]
    return total


def norm_backward(hat, scale, gain, error):
    weighted = error * gain
    mean_one = jnp.mean(weighted, axis=-1, keepdims=True)
    mean_two = jnp.mean(weighted * hat, axis=-1, keepdims=True)
    return scale * (weighted - mean_one - hat * mean_two)


def col_sum(values):
    return jnp.sum(values, axis=0, keepdims=True)


def call(kernel, scalars, grid, ins, outs, scratch=(), flops=0, moved=0):
    arrays = [a for a, _, _ in ins]
    in_specs = [pl.BlockSpec(b, m) for _, b, m in ins]
    aliases = {}
    for number, out in enumerate(outs):
        if out[4] is not None:
            aliases[1 + len(arrays)] = number
            arrays.append(out[4])
            in_specs.append(pl.BlockSpec(memory_space=pl.ANY))
    extra = len(aliases)
    in_count = len(ins)

    def body(*refs):
        kernel(*refs[: 1 + in_count], *refs[1 + in_count + extra :])

    return pl.pallas_call(
        body,
        out_shape=[jax.ShapeDtypeStruct(s, d) for s, d, _, _, _ in outs],
        grid_spec=pltpu.PrefetchScalarGridSpec(
            num_scalar_prefetch=1,
            grid=grid,
            in_specs=in_specs,
            out_specs=[pl.BlockSpec(b, m) for _, _, b, m, _ in outs],
            scratch_shapes=list(scratch),
        ),
        input_output_aliases=aliases,
        compiler_params=pltpu.CompilerParams(
            dimension_semantics=("arbitrary",) * len(grid), vmem_limit_bytes=VMEM_MIB * MIB
        ),
        cost_estimate=pl.CostEstimate(
            flops=int(flops), bytes_accessed=int(moved), transcendentals=0
        ),
    )(scalars, *arrays)


def manual(kernel, scalars, ins, outs, scratch, flops=0, moved=0, vmem=VMEM_MIB):
    any_space = pl.BlockSpec(memory_space=pl.ANY)
    vmem_space = pl.BlockSpec(memory_space=pltpu.VMEM)
    arrays = [a for a, _ in ins]
    in_specs = [vmem_space if inside else any_space for _, inside in ins]
    aliases = {}
    for number, out in enumerate(outs):
        if out[3] is not None:
            aliases[1 + len(arrays)] = number
            arrays.append(out[3])
            in_specs.append(any_space)
    extra = len(aliases)
    in_count = len(ins)

    def body(*refs):
        kernel(*refs[: 1 + in_count], *refs[1 + in_count + extra :])

    return pl.pallas_call(
        body,
        out_shape=[jax.ShapeDtypeStruct(s, d) for s, d, _, _ in outs],
        in_specs=[pl.BlockSpec(memory_space=pltpu.SMEM)] + in_specs,
        out_specs=[vmem_space if inside else any_space for _, _, inside, _ in outs],
        scratch_shapes=list(scratch),
        input_output_aliases=aliases,
        compiler_params=pltpu.CompilerParams(vmem_limit_bytes=vmem * MIB),
        cost_estimate=pl.CostEstimate(
            flops=int(flops), bytes_accessed=int(moved), transcendentals=0
        ),
    )(scalars, *arrays)


def begin(src, dst, sem):
    copy = pltpu.make_async_copy(src, dst, sem)
    copy.start()
    return copy


def dma_sems(count):
    return pltpu.SemaphoreType.DMA((count,))


def whole2(i, s):
    return (0, 0)


def slot3(i, s):
    return (s[0], 0, 0)


def token_copies(s, source, number, refs, target, sems):
    rows, width = target.shape
    half = width // 2
    rank = s[RANK]
    if source == "relay":
        return [begin(refs[0], target, sems.at[0])]
    first = pl.multiple_of(rank * half, half)
    second = pl.multiple_of((1 - rank) * half, half)
    whole, other = refs
    return [
        begin(
            whole.at[number, 0, pl.ds(pl.multiple_of(rank * rows, rows), rows)],
            target.at[:, pl.ds(first, half)],
            sems.at[0],
        ),
        begin(other, target.at[:, pl.ds(second, half)], sems.at[1]),
    ]


def norm_kv(info, owner, number, source, tokens, vec, w_own, w_oth, bias_v, kept):
    rows, width = tokens[-1].shape[0], vec.shape[1]
    half = width // 2
    count = len(tokens)

    def kernel(s, *refs):
        token_refs = refs[:count]
        (v, own, oth, bv, x_out, n_out, kv_out, x_v, n_v, w_v, kv_v, tok_sems, w_sems,
         out_sems) = refs[count:]

        @pl.when(s[ACTIVE + owner] == 1)
        def _():
            arriving = token_copies(s, source, number, token_refs, x_v, tok_sems)
            loads = []
            for part in range(4):
                ref = own if part < 2 else oth
                loads.append(begin(ref.at[1 + part % 2], w_v.at[part], w_sems.at[part]))
            for copy in arriving:
                copy.wait()
            outs = [begin(x_v, x_out.at[number], out_sems.at[0])]
            for t in tiles(rows):
                hat, _ = norm_stats(x_v[t].astype(F32))
                n_v[t] = (hat * v[LN1G : LN1G + 1] + v[LN1B : LN1B + 1]).astype(BF16)
            outs.append(begin(n_v, n_out.at[number], out_sems.at[1]))
            for part in range(4):
                loads[part].wait()
                result = dot(n_v[...], w_v[part])
                kind, side = part % 2, part // 2
                columns = slice(side * half, (side + 1) * half)
                if kind == 1:
                    result = result + bv[:, columns]
                kv_v[part] = result.astype(BF16)
                outs.append(
                    begin(
                        kv_v.at[part],
                        kv_out.at[kind, :, pl.ds(side * half, half)],
                        out_sems.at[2 + part],
                    )
                )
            for copy in outs:
                copy.wait()

    stack = (MICRO, rows, width)
    return manual(
        kernel,
        info,
        [(array, False) for array in tokens]
        + [(vec, True), (w_own, False), (w_oth, False), (bias_v, True)],
        [
            (stack, BF16, False, kept.get("x")),
            (stack, BF16, False, kept.get("normed1")),
            ((2, rows, width), BF16, False, None),
        ],
        [
            pltpu.VMEM((rows, width), BF16),
            pltpu.VMEM((rows, width), BF16),
            pltpu.VMEM((4, width, half), BF16),
            pltpu.VMEM((4, rows, half), BF16),
            dma_sems(2),
            dma_sems(4),
            dma_sems(6),
        ],
        flops=2 * rows * width * 2 * width,
        moved=4 * width * width + 10 * rows * width,
    )


def project_q(info, owner, number, normed, w_own, w_oth, bias_q, kept):
    _, rows, width = normed.shape
    half = width // 2

    def kernel(s, n, own, oth, bq, q_out, n_v, w_v, q_v, in_sems, out_sems):
        @pl.when(s[ACTIVE + owner] == 1)
        def _():
            load = begin(n.at[number], n_v, in_sems.at[0])
            loads = [
                begin(own.at[0], w_v.at[0], in_sems.at[1]),
                begin(oth.at[0], w_v.at[1], in_sems.at[2]),
            ]
            load.wait()
            outs = []
            for side in range(2):
                loads[side].wait()
                columns = slice(side * half, (side + 1) * half)
                q_v[side] = (dot(n_v[...], w_v[side]) + bq[:, columns]).astype(BF16)
                outs.append(
                    begin(
                        q_v.at[side],
                        q_out.at[number, :, pl.ds(side * half, half)],
                        out_sems.at[side],
                    )
                )
            for copy in outs:
                copy.wait()

    return manual(
        kernel,
        info,
        [(normed, False), (w_own, False), (w_oth, False), (bias_q, True)],
        [((MICRO, rows, width), BF16, False, kept.get("q"))],
        [
            pltpu.VMEM((rows, width), BF16),
            pltpu.VMEM((2, width, half), BF16),
            pltpu.VMEM((2, rows, half), BF16),
            dma_sems(3),
            dma_sems(2),
        ],
        flops=2 * rows * width * width,
        moved=2 * width * width + 4 * rows * width,
    )[0]


def attend(info, owner, number, q, kv_here, kv_there, kept):
    _, rows, width = q.shape
    heads = width // HEAD_DIM
    factor = HEAD_DIM**-0.5 * math.log2(math.e)
    lanes = 2 * HEAD_DIM
    block = 2 * lanes
    steps = width // block

    def kernel(s, *refs):
        @pl.when(s[ACTIVE + owner] == 1)
        def _():
            compute(*refs)

    def compute(q_ref, here, there, e_out, o_out, mixed_out, inv_out, kv_out, *scratch):
        scores, results = scratch[:4], scratch[4:]
        kv_out[0, :, :rows] = here[...]
        kv_out[0, :, rows:] = there[...]
        first_q = lax.broadcasted_iota(jnp.int32, (rows, lanes), 1) < HEAD_DIM
        first_k = lax.broadcasted_iota(jnp.int32, (2 * rows, lanes), 1) < HEAD_DIM
        first_t = lax.broadcasted_iota(jnp.int32, (TILE, lanes), 1) < HEAD_DIM

        def columns(head):
            return slice(head // 2 * lanes, (head // 2 + 1) * lanes)

        def score(head):
            mine = first_q if head % 2 == 0 else ~first_q
            masked = jnp.where(mine, q_ref[0, :, columns(head)], 0)
            scores[head][...] = dot_nt(masked, kv_out[0, 0, :, columns(head)])

        score(0)
        for head in range(4):
            if head < 3:
                score(head + 1)
            for t in tiles(rows):
                tile = scores[head][t]
                top = jnp.max(tile, axis=-1, keepdims=True)
                e_out[0, head, t] = jnp.exp2((tile - top) * factor).astype(BF16)
            mine = first_k if head % 2 == 0 else ~first_k
            values = jnp.where(mine, kv_out[0, 1, :, columns(head)], 1)
            results[head][...] = dot(e_out[0, head], values)
        for pair in range(2):
            place = slice(pair * lanes, (pair + 1) * lanes)
            for t in tiles(rows):
                one, two = results[2 * pair][t], results[2 * pair + 1][t]
                total = jnp.where(
                    first_t, pltpu.roll(one, HEAD_DIM, 1), pltpu.roll(two, HEAD_DIM, 1)
                )
                inverse = 1.0 / total
                mixed = jnp.where(first_t, one, two) * inverse
                o_out[0, t, place] = mixed
                mixed_out[t, place] = mixed.astype(BF16)
                inv_out[0, t, place] = inverse

    def on(s):
        return s[ACTIVE + owner]

    def slot(s):
        return jnp.where(on(s) == 1, number, SPARE)

    column = lambda i, s: (slot(s), 0, i * on(s))
    spare = MICRO + 1
    return call(
        kernel,
        info,
        (steps,),
        [
            (q, (1, rows, block), lambda i, s: (number, 0, i * on(s))),
            (kv_here, (2, rows, block), lambda i, s: (0, 0, i * on(s))),
            (
                kv_there,
                (2, rows, block),
                lambda i, s: (0, 0, lax.rem(i + steps // 2, steps) * on(s)),
            ),
        ],
        [
            (
                (spare, heads, rows, 2 * rows),
                BF16,
                (1, 4, rows, 2 * rows),
                lambda i, s: (slot(s), i * on(s), 0, 0),
                kept.get("grown"),
            ),
            ((spare, rows, width), F32, (1, rows, block), column, kept.get("mixed_full")),
            ((rows, width), BF16, (rows, block), lambda i, s: (0, i * on(s)), None),
            ((spare, rows, width), F32, (1, rows, block), column, kept.get("inverse")),
            (
                (spare, 2, 2 * rows, width),
                BF16,
                (1, 2, 2 * rows, block),
                lambda i, s: (slot(s), 0, 0, i * on(s)),
                kept.get("kv"),
            ),
        ],
        [pltpu.VMEM((rows, 2 * rows), F32)] * 4 + [pltpu.VMEM((rows, lanes), F32)] * 4,
        flops=8 * rows * rows * width,
        moved=4 * heads * rows * rows + 30 * rows * width,
    )


def gelu_parts(x):
    size = jnp.abs(x)
    base = 1.0 + (0.3275911 * math.sqrt(0.5)) * size
    t = pl.reciprocal(base, approx=True)
    t = t * (2.0 - base * t)
    grown = jnp.exp2(x * x * (-0.5 * math.log2(math.e)))
    poly = 0.5 * 1.061405429
    for factor in (-1.453152027, 1.421413741, -0.284496736, 0.254829592):
        poly = poly * t + 0.5 * factor
    tail = poly * t * grown
    below = jnp.where(x < 0.0, tail, 1.0 - tail)
    return x * below, below + x * grown * (1.0 / math.sqrt(2.0 * math.pi))


CHUNK = 512


def mlp_forward(info, owner, number, mixed, x, vec, wo_own, wo_oth, wu_own, wu_oth, wd_own, wd_oth, b_up, kept):
    _, rows, width = x.shape
    side_hidden = wu_own.shape[1]
    hidden = 2 * side_hidden
    half = width // 2
    steps = hidden // CHUNK
    split = steps // 2

    def kernel(
        s, m, x_ref, v, woo, wot, wuo, wut, wdo, wdt, bu,
        att_out, res_out, n_out, act_out, slope_out, branch_out, y_out, relay_out, m_out,
        m_v, x_v, wo_v, wu_v, wd_v, att_v, res_v, n_v, h_v, act_v, slope_v, branch_v, y_v, acc,
        in_sems, wu_sems, wd_sems, out_sems, act_sems, slope_sems,
    ):
        @pl.when(s[ACTIVE + owner] == 1)
        def _():
            slot = number
            first = [
                begin(m, m_v, in_sems.at[0]),
                begin(woo, wo_v.at[0], in_sems.at[1]),
                begin(wot, wo_v.at[1], in_sems.at[2]),
                begin(x_ref.at[slot], x_v, in_sems.at[3]),
            ]
            ups, downs = [], []

            def prefetch(i):
                if i < steps:
                    part = pl.ds((i % split) * CHUNK, CHUNK)
                    up, down = (wuo, wdo) if i < split else (wut, wdt)
                    ups.append(begin(up.at[:, part], wu_v.at[i], wu_sems.at[i]))
                    downs.append(begin(down.at[part], wd_v.at[i], wd_sems.at[i]))

            prefetch(0)
            prefetch(1)
            for copy in first:
                copy.wait()
            acc[...] = dot(m_v[:, :half], wo_v[0]) + dot(m_v[:, half:], wo_v[1])
            for t in tiles(rows):
                attended = acc[t] + v[OUTB : OUTB + 1]
                att_v[t] = attended.astype(BF16)
                residual = x_v[t].astype(F32) + v[SATT : SATT + 1] * attended
                res_v[t] = residual
                hat, _ = norm_stats(residual)
                n_v[t] = (hat * v[LN2G : LN2G + 1] + v[LN2B : LN2B + 1]).astype(BF16)
            outs = [
                begin(att_v, att_out.at[slot], out_sems.at[0]),
                begin(res_v, res_out.at[slot], out_sems.at[1]),
                begin(n_v, n_out.at[slot], out_sems.at[2]),
                begin(m_v, m_out.at[slot], out_sems.at[6]),
            ]

            def up_product(i):
                ups[i].wait()
                h_v[i % 2] = dot(n_v[...], wu_v[i])

            def down_product(i):
                downs[i].wait()
                part = pl.ds(i * CHUNK, CHUNK)
                outs.append(begin(act_v.at[i], act_out.at[slot, :, part], act_sems.at[i]))
                outs.append(begin(slope_v.at[i], slope_out.at[slot, :, part], slope_sems.at[i]))
                product = dot(act_v[i], wd_v[i])
                acc[...] = product if i == 0 else acc[...] + product

            up_product(0)
            for i in range(steps):
                prefetch(i + 2)
                if i > 0:
                    down_product(i - 1)
                if i + 1 < steps:
                    up_product(i + 1)
                for t in tiles(rows):
                    active, slope = gelu_parts(h_v[i % 2, t] + bu[i : i + 1])
                    act_v[i, t] = active.astype(BF16)
                    slope_v[i, t] = slope.astype(BF16)
            down_product(steps - 1)
            for t in tiles(rows):
                branch = acc[t] + v[FC2B : FC2B + 1]
                y_v[t] = (res_v[t] + v[SMLP : SMLP + 1] * branch).astype(BF16)
                branch_v[t] = branch.astype(BF16)
            outs.append(begin(y_v, relay_out, out_sems.at[3]))
            outs.append(begin(y_v, y_out.at[slot], out_sems.at[4]))
            outs.append(begin(branch_v, branch_out.at[slot], out_sems.at[5]))
            for copy in outs:
                copy.wait()

    stack = (MICRO, rows, width)
    tall = (MICRO, rows, hidden)
    plain = pltpu.VMEM((rows, width), BF16)
    full = pltpu.VMEM((rows, width), F32)
    chunks = pltpu.VMEM((steps, rows, CHUNK), BF16)
    return manual(
        kernel,
        info,
        [
            (mixed, False),
            (x, False),
            (vec, True),
            (wo_own, False),
            (wo_oth, False),
            (wu_own, False),
            (wu_oth, False),
            (wd_own, False),
            (wd_oth, False),
            (b_up, True),
        ],
        [
            (stack, BF16, False, kept.get("attended")),
            (stack, F32, False, kept.get("residual")),
            (stack, BF16, False, kept.get("normed2")),
            (tall, BF16, False, kept.get("active")),
            (tall, BF16, False, kept.get("slope")),
            (stack, BF16, False, kept.get("branch")),
            (stack, BF16, False, kept.get("output")),
            ((rows, width), BF16, False, None),
            (stack, BF16, False, kept.get("mixed")),
        ],
        [
            plain,
            plain,
            pltpu.VMEM((2, half, width), BF16),
            pltpu.VMEM((steps, width, CHUNK), BF16),
            pltpu.VMEM((steps, CHUNK, width), BF16),
            plain,
            full,
            plain,
            pltpu.VMEM((2, rows, CHUNK), F32),
            chunks,
            chunks,
            plain,
            plain,
            full,
            dma_sems(4),
            dma_sems(steps),
            dma_sems(steps),
            dma_sems(7),
            dma_sems(steps),
            dma_sems(steps),
        ],
        flops=4 * rows * width * hidden + 2 * rows * width * width,
        moved=4 * width * hidden + 2 * width * width + 8 * rows * hidden,
    )


def scale_branch(info, owner, number, relay, vec, earlier):
    rows, width = relay.shape

    def kernel(s, g, v, gb_out, g_v, gb_v, sems):
        @pl.when(s[ACTIVE + owner] == 1)
        def _():
            begin(g, g_v, sems.at[0]).wait()
            gb_v[...] = (v[SMLP : SMLP + 1] * g_v[...].astype(F32)).astype(BF16)
            begin(gb_v, gb_out.at[number], sems.at[1]).wait()

    return manual(
        kernel,
        info,
        [(relay, False), (vec, True)],
        [((MICRO, rows, width), BF16, False, earlier)],
        [pltpu.VMEM((rows, width), BF16), pltpu.VMEM((rows, width), BF16), dma_sems(2)],
        moved=4 * rows * width,
    )[0]


def mlp_backward(info, owner, number, source, tokens, vec, wo_own, wo_oth, wu_own, wu_oth, wd_own, wd_oth, kept, grads, scaled):
    count = len(tokens)
    _, rows, width = kept["x"].shape
    side_hidden = wu_own.shape[1]
    hidden = 2 * side_hidden
    half = width // 2
    steps = hidden // CHUNK
    split = steps // 2

    def kernel(s, *refs):
        work(s, refs[:count], *refs[count:])

    def work(
        s, token_refs, branch, slope, res, att, v, woo, wot, wuo, wut, wdo, wdt,
        gb_out, before_out, ga_out, gm_out, gr_out, small_out, shift_out,
        g_v, branch_v, slope_v, res_v, att_v, wo_v, wu_v, wd_v, gb_v, d_v, before_v, ga_v, gm_v,
        gr_v, acc, sums, tok_sems, in_sems, slope_sems, wu_sems, wd_sems, out_sems, before_sems,
    ):
        @pl.when(s[ACTIVE + owner] == 0)
        def _():
            small_out[...] = jnp.zeros_like(small_out)
            shift_out[...] = jnp.zeros_like(shift_out)

        @pl.when(s[ACTIVE + owner] == 1)
        def _():
            slot = number
            arriving = token_copies(s, source, number, token_refs, g_v, tok_sems)
            ups, downs, slopes = [], [], []

            def prefetch(i):
                if i < steps:
                    part = pl.ds((i % split) * CHUNK, CHUNK)
                    up, down = (wuo, wdo) if i < split else (wut, wdt)
                    here = pl.ds(i * CHUNK, CHUNK)
                    downs.append(begin(down.at[part], wd_v.at[i], wd_sems.at[i]))
                    slopes.append(begin(slope.at[slot, :, here], slope_v.at[i], slope_sems.at[i]))
                    ups.append(begin(up.at[:, part], wu_v.at[i], wu_sems.at[i]))

            prefetch(0)
            branch_in = begin(branch.at[slot], branch_v, in_sems.at[0])
            prefetch(1)
            last = []
            for copy in arriving:
                copy.wait()
            for t in tiles(rows):
                gb_v[t] = (v[SMLP : SMLP + 1] * g_v[t].astype(F32)).astype(BF16)
            outs = []
            if not scaled:
                outs.append(begin(gb_v, gb_out.at[slot], out_sems.at[0]))

            def down_product(i):
                downs[i].wait()
                d_v[i % 2] = dot_nt(gb_v[...], wd_v[i])

            down_product(0)
            branch_in.wait()
            sums[...] = jnp.zeros_like(sums)
            for t in tiles(rows):
                sums[0] += eights(g_v[t].astype(F32) * branch_v[t].astype(F32))
                sums[1] += eights(gb_v[t].astype(F32))

            def up_product(i):
                ups[i].wait()
                part = pl.ds(i * CHUNK, CHUNK)
                outs.append(begin(before_v.at[i], before_out.at[slot, :, part], before_sems.at[i]))
                product = dot_nt(before_v[i], wu_v[i])
                acc[...] = product if i == 0 else acc[...] + product

            for i in range(steps):
                prefetch(i + 2)
                if i == steps - 2:
                    last = [
                        begin(res.at[slot], res_v, in_sems.at[1]),
                        begin(att.at[slot], att_v, in_sems.at[2]),
                        begin(woo, wo_v.at[0], in_sems.at[3]),
                        begin(wot, wo_v.at[1], in_sems.at[4]),
                    ]
                slopes[i].wait()
                if i > 0:
                    up_product(i - 1)
                if i + 1 < steps:
                    down_product(i + 1)
                total = jnp.zeros((8, CHUNK), F32)
                for t in tiles(rows):
                    grad_before = (d_v[i % 2, t] * slope_v[i, t].astype(F32)).astype(BF16)
                    before_v[i, t] = grad_before
                    total = total + eights(grad_before.astype(F32))
                shift_out[i : i + 1] = col_sum(total)
            up_product(steps - 1)
            for copy in last:
                copy.wait()
            for t in tiles(rows):
                hat, scale = norm_stats(res_v[t])
                error = acc[t]
                sums[2] += eights(error * hat)
                sums[3] += eights(error)
                grad = g_v[t].astype(F32) + norm_backward(hat, scale, v[LN2G : LN2G + 1], error)
                gr_v[t] = grad
                sums[4] += eights(grad * att_v[t].astype(F32))
                ga = (v[SATT : SATT + 1] * grad).astype(BF16)
                ga_v[t] = ga
                sums[5] += eights(ga.astype(F32))
            outs.append(begin(ga_v, ga_out.at[slot], out_sems.at[1]))
            outs.append(begin(gr_v, gr_out, out_sems.at[3]))
            gm_v[:, :half] = dot_nt(ga_v[...], wo_v[0]).astype(BF16)
            gm_v[:, half:] = dot_nt(ga_v[...], wo_v[1]).astype(BF16)
            outs.append(begin(gm_v, gm_out, out_sems.at[2]))
            small_out[...] = jnp.zeros_like(small_out)
            for row in range(6):
                small_out[row : row + 1] = col_sum(sums[row])
            for copy in outs:
                copy.wait()

    stack = (MICRO, rows, width)
    plain = pltpu.VMEM((rows, width), BF16)
    full = pltpu.VMEM((rows, width), F32)
    chunks = pltpu.VMEM((steps, rows, CHUNK), BF16)
    return manual(
        kernel,
        info,
        [(array, False) for array in tokens]
        + [
            (kept["branch"], False),
            (kept["slope"], False),
            (kept["residual"], False),
            (kept["attended"], False),
            (vec, True),
            (wo_own, False),
            (wo_oth, False),
            (wu_own, False),
            (wu_oth, False),
            (wd_own, False),
            (wd_oth, False),
        ],
        [
            (stack, BF16, False, None if scaled else grads.get("branch")),
            ((MICRO, rows, hidden), BF16, False, grads.get("before")),
            (stack, BF16, False, grads.get("attended")),
            ((rows, width), BF16, False, None),
            ((rows, width), F32, False, None),
            ((8, width), F32, True, None),
            ((steps, CHUNK), F32, True, None),
        ],
        [
            plain,
            plain,
            chunks,
            full,
            plain,
            pltpu.VMEM((2, half, width), BF16),
            pltpu.VMEM((steps, width, CHUNK), BF16),
            pltpu.VMEM((steps, CHUNK, width), BF16),
            plain,
            pltpu.VMEM((2, rows, CHUNK), F32),
            chunks,
            plain,
            plain,
            full,
            full,
            pltpu.VMEM((6, 8, width), F32),
            dma_sems(2),
            dma_sems(5),
            dma_sems(steps),
            dma_sems(steps),
            dma_sems(steps),
            dma_sems(4),
            dma_sems(steps),
        ],
        flops=4 * rows * width * hidden + 2 * rows * width * width,
        moved=4 * width * hidden + 2 * width * width + 8 * rows * hidden,
    )


def attend_backward(info, owner, number, grad_mixed, kept):
    _, rows, width = kept["q"].shape
    heads = width // HEAD_DIM
    lanes = 2 * HEAD_DIM
    block = 2 * lanes
    steps = width // block
    score_scale = HEAD_DIM**-0.5

    def kernel(s, *refs):
        @pl.when(s[ACTIVE + owner] == 1)
        def _():
            compute(*refs)

    def compute(gm, q_ref, kv, grown, full, inv, dq_out, here_out, there_out, *scratch):
        probs, scores = scratch[:4], scratch[4:8]
        own_v, centre_v = scratch[8:]
        first_q = lax.broadcasted_iota(jnp.int32, (rows, lanes), 1) < HEAD_DIM
        first_t = lax.broadcasted_iota(jnp.int32, (TILE, lanes), 1) < HEAD_DIM

        def columns(head):
            return slice(head // 2 * lanes, (head // 2 + 1) * lanes)

        for pair in range(2):
            place = columns(2 * pair)
            for t in tiles(rows):
                scaled = (gm[t, place].astype(F32) * inv[0, t, place]).astype(BF16)
                product = scaled.astype(F32) * full[0, t, place]
                for side in range(2):
                    mine = first_t if side == 0 else ~first_t
                    own_v[2 * pair + side, t] = jnp.where(mine, scaled, 0)
                    centre_v[2 * pair + side, t] = jnp.sum(
                        jnp.where(mine, product, 0.0), axis=-1, keepdims=True
                    )

        def prob(head):
            probs[head][...] = dot_nt(own_v[head], kv[0, 1, :, columns(head)])

        prob(0)
        grad_q, grad_k, grad_v = [], [], []
        for head in range(4):
            if head < 3:
                prob(head + 1)
            for t in tiles(rows):
                weight = grown[0, head, t].astype(F32)
                scores[head][t] = (weight * (probs[head][t] - centre_v[head, t])).astype(BF16)
            mine = first_q if head % 2 == 0 else ~first_q
            grad_v.append(dot_tn(grown[0, head], own_v[head]))
            grad_q.append(dot(scores[head][...], kv[0, 0, :, columns(head)]))
            masked = jnp.where(mine, q_ref[0, :, columns(head)], 0)
            grad_k.append(dot_tn(scores[head][...], masked))
            if head % 2 == 1:
                place = columns(head)
                dq = jnp.where(first_q, grad_q[head - 1], grad_q[head]) * score_scale
                dq_out[:, place] = dq.astype(BF16)
                dk = ((grad_k[head - 1] + grad_k[head]) * score_scale).astype(BF16)
                dv = (grad_v[head - 1] + grad_v[head]).astype(BF16)
                here_out[0, :, place] = dk[:rows]
                here_out[1, :, place] = dv[:rows]
                there_out[0, :, place] = dk[rows:]
                there_out[1, :, place] = dv[rows:]

    def on(s):
        return s[ACTIVE + owner]

    def slot(s):
        return jnp.where(on(s) == 1, number, SPARE)

    column = lambda i, s: (slot(s), 0, i * on(s))
    plain = lambda i, s: (0, i * on(s))
    return call(
        kernel,
        info,
        (steps,),
        [
            (grad_mixed, (rows, block), plain),
            (kept["q"], (1, rows, block), lambda i, s: (number, 0, i * on(s))),
            (kept["kv"], (1, 2, 2 * rows, block), lambda i, s: (slot(s), 0, 0, i * on(s))),
            (kept["grown"], (1, 4, rows, 2 * rows), lambda i, s: (slot(s), i * on(s), 0, 0)),
            (kept["mixed_full"], (1, rows, block), column),
            (kept["inverse"], (1, rows, block), column),
        ],
        [
            ((rows, width), BF16, (rows, block), plain, None),
            ((2, rows, width), BF16, (2, rows, block), lambda i, s: (0, 0, i * on(s)), None),
            ((2, rows, width), BF16, (2, rows, block), lambda i, s: (0, 0, i * on(s)), None),
        ],
        [pltpu.VMEM((rows, 2 * rows), F32)] * 4
        + [pltpu.VMEM((rows, 2 * rows), BF16)] * 4
        + [pltpu.VMEM((4, rows, lanes), BF16), pltpu.VMEM((4, rows, 1), F32)],
        flops=16 * rows * rows * width,
        moved=4 * heads * rows * rows + 30 * rows * width,
    )


def qkv_backward(info, owner, number, dq, dkv_here, dkv_there, w_own, w_oth, grad_res, vec, kept, grads):
    _, rows, width = kept["x"].shape
    half = width // 2

    def kernel(s, dq_ref, here, there, own, oth, gr, x_ref, v, packed_out, gx_out, relay_out,
               small_out, shift_out, a_v, b_v, p_v, w_v, gr_v, x_v, gx_v, acc, sums,
               a_sems, b_sems, w_sems, in_sems, packed_sems, out_sems):
        @pl.when(s[ACTIVE + owner] == 0)
        def _():
            small_out[...] = jnp.zeros_like(small_out)
            shift_out[...] = jnp.zeros_like(shift_out)

        @pl.when(s[ACTIVE + owner] == 1)
        def _():
            slot = number
            loads = []
            for part in range(6):
                kind, side = part % 3, part // 3
                columns = pl.ds(side * half, half)
                if kind == 0:
                    copies = [begin(dq_ref.at[:, columns], a_v.at[part], a_sems.at[part])]
                else:
                    turned = pl.ds((1 - side) * half, half)
                    copies = [
                        begin(here.at[kind - 1, :, columns], a_v.at[part], a_sems.at[part]),
                        begin(there.at[kind - 1, :, turned], b_v.at[part], b_sems.at[part]),
                    ]
                weight = own if side == 0 else oth
                copies.append(begin(weight.at[kind], w_v.at[part], w_sems.at[part]))
                loads.append(copies)
            last = [
                begin(x_ref.at[slot], x_v, in_sems.at[0]),
                begin(gr, gr_v, in_sems.at[1]),
            ]
            outs = []
            for part in range(6):
                for copy in loads[part]:
                    copy.wait()
                total = jnp.zeros((8, half), F32)
                for t in tiles(rows):
                    packed = a_v[part, t]
                    if part % 3 > 0:
                        packed = (packed.astype(F32) + b_v[part, t].astype(F32)).astype(BF16)
                    p_v[part, t] = packed
                    total = total + eights(packed.astype(F32))
                shift_out[part : part + 1] = col_sum(total)
                outs.append(
                    begin(
                        p_v.at[part],
                        packed_out.at[slot, :, pl.ds(part * half, half)],
                        packed_sems.at[part],
                    )
                )
                product = dot_nt(p_v[part], w_v[part])
                acc[...] = product if part == 0 else acc[...] + product
            for copy in last:
                copy.wait()
            sums[...] = jnp.zeros_like(sums)
            for t in tiles(rows):
                hat, scale = norm_stats(x_v[t].astype(F32))
                error = acc[t]
                grad = gr_v[t] + norm_backward(hat, scale, v[LN1G : LN1G + 1], error)
                gx_v[t] = grad.astype(BF16)
                sums[0] += eights(error * hat)
                sums[1] += eights(error)
            outs.append(begin(gx_v, relay_out, out_sems.at[0]))
            outs.append(begin(gx_v, gx_out.at[slot], out_sems.at[1]))
            small_out[...] = jnp.zeros_like(small_out)
            for row in range(2):
                small_out[row : row + 1] = col_sum(sums[row])
            for copy in outs:
                copy.wait()

    stack = (MICRO, rows, width)
    parts = pltpu.VMEM((6, rows, half), BF16)
    return manual(
        kernel,
        info,
        [
            (dq, False),
            (dkv_here, False),
            (dkv_there, False),
            (w_own, False),
            (w_oth, False),
            (grad_res, False),
            (kept["x"], False),
            (vec, True),
        ],
        [
            ((MICRO, rows, 3 * width), BF16, False, grads.get("packed")),
            (stack, BF16, False, grads.get("input")),
            ((rows, width), BF16, False, None),
            ((8, width), F32, True, None),
            ((8, half), F32, True, None),
        ],
        [
            parts,
            parts,
            parts,
            pltpu.VMEM((6, width, half), BF16),
            pltpu.VMEM((rows, width), F32),
            pltpu.VMEM((rows, width), BF16),
            pltpu.VMEM((rows, width), BF16),
            pltpu.VMEM((rows, width), F32),
            pltpu.VMEM((2, 8, width), F32),
            dma_sems(6),
            dma_sems(6),
            dma_sems(6),
            dma_sems(2),
            dma_sems(6),
            dma_sems(2),
        ],
        flops=6 * rows * width * width,
        moved=6 * width * width + 16 * rows * width,
    )


def swap(block):
    return lax.ppermute(block, "tensor", [(0, 1), (1, 0)])


def ring_order(count):
    return list(range(0, count, 2)) + list(range(count - 1, 0, -2))


def tied(value, *others):
    return lax.optimization_barrier((value, *others))[0]


class Ring:
    def __init__(self, info, parts, shapes, places):
        self.info, self.parts, self.shapes, self.places = info, parts, shapes, places
        self.count = lax.axis_size("dp")
        order = ring_order(self.count)
        n = self.count
        self.chunk = parts[0][0].shape[0] // (2 * n)
        self.widths = [pair[0].shape[1] for pair in parts]
        self.signs = (1, -1)
        self.routes = [[(order[i], order[(i + s) % n]) for i in range(n)] for s in self.signs]
        self.step = 0
        self.steps = 2 * (n - 1)
        self.totals = [None] * len(shapes)
        self.moving = self.add([0, 0], None)

    def unit(self, way, ahead):
        return UNITS + way * self.count + ahead % self.count

    def add(self, ahead, arrived):
        chunk, width, parts = self.chunk, sum(self.widths), len(self.parts)
        units = [self.unit(w, ahead[w]) for w in range(2)]
        terms = 2 if arrived is None else 3

        def kernel(s, *refs):
            halves = refs[: 2 * parts]
            refs = refs[2 * parts :]
            if terms == 3:
                arrivals, refs = refs[:2], refs[2:]
            outs, (held, sems) = refs[:2], refs[2:]
            copies = []
            for w in range(2):
                rows = pl.ds(pl.multiple_of(s[units[w]] * chunk, chunk), chunk)
                base = 0
                for number, columns in enumerate(self.widths):
                    for term in range(2):
                        copies.append(
                            begin(
                                halves[2 * number + term].at[rows],
                                held.at[w, term, :, pl.ds(base, columns)],
                                sems.at[w, term, number],
                            )
                        )
                    base += columns
                if terms == 3:
                    copies.append(begin(arrivals[w], held.at[w, 2], sems.at[w, 2, 0]))
            for copy in copies:
                copy.wait()
            for w in range(2):
                for t in tiles(chunk):
                    for first in range(0, width, 512):
                        c = slice(first, min(first + 512, width))
                        total = held[w, 0, t, c].astype(F32) + held[w, 1, t, c].astype(F32)
                        if terms == 3:
                            total = total + held[w, 2, t, c].astype(F32)
                        outs[w][t, c] = total.astype(BF16)

        arrays = [(term, False) for pair in self.parts for term in pair]
        if arrived is not None:
            arrays += [(block, False) for block in arrived]
        return manual(
            kernel,
            self.info,
            arrays,
            [((chunk, width), BF16, True, None)] * 2,
            [pltpu.VMEM((2, terms, chunk, width), BF16), pltpu.SemaphoreType.DMA((2, 3, parts))],
            moved=2 * (terms + 1) * 2 * chunk * width,
            vmem=16,
        )

    def put(self, ahead, blocks):
        chunk, width = self.chunk, sum(self.widths)
        units = [self.unit(w, ahead[w]) for w in range(2)]
        count = len(self.shapes)
        pieces = sum(len(self.places.columns(c)) for c in range(count))

        def kernel(s, *refs):
            sources, outs, (held, wide, in_sems, out_sems) = (
                refs[:2],
                refs[2 : 2 + count],
                refs[2 + count :],
            )
            loads = [begin(sources[w], held.at[w], in_sems.at[w]) for w in range(2)]
            copies = []
            for w in range(2):
                loads[w].wait()
                for t in tiles(chunk):
                    for first in range(0, width, 512):
                        c = slice(first, min(first + 512, width))
                        wide[w, t, c] = held[w, t, c].astype(F32)
                number = 0
                for target in range(count):
                    for first, columns in self.places.columns(target):
                        ref = self.places.ref(
                            outs[target], target, first, columns, s[units[w]], chunk
                        )
                        copies.append(
                            begin(
                                wide.at[w, :, pl.ds(first, columns)],
                                ref,
                                out_sems.at[w, number],
                            )
                        )
                        number += 1
            for copy in copies:
                copy.wait()

        self.totals = manual(
            kernel,
            self.info,
            [(block, False) for block in blocks],
            [(shape, F32, False, old) for shape, old in zip(self.shapes, self.totals)],
            [
                pltpu.VMEM((2, chunk, width), BF16),
                pltpu.VMEM((2, chunk, width), F32),
                dma_sems(2),
                pltpu.SemaphoreType.DMA((2, pieces)),
            ],
            moved=2 * 6 * chunk * width,
            vmem=16,
        )

    def advance(self, *after):
        arrived = [lax.ppermute(self.moving[w], "dp", self.routes[w]) for w in range(2)]
        if after:
            arrived = list(lax.optimization_barrier((*arrived, *after))[:2])
        step = self.step
        if step < self.count - 1:
            self.moving = self.add([-s * (step + 1) for s in self.signs], arrived)
        else:
            if step == self.count - 1:
                self.put(self.signs, self.moving)
            self.moving = arrived
            self.put([-s * (step - self.count + 1) for s in self.signs], arrived)
        self.step += 1

    def done(self):
        return self.step == self.steps

    def finish(self):
        while not self.done():
            self.advance()
        return self.totals


class WholeRows:
    def __init__(self, width):
        self.width = width

    def columns(self, target):
        return [(0, self.width)]

    def ref(self, out, target, first, columns, unit, chunk):
        return out.at[pl.ds(pl.multiple_of(unit * chunk, chunk), chunk)]


class TailPlaces:
    def __init__(self, half, lanes):
        self.half, self.lanes = half, lanes

    def columns(self, target):
        half = self.half
        if target == 0:
            return [(j * half, half) for j in range(3)]
        return [(3 * half, half)] if target == 1 else [(4 * half, self.lanes)]

    def ref(self, out, target, first, columns, unit, chunk):
        rows = pl.ds(pl.multiple_of(unit * chunk, chunk), chunk)
        if target == 0:
            return out.at[first // self.half, rows]
        if target == 2:
            return out.at[rows]
        each = self.half // chunk
        return out.at[
            pl.ds(pl.multiple_of(lax.rem(unit, each) * chunk, chunk), chunk),
            pl.ds(pl.multiple_of(lax.div(unit, each) * self.half, self.half), self.half),
        ]


def partner_tokens(info, block, numbers):
    _, _, seq, half = block.shape
    rows = seq // 2

    def kernel(s, ref, out, sems):
        start = pl.multiple_of((1 - s[RANK]) * rows, rows)
        copies = [
            begin(ref.at[number, 0, pl.ds(start, rows)], out.at[place], sems.at[place])
            for place, number in enumerate(numbers)
        ]
        for copy in copies:
            copy.wait()

    return manual(
        kernel,
        info,
        [(block, False)],
        [((len(numbers), rows, half), BF16, False, None)],
        [dma_sems(len(numbers))],
        vmem=4,
    )[0]


def partner_features(info, block):
    micro, rows, width = block.shape
    half = width // 2

    def kernel(s, ref, out, sems):
        start = pl.multiple_of((1 - s[RANK]) * half, half)
        copies = [
            begin(ref.at[m, :, pl.ds(start, half)], out.at[m], sems.at[m]) for m in range(micro)
        ]
        for copy in copies:
            copy.wait()

    return manual(
        kernel,
        info,
        [(block, False)],
        [((micro, rows, half), BF16, False, None)],
        [dma_sems(micro)],
        vmem=4,
    )[0]


def join_tokens(info, block, received):
    micro, rows, width = block.shape
    half = width // 2

    def kernel(s, ref, other, out, sems):
        rank = s[RANK]
        features = pl.ds(pl.multiple_of(rank * half, half), half)
        here = pl.ds(pl.multiple_of(rank * rows, rows), rows)
        there = pl.ds(pl.multiple_of((1 - rank) * rows, rows), rows)
        copies = []
        for m in range(micro):
            copies.append(begin(ref.at[m, :, features], out.at[0, m, 0, here], sems.at[0, m]))
            copies.append(begin(other.at[m], out.at[0, m, 0, there], sems.at[1, m]))
        for copy in copies:
            copy.wait()

    return manual(
        kernel,
        info,
        [(block, False), (received, False)],
        [((1, micro, 1, 2 * rows, half), BF16, False, None)],
        [pltpu.SemaphoreType.DMA((2, micro))],
        vmem=4,
    )[0]


LANES = 128


def gather_vectors(info, sums, rows_out):
    calls = len(sums)
    width = sums[0][0].shape[1]
    half = width // 2

    def kernel(s, *refs):
        own, oth = refs[4 * calls :]
        low = s[RANK] == 0

        def total(kind):
            blocks = [refs[4 * c + kind][...] for c in range(calls)]
            return sum(blocks[1:], blocks[0])

        two, up, one, qkv = [total(kind) for kind in range(4)]
        own[...] = jnp.zeros_like(own)
        oth[...] = jnp.zeros_like(oth)
        place = 0

        def write(first, second):
            nonlocal place
            for c in range(0, half, LANES):
                own[place : place + 1] = first[:, c : c + LANES].astype(BF16)
                oth[place : place + 1] = second[:, c : c + LANES].astype(BF16)
                place += 1

        for block, count in ((one, 2), (two, 6)):
            for row in range(count):
                line = block[row : row + 1]
                left, right = line[:, :half], line[:, half:]
                write(jnp.where(low, left, right), jnp.where(low, right, left))
        for row in range(3):
            write(qkv[row : row + 1], qkv[3 + row : 4 + row])
        hidden_rows = up.shape[0] // 2
        for row in range(hidden_rows):
            write(up[row : row + 1], up[hidden_rows + row : hidden_rows + row + 1])

    vmem = pl.BlockSpec(memory_space=pltpu.VMEM)
    return pl.pallas_call(
        kernel,
        in_specs=[pl.BlockSpec(memory_space=pltpu.SMEM)] + [vmem] * (4 * calls),
        out_specs=[vmem] * 2,
        out_shape=[jax.ShapeDtypeStruct((rows_out, LANES), BF16)] * 2,
    )(info, *[block for group in sums for block in group])


def spread_vectors(sums, half, hidden_half):
    def kernel(ref, *outs):
        def line(number, out, row=0, columns=half, first=0):
            for c in range(0, columns, LANES):
                place = (number * half + c) // LANES
                out[row : row + 1, first + c : first + c + LANES] = ref[place : place + 1]

        for number in range(8):
            line(number, outs[number])
        line(8, outs[8])
        line(10, outs[8], row=1)
        line(11, outs[9], columns=hidden_half)

    vmem = pl.BlockSpec(memory_space=pltpu.VMEM)
    shapes = [(1, half)] * 8 + [(2, half), (1, hidden_half)]
    return pl.pallas_call(
        kernel,
        in_specs=[vmem],
        out_specs=[vmem] * 10,
        out_shape=[jax.ShapeDtypeStruct(shape, F32) for shape in shapes],
    )(sums)


def pack_vectors(blocks, hidden_bias):
    half = blocks[0].shape[1]
    hidden_rows = hidden_bias.shape[1] // half
    filled = sum(b.shape[0] for b in blocks)

    def kernel(*refs):
        out = refs[-1]
        place = 0
        for ref in refs[: len(blocks)]:
            for row in range(ref.shape[0]):
                out[place : place + 1] = ref[row : row + 1].astype(F32)
                place += 1
        for row in range(hidden_rows):
            columns = slice(row * half, (row + 1) * half)
            out[place : place + 1] = refs[len(blocks)][:, columns].astype(F32)
            place += 1

    return pl.pallas_call(
        kernel, out_shape=jax.ShapeDtypeStruct((filled + hidden_rows, half), F32)
    )(*blocks, hidden_bias)


def join_vectors(scalars, own, oth, hidden_rows):
    half = own.shape[1]

    def kernel(s, own_ref, oth_ref, vec, bias_q, bias_v, bias_up):
        low = s[RANK] == 0
        vec[:, :half] = jnp.where(low, own_ref[:8], oth_ref[:8])
        vec[:, half:] = jnp.where(low, oth_ref[:8], own_ref[:8])
        for row, out in ((8, bias_q), (9, bias_v)):
            out[:, :half] = own_ref[row : row + 1]
            out[:, half:] = oth_ref[row : row + 1]
        bias_up[:hidden_rows] = own_ref[10 : 10 + hidden_rows]
        bias_up[hidden_rows:] = oth_ref[10 : 10 + hidden_rows]

    vmem = pl.BlockSpec(memory_space=pltpu.VMEM)
    return pl.pallas_call(
        kernel,
        in_specs=[pl.BlockSpec(memory_space=pltpu.SMEM), vmem, vmem],
        out_specs=[vmem] * 4,
        out_shape=[
            jax.ShapeDtypeStruct((8, 2 * half), F32),
            jax.ShapeDtypeStruct((1, 2 * half), F32),
            jax.ShapeDtypeStruct((1, 2 * half), F32),
            jax.ShapeDtypeStruct((2 * hidden_rows, half), F32),
        ],
    )(scalars, own, oth)


def shards(
    inputs,
    cotangent,
    ln1_gain,
    ln1_bias,
    qkv_weight,
    qv_bias,
    out_weight,
    out_bias,
    scale_attn,
    ln2_gain,
    ln2_bias,
    fc1_weight,
    fc1_bias,
    fc2_weight,
    fc2_bias,
    scale_mlp,
):
    micro, images, seq_len, half = inputs.shape
    assert micro == MICRO and images == 1
    width = 2 * half
    hidden_half = fc1_weight.shape[2]

    count = lax.axis_size("dp")
    order = ring_order(count)
    table = [
        [rank, int(section == 0), int(section == 1)]
        + [way * count + (order.index(i) + ahead) % count for way in range(2) for ahead in range(count)]
        for section in range(2)
        for rank in range(2)
        for i in range(count)
    ]
    info = lax.dynamic_slice(
        jnp.asarray(table, jnp.int32),
        (lax.axis_index(("section", "tensor", "dp")), 0),
        (1, len(table[0])),
        allow_negative_indices=False,
    ).reshape(-1)

    first_oth = swap(partner_tokens(info, inputs, (0,))[0])
    vectors = pack_vectors(
        [
            ln1_gain, ln1_bias, out_bias, scale_attn, ln2_gain, ln2_bias, fc2_bias, scale_mlp,
            qv_bias[0],
        ],
        fc1_bias,
    )
    vectors_oth = swap(vectors)
    wq_own = jnp.transpose(qkv_weight[0], (1, 0, 2))
    wq_oth = swap(tied(wq_own, vectors))
    vec, bias_q, bias_v, b_up = join_vectors(info, vectors, vectors_oth, hidden_half // half)
    b_up = b_up.reshape(2 * hidden_half // CHUNK, CHUNK)
    wo_own, wu_own, wd_own = out_weight[0], fc1_weight[0], fc2_weight[0]
    wo_oth = swap(tied(wo_own, first_oth, vectors_oth))
    wu_oth = swap(tied(wu_own, first_oth, vectors_oth))
    wd_oth = swap(tied(wd_own, first_oth, vectors_oth))
    second_oth = swap(partner_tokens(info, tied(inputs, wd_oth), (1,))[0])
    cot_oth = swap(partner_tokens(info, tied(cotangent, wd_oth), (0, 1)))

    kept = {}

    def forward(owner, number, source, tokens):
        kept["x"], kept["normed1"], kv_here = norm_kv(
            info, owner, number, source, tokens, vec, wq_own, wq_oth, bias_v, kept
        )
        kv_there = swap(kv_here)
        kept["q"] = project_q(info, owner, number, kept["normed1"], wq_own, wq_oth, bias_q, kept)
        kept["grown"], kept["mixed_full"], mixed, kept["inverse"], kept["kv"] = attend(
            info, owner, number, kept["q"], kv_here, kv_there, kept
        )
        (
            kept["attended"],
            kept["residual"],
            kept["normed2"],
            kept["active"],
            kept["slope"],
            kept["branch"],
            kept["output"],
            relayed,
            kept["mixed"],
        ) = mlp_forward(
            info, owner, number, mixed, kept["x"], vec, wo_own, wo_oth, wu_own, wu_oth, wd_own,
            wd_oth, b_up, kept,
        )
        return relayed

    relayed = forward(0, 0, "argument", (inputs, first_oth))
    first = lax.ppermute(relayed, "section", [(0, 1)])
    relayed = forward(0, 1, "argument", (inputs, second_oth))
    relayed, first = lax.optimization_barrier((relayed, first))
    second = lax.ppermute(relayed, "section", [(0, 1)])
    forward(1, 0, "relay", (first,))
    forward(1, 1, "relay", (second,))

    grads = {}
    sums = []

    def backward_mlp(owner, number, source, tokens, scaled=False):
        (
            branch,
            grads["before"],
            grads["attended"],
            grad_mixed,
            grad_res,
            small,
            shift,
        ) = mlp_backward(
            info, owner, number, source, tokens, vec, wo_own, wo_oth, wu_own, wu_oth, wd_own,
            wd_oth, kept, grads, scaled,
        )
        if not scaled:
            grads["branch"] = branch
        return grad_mixed, grad_res, small, shift

    def backward_attention(owner, number, grad_mixed):
        dq, dkv_here, dkv_send = attend_backward(info, owner, number, grad_mixed, kept)
        return dq, dkv_here, swap(dkv_send)

    def backward_qkv(owner, number, dq, dkv_here, dkv_there, grad_res, small, shift):
        grads["packed"], grads["input"], relayed, small_one, shift_qkv = qkv_backward(
            info, owner, number, dq, dkv_here, dkv_there, wq_own, wq_oth, grad_res, vec, kept,
            grads,
        )
        sums.append((small, shift, small_one, shift_qkv))
        return relayed

    def backward(owner, number, source, tokens):
        grad_mixed, grad_res, small, shift = backward_mlp(owner, number, source, tokens)
        flows = backward_attention(owner, number, grad_mixed)
        return backward_qkv(owner, number, *flows, grad_res, small, shift)

    relayed = backward(1, 0, "argument", (cotangent, cot_oth[0]))
    first = lax.ppermute(relayed, "section", [(1, 0)])
    relayed = backward(1, 1, "argument", (cotangent, cot_oth[1]))
    relayed, first = lax.optimization_barrier((relayed, first))
    second = lax.ppermute(relayed, "section", [(1, 0)])
    backward(0, 0, "relay", (first,))

    def weight_grad(left, right):
        return lax.dot_general(
            left, right, (((0, 1), (0, 1)), ((), ())), preferred_element_type=F32
        ).astype(BF16)

    grads["branch"] = scale_branch(info, 0, 1, second, vec, grads["branch"])
    active, g_branch = kept["active"], grads["branch"]
    down_oth = weight_grad(active[:, :, hidden_half:], g_branch)
    down_sent = swap(down_oth)
    down_own = weight_grad(active[:, :, :hidden_half], tied(g_branch, down_oth))
    ring_down = Ring(info, [(down_own, down_sent)], [down_own.shape], WholeRows(width))
    second = tied(second, *ring_down.moving)
    grad_mixed, grad_res, small, shift = backward_mlp(0, 1, "relay", (second,), scaled=True)
    ring_down.advance(grad_mixed)
    normed2 = tied(kept["normed2"], *ring_down.moving)
    before = grads["before"]
    up_oth = weight_grad(normed2, before[:, :, hidden_half:])
    up_sent = swap(up_oth)
    ring_down.advance(up_oth)
    normed2 = tied(normed2, *ring_down.moving)
    up_own = weight_grad(normed2, before[:, :, :hidden_half])
    ring_down.advance(up_own)
    ring_up = Ring(info, [(up_own, up_sent)], [up_own.shape], WholeRows(hidden_half))
    grad_mixed = tied(grad_mixed, *ring_down.moving, *ring_up.moving)
    flows = backward_attention(0, 1, grad_mixed)
    ring_down.advance(flows[0])
    ring_up.advance(flows[0])
    grad_res = tied(grad_res, *ring_down.moving, *ring_up.moving)
    backward_qkv(0, 1, *flows, grad_res, small, shift)
    packed = grads["packed"]
    ring_down.advance(packed)
    ring_up.advance(packed)
    normed1 = tied(kept["normed1"], *ring_down.moving, *ring_up.moving)
    vectors = gather_vectors(info, sums, width)

    def tail(index):
        columns = packed[:, :, index * 3 * half : (index + 1) * 3 * half]
        mixed = kept["mixed"][:, :, index * half : (index + 1) * half]
        g_att = grads["attended"]
        outs = [weight_grad(mixed, g_att[:, :, half * j : half * (j + 1)]) for j in range(2)]
        return [weight_grad(normed1, columns), jnp.concatenate(outs, axis=0), vectors[index]]

    tail_oth = tail(1)
    tail_sent = [swap(block) for block in tail_oth]
    ring_down.advance(tail_oth[0])
    ring_up.advance(tail_oth[0])
    normed1 = tied(normed1, *ring_down.moving, *ring_up.moving)
    tail_own = tail(0)
    ring_down.advance(tail_own[0])
    ring_up.advance(tail_own[0])
    ring_tail = Ring(
        info,
        list(zip(tail_own, tail_sent)),
        [(3, width, half), (half, width), (width, LANES)],
        TailPlaces(half, LANES),
    )
    rings = [ring_down, ring_up, ring_tail]
    before_it = ring_tail
    while not all(ring.done() for ring in rings):
        for ring in rings:
            if not ring.done():
                ring.advance(*before_it.moving)
                before_it = ring
    (total_down,) = ring_down.finish()
    (total_up,) = ring_up.finish()
    total_qkv, total_out, total_vectors = ring_tail.finish()
    block_outputs = join_tokens(info, kept["output"], swap(partner_features(info, kept["output"])))
    input_grads = join_tokens(info, grads["input"], swap(partner_features(info, grads["input"])))
    rows = spread_vectors(total_vectors, half, hidden_half)
    return (
        block_outputs,
        input_grads,
        rows[0],
        rows[1],
        jnp.transpose(total_qkv, (1, 0, 2))[None],
        rows[8][None],
        total_out[None],
        rows[7],
        rows[6],
        rows[4],
        rows[5],
        total_up[None],
        rows[9],
        total_down[None],
        rows[3],
        rows[2],
    )


def solution(mesh):
    placed = (
        P(None, "dp", None, "tensor"),
        P(None, "dp", None, "tensor"),
        P("section", "tensor"),
        P("section", "tensor"),
        P("section", None, None, "tensor"),
        P("section", None, "tensor"),
        P("section", "tensor", None),
        P("section", "tensor"),
        P("section", "tensor"),
        P("section", "tensor"),
        P("section", "tensor"),
        P("section", None, "tensor"),
        P("section", "tensor"),
        P("section", "tensor", None),
        P("section", "tensor"),
        P("section", "tensor"),
    )
    return jax.shard_map(
        shards,
        mesh=mesh,
        in_specs=placed,
        out_specs=(
            P("section", None, "dp", None, "tensor"),
            P("section", None, "dp", None, "tensor"),
            P("section", "tensor"),
            P("section", "tensor"),
            P("section", None, None, "tensor"),
            P("section", None, "tensor"),
            P("section", "tensor", None),
            P("section", "tensor"),
            P("section", "tensor"),
            P("section", "tensor"),
            P("section", "tensor"),
            P("section", None, "tensor"),
            P("section", "tensor"),
            P("section", "tensor", None),
            P("section", "tensor"),
            P("section", "tensor"),
        ),
        check_vma=False,
    )
```

time: 813 us -> 752 us (0.925)
  Pallas kernels: 216 us -> 311 us
  waiting for transfers between devices: 314 us -> 248 us
  other arithmetic: 62.4 us -> 1.11 us
  between operations: 27.6 us -> 2.23 us
    pallas_call x15 -> x76, Pallas kernels: 135 us -> 232 us  [manual(): pl.pallas_call(body, out_shape=[jax.ShapeDtypeStruct(s, d) for s, d, _, _...]
    ppermute x60 -> x88, waiting for transfers between devices: 291 us -> 239 us  [the longest x1 115 us: shards(): first = lax.ppermute(relayed, 'section', [(1, 0)])]
    convert_element_type x29 -> x0, other arithmetic: 24.6 us -> none  [the longest x5 14.6 us: paired(): return (own.astype(F32) + swap(oth).astype(F32)).astype(BF16)]
    dynamic_update_slice x65 -> x0, other arithmetic: 16.2 us -> none  [put(): lax.dynamic_update_slice_in_dim(total, piece, start(way, owner, chunk), 0)]
    unnamed x132 -> x112, local copies, waits for them, and re-layouts: 16.9 us -> 32.1 us
    ppermute x20 -> x23, waiting for transfers between devices: 22.9 us -> 9.28 us  [swap(): return lax.ppermute(block, 'tensor', [(0, 1), (1, 0)])]
    pallas_call x6 -> x8, Pallas kernels: 81.4 us -> 72 us  [call(): pl.pallas_call(body, out_shape=[jax.ShapeDtypeStruct(s, d) for s, d, _, _...]
    broadcast_in_dim x3 -> x0, other arithmetic: 8.69 us -> none  [the longest x1 6.63 us: shards(): total_down[None]]
  transfers between devices with their start and end apart: 81 -> 111, of which waited for: 48 -> 45; matrix products, arithmetic and copies ran while one was open for 14% -> 3% of each run, Pallas kernels for 10% -> 37%
where the time goes in v2:
time: 752 us; the launch traced here: 739 us
  Pallas kernels  311 us (41%)
  waiting for transfers between devices  248 us (33%)
  starting transfers between devices  109 us (14%)
  matrix products  34.4 us (5%)
  local copies, waits for them, and re-layouts  33.7 us (4%)
    pallas_call x76, Pallas kernels, manual(): pl.pallas_call(body, out_shape=[jax.ShapeDtypeStruct(s, d) for s, d, _, _...  232 us
    ppermute x1, waiting for transfers between devices, shards(): first = lax.ppermute(relayed, 'section', [(1, 0)])  115 us
    ppermute x84, waiting for transfers between devices, advance(): lax.ppermute(self.moving[w], 'dp', self.routes[w])  112 us
    ppermute x84, starting transfers between devices, advance(): lax.ppermute(self.moving[w], 'dp', self.routes[w])  96.8 us
    pallas_call x8, Pallas kernels, call(): pl.pallas_call(body, out_shape=[jax.ShapeDtypeStruct(s, d) for s, d, _, _...  72 us
    dot_general x10, matrix products, weight_grad(): lax.dot_general(left, right, (((0, 1), (0, 1)), ((), ())), preferred_elem...  34.4 us
    unnamed x112, local copies, waits for them, and re-layouts  32.1 us
  transfers between devices with their start and end apart: 111, of which 45 were waited for; matrix products, arithmetic and copies ran while one was open for 3% of the time, Pallas kernels for 37%

profile of v2, /device:TPU:0, one launch (start us, length us, event | category | flops | bytes accessed | tf_op | source)
XLA Modules:
  0.0 738.9 jit_solution(16819164053788209390)
XLA Ops:
  10.4 6.5 shard_map.292
  17.5 4.2 shard_map.294.refs_5_.refs_1_
  24.2 12.2 %shard_map.296 = (bf16[3,16,384,768]{3,2,1,0:T(8,128)(2,1)}, f32[3,384,1024]{2,1,0:T(8,128)}, bf16[384,1024]{1,0:T(8,128)(2,1)}, f32[3,384,1024]{2,1,0:T(8,128)}, bf16[3,2,768,1024]{3,2,1,0:T(8,128)(2,1)}) custom-call(s32[19]{0:T(128)} %copy-done.26, bf16[2,384,1024]{2,1,0:T(8,128)(2,1)} %shard_map.294.refs_5_.refs_1_, ...), custom_call_target="tpu_custom_call" | custom-call | flops 1207959552 | bytes 21233664 | tf_op jit(solution)/shard_map/pallas_call | solution.py:80
  36.4 22.6 %shard_map.298 = (bf16[2,384,1024]{2,1,0:T(8,128)(2,1)}, f32[2,384,1024]{2,1,0:T(8,128)}, bf16[2,384,1024]{2,1,0:T(8,128)(2,1)}, bf16[2,384,4096]{2,1,0:T(8,128)...) custom-call(s32[19]{0:T(128)} %copy-done.26, ...), custom_call_target="tpu_custom_call" | custom-call | flops 7247757312 | bytes 31457280 | tf_op jit(solution)/shard_map/pallas_call | solution.py:117
  59.8 6.7 shard_map.293
  69.1 4.1 shard_map.295.refs_1_.refs_5_
  74.4 12.3 %shard_map.297 = (bf16[3,16,384,768]{3,2,1,0:T(8,128)(2,1)}, f32[3,384,1024]{2,1,0:T(8,128)}, bf16[384,1024]{1,0:T(8,128)(2,1)}, f32[3,384,1024]{2,1,0:T(8,128)}, bf16[3,2,768,1024]{3,2,1,0:T(8,128)(2,1)}) custom-call(s32[19]{0:T(128)} %copy-done.26, ...), custom_call_target="tpu_custom_call", output_to_operand_aliasing={{0}: (4, {}), {1}: (5, {}), {3}: (6, {}), {4}: (7, {})} | custom-call | flops 1207959552 | bytes 21233664 | tf_op jit(solution)/shard_map/pallas_call | solution.py:80
  86.7 21.1 %shard_map.299 = (bf16[2,384,1024]{2,1,0:T(8,128)(2,1)}, f32[2,384,1024]{2,1,0:T(8,128)}, bf16[2,384,1024]{2,1,0:T(8,128)(2,1)}, bf16[2,384,4096]{2,1,0:T(8,128)...) custom-call(s32[19]{0:T(128)} %copy-done.26, ...), custom_call_target="tpu_custom_call", output_to_operand_aliasing={{0}: (11, {}), {1}: (12, {}), {2}: (13, {}), {3}: (14, {}),... | custom-call | flops 7247757312 | bytes 31457280 | tf_op jit(solution)/shard_map/pallas_call | solution.py:117
  119.0 9.4 %collective-permute-done.10.refs_1_ = bf16[384,1024]{1,0:T(8,128)(2,1)} collective-permute-done((bf16[384,1024]{1,0:T(8,128)(2,1)}, bf16[384,1024]{1,0:T(8,128)(2,1)}, u32[]{:S(2)}, u32[]{:S(2)}) %collective-permute-start.10) | collective-permute-done | bytes 786464 | tf_op jit(solution)/shard_map/ppermute | solution.py:1414
  147.4 10.0 %shard_map.312 = (bf16[2,384,1024]{2,1,0:T(8,128)(2,1)}, bf16[2,384,4096]{2,1,0:T(8,128)(2,1)}, bf16[2,384,1024]{2,1,0:T(8,128)(2,1)}, bf16[384,1024]{1,0:T(8,12...) custom-call(s32[19]{0:T(128)} %copy-done.26, ...), custom_call_target="tpu_custom_call", output_to_operand_aliasing={{0}: (14, {}), {1}: (15, {}), {2}: (16, {})} | custom-call | flops 7247757312 | bytes 31457280 | tf_op jit(solution)/shard_map/pallas_call | solution.py:117
  167.9 115.3 %collective-permute-done.17.refs_1_ = bf16[384,1024]{1,0:T(8,128)(2,1)} collective-permute-done((bf16[384,1024]{1,0:T(8,128)(2,1)}, bf16[384,1024]{1,0:T(8,128)(2,1)}, u32[]{:S(2)}, u32[]{:S(2)}) %collective-permute-start.17) | collective-permute-done | bytes 786464 | tf_op jit(solution)/shard_map/ppermute | solution.py:1456
  284.5 17.9 %shard_map.317 = (bf16[2,384,1024]{2,1,0:T(8,128)(2,1)}, bf16[2,384,4096]{2,1,0:T(8,128)(2,1)}, bf16[2,384,1024]{2,1,0:T(8,128)(2,1)}, bf16[384,1024]{1,0:T(8,12...) custom-call(s32[19]{0:T(128)} %copy-done.26, ...), custom_call_target="tpu_custom_call", output_to_operand_aliasing={{0}: (13, {}), {1}: (14, {}), {2}: (15, {})} | custom-call | flops 7247757312 | bytes 31457280 | tf_op jit(solution)/shard_map/pallas_call | solution.py:117
  308.4 5.9 bitcast_convert_fusion.3
  314.5 5.6 bitcast_convert_fusion.2.refs_1_
  326.6 18.0 %shard_map.320 = (bf16[2,384,1024]{2,1,0:T(8,128)(2,1)}, bf16[2,384,4096]{2,1,0:T(8,128)(2,1)}, bf16[2,384,1024]{2,1,0:T(8,128)(2,1)}, bf16[384,1024]{1,0:T(8,12...) custom-call(s32[19]{0:T(128)} %copy-done.26, ...), custom_call_target="tpu_custom_call", output_to_operand_aliasing={{1}: (13, {}), {2}: (14, {})} | custom-call | flops 7247757312 | bytes 31457280 | tf_op jit(solution)/shard_map/pallas_call | solution.py:117
  352.2 5.0 bitcast_convert_fusion.1
  359.5 15.8 %shard_map.328 = (bf16[384,1024]{1,0:T(8,128)(2,1)}, bf16[2,384,1024]{2,1,0:T(8,128)(2,1)}, bf16[2,384,1024]{2,1,0:T(8,128)(2,1)}) custom-call(s32[19]{0:T(128)} %copy-done.26, bf16[384,1024]{1,0:T(8,128)(2,1)} %get-tuple-element.467.refs_1_, bf16[2,384,1024]{2,1,0:T(8,128)(2,1)} %shard_map.303.refs_1_.refs_2_, ...), custom_call_target="tpu_custom_call" | custom-call | flops 2415919104 | bytes 21233664 | tf_op jit(solution)/shard_map/pallas_call | solution.py:80
  382.9 5.8 bitcast_convert_fusion.refs_1_
  394.6 15.7 %shard_map.325 = (bf16[384,1024]{1,0:T(8,128)(2,1)}, bf16[2,384,1024]{2,1,0:T(8,128)(2,1)}, bf16[2,384,1024]{2,1,0:T(8,128)(2,1)}) custom-call(s32[19]{0:T(128)} %copy-done.26, bf16[384,1024]{1,0:T(8,128)(2,1)} %get-tuple-element.453.refs_1_, bf16[2,384,1024]{2,1,0:T(8,128)(2,1)} %shard_map.303.refs_1_.refs_2_, ...), custom_call_target="tpu_custom_call" | custom-call | flops 2415919104 | bytes 21233664 | tf_op jit(solution)/shard_map/pallas_call | solution.py:80
  413.9 5.5 collective-permute-done.28.refs_3_
  432.2 9.7 %shard_map.329 = (bf16[2,384,3072]{2,1,0:T(8,128)(2,1)}, bf16[2,384,1024]{2,1,0:T(8,128)(2,1)}, bf16[384,1024]{1,0:T(8,128)(2,1)}, f32[8,1024]{1,0:T(8,128)}, f32[8,512]{1,0:T(8,128)}) custom-call(s32[19]{0:T(128)} %copy-done.26, bf16[384,1024]{1,0:T(8,128)(2,1)} %get-tuple-element.468.refs_1_, ...), custom_call_target="tpu_custom_call", output_to_operand_aliasing={{0}: (9, {}), {1}: (10, {})} | custom-call | flops 2415919104 | bytes 12582912 | tf_op jit(solution)/shard_map/pallas_call | solution.py:117
  441.9 9.3 %shard_map.330 = (bf16[2,384,3072]{2,1,0:T(8,128)(2,1)}, bf16[2,384,1024]{2,1,0:T(8,128)(2,1)}, bf16[384,1024]{1,0:T(8,128)(2,1)}, f32[8,1024]{1,0:T(8,128)}, f32[8,512]{1,0:T(8,128)}) custom-call(s32[19]{0:T(128)} %copy-done.26, bf16[384,1024]{1,0:T(8,128)(2,1)} %get-tuple-element.454.refs_1_, ...), custom_call_target="tpu_custom_call", output_to_operand_aliasing={{0}: (9, {}), {1}: (10, {})} | custom-call | flops 2415919104 | bytes 12582912 | tf_op jit(solution)/shard_map/pallas_call | solution.py:117
  489.4 4.7 bitcast_convert_fusion.4.refs_1_
  580.4 7.0 collective-permute-done.76.refs_2_
  594.9 9.7 %collective-permute-done.81.refs_1_ = bf16[64,2048]{1,0:T(8,128)(2,1)S(1)} collective-permute-done((bf16[64,2048]{1,0:T(8,128)(2,1)S(1)}, bf16[64,2048]{1,0:T(8,128)(2,1)S(1)}, u32[]{:S(2)}, u32[]{:S(2)}) %collective-permute-start.81) | collective-permute-done | bytes 262176 | tf_op jit(solution)/shard_map/ppermute | solution.py:1077
  611.3 7.7 %collective-permute-done.90.refs_2_ = bf16[128,1024]{1,0:T(8,128)(2,1)S(1)} collective-permute-done((bf16[128,1024]{1,0:T(8,128)(2,1)S(1)}, bf16[128,1024]{1,0:T(8,128)(2,1)S(1)}, u32[]{:S(2)}, u32[]{:S(2)}) %collective-permute-start.90) | collective-permute-done | bytes 262176 | tf_op jit(solution)/shard_map/ppermute | solution.py:1077
  628.2 5.9 collective-permute-done.93.refs_1_
  642.1 5.9 collective-permute-done.97.refs_1_
  648.0 5.7 collective-permute-done.98.refs_2_
  658.1 8.0 %collective-permute-done.101.refs_1_ = bf16[64,2048]{1,0:T(8,128)(2,1)S(1)} collective-permute-done((bf16[64,2048]{1,0:T(8,128)(2,1)S(1)}, bf16[64,2048]{1,0:T(8,128)(2,1)S(1)}, u32[]{:S(2)}, u32[]{:S(2)}) %collective-permute-start.101) | collective-permute-done | bytes 262176 | tf_op jit(solution)/shard_map/ppermute | solution.py:1077
  668.4 5.5 collective-permute-done.103.refs_1_
  684.3 5.8 collective-permute-done.107.refs_1_
  (404 shorter events, 332.2 us)
Async XLA Ops:
  8.8 27.6 %collective-permute-start.8 = (bf16[1024,2048]{1,0:T(8,128)(2,1)}, bf16[1024,2048]{1,0:T(8,128)(2,1)}, u32[]{:S(2)}, u32[]{:S(2)}) collective-permute-start(bf16[1024,2048]{1,0:T(8,128)(2,1)} %bitcast.74), channel_id=1, source_target_pairs={{0,8},{8,0},{1,9},{9,1},{2,10},{10,2},{3,11},{11,3},{4,12},{12,4},... | collective-permute-start | bytes 12582920 | tf_op jit(solution)/shard_map/ppermute | solution.py:944
  17.4 19.1 %collective-permute-start.7 = (bf16[512,1024]{1,0:T(8,128)(2,1)}, bf16[512,1024]{1,0:T(8,128)(2,1)}, u32[]{:S(2)}, u32[]{:S(2)}) collective-permute-start(bf16[512,1024]{1,0:T(8,128)(2,1)} %bitcast.8.refs_4_.refs_8_.refs_7_), channel_id=1, source_target_pairs={{0,8},{8,0},{1,9},{9,1},{2,10},{10,2},{3,11},{11,3},{4,12},{12,4},... | collective-permute-start | bytes 3145736 | tf_op jit(solution)/shard_map/ppermute | solution.py:944
  22.5 36.5 %collective-permute-start.3 = (bf16[384,512]{1,0:T(8,128)(2,1)S(1)}, bf16[384,512]{1,0:T(8,128)(2,1)S(1)}, u32[]{:S(2)}, u32[]{:S(2)}) collective-permute-start(bf16[384,512]{1,0:T(8,128)(2,1)S(1)} %bitcast.56), channel_id=1, source_target_pairs={{0,8},{8,0},{1,9},{9,1},{2,10},{10,2},{3,11},{11,3},{4,12},{12,4},... | collective-permute-start | bytes 1179656 | tf_op jit(solution)/shard_map/ppermute | solution.py:944
  66.9 40.9 %collective-permute-start.9 = (bf16[384,1024]{1,0:T(8,128)(2,1)}, bf16[384,1024]{1,0:T(8,128)(2,1)}, u32[]{:S(2)}, u32[]{:S(2)}) collective-permute-start(bf16[384,1024]{1,0:T(8,128)(2,1)} %get-tuple-element.359), channel_id=1, source_target_pairs={{0,16},{1,17},{2,18},{3,19},{4,20},{5,21},{6,22},{7,23},{8,24},{9,... | collective-permute-start | bytes 2359304 | tf_op jit(solution)/shard_map/ppermute | solution.py:1411
  109.3 19.2 %collective-permute-start.10 = (bf16[384,1024]{1,0:T(8,128)(2,1)}, bf16[384,1024]{1,0:T(8,128)(2,1)}, u32[]{:S(2)}, u32[]{:S(2)}) collective-permute-start(bf16[384,1024]{1,0:T(8,128)(2,1)} %get-tuple-element.360), channel_id=1, source_target_pairs={{0,16},{1,17},{2,18},{3,19},{4,20},{5,21},{6,22},{7,23},{8,24},{9,... | collective-permute-start | bytes 2359304 | tf_op jit(solution)/shard_map/ppermute | solution.py:1414
  163.2 120.0 %collective-permute-start.17 = (bf16[384,1024]{1,0:T(8,128)(2,1)}, bf16[384,1024]{1,0:T(8,128)(2,1)}, u32[]{:S(2)}, u32[]{:S(2)}) collective-permute-start(bf16[384,1024]{1,0:T(8,128)(2,1)} %get-tuple-element.420), channel_id=1, source_target_pairs={{16,0},{17,1},{18,2},{19,3},{20,4},{21,5},{22,6},{23,7},{24,8},{25... | collective-permute-start | bytes 2359304 | tf_op jit(solution)/shard_map/ppermute | solution.py:1456
  283.2 21.3 %collective-permute-start.18 = (bf16[384,1024]{1,0:T(8,128)(2,1)}, bf16[384,1024]{1,0:T(8,128)(2,1)S(1)}, u32[]{:S(2)}, u32[]{:S(2)}) collective-permute-start(bf16[384,1024]{1,0:T(8,128)(2,1)} %get-tuple-element.421), channel_id=1, source_target_pairs={{16,0},{17,1},{18,2},{19,3},{20,4},{21,5},{22,6},{23,7},{24,8},{25... | collective-permute-start | bytes 2359304 | tf_op jit(solution)/shard_map/ppermute | solution.py:1459
  323.6 21.0 %collective-permute-start.20 = (bf16[128,1024]{1,0:T(8,128)(2,1)S(1)}, bf16[128,1024]{1,0:T(8,128)(2,1)S(1)}, u32[]{:S(2)}, u32[]{:S(2)}) collective-permute-start(bf16[128,1024]{1,0:T(8,128)(2,1)S(1)} %get-tuple-element.429), channel_id=1, source_target_pairs={{0,2},{2,4},{4,6},{6,7},{7,5},{5,3},{3,1},{1,0},{8,10},{10,12},{12... | collective-permute-start | bytes 786440 | tf_op jit(solution)/shard_map/ppermute | solution.py:1077
  326.6 18.0 %collective-permute-start.21 = (bf16[128,1024]{1,0:T(8,128)(2,1)S(1)}, bf16[128,1024]{1,0:T(8,128)(2,1)S(1)}, u32[]{:S(2)}, u32[]{:S(2)}) collective-permute-start(bf16[128,1024]{1,0:T(8,128)(2,1)S(1)} %get-tuple-element.430), channel_id=1, source_target_pairs={{0,1},{2,0},{4,2},{6,4},{7,6},{5,7},{3,5},{1,3},{8,9},{10,8},{12,1... | collective-permute-start | bytes 786440 | tf_op jit(solution)/shard_map/ppermute | solution.py:1077
  357.3 34.8 %collective-permute-start.26 = (bf16[1024,2048]{1,0:T(8,128)(2,1)}, bf16[1024,2048]{1,0:T(8,128)(2,1)}, u32[]{:S(2)}, u32[]{:S(2)}) collective-permute-start(bf16[1024,2048]{1,0:T(8,128)(2,1)} %bitcast_convert_fusion.1), channel_id=1, source_target_pairs={{0,8},{8,0},{1,9},{9,1},{2,10},{10,2},{3,11},{11,3},{4,12},{12,4},... | collective-permute-start | bytes 12582920 | tf_op jit(solution)/shard_map/ppermute | solution.py:944
  357.3 18.3 %collective-permute-start.22 = (bf16[128,1024]{1,0:T(8,128)(2,1)S(1)}, bf16[128,1024]{1,0:T(8,128)(2,1)S(1)}, u32[]{:S(2)}, u32[]{:S(2)}) collective-permute-start(bf16[128,1024]{1,0:T(8,128)(2,1)S(1)} %get-tuple-element.437), channel_id=1, source_target_pairs={{0,2},{2,4},{4,6},{6,7},{7,5},{5,3},{3,1},{1,0},{8,10},{10,12},{12... | collective-permute-start | bytes 786440 | tf_op jit(solution)/shard_map/ppermute | solution.py:1077
  359.3 16.2 %collective-permute-start.23 = (bf16[128,1024]{1,0:T(8,128)(2,1)S(1)}, bf16[128,1024]{1,0:T(8,128)(2,1)S(1)}, u32[]{:S(2)}, u32[]{:S(2)}) collective-permute-start(bf16[128,1024]{1,0:T(8,128)(2,1)S(1)} %get-tuple-element.438), channel_id=1, source_target_pairs={{0,1},{2,0},{4,2},{6,4},{7,6},{5,7},{3,5},{1,3},{8,9},{10,8},{12,1... | collective-permute-start | bytes 786440 | tf_op jit(solution)/shard_map/ppermute | solution.py:1077
  375.3 56.5 %collective-permute-start.32 = (bf16[2,384,1024]{2,1,0:T(8,128)(2,1)}, bf16[2,384,1024]{2,1,0:T(8,128)(2,1)}, u32[]{:S(2)}, u32[]{:S(2)}) collective-permute-start(bf16[2,384,1024]{2,1,0:T(8,128)(2,1)} %get-tuple-element.470), channel_id=1, source_target_pairs={{0,8},{8,0},{1,9},{9,1},{2,10},{10,2},{3,11},{11,3},{4,12},{12,4},... | collective-permute-start | bytes 4718600 | tf_op jit(solution)/shard_map/ppermute | solution.py:944
  410.2 31.7 %collective-permute-start.27 = (bf16[2,384,1024]{2,1,0:T(8,128)(2,1)}, bf16[2,384,1024]{2,1,0:T(8,128)(2,1)}, u32[]{:S(2)}, u32[]{:S(2)}) collective-permute-start(bf16[2,384,1024]{2,1,0:T(8,128)(2,1)} %get-tuple-element.456), channel_id=1, source_target_pairs={{0,8},{8,0},{1,9},{9,1},{2,10},{10,2},{3,11},{11,3},{4,12},{12,4},... | collective-permute-start | bytes 4718600 | tf_op jit(solution)/shard_map/ppermute | solution.py:944
  425.6 25.7 %collective-permute-start.34 = (bf16[128,1024]{1,0:T(8,128)(2,1)S(1)}, bf16[128,1024]{1,0:T(8,128)(2,1)S(1)}, u32[]{:S(2)}, u32[]{:S(2)}) collective-permute-start(bf16[128,1024]{1,0:T(8,128)(2,1)S(1)} %get-tuple-element.460), channel_id=1, source_target_pairs={{0,2},{2,4},{4,6},{6,7},{7,5},{5,3},{3,1},{1,0},{8,10},{10,12},{12... | collective-permute-start | bytes 786440 | tf_op jit(solution)/shard_map/ppermute | solution.py:1077
  427.2 24.1 %collective-permute-start.35 = (bf16[128,1024]{1,0:T(8,128)(2,1)S(1)}, bf16[128,1024]{1,0:T(8,128)(2,1)S(1)}, u32[]{:S(2)}, u32[]{:S(2)}) collective-permute-start(bf16[128,1024]{1,0:T(8,128)(2,1)S(1)} %get-tuple-element.461), channel_id=1, source_target_pairs={{0,1},{2,0},{4,2},{6,4},{7,6},{5,7},{3,5},{1,3},{8,9},{10,8},{12,1... | collective-permute-start | bytes 786440 | tf_op jit(solution)/shard_map/ppermute | solution.py:1077
  430.1 21.2 %collective-permute-start.36 = (bf16[64,2048]{1,0:T(8,128)(2,1)}, bf16[64,2048]{1,0:T(8,128)(2,1)S(1)}, u32[]{:S(2)}, u32[]{:S(2)}) collective-permute-start(bf16[64,2048]{1,0:T(8,128)(2,1)} %get-tuple-element.464), channel_id=1, source_target_pairs={{0,2},{2,4},{4,6},{6,7},{7,5},{5,3},{3,1},{1,0},{8,10},{10,12},{12... | collective-permute-start | bytes 786440 | tf_op jit(solution)/shard_map/ppermute | solution.py:1077
  431.8 19.5 %collective-permute-start.37 = (bf16[64,2048]{1,0:T(8,128)(2,1)S(1)}, bf16[64,2048]{1,0:T(8,128)(2,1)S(1)}, u32[]{:S(2)}, u32[]{:S(2)}) collective-permute-start(bf16[64,2048]{1,0:T(8,128)(2,1)S(1)} %get-tuple-element.465), channel_id=1, source_target_pairs={{0,1},{2,0},{4,2},{6,4},{7,6},{5,7},{3,5},{1,3},{8,9},{10,8},{12,1... | collective-permute-start | bytes 786440 | tf_op jit(solution)/shard_map/ppermute | solution.py:1077
  464.3 37.7 %collective-permute-start.42 = (bf16[1024,1536]{1,0:T(8,128)(2,1)}, bf16[1024,1536]{1,0:T(8,128)(2,1)S(1)}, u32[]{:S(2)}, u32[]{:S(2)}) collective-permute-start(bf16[1024,1536]{1,0:T(8,128)(2,1)} %bitcast_convert_fusion.5), channel_id=1, source_target_pairs={{0,8},{8,0},{1,9},{9,1},{2,10},{10,2},{3,11},{11,3},{4,12},{12,4},... | collective-permute-start | bytes 9437192 | tf_op jit(solution)/shard_map/ppermute | solution.py:944
  468.6 31.2 %collective-permute-start.43 = (bf16[1024,512]{1,0:T(8,128)(2,1)}, bf16[1024,512]{1,0:T(8,128)(2,1)}, u32[]{:S(2)}, u32[]{:S(2)}) collective-permute-start(bf16[1024,512]{1,0:T(8,128)(2,1)} %pad_maximum_fusion.1), channel_id=1, source_target_pairs={{0,8},{8,0},{1,9},{9,1},{2,10},{10,2},{3,11},{11,3},{4,12},{12,4},... | collective-permute-start | bytes 3145736 | tf_op jit(solution)/shard_map/ppermute | solution.py:944
  506.0 15.6 %collective-permute-start.59 = (bf16[128,1024]{1,0:T(8,128)(2,1)S(1)}, bf16[128,1024]{1,0:T(8,128)(2,1)S(1)}, u32[]{:S(2)}, u32[]{:S(2)}) collective-permute-start(bf16[128,1024]{1,0:T(8,128)(2,1)S(1)} %collective-permute-done.53.refs_1_), channel_id=1, source_target_pairs={{0,2},{2,4},{4,6},{6,7},{7,5},{5,3},{3,1},{1,0},{8,10},{10,12},{12... | collective-permute-start | bytes 786440 | tf_op jit(solution)/shard_map/ppermute | solution.py:1077
  523.2 15.6 %collective-permute-start.65 = (bf16[128,1024]{1,0:T(8,128)(2,1)S(1)}, bf16[128,1024]{1,0:T(8,128)(2,1)S(1)}, u32[]{:S(2)}, u32[]{:S(2)}) collective-permute-start(bf16[128,1024]{1,0:T(8,128)(2,1)S(1)} %collective-permute-done.59.refs_1_), channel_id=1, source_target_pairs={{0,2},{2,4},{4,6},{6,7},{7,5},{5,3},{3,1},{1,0},{8,10},{10,12},{12... | collective-permute-start | bytes 786440 | tf_op jit(solution)/shard_map/ppermute | solution.py:1077
  540.4 15.6 %collective-permute-start.71 = (bf16[128,1024]{1,0:T(8,128)(2,1)S(1)}, bf16[128,1024]{1,0:T(8,128)(2,1)S(1)}, u32[]{:S(2)}, u32[]{:S(2)}) collective-permute-start(bf16[128,1024]{1,0:T(8,128)(2,1)S(1)} %collective-permute-done.65.refs_1_), channel_id=1, source_target_pairs={{0,2},{2,4},{4,6},{6,7},{7,5},{5,3},{3,1},{1,0},{8,10},{10,12},{12... | collective-permute-start | bytes 786440 | tf_op jit(solution)/shard_map/ppermute | solution.py:1077
  557.6 15.6 %collective-permute-start.77 = (bf16[128,1024]{1,0:T(8,128)(2,1)S(1)}, bf16[128,1024]{1,0:T(8,128)(2,1)S(1)}, u32[]{:S(2)}, u32[]{:S(2)}) collective-permute-start(bf16[128,1024]{1,0:T(8,128)(2,1)S(1)} %collective-permute-done.71.refs_1_), channel_id=1, source_target_pairs={{0,2},{2,4},{4,6},{6,7},{7,5},{5,3},{3,1},{1,0},{8,10},{10,12},{12... | collective-permute-start | bytes 786440 | tf_op jit(solution)/shard_map/ppermute | solution.py:1077
  563.2 15.6 %collective-permute-start.75 = (bf16[64,2048]{1,0:T(8,128)(2,1)S(1)}, bf16[64,2048]{1,0:T(8,128)(2,1)S(1)}, u32[]{:S(2)}, u32[]{:S(2)}) collective-permute-start(bf16[64,2048]{1,0:T(8,128)(2,1)S(1)} %collective-permute-done.69.refs_1_), channel_id=1, source_target_pairs={{0,2},{2,4},{4,6},{6,7},{7,5},{5,3},{3,1},{1,0},{8,10},{10,12},{12... | collective-permute-start | bytes 786440 | tf_op jit(solution)/shard_map/ppermute | solution.py:1077
  570.7 16.6 %collective-permute-start.73 = (bf16[64,2176]{1,0:T(8,128)(2,1)S(1)}, bf16[64,2176]{1,0:T(8,128)(2,1)S(1)}, u32[]{:S(2)}, u32[]{:S(2)}) collective-permute-start(bf16[64,2176]{1,0:T(8,128)(2,1)S(1)} %get-tuple-element.562), channel_id=1, source_target_pairs={{0,2},{2,4},{4,6},{6,7},{7,5},{5,3},{3,1},{1,0},{8,10},{10,12},{12... | collective-permute-start | bytes 835592 | tf_op jit(solution)/shard_map/ppermute | solution.py:1077
  574.8 18.1 %collective-permute-start.83 = (bf16[128,1024]{1,0:T(8,128)(2,1)S(1)}, bf16[128,1024]{1,0:T(8,128)(2,1)S(1)}, u32[]{:S(2)}, u32[]{:S(2)}) collective-permute-start(bf16[128,1024]{1,0:T(8,128)(2,1)S(1)} %collective-permute-done.77.refs_1_), channel_id=1, source_target_pairs={{0,2},{2,4},{4,6},{6,7},{7,5},{5,3},{3,1},{1,0},{8,10},{10,12},{12... | collective-permute-start | bytes 786440 | tf_op jit(solution)/shard_map/ppermute | solution.py:1077
  593.4 17.3 %collective-permute-start.89 = (bf16[128,1024]{1,0:T(8,128)(2,1)S(1)}, bf16[128,1024]{1,0:T(8,128)(2,1)S(1)}, u32[]{:S(2)}, u32[]{:S(2)}) collective-permute-start(bf16[128,1024]{1,0:T(8,128)(2,1)S(1)} %collective-permute-done.83.refs_1_), channel_id=1, source_target_pairs={{0,2},{2,4},{4,6},{6,7},{7,5},{5,3},{3,1},{1,0},{8,10},{10,12},{12... | collective-permute-start | bytes 786440 | tf_op jit(solution)/shard_map/ppermute | solution.py:1077
  636.1 17.6 %collective-permute-start.95 = (bf16[64,2176]{1,0:T(8,128)(2,1)S(1)}, bf16[64,2176]{1,0:T(8,128)(2,1)S(1)}, u32[]{:S(2)}, u32[]{:S(2)}) collective-permute-start(bf16[64,2176]{1,0:T(8,128)(2,1)S(1)} %collective-permute-done.91.refs_1_), channel_id=1, source_target_pairs={{0,2},{2,4},{4,6},{6,7},{7,5},{5,3},{3,1},{1,0},{8,10},{10,12},{12... | collective-permute-start | bytes 835592 | tf_op jit(solution)/shard_map/ppermute | solution.py:1077
  678.3 17.9 %collective-permute-start.33 = (bf16[2,384,512]{2,1,0:T(8,128)(2,1)S(1)}, bf16[2,384,512]{2,1,0:T(8,128)(2,1)S(1)}, u32[]{:S(2)}, u32[]{:S(2)}) collective-permute-start(bf16[2,384,512]{2,1,0:T(8,128)(2,1)S(1)} %shard_map.331), channel_id=1, source_target_pairs={{0,8},{8,0},{1,9},{9,1},{2,10},{10,2},{3,11},{11,3},{4,12},{12,4},... | collective-permute-start | bytes 2359304 | tf_op jit(solution)/shard_map/ppermute | solution.py:944
  690.9 43.6 %collective-permute-start.109 = (bf16[64,2176]{1,0:T(8,128)(2,1)S(1)}, bf16[64,2176]{1,0:T(8,128)(2,1)S(1)}, u32[]{:S(2)}, u32[]{:S(2)}) collective-permute-start(bf16[64,2176]{1,0:T(8,128)(2,1)S(1)} %collective-permute-done.107.refs_1_), channel_id=1, source_target_pairs={{0,2},{2,4},{4,6},{6,7},{7,5},{5,3},{3,1},{1,0},{8,10},{10,12},{12... | collective-permute-start | bytes 835592 | tf_op jit(solution)/shard_map/ppermute | solution.py:1077
  691.2 43.3 %collective-permute-start.110 = (bf16[64,2176]{1,0:T(8,128)(2,1)S(1)}, bf16[64,2176]{1,0:T(8,128)(2,1)S(1)}, u32[]{:S(2)}, u32[]{:S(2)}) collective-permute-start(bf16[64,2176]{1,0:T(8,128)(2,1)S(1)} %collective-permute-done.108.refs_2_), channel_id=1, source_target_pairs={{0,1},{2,0},{4,2},{6,4},{7,6},{5,7},{3,5},{1,3},{8,9},{10,8},{12,1... | collective-permute-start | bytes 835592 | tf_op jit(solution)/shard_map/ppermute | solution.py:1077
  (135 other events, 1198.4 us)

commit v3 on v2

--- a/solution.py
+++ b/solution.py
@@ -13,6 +13,7 @@
 BF16 = jnp.bfloat16
 MIB = 1 << 20
 VMEM_MIB = 62
+RING_MIB = 61
 TILE = 16
 MICRO = 2
 SPARE = MICRO
@@ -62,7 +63,7 @@
     return jnp.sum(values, axis=0, keepdims=True)
 
 
-def call(kernel, scalars, grid, ins, outs, scratch=(), flops=0, moved=0):
+def call(kernel, scalars, grid, ins, outs, scratch=(), flops=0, moved=0, after=()):
     arrays = [a for a, _, _ in ins]
     in_specs = [pl.BlockSpec(b, m) for _, b, m in ins]
     aliases = {}
@@ -71,7 +72,9 @@
             aliases[1 + len(arrays)] = number
             arrays.append(out[4])
             in_specs.append(pl.BlockSpec(memory_space=pl.ANY))
-    extra = len(aliases)
+    arrays += after
+    in_specs += [pl.BlockSpec(memory_space=pl.ANY)] * len(after)
+    extra = len(aliases) + len(after)
     in_count = len(ins)
 
     def body(*refs):
@@ -97,18 +100,21 @@
     )(scalars, *arrays)
 
 
-def manual(kernel, scalars, ins, outs, scratch, flops=0, moved=0, vmem=VMEM_MIB):
+def manual(kernel, scalars, ins, outs, scratch, flops=0, moved=0, vmem=VMEM_MIB, after=(), same=None):
     any_space = pl.BlockSpec(memory_space=pl.ANY)
     vmem_space = pl.BlockSpec(memory_space=pltpu.VMEM)
     arrays = [a for a, _ in ins]
     in_specs = [vmem_space if inside else any_space for _, inside in ins]
-    aliases = {}
+    aliases = {1 + i: o for i, o in (same or {}).items()}
+    before = len(arrays)
     for number, out in enumerate(outs):
         if out[3] is not None:
             aliases[1 + len(arrays)] = number
             arrays.append(out[3])
             in_specs.append(any_space)
-    extra = len(aliases)
+    arrays += after
+    in_specs += [any_space] * len(after)
+    extra = len(arrays) - before
     in_count = len(ins)
 
     def body(*refs):
@@ -165,7 +171,7 @@
     ]
 
 
-def norm_kv(info, owner, number, source, tokens, vec, w_own, w_oth, bias_v, kept):
+def norm_kv(info, owner, number, source, tokens, vec, w_own, w_oth, bias_v, kept, after=()):
     rows, width = tokens[-1].shape[0], vec.shape[1]
     half = width // 2
     count = len(tokens)
@@ -229,6 +235,7 @@
         ],
         flops=2 * rows * width * 2 * width,
         moved=4 * width * width + 10 * rows * width,
+        after=after,
     )
 
 
@@ -393,7 +400,7 @@
 CHUNK = 512
 
 
-def mlp_forward(info, owner, number, mixed, x, vec, wo_own, wo_oth, wu_own, wu_oth, wd_own, wd_oth, b_up, kept):
+def mlp_forward(info, owner, number, mixed, x, vec, wo_own, wo_oth, wu_own, wu_oth, wd_own, wd_oth, b_up, kept, after=()):
     _, rows, width = x.shape
     side_hidden = wu_own.shape[1]
     hidden = 2 * side_hidden
@@ -533,10 +540,11 @@
         ],
         flops=4 * rows * width * hidden + 2 * rows * width * width,
         moved=4 * width * hidden + 2 * width * width + 8 * rows * hidden,
+        after=after,
     )
 
 
-def scale_branch(info, owner, number, relay, vec, earlier):
+def scale_branch(info, owner, number, relay, vec, earlier, after=()):
     rows, width = relay.shape
 
     def kernel(s, g, v, gb_out, g_v, gb_v, sems):
@@ -553,10 +561,11 @@
         [((MICRO, rows, width), BF16, False, earlier)],
         [pltpu.VMEM((rows, width), BF16), pltpu.VMEM((rows, width), BF16), dma_sems(2)],
         moved=4 * rows * width,
+        after=after,
     )[0]
 
 
-def mlp_backward(info, owner, number, source, tokens, vec, wo_own, wo_oth, wu_own, wu_oth, wd_own, wd_oth, kept, grads, scaled):
+def mlp_backward(info, owner, number, source, tokens, vec, wo_own, wo_oth, wu_own, wu_oth, wd_own, wd_oth, kept, grads, scaled, after):
     count = len(tokens)
     _, rows, width = kept["x"].shape
     side_hidden = wu_own.shape[1]
@@ -726,10 +735,11 @@
         ],
         flops=4 * rows * width * hidden + 2 * rows * width * width,
         moved=4 * width * hidden + 2 * width * width + 8 * rows * hidden,
+        after=after,
     )
 
 
-def attend_backward(info, owner, number, grad_mixed, kept):
+def attend_backward(info, owner, number, grad_mixed, kept, after=()):
     _, rows, width = kept["q"].shape
     heads = width // HEAD_DIM
     lanes = 2 * HEAD_DIM
@@ -820,10 +830,11 @@
         + [pltpu.VMEM((4, rows, lanes), BF16), pltpu.VMEM((4, rows, 1), F32)],
         flops=16 * rows * rows * width,
         moved=4 * heads * rows * rows + 30 * rows * width,
+        after=after,
     )
 
 
-def qkv_backward(info, owner, number, dq, dkv_here, dkv_there, w_own, w_oth, grad_res, vec, kept, grads):
+def qkv_backward(info, owner, number, dq, dkv_here, dkv_there, w_own, w_oth, grad_res, vec, kept, grads, after=()):
     _, rows, width = kept["x"].shape
     half = width // 2
 
@@ -937,6 +948,7 @@
         ],
         flops=6 * rows * width * width,
         moved=6 * width * width + 16 * rows * width,
+        after=after,
     )
 
 
@@ -970,7 +982,7 @@
     def unit(self, way, ahead):
         return UNITS + way * self.count + ahead % self.count
 
-    def add(self, ahead, arrived):
+    def add(self, ahead, arrived, after=()):
         chunk, width, parts = self.chunk, sum(self.widths), len(self.parts)
         units = [self.unit(w, ahead[w]) for w in range(2)]
         terms = 2 if arrived is None else 3
@@ -1018,24 +1030,23 @@
             [((chunk, width), BF16, True, None)] * 2,
             [pltpu.VMEM((2, terms, chunk, width), BF16), pltpu.SemaphoreType.DMA((2, 3, parts))],
             moved=2 * (terms + 1) * 2 * chunk * width,
-            vmem=16,
+            vmem=RING_MIB,
+            after=after,
         )
 
-    def put(self, ahead, blocks):
+    def put(self, ahead, blocks, after=()):
         chunk, width = self.chunk, sum(self.widths)
-        units = [self.unit(w, ahead[w]) for w in range(2)]
+        units = [self.unit(w, pair[w]) for pair in ahead for w in range(2)]
+        size = len(units)
         count = len(self.shapes)
         pieces = sum(len(self.places.columns(c)) for c in range(count))
 
         def kernel(s, *refs):
-            sources, outs, (held, wide, in_sems, out_sems) = (
-                refs[:2],
-                refs[2 : 2 + count],
-                refs[2 + count :],
-            )
-            loads = [begin(sources[w], held.at[w], in_sems.at[w]) for w in range(2)]
+            sources, outs = refs[:size], refs[size : size + count]
+            held, wide, in_sems, out_sems = refs[size + count + 2 :]
+            loads = [begin(sources[w], held.at[w], in_sems.at[w]) for w in range(size)]
             copies = []
-            for w in range(2):
+            for w in range(size):
                 loads[w].wait()
                 for t in tiles(chunk):
                     for first in range(0, width, 512):
@@ -1058,20 +1069,25 @@
             for copy in copies:
                 copy.wait()
 
-        self.totals = manual(
+        results = manual(
             kernel,
             self.info,
-            [(block, False) for block in blocks],
-            [(shape, F32, False, old) for shape, old in zip(self.shapes, self.totals)],
+            [(block, False) for block in blocks[:-2]] + [(block, False) for block in blocks[-2:]],
+            [(shape, F32, False, old) for shape, old in zip(self.shapes, self.totals)]
+            + [((chunk, width), BF16, False, None)] * 2,
             [
-                pltpu.VMEM((2, chunk, width), BF16),
-                pltpu.VMEM((2, chunk, width), F32),
-                dma_sems(2),
-                pltpu.SemaphoreType.DMA((2, pieces)),
+                pltpu.VMEM((size, chunk, width), BF16),
+                pltpu.VMEM((size, chunk, width), F32),
+                dma_sems(size),
+                pltpu.SemaphoreType.DMA((size, pieces)),
             ],
             moved=2 * 6 * chunk * width,
-            vmem=16,
+            vmem=RING_MIB,
+            after=after,
+            same={size - 2: count, size - 1: count + 1},
         )
+        self.totals = list(results[:count])
+        return list(results[count:])
 
     def advance(self, *after):
         arrived = [lax.ppermute(self.moving[w], "dp", self.routes[w]) for w in range(2)]
@@ -1081,10 +1097,12 @@
         if step < self.count - 1:
             self.moving = self.add([-s * (step + 1) for s in self.signs], arrived)
         else:
+            ahead = [[-s * (step - self.count + 1) for s in self.signs]]
+            blocks = arrived
             if step == self.count - 1:
-                self.put(self.signs, self.moving)
-            self.moving = arrived
-            self.put([-s * (step - self.count + 1) for s in self.signs], arrived)
+                ahead.insert(0, self.signs)
+                blocks = list(self.moving) + arrived
+            self.moving = self.put(ahead, blocks)
         self.step += 1
 
     def done(self):
@@ -1147,9 +1165,9 @@
         kernel,
         info,
         [(block, False)],
-        [((len(numbers), rows, half), BF16, False, None)],
+        [((len(numbers), rows, half), BF16, True, None)],
         [dma_sems(len(numbers))],
-        vmem=4,
+        vmem=8,
     )[0]
 
 
@@ -1169,9 +1187,9 @@
         kernel,
         info,
         [(block, False)],
-        [((micro, rows, half), BF16, False, None)],
+        [((micro, rows, half), BF16, True, None)],
         [dma_sems(micro)],
-        vmem=4,
+        vmem=8,
     )[0]
 
 
@@ -1195,9 +1213,9 @@
         kernel,
         info,
         [(block, False), (received, False)],
-        [((1, micro, 1, 2 * rows, half), BF16, False, None)],
+        [((1, micro, 1, 2 * rows, half), BF16, True, None)],
         [pltpu.SemaphoreType.DMA((2, micro))],
-        vmem=4,
+        vmem=8,
     )[0]
 
 
@@ -1382,9 +1400,9 @@
 
     kept = {}
 
-    def forward(owner, number, source, tokens):
+    def forward(owner, number, source, tokens, after=(), late=()):
         kept["x"], kept["normed1"], kv_here = norm_kv(
-            info, owner, number, source, tokens, vec, wq_own, wq_oth, bias_v, kept
+            info, owner, number, source, tokens, vec, wq_own, wq_oth, bias_v, kept, after
         )
         kv_there = swap(kv_here)
         kept["q"] = project_q(info, owner, number, kept["normed1"], wq_own, wq_oth, bias_q, kept)
@@ -1403,22 +1421,14 @@
             kept["mixed"],
         ) = mlp_forward(
             info, owner, number, mixed, kept["x"], vec, wo_own, wo_oth, wu_own, wu_oth, wd_own,
-            wd_oth, b_up, kept,
+            wd_oth, b_up, kept, late,
         )
         return relayed
 
-    relayed = forward(0, 0, "argument", (inputs, first_oth))
-    first = lax.ppermute(relayed, "section", [(0, 1)])
-    relayed = forward(0, 1, "argument", (inputs, second_oth))
-    relayed, first = lax.optimization_barrier((relayed, first))
-    second = lax.ppermute(relayed, "section", [(0, 1)])
-    forward(1, 0, "relay", (first,))
-    forward(1, 1, "relay", (second,))
-
     grads = {}
     sums = []
 
-    def backward_mlp(owner, number, source, tokens, scaled=False):
+    def backward_mlp(owner, number, source, tokens, after, scaled=False):
         (
             branch,
             grads["before"],
@@ -1429,49 +1439,56 @@
             shift,
         ) = mlp_backward(
             info, owner, number, source, tokens, vec, wo_own, wo_oth, wu_own, wu_oth, wd_own,
-            wd_oth, kept, grads, scaled,
+            wd_oth, kept, grads, scaled, after,
         )
         if not scaled:
             grads["branch"] = branch
         return grad_mixed, grad_res, small, shift
 
-    def backward_attention(owner, number, grad_mixed):
-        dq, dkv_here, dkv_send = attend_backward(info, owner, number, grad_mixed, kept)
+    def backward_attention(owner, number, grad_mixed, after=()):
+        dq, dkv_here, dkv_send = attend_backward(info, owner, number, grad_mixed, kept, after)
         return dq, dkv_here, swap(dkv_send)
 
-    def backward_qkv(owner, number, dq, dkv_here, dkv_there, grad_res, small, shift):
+    def backward_qkv(owner, number, dq, dkv_here, dkv_there, grad_res, small, shift, after=()):
         grads["packed"], grads["input"], relayed, small_one, shift_qkv = qkv_backward(
             info, owner, number, dq, dkv_here, dkv_there, wq_own, wq_oth, grad_res, vec, kept,
-            grads,
+            grads, after,
         )
         sums.append((small, shift, small_one, shift_qkv))
         return relayed
 
-    def backward(owner, number, source, tokens):
-        grad_mixed, grad_res, small, shift = backward_mlp(owner, number, source, tokens)
+    def backward(owner, number, source, tokens, after):
+        grad_mixed, grad_res, small, shift = backward_mlp(owner, number, source, tokens, after)
         flows = backward_attention(owner, number, grad_mixed)
         return backward_qkv(owner, number, *flows, grad_res, small, shift)
 
-    relayed = backward(1, 0, "argument", (cotangent, cot_oth[0]))
+    relayed = forward(0, 0, "argument", (inputs, first_oth))
+    first = lax.ppermute(relayed, "section", [(0, 1)])
+    relayed = forward(0, 1, "argument", (inputs, second_oth), [relayed])
+    second = lax.ppermute(relayed, "section", [(0, 1)])
+    relayed = forward(1, 0, "relay", (first,), [relayed])
+    relayed = backward(1, 0, "argument", (cotangent, cot_oth[0]), [relayed, second])
     first = lax.ppermute(relayed, "section", [(1, 0)])
-    relayed = backward(1, 1, "argument", (cotangent, cot_oth[1]))
-    relayed, first = lax.optimization_barrier((relayed, first))
+    relayed = forward(1, 1, "relay", (second,), [relayed], [first])
+    relayed = backward(1, 1, "argument", (cotangent, cot_oth[1]), [relayed])
     second = lax.ppermute(relayed, "section", [(1, 0)])
-    backward(0, 0, "relay", (first,))
+    relayed = backward(0, 0, "relay", (first,), [relayed])
 
     def weight_grad(left, right):
         return lax.dot_general(
             left, right, (((0, 1), (0, 1)), ((), ())), preferred_element_type=F32
         ).astype(BF16)
 
-    grads["branch"] = scale_branch(info, 0, 1, second, vec, grads["branch"])
+    grads["branch"] = scale_branch(info, 0, 1, second, vec, grads["branch"], [relayed])
     active, g_branch = kept["active"], grads["branch"]
     down_oth = weight_grad(active[:, :, hidden_half:], g_branch)
     down_sent = swap(down_oth)
-    down_own = weight_grad(active[:, :, :hidden_half], tied(g_branch, down_oth))
+    down_own = weight_grad(active[:, :, :hidden_half], g_branch)
     ring_down = Ring(info, [(down_own, down_sent)], [down_own.shape], WholeRows(width))
     second = tied(second, *ring_down.moving)
-    grad_mixed, grad_res, small, shift = backward_mlp(0, 1, "relay", (second,), scaled=True)
+    grad_mixed, grad_res, small, shift = backward_mlp(
+        0, 1, "relay", (second,), list(ring_down.moving), scaled=True
+    )
     ring_down.advance(grad_mixed)
     normed2 = tied(kept["normed2"], *ring_down.moving)
     before = grads["before"]

time: 752 us -> 779 us (1.036)
  Pallas kernels: 311 us -> 376 us
  waiting for transfers between devices: 248 us -> 206 us
  starting transfers between devices: 109 us -> 99 us
  matrix products: 34.4 us -> 43.5 us
    pallas_call x76 -> x73, Pallas kernels: 232 us -> 297 us  [manual(): pl.pallas_call(body, out_shape=[jax.ShapeDtypeStruct(s, d) for s, d, _, _...]
    ppermute x1, waiting for transfers between devices: 115 us -> 51.5 us  [shards(): first = lax.ppermute(relayed, 'section', [(1, 0)])]
    ppermute x1, waiting for transfers between devices: 2.09 us -> 32.5 us  [shards(): second = lax.ppermute(relayed, 'section', [(1, 0)])]
    ppermute x84, waiting for transfers between devices: 112 us -> 91.9 us  [advance(): lax.ppermute(self.moving[w], 'dp', self.routes[w])]
    dot_general x10, matrix products: 34.4 us -> 43.5 us  [weight_grad(): lax.dot_general(left, right, (((0, 1), (0, 1)), ((), ())), preferred_elem...]
    ppermute x23, waiting for transfers between devices: 9.28 us -> 18.1 us  [swap(): return lax.ppermute(block, 'tensor', [(0, 1), (1, 0)])]
    ppermute x84, starting transfers between devices: 96.8 us -> 88.3 us  [advance(): lax.ppermute(self.moving[w], 'dp', self.routes[w])]
    unnamed x112 -> x234, local copies, waits for them, and re-layouts: 32.1 us -> 35.5 us
  transfers between devices with their start and end apart: 111 -> 111, of which waited for: 45 -> 41; matrix products, arithmetic and copies ran while one was open for 3% -> 4% of each run, Pallas kernels for 37% -> 32%
where the time goes in v3:
time: 779 us; the launch traced here: 765 us
  Pallas kernels  376 us (48%)
  waiting for transfers between devices  206 us (26%)
  starting transfers between devices  99 us (13%)
  matrix products  43.5 us (6%)
  local copies, waits for them, and re-layouts  37.1 us (5%)
    pallas_call x73, Pallas kernels, manual(): pl.pallas_call(body, out_shape=[jax.ShapeDtypeStruct(s, d) for s, d, _, _...  297 us
    ppermute x84, waiting for transfers between devices, advance(): lax.ppermute(self.moving[w], 'dp', self.routes[w])  91.9 us
    ppermute x84, starting transfers between devices, advance(): lax.ppermute(self.moving[w], 'dp', self.routes[w])  88.3 us
    pallas_call x8, Pallas kernels, call(): pl.pallas_call(body, out_shape=[jax.ShapeDtypeStruct(s, d) for s, d, _, _...  72.2 us
    ppermute x1, waiting for transfers between devices, shards(): first = lax.ppermute(relayed, 'section', [(1, 0)])  51.5 us
    dot_general x10, matrix products, weight_grad(): lax.dot_general(left, right, (((0, 1), (0, 1)), ((), ())), preferred_elem...  43.5 us
    unnamed x234, local copies, waits for them, and re-layouts  35.5 us
    ppermute x1, waiting for transfers between devices, shards(): second = lax.ppermute(relayed, 'section', [(1, 0)])  32.5 us
  transfers between devices with their start and end apart: 111, of which 41 were waited for; matrix products, arithmetic and copies ran while one was open for 4% of the time, Pallas kernels for 32%

profile of v3, /device:TPU:0, one launch (start us, length us, event | category | flops | bytes accessed | tf_op | source)
XLA Modules:
  0.0 765.3 jit_solution(12752961988700295738)
XLA Ops:
  10.4 6.5 shard_map.292
  24.2 12.3 %shard_map.294 = (bf16[3,16,384,768]{3,2,1,0:T(8,128)(2,1)}, f32[3,384,1024]{2,1,0:T(8,128)}, bf16[384,1024]{1,0:T(8,128)(2,1)}, f32[3,384,1024]{2,1,0:T(8,128)}, bf16[3,2,768,1024]{3,2,1,0:T(8,128)(2,1)}) custom-call(s32[19]{0:T(128)} %copy-done.6, bf16[2,384,1024]{2,1,0:T(8,128)(2,1)} %shard_map.293.refs_1_.refs_5_, ...), custom_call_target="tpu_custom_call" | custom-call | flops 1207959552 | bytes 21233664 | tf_op jit(solution)/shard_map/pallas_call | solution.py:83
  36.6 22.3 %shard_map.295 = (bf16[2,384,1024]{2,1,0:T(8,128)(2,1)}, f32[2,384,1024]{2,1,0:T(8,128)}, bf16[2,384,1024]{2,1,0:T(8,128)(2,1)}, bf16[2,384,4096]{2,1,0:T(8,128)...) custom-call(s32[19]{0:T(128)} %copy-done.6, ...), custom_call_target="tpu_custom_call" | custom-call | flops 7247757312 | bytes 31457280 | tf_op jit(solution)/shard_map/pallas_call | solution.py:123
  59.6 6.9 shard_map.296
  74.5 12.2 %shard_map.298 = (bf16[3,16,384,768]{3,2,1,0:T(8,128)(2,1)}, f32[3,384,1024]{2,1,0:T(8,128)}, bf16[384,1024]{1,0:T(8,128)(2,1)}, f32[3,384,1024]{2,1,0:T(8,128)}, bf16[3,2,768,1024]{3,2,1,0:T(8,128)(2,1)}) custom-call(s32[19]{0:T(128)} %copy-done.6, ...), custom_call_target="tpu_custom_call", output_to_operand_aliasing={{0}: (4, {}), {1}: (5, {}), {3}: (6, {}), {4}: (7, {})} | custom-call | flops 1207959552 | bytes 21233664 | tf_op jit(solution)/shard_map/pallas_call | solution.py:83
  86.7 21.1 %shard_map.299 = (bf16[2,384,1024]{2,1,0:T(8,128)(2,1)}, f32[2,384,1024]{2,1,0:T(8,128)}, bf16[2,384,1024]{2,1,0:T(8,128)(2,1)}, bf16[2,384,4096]{2,1,0:T(8,128)...) custom-call(s32[19]{0:T(128)} %copy-done.6, ...), custom_call_target="tpu_custom_call", output_to_operand_aliasing={{0}: (11, {}), {1}: (12, {}), {2}: (13, {}), {3}: (14, {}),... | custom-call | flops 7247757312 | bytes 31457280 | tf_op jit(solution)/shard_map/pallas_call | solution.py:123
  121.8 11.7 %collective-permute-done.9.refs_15_.refs_1_ = bf16[384,1024]{1,0:T(8,128)(2,1)S(1)} collective-permute-done((bf16[384,1024]{1,0:T(8,128)(2,1)}, bf16[384,1024]{1,0:T(8,128)(2,1)S(1)}, u32[]{:S(2)}, u32[]{:S(2)}) %collective-permute-start.9) | collective-permute-done | bytes 786464 | tf_op jit(solution)/shard_map/ppermute | solution.py:1468
  134.3 10.3 %shard_map.305 = (bf16[2,384,1024]{2,1,0:T(8,128)(2,1)}, bf16[2,384,4096]{2,1,0:T(8,128)(2,1)}, bf16[2,384,1024]{2,1,0:T(8,128)(2,1)}, bf16[384,1024]{1,0:T(8,12...) custom-call(s32[19]{0:T(128)} %copy-done.6, bf16[2,1,768,512]{3,2,1,0:T(8,128)(2,1)} %refs_1_.13, ...), custom_call_target="tpu_custom_call" | custom-call | flops 7247757312 | bytes 31457280 | tf_op jit(solution)/shard_map/pallas_call | solution.py:123
  163.9 51.5 %collective-permute-done.15.refs_19_.refs_1_ = bf16[384,1024]{1,0:T(8,128)(2,1)S(1)} collective-permute-done((bf16[384,1024]{1,0:T(8,128)(2,1)S(1)}, bf16[384,1024]{1,0:T(8,128)(2,1)S(1)}, u32[]{:S(2)}, u32[]{:S(2)}) %collective-permute-start.15) | collective-permute-done | bytes 786464 | tf_op jit(solution)/shard_map/ppermute | solution.py:1471
  217.6 12.6 %shard_map.314 = (bf16[2,384,1024]{2,1,0:T(8,128)(2,1)}, bf16[2,384,4096]{2,1,0:T(8,128)(2,1)}, bf16[2,384,1024]{2,1,0:T(8,128)(2,1)}, bf16[384,1024]{1,0:T(8,12...) custom-call(s32[19]{0:T(128)} %copy-done.6, ...), custom_call_target="tpu_custom_call", output_to_operand_aliasing={{0}: (14, {}), {1}: (15, {}), {2}: (16, {})} | custom-call | flops 7247757312 | bytes 31457280 | tf_op jit(solution)/shard_map/pallas_call | solution.py:123
  240.8 17.9 %shard_map.317 = (bf16[2,384,1024]{2,1,0:T(8,128)(2,1)}, bf16[2,384,4096]{2,1,0:T(8,128)(2,1)}, bf16[2,384,1024]{2,1,0:T(8,128)(2,1)}, bf16[384,1024]{1,0:T(8,12...) custom-call(s32[19]{0:T(128)} %copy-done.6, ...), custom_call_target="tpu_custom_call", output_to_operand_aliasing={{0}: (13, {}), {1}: (14, {}), {2}: (15, {})} | custom-call | flops 7247757312 | bytes 31457280 | tf_op jit(solution)/shard_map/pallas_call | solution.py:123
  258.7 15.8 %shard_map.318 = (bf16[384,1024]{1,0:T(8,128)(2,1)}, bf16[2,384,1024]{2,1,0:T(8,128)(2,1)}, bf16[2,384,1024]{2,1,0:T(8,128)(2,1)}) custom-call(s32[19]{0:T(128)} %copy-done.6, bf16[384,1024]{1,0:T(8,128)(2,1)} %get-tuple-element.471.refs_1_, bf16[2,384,1024]{2,1,0:T(8,128)(2,1)} %shard_map.309.refs_1_.refs_2_, ...), custom_call_target="tpu_custom_call" | custom-call | flops 2415919104 | bytes 21233664 | tf_op jit(solution)/shard_map/pallas_call | solution.py:83
  278.3 9.3 %shard_map.319 = (bf16[2,384,3072]{2,1,0:T(8,128)(2,1)}, bf16[2,384,1024]{2,1,0:T(8,128)(2,1)}, bf16[384,1024]{1,0:T(8,128)(2,1)}, f32[8,1024]{1,0:T(8,128)}, f32[8,512]{1,0:T(8,128)}) custom-call(s32[19]{0:T(128)} %copy-done.6, bf16[384,1024]{1,0:T(8,128)(2,1)} %get-tuple-element.472.refs_1_, ...), custom_call_target="tpu_custom_call", output_to_operand_aliasing={{0}: (9, {}), {1}: (10, {})} | custom-call | flops 2415919104 | bytes 12582912 | tf_op jit(solution)/shard_map/pallas_call | solution.py:123
  287.6 32.5 %collective-permute-done.18.refs_1_ = bf16[384,1024]{1,0:T(8,128)(2,1)S(1)} collective-permute-done((bf16[384,1024]{1,0:T(8,128)(2,1)S(1)}, bf16[384,1024]{1,0:T(8,128)(2,1)S(1)}, u32[]{:S(2)}, u32[]{:S(2)}) %collective-permute-start.18) | collective-permute-done | bytes 786464 | tf_op jit(solution)/shard_map/ppermute | solution.py:1474
  323.9 5.9 bitcast_convert_fusion.2
  330.0 7.0 bitcast_convert_fusion.3.refs_1_
  343.0 17.9 %shard_map.322 = (bf16[2,384,1024]{2,1,0:T(8,128)(2,1)}, bf16[2,384,4096]{2,1,0:T(8,128)(2,1)}, bf16[2,384,1024]{2,1,0:T(8,128)(2,1)}, bf16[384,1024]{1,0:T(8,12...) custom-call(s32[19]{0:T(128)} %copy-done.6, ...), custom_call_target="tpu_custom_call", output_to_operand_aliasing={{1}: (13, {}), {2}: (14, {})} | custom-call | flops 7247757312 | bytes 31457280 | tf_op jit(solution)/shard_map/pallas_call | solution.py:123
  364.9 7.0 bitcast_convert_fusion.1
  373.9 6.9 collective-permute-done.23.refs_3_
  388.3 6.9 bitcast_convert_fusion.refs_1_
  402.4 15.7 %shard_map.327 = (bf16[384,1024]{1,0:T(8,128)(2,1)}, bf16[2,384,1024]{2,1,0:T(8,128)(2,1)}, bf16[2,384,1024]{2,1,0:T(8,128)(2,1)}) custom-call(s32[19]{0:T(128)} %copy-done.6, bf16[384,1024]{1,0:T(8,128)(2,1)} %get-tuple-element.503.refs_1_, bf16[2,384,1024]{2,1,0:T(8,128)(2,1)} %shard_map.309.refs_1_.refs_2_, ...), custom_call_target="tpu_custom_call" | custom-call | flops 2415919104 | bytes 21233664 | tf_op jit(solution)/shard_map/pallas_call | solution.py:83
  422.3 5.3 collective-permute-done.29.refs_3_
  445.8 9.7 %shard_map.330 = (bf16[2,384,3072]{2,1,0:T(8,128)(2,1)}, bf16[2,384,1024]{2,1,0:T(8,128)(2,1)}, bf16[384,1024]{1,0:T(8,128)(2,1)}, f32[8,1024]{1,0:T(8,128)}, f32[8,512]{1,0:T(8,128)}) custom-call(s32[19]{0:T(128)} %copy-done.6, bf16[384,1024]{1,0:T(8,128)(2,1)} %get-tuple-element.504.refs_1_, ...), custom_call_target="tpu_custom_call", output_to_operand_aliasing={{0}: (9, {}), {1}: (10, {})} | custom-call | flops 2415919104 | bytes 12582912 | tf_op jit(solution)/shard_map/pallas_call | solution.py:123
  462.3 5.8 bitcast_convert_fusion.5
  482.1 5.9 collective-permute-done.41.refs_4_
  497.3 5.7 bitcast_convert_fusion.4.refs_1_
  582.2 5.4 collective-permute-done.70.refs_4_
  638.4 6.6 collective-permute-done.87.refs_1_
  657.1 7.6 collective-permute-done.91.refs_1_
  677.0 8.4 %collective-permute-done.95.refs_1_ = bf16[64,2048]{1,0:T(8,128)(2,1)S(1)} collective-permute-done((bf16[64,2048]{1,0:T(8,128)(2,1)}, bf16[64,2048]{1,0:T(8,128)(2,1)S(1)}, u32[]{:S(2)}, u32[]{:S(2)}) %collective-permute-start.95) | collective-permute-done | bytes 262176 | tf_op jit(solution)/shard_map/ppermute | solution.py:1093
  696.4 4.7 collective-permute-done.97.refs_1_
  733.1 4.7 collective-permute-done.103.refs_1_
  (523 shorter events, 382.9 us)
Async XLA Ops:
  8.8 27.7 %collective-permute-start.7 = (bf16[1024,2048]{1,0:T(8,128)(2,1)}, bf16[1024,2048]{1,0:T(8,128)(2,1)}, u32[]{:S(2)}, u32[]{:S(2)}) collective-permute-start(bf16[1024,2048]{1,0:T(8,128)(2,1)} %bitcast.74), channel_id=1, source_target_pairs={{0,8},{8,0},{1,9},{9,1},{2,10},{10,2},{3,11},{11,3},{4,12},{12,4},... | collective-permute-start | bytes 12582920 | tf_op jit(solution)/shard_map/ppermute | solution.py:956
  17.4 19.2 %collective-permute-start.6 = (bf16[512,1024]{1,0:T(8,128)(2,1)}, bf16[512,1024]{1,0:T(8,128)(2,1)}, u32[]{:S(2)}, u32[]{:S(2)}) collective-permute-start(bf16[512,1024]{1,0:T(8,128)(2,1)} %bitcast.8.refs_4_.refs_8_.refs_7_), channel_id=1, source_target_pairs={{0,8},{8,0},{1,9},{9,1},{2,10},{10,2},{3,11},{11,3},{4,12},{12,4},... | collective-permute-start | bytes 3145736 | tf_op jit(solution)/shard_map/ppermute | solution.py:956
  22.5 36.3 %collective-permute-start.3 = (bf16[384,512]{1,0:T(8,128)(2,1)S(1)}, bf16[384,512]{1,0:T(8,128)(2,1)S(1)}, u32[]{:S(2)}, u32[]{:S(2)}) collective-permute-start(bf16[384,512]{1,0:T(8,128)(2,1)S(1)} %bitcast.56), channel_id=1, source_target_pairs={{0,8},{8,0},{1,9},{9,1},{2,10},{10,2},{3,11},{11,3},{4,12},{12,4},... | collective-permute-start | bytes 1179656 | tf_op jit(solution)/shard_map/ppermute | solution.py:956
  66.9 40.8 %collective-permute-start.10 = (bf16[384,1024]{1,0:T(8,128)(2,1)}, bf16[384,1024]{1,0:T(8,128)(2,1)}, u32[]{:S(2)}, u32[]{:S(2)}) collective-permute-start(bf16[384,1024]{1,0:T(8,128)(2,1)} %get-tuple-element.387.refs_9_), channel_id=1, source_target_pairs={{0,16},{1,17},{2,18},{3,19},{4,20},{5,21},{6,22},{7,23},{8,24},{9,... | collective-permute-start | bytes 2359304 | tf_op jit(solution)/shard_map/ppermute | solution.py:1466
  114.5 19.0 %collective-permute-start.9 = (bf16[384,1024]{1,0:T(8,128)(2,1)}, bf16[384,1024]{1,0:T(8,128)(2,1)S(1)}, u32[]{:S(2)}, u32[]{:S(2)}) collective-permute-start(bf16[384,1024]{1,0:T(8,128)(2,1)} %get-tuple-element.404.refs_8_), channel_id=1, source_target_pairs={{0,16},{1,17},{2,18},{3,19},{4,20},{5,21},{6,22},{7,23},{8,24},{9,... | collective-permute-start | bytes 2359304 | tf_op jit(solution)/shard_map/ppermute | solution.py:1468
  156.3 59.1 %collective-permute-start.15 = (bf16[384,1024]{1,0:T(8,128)(2,1)S(1)}, bf16[384,1024]{1,0:T(8,128)(2,1)S(1)}, u32[]{:S(2)}, u32[]{:S(2)}) collective-permute-start(bf16[384,1024]{1,0:T(8,128)(2,1)S(1)} %copy-done.26), channel_id=1, source_target_pairs={{16,0},{17,1},{18,2},{19,3},{20,4},{21,5},{22,6},{23,7},{24,8},{25... | collective-permute-start | bytes 2359304 | tf_op jit(solution)/shard_map/ppermute | solution.py:1471
  274.7 45.4 %collective-permute-start.18 = (bf16[384,1024]{1,0:T(8,128)(2,1)S(1)}, bf16[384,1024]{1,0:T(8,128)(2,1)S(1)}, u32[]{:S(2)}, u32[]{:S(2)}) collective-permute-start(bf16[384,1024]{1,0:T(8,128)(2,1)S(1)} %copy-done.27), channel_id=1, source_target_pairs={{16,0},{17,1},{18,2},{19,3},{20,4},{21,5},{22,6},{23,7},{24,8},{25... | collective-permute-start | bytes 2359304 | tf_op jit(solution)/shard_map/ppermute | solution.py:1474
  340.0 20.9 %collective-permute-start.21 = (bf16[128,1024]{1,0:T(8,128)(2,1)}, bf16[128,1024]{1,0:T(8,128)(2,1)S(1)}, u32[]{:S(2)}, u32[]{:S(2)}) collective-permute-start(bf16[128,1024]{1,0:T(8,128)(2,1)} %get-tuple-element.479.refs_15_), channel_id=1, source_target_pairs={{0,2},{2,4},{4,6},{6,7},{7,5},{5,3},{3,1},{1,0},{8,10},{10,12},{12... | collective-permute-start | bytes 786440 | tf_op jit(solution)/shard_map/ppermute | solution.py:1093
  343.0 17.9 %collective-permute-start.22 = (bf16[128,1024]{1,0:T(8,128)(2,1)}, bf16[128,1024]{1,0:T(8,128)(2,1)S(1)}, u32[]{:S(2)}, u32[]{:S(2)}) collective-permute-start(bf16[128,1024]{1,0:T(8,128)(2,1)} %get-tuple-element.480.refs_16_), channel_id=1, source_target_pairs={{0,1},{2,0},{4,2},{6,4},{7,6},{5,7},{3,5},{1,3},{8,9},{10,8},{12,1... | collective-permute-start | bytes 786440 | tf_op jit(solution)/shard_map/ppermute | solution.py:1093
  371.9 27.7 %collective-permute-start.27 = (bf16[1024,2048]{1,0:T(8,128)(2,1)}, bf16[1024,2048]{1,0:T(8,128)(2,1)}, u32[]{:S(2)}, u32[]{:S(2)}) collective-permute-start(bf16[1024,2048]{1,0:T(8,128)(2,1)} %bitcast_convert_fusion.1), channel_id=1, source_target_pairs={{0,8},{8,0},{1,9},{9,1},{2,10},{10,2},{3,11},{11,3},{4,12},{12,4},... | collective-permute-start | bytes 12582920 | tf_op jit(solution)/shard_map/ppermute | solution.py:956
  418.2 26.5 %collective-permute-start.28 = (bf16[2,384,1024]{2,1,0:T(8,128)(2,1)}, bf16[2,384,1024]{2,1,0:T(8,128)(2,1)S(1)}, u32[]{:S(2)}, u32[]{:S(2)}) collective-permute-start(bf16[2,384,1024]{2,1,0:T(8,128)(2,1)} %get-tuple-element.506), channel_id=1, source_target_pairs={{0,8},{8,0},{1,9},{9,1},{2,10},{10,2},{3,11},{11,3},{4,12},{12,4},... | collective-permute-start | bytes 4718600 | tf_op jit(solution)/shard_map/ppermute | solution.py:956
  437.5 18.0 %collective-permute-start.36 = (bf16[64,2048]{1,0:T(8,128)(2,1)}, bf16[64,2048]{1,0:T(8,128)(2,1)S(1)}, u32[]{:S(2)}, u32[]{:S(2)}) collective-permute-start(bf16[64,2048]{1,0:T(8,128)(2,1)} %get-tuple-element.514), channel_id=1, source_target_pairs={{0,2},{2,4},{4,6},{6,7},{7,5},{5,3},{3,1},{1,0},{8,10},{10,12},{12... | collective-permute-start | bytes 786440 | tf_op jit(solution)/shard_map/ppermute | solution.py:1093
  439.1 16.4 %collective-permute-start.37 = (bf16[64,2048]{1,0:T(8,128)(2,1)}, bf16[64,2048]{1,0:T(8,128)(2,1)}, u32[]{:S(2)}, u32[]{:S(2)}) collective-permute-start(bf16[64,2048]{1,0:T(8,128)(2,1)} %get-tuple-element.515), channel_id=1, source_target_pairs={{0,1},{2,0},{4,2},{6,4},{7,6},{5,7},{3,5},{1,3},{8,9},{10,8},{12,1... | collective-permute-start | bytes 786440 | tf_op jit(solution)/shard_map/ppermute | solution.py:1093
  468.2 51.5 %collective-permute-start.42 = (bf16[1024,1536]{1,0:T(8,128)(2,1)}, bf16[1024,1536]{1,0:T(8,128)(2,1)}, u32[]{:S(2)}, u32[]{:S(2)}) collective-permute-start(bf16[1024,1536]{1,0:T(8,128)(2,1)} %bitcast_convert_fusion.5), channel_id=1, source_target_pairs={{0,8},{8,0},{1,9},{9,1},{2,10},{10,2},{3,11},{11,3},{4,12},{12,4},... | collective-permute-start | bytes 9437192 | tf_op jit(solution)/shard_map/ppermute | solution.py:956
  472.4 44.2 %collective-permute-start.43 = (bf16[1024,512]{1,0:T(8,128)(2,1)}, bf16[1024,512]{1,0:T(8,128)(2,1)S(1)}, u32[]{:S(2)}, u32[]{:S(2)}) collective-permute-start(bf16[1024,512]{1,0:T(8,128)(2,1)} %pad_maximum_fusion.1), channel_id=1, source_target_pairs={{0,8},{8,0},{1,9},{9,1},{2,10},{10,2},{3,11},{11,3},{4,12},{12,4},... | collective-permute-start | bytes 3145736 | tf_op jit(solution)/shard_map/ppermute | solution.py:956
  472.4 15.7 %collective-permute-start.38 = (bf16[128,1024]{1,0:T(8,128)(2,1)}, bf16[128,1024]{1,0:T(8,128)(2,1)}, u32[]{:S(2)}, u32[]{:S(2)}) collective-permute-start(bf16[128,1024]{1,0:T(8,128)(2,1)} %get-tuple-element.523), channel_id=1, source_target_pairs={{0,2},{2,4},{4,6},{6,7},{7,5},{5,3},{3,1},{1,0},{8,10},{10,12},{12... | collective-permute-start | bytes 786440 | tf_op jit(solution)/shard_map/ppermute | solution.py:1093
  507.6 16.4 %collective-permute-start.53 = (bf16[128,1024]{1,0:T(8,128)(2,1)}, bf16[128,1024]{1,0:T(8,128)(2,1)}, u32[]{:S(2)}, u32[]{:S(2)}) collective-permute-start(bf16[128,1024]{1,0:T(8,128)(2,1)} %get-tuple-element.567.refs_1_), channel_id=1, source_target_pairs={{0,2},{2,4},{4,6},{6,7},{7,5},{5,3},{3,1},{1,0},{8,10},{10,12},{12... | collective-permute-start | bytes 786440 | tf_op jit(solution)/shard_map/ppermute | solution.py:1093
  573.6 17.8 %collective-permute-start.67 = (bf16[64,2176]{1,0:T(8,128)(2,1)}, bf16[64,2176]{1,0:T(8,128)(2,1)S(1)}, u32[]{:S(2)}, u32[]{:S(2)}) collective-permute-start(bf16[64,2176]{1,0:T(8,128)(2,1)} %get-tuple-element.605), channel_id=1, source_target_pairs={{0,2},{2,4},{4,6},{6,7},{7,5},{5,3},{3,1},{1,0},{8,10},{10,12},{12... | collective-permute-start | bytes 835592 | tf_op jit(solution)/shard_map/ppermute | solution.py:1093
  574.6 16.7 %collective-permute-start.68 = (bf16[64,2176]{1,0:T(8,128)(2,1)}, bf16[64,2176]{1,0:T(8,128)(2,1)S(1)}, u32[]{:S(2)}, u32[]{:S(2)}) collective-permute-start(bf16[64,2176]{1,0:T(8,128)(2,1)} %get-tuple-element.606), channel_id=1, source_target_pairs={{0,1},{2,0},{4,2},{6,4},{7,6},{5,7},{3,5},{1,3},{8,9},{10,8},{12,1... | collective-permute-start | bytes 835592 | tf_op jit(solution)/shard_map/ppermute | solution.py:1093
  580.1 18.0 %collective-permute-start.77 = (bf16[128,1024]{1,0:T(8,128)(2,1)}, bf16[128,1024]{1,0:T(8,128)(2,1)S(1)}, u32[]{:S(2)}, u32[]{:S(2)}) collective-permute-start(bf16[128,1024]{1,0:T(8,128)(2,1)} %get-tuple-element.610), channel_id=1, source_target_pairs={{0,2},{2,4},{4,6},{6,7},{7,5},{5,3},{3,1},{1,0},{8,10},{10,12},{12... | collective-permute-start | bytes 786440 | tf_op jit(solution)/shard_map/ppermute | solution.py:1093
  581.4 18.3 %collective-permute-start.78 = (bf16[128,1024]{1,0:T(8,128)(2,1)}, bf16[128,1024]{1,0:T(8,128)(2,1)S(1)}, u32[]{:S(2)}, u32[]{:S(2)}) collective-permute-start(bf16[128,1024]{1,0:T(8,128)(2,1)} %get-tuple-element.611), channel_id=1, source_target_pairs={{0,1},{2,0},{4,2},{6,4},{7,6},{5,7},{3,5},{1,3},{8,9},{10,8},{12,1... | collective-permute-start | bytes 786440 | tf_op jit(solution)/shard_map/ppermute | solution.py:1093
  613.2 16.9 %collective-permute-start.79 = (bf16[64,2176]{1,0:T(8,128)(2,1)}, bf16[64,2176]{1,0:T(8,128)(2,1)S(1)}, u32[]{:S(2)}, u32[]{:S(2)}) collective-permute-start(bf16[64,2176]{1,0:T(8,128)(2,1)} %get-tuple-element.632), channel_id=1, source_target_pairs={{0,2},{2,4},{4,6},{6,7},{7,5},{5,3},{3,1},{1,0},{8,10},{10,12},{12... | collective-permute-start | bytes 835592 | tf_op jit(solution)/shard_map/ppermute | solution.py:1093
  613.7 16.4 %collective-permute-start.80 = (bf16[64,2176]{1,0:T(8,128)(2,1)}, bf16[64,2176]{1,0:T(8,128)(2,1)S(1)}, u32[]{:S(2)}, u32[]{:S(2)}) collective-permute-start(bf16[64,2176]{1,0:T(8,128)(2,1)} %get-tuple-element.633), channel_id=1, source_target_pairs={{0,1},{2,0},{4,2},{6,4},{7,6},{5,7},{3,5},{1,3},{8,9},{10,8},{12,1... | collective-permute-start | bytes 835592 | tf_op jit(solution)/shard_map/ppermute | solution.py:1093
  634.3 14.3 %collective-permute-start.85 = (bf16[64,2176]{1,0:T(8,128)(2,1)}, bf16[64,2176]{1,0:T(8,128)(2,1)S(1)}, u32[]{:S(2)}, u32[]{:S(2)}) collective-permute-start(bf16[64,2176]{1,0:T(8,128)(2,1)} %get-tuple-element.646), channel_id=1, source_target_pairs={{0,2},{2,4},{4,6},{6,7},{7,5},{5,3},{3,1},{1,0},{8,10},{10,12},{12... | collective-permute-start | bytes 835592 | tf_op jit(solution)/shard_map/ppermute | solution.py:1093
  652.9 15.9 %collective-permute-start.89 = (bf16[64,2176]{1,0:T(8,128)(2,1)}, bf16[64,2176]{1,0:T(8,128)(2,1)S(1)}, u32[]{:S(2)}, u32[]{:S(2)}) collective-permute-start(bf16[64,2176]{1,0:T(8,128)(2,1)} %get-tuple-element.655.refs_1_), channel_id=1, source_target_pairs={{0,2},{2,4},{4,6},{6,7},{7,5},{5,3},{3,1},{1,0},{8,10},{10,12},{12... | collective-permute-start | bytes 835592 | tf_op jit(solution)/shard_map/ppermute | solution.py:1093
  653.8 15.0 %collective-permute-start.90 = (bf16[64,2176]{1,0:T(8,128)(2,1)}, bf16[64,2176]{1,0:T(8,128)(2,1)S(1)}, u32[]{:S(2)}, u32[]{:S(2)}) collective-permute-start(bf16[64,2176]{1,0:T(8,128)(2,1)} %get-tuple-element.656.refs_2_), channel_id=1, source_target_pairs={{0,1},{2,0},{4,2},{6,4},{7,6},{5,7},{3,5},{1,3},{8,9},{10,8},{12,1... | collective-permute-start | bytes 835592 | tf_op jit(solution)/shard_map/ppermute | solution.py:1093
  672.8 18.0 %collective-permute-start.93 = (bf16[64,2176]{1,0:T(8,128)(2,1)}, bf16[64,2176]{1,0:T(8,128)(2,1)S(1)}, u32[]{:S(2)}, u32[]{:S(2)}) collective-permute-start(bf16[64,2176]{1,0:T(8,128)(2,1)} %get-tuple-element.664), channel_id=1, source_target_pairs={{0,2},{2,4},{4,6},{6,7},{7,5},{5,3},{3,1},{1,0},{8,10},{10,12},{12... | collective-permute-start | bytes 835592 | tf_op jit(solution)/shard_map/ppermute | solution.py:1093
  674.7 16.0 %collective-permute-start.94 = (bf16[64,2176]{1,0:T(8,128)(2,1)}, bf16[64,2176]{1,0:T(8,128)(2,1)S(1)}, u32[]{:S(2)}, u32[]{:S(2)}) collective-permute-start(bf16[64,2176]{1,0:T(8,128)(2,1)} %get-tuple-element.665), channel_id=1, source_target_pairs={{0,1},{2,0},{4,2},{6,4},{7,6},{5,7},{3,5},{1,3},{8,9},{10,8},{12,1... | collective-permute-start | bytes 835592 | tf_op jit(solution)/shard_map/ppermute | solution.py:1093
  710.3 33.3 %collective-permute-start.16 = (bf16[2,384,512]{2,1,0:T(8,128)(2,1)}, bf16[2,384,512]{2,1,0:T(8,128)(2,1)}, u32[]{:S(2)}, u32[]{:S(2)}) collective-permute-start(bf16[2,384,512]{2,1,0:T(8,128)(2,1)} %shard_map.312), channel_id=1, source_target_pairs={{0,8},{8,0},{1,9},{9,1},{2,10},{10,2},{3,11},{11,3},{4,12},{12,4},... | collective-permute-start | bytes 2359304 | tf_op jit(solution)/shard_map/ppermute | solution.py:956
  711.0 34.4 %collective-permute-start.33 = (bf16[2,384,512]{2,1,0:T(8,128)(2,1)S(1)}, bf16[2,384,512]{2,1,0:T(8,128)(2,1)}, u32[]{:S(2)}, u32[]{:S(2)}) collective-permute-start(bf16[2,384,512]{2,1,0:T(8,128)(2,1)S(1)} %shard_map.331), channel_id=1, source_target_pairs={{0,8},{8,0},{1,9},{9,1},{2,10},{10,2},{3,11},{11,3},{4,12},{12,4},... | collective-permute-start | bytes 2359304 | tf_op jit(solution)/shard_map/ppermute | solution.py:956
  741.5 18.3 %collective-permute-start.105 = (bf16[64,2176]{1,0:T(8,128)(2,1)}, bf16[64,2176]{1,0:T(8,128)(2,1)S(1)}, u32[]{:S(2)}, u32[]{:S(2)}) collective-permute-start(bf16[64,2176]{1,0:T(8,128)(2,1)} %get-tuple-element.704), channel_id=1, source_target_pairs={{0,2},{2,4},{4,6},{6,7},{7,5},{5,3},{3,1},{1,0},{8,10},{10,12},{12... | collective-permute-start | bytes 835592 | tf_op jit(solution)/shard_map/ppermute | solution.py:1093
  743.0 16.8 %collective-permute-start.106 = (bf16[64,2176]{1,0:T(8,128)(2,1)}, bf16[64,2176]{1,0:T(8,128)(2,1)S(1)}, u32[]{:S(2)}, u32[]{:S(2)}) collective-permute-start(bf16[64,2176]{1,0:T(8,128)(2,1)} %get-tuple-element.705), channel_id=1, source_target_pairs={{0,1},{2,0},{4,2},{6,4},{7,6},{5,7},{3,5},{1,3},{8,9},{10,8},{12,1... | collective-permute-start | bytes 835592 | tf_op jit(solution)/shard_map/ppermute | solution.py:1093
  (196 other events, 1104.1 us)

commit v4 on v3

--- a/solution.py
+++ b/solution.py
@@ -43,6 +43,14 @@
 
 def tiles(rows):
     return [slice(r, r + TILE) for r in range(0, rows, TILE)]
+
+
+def each_tile(rows, body):
+    def step(i, carry):
+        body(pl.ds(pl.multiple_of(i * TILE, TILE), TILE))
+        return carry
+
+    lax.fori_loop(0, rows // TILE, step, 0, unroll=2)
 
 
 def eights(values):
@@ -184,34 +192,39 @@
         @pl.when(s[ACTIVE + owner] == 1)
         def _():
             arriving = token_copies(s, source, number, token_refs, x_v, tok_sems)
-            loads = []
             for part in range(4):
                 ref = own if part < 2 else oth
-                loads.append(begin(ref.at[1 + part % 2], w_v.at[part], w_sems.at[part]))
+                begin(ref.at[1 + part % 2], w_v.at[part], w_sems.at[part])
             for copy in arriving:
                 copy.wait()
             outs = [begin(x_v, x_out.at[number], out_sems.at[0])]
-            for t in tiles(rows):
+
+            def norm(t):
                 hat, _ = norm_stats(x_v[t].astype(F32))
                 n_v[t] = (hat * v[LN1G : LN1G + 1] + v[LN1B : LN1B + 1]).astype(BF16)
+
+            each_tile(rows, norm)
             outs.append(begin(n_v, n_out.at[number], out_sems.at[1]))
-            for part in range(4):
-                loads[part].wait()
-                result = dot(n_v[...], w_v[part])
-                kind, side = part % 2, part // 2
-                columns = slice(side * half, (side + 1) * half)
-                if kind == 1:
-                    result = result + bv[:, columns]
-                kv_v[part] = result.astype(BF16)
-                outs.append(
-                    begin(
-                        kv_v.at[part],
-                        kv_out.at[kind, :, pl.ds(side * half, half)],
-                        out_sems.at[2 + part],
-                    )
+
+            def out_copy(part):
+                columns = pl.ds(pl.multiple_of(part // 2 * half, half), half)
+                return pltpu.make_async_copy(
+                    kv_v.at[part], kv_out.at[part % 2, :, columns], out_sems.at[2 + part]
                 )
+
+            def project(part, carry):
+                pltpu.make_async_copy(own.at[0], w_v.at[part], w_sems.at[part]).wait()
+                columns = pl.ds(pl.multiple_of(part // 2 * half, half), half)
+                shift = bv[:, columns] * (part % 2).astype(F32)
+                kv_v[part] = (dot(n_v[...], w_v[part]) + shift).astype(BF16)
+                out_copy(part).start()
+                return carry
+
+            lax.fori_loop(0, 4, project, 0)
             for copy in outs:
                 copy.wait()
+            for part in range(4):
+                out_copy(part).wait()
 
     stack = (MICRO, rows, width)
     return manual(
@@ -411,7 +424,8 @@
     def kernel(
         s, m, x_ref, v, woo, wot, wuo, wut, wdo, wdt, bu,
         att_out, res_out, n_out, act_out, slope_out, branch_out, y_out, relay_out, m_out,
-        m_v, x_v, wo_v, wu_v, wd_v, att_v, res_v, n_v, h_v, act_v, slope_v, branch_v, y_v, acc,
+        m_v, x_v, wo_v, wu_v, wd_v, att_v, res_v, n_v, h_one, h_two, act_v, slope_v, branch_v, y_v,
+        acc,
         in_sems, wu_sems, wd_sems, out_sems, act_sems, slope_sems,
     ):
         @pl.when(s[ACTIVE + owner] == 1)
@@ -423,27 +437,24 @@
                 begin(wot, wo_v.at[1], in_sems.at[2]),
                 begin(x_ref.at[slot], x_v, in_sems.at[3]),
             ]
-            ups, downs = [], []
-
-            def prefetch(i):
-                if i < steps:
-                    part = pl.ds((i % split) * CHUNK, CHUNK)
-                    up, down = (wuo, wdo) if i < split else (wut, wdt)
-                    ups.append(begin(up.at[:, part], wu_v.at[i], wu_sems.at[i]))
-                    downs.append(begin(down.at[part], wd_v.at[i], wd_sems.at[i]))
-
-            prefetch(0)
-            prefetch(1)
+            for i in range(steps):
+                part = pl.ds((i % split) * CHUNK, CHUNK)
+                up, down = (wuo, wdo) if i < split else (wut, wdt)
+                begin(up.at[:, part], wu_v.at[i], wu_sems.at[i])
+                begin(down.at[part], wd_v.at[i], wd_sems.at[i])
             for copy in first:
                 copy.wait()
             acc[...] = dot(m_v[:, :half], wo_v[0]) + dot(m_v[:, half:], wo_v[1])
-            for t in tiles(rows):
+
+            def first_norm(t):
                 attended = acc[t] + v[OUTB : OUTB + 1]
                 att_v[t] = attended.astype(BF16)
                 residual = x_v[t].astype(F32) + v[SATT : SATT + 1] * attended
                 res_v[t] = residual
                 hat, _ = norm_stats(residual)
                 n_v[t] = (hat * v[LN2G : LN2G + 1] + v[LN2B : LN2B + 1]).astype(BF16)
+
+            each_tile(rows, first_norm)
             outs = [
                 begin(att_v, att_out.at[slot], out_sems.at[0]),
                 begin(res_v, res_out.at[slot], out_sems.at[1]),
@@ -451,34 +462,75 @@
                 begin(m_v, m_out.at[slot], out_sems.at[6]),
             ]
 
-            def up_product(i):
-                ups[i].wait()
-                h_v[i % 2] = dot(n_v[...], wu_v[i])
-
-            def down_product(i):
-                downs[i].wait()
-                part = pl.ds(i * CHUNK, CHUNK)
-                outs.append(begin(act_v.at[i], act_out.at[slot, :, part], act_sems.at[i]))
-                outs.append(begin(slope_v.at[i], slope_out.at[slot, :, part], slope_sems.at[i]))
-                product = dot(act_v[i], wd_v[i])
-                acc[...] = product if i == 0 else acc[...] + product
-
-            up_product(0)
-            for i in range(steps):
-                prefetch(i + 2)
-                if i > 0:
-                    down_product(i - 1)
-                if i + 1 < steps:
-                    up_product(i + 1)
+            def up_product(i, target):
+                target[...] = dot(n_v[...], wu_v[i])
+
+            def up_wait(i):
+                pltpu.make_async_copy(
+                    wuo.at[:, pl.ds(0, CHUNK)], wu_v.at[i], wu_sems.at[i]
+                ).wait()
+
+            def down_wait(i):
+                pltpu.make_async_copy(wdo.at[pl.ds(0, CHUNK)], wd_v.at[i], wd_sems.at[i]).wait()
+
+            def copies(i, side):
+                part = pl.ds(pl.multiple_of(i * CHUNK, CHUNK), CHUNK)
+                return [
+                    pltpu.make_async_copy(
+                        act_v.at[side], act_out.at[slot, :, part], act_sems.at[side]
+                    ),
+                    pltpu.make_async_copy(
+                        slope_v.at[side], slope_out.at[slot, :, part], slope_sems.at[side]
+                    ),
+                ]
+
+            def activate(i, source, side):
+                shift = bu[pl.ds(i, 1), :]
                 for t in tiles(rows):
-                    active, slope = gelu_parts(h_v[i % 2, t] + bu[i : i + 1])
-                    act_v[i, t] = active.astype(BF16)
-                    slope_v[i, t] = slope.astype(BF16)
-            down_product(steps - 1)
-            for t in tiles(rows):
+                    active, slope = gelu_parts(source[t] + shift)
+                    act_v[side, t] = active.astype(BF16)
+                    slope_v[side, t] = slope.astype(BF16)
+
+            def pair(j, carry):
+                i = 2 * j
+                up_wait(i + 1)
+
+                @pl.when(j > 0)
+                def _():
+                    for copy in copies(i - 2, 0) + copies(i - 1, 1):
+                        copy.wait()
+
+                up_product(i + 1, h_two)
+                activate(i, h_one, 0)
+                for copy in copies(i, 0):
+                    copy.start()
+                down_wait(i)
+
+                @pl.when(i + 2 < steps)
+                def _():
+                    up_wait(i + 2)
+
+                up_product(jnp.minimum(i + 2, steps - 1), h_one)
+                acc[...] += dot(act_v[0], wd_v[i])
+                activate(i + 1, h_two, 1)
+                for copy in copies(i + 1, 1):
+                    copy.start()
+                down_wait(i + 1)
+                acc[...] += dot(act_v[1], wd_v[i + 1])
+                return carry
+
+            acc[...] = jnp.zeros_like(acc)
+            up_wait(0)
+            up_product(0, h_one)
+            lax.fori_loop(0, steps // 2, pair, 0)
+
+            def finish(t):
                 branch = acc[t] + v[FC2B : FC2B + 1]
                 y_v[t] = (res_v[t] + v[SMLP : SMLP + 1] * branch).astype(BF16)
                 branch_v[t] = branch.astype(BF16)
+
+            each_tile(rows, finish)
+            outs += copies(steps - 2, 0) + copies(steps - 1, 1)
             outs.append(begin(y_v, relay_out, out_sems.at[3]))
             outs.append(begin(y_v, y_out.at[slot], out_sems.at[4]))
             outs.append(begin(branch_v, branch_out.at[slot], out_sems.at[5]))
@@ -489,7 +541,7 @@
     tall = (MICRO, rows, hidden)
     plain = pltpu.VMEM((rows, width), BF16)
     full = pltpu.VMEM((rows, width), F32)
-    chunks = pltpu.VMEM((steps, rows, CHUNK), BF16)
+    chunks = pltpu.VMEM((2, rows, CHUNK), BF16)
     return manual(
         kernel,
         info,
@@ -525,7 +577,8 @@
             plain,
             full,
             plain,
-            pltpu.VMEM((2, rows, CHUNK), F32),
+            pltpu.VMEM((rows, CHUNK), F32),
+            pltpu.VMEM((rows, CHUNK), F32),
             chunks,
             chunks,
             plain,
@@ -535,8 +588,8 @@
             dma_sems(steps),
             dma_sems(steps),
             dma_sems(7),
-            dma_sems(steps),
-            dma_sems(steps),
+            dma_sems(2),
+            dma_sems(2),
         ],
         flops=4 * rows * width * hidden + 2 * rows * width * width,
         moved=4 * width * hidden + 2 * width * width + 8 * rows * hidden,
@@ -580,7 +633,7 @@
     def work(
         s, token_refs, branch, slope, res, att, v, woo, wot, wuo, wut, wdo, wdt,
         gb_out, before_out, ga_out, gm_out, gr_out, small_out, shift_out,
-        g_v, branch_v, slope_v, res_v, att_v, wo_v, wu_v, wd_v, gb_v, d_v, before_v, ga_v, gm_v,
+        g_v, branch_v, slope_v, res_v, att_v, wo_v, wu_v, wd_v, gb_v, d_one, d_two, before_v, ga_v, gm_v,
         gr_v, acc, sums, tok_sems, in_sems, slope_sems, wu_sems, wd_sems, out_sems, before_sems,
     ):
         @pl.when(s[ACTIVE + owner] == 0)
@@ -592,71 +645,106 @@
         def _():
             slot = number
             arriving = token_copies(s, source, number, token_refs, g_v, tok_sems)
-            ups, downs, slopes = [], [], []
-
-            def prefetch(i):
-                if i < steps:
-                    part = pl.ds((i % split) * CHUNK, CHUNK)
-                    up, down = (wuo, wdo) if i < split else (wut, wdt)
-                    here = pl.ds(i * CHUNK, CHUNK)
-                    downs.append(begin(down.at[part], wd_v.at[i], wd_sems.at[i]))
-                    slopes.append(begin(slope.at[slot, :, here], slope_v.at[i], slope_sems.at[i]))
-                    ups.append(begin(up.at[:, part], wu_v.at[i], wu_sems.at[i]))
-
-            prefetch(0)
             branch_in = begin(branch.at[slot], branch_v, in_sems.at[0])
-            prefetch(1)
-            last = []
+            for i in range(steps):
+                part = pl.ds((i % split) * CHUNK, CHUNK)
+                up, down = (wuo, wdo) if i < split else (wut, wdt)
+                here = pl.ds(i * CHUNK, CHUNK)
+                begin(down.at[part], wd_v.at[i], wd_sems.at[i])
+                begin(slope.at[slot, :, here], slope_v.at[i], slope_sems.at[i])
+                begin(up.at[:, part], wu_v.at[i], wu_sems.at[i])
+            last = [
+                begin(res.at[slot], res_v, in_sems.at[1]),
+                begin(att.at[slot], att_v, in_sems.at[2]),
+                begin(woo, wo_v.at[0], in_sems.at[3]),
+                begin(wot, wo_v.at[1], in_sems.at[4]),
+            ]
             for copy in arriving:
                 copy.wait()
-            for t in tiles(rows):
+
+            def scale(t):
                 gb_v[t] = (v[SMLP : SMLP + 1] * g_v[t].astype(F32)).astype(BF16)
+
+            each_tile(rows, scale)
             outs = []
             if not scaled:
                 outs.append(begin(gb_v, gb_out.at[slot], out_sems.at[0]))
 
-            def down_product(i):
-                downs[i].wait()
-                d_v[i % 2] = dot_nt(gb_v[...], wd_v[i])
-
-            down_product(0)
+            def down_product(i, target):
+                target[...] = dot_nt(gb_v[...], wd_v[i])
+
+            def down_wait(i):
+                pltpu.make_async_copy(wdo.at[pl.ds(0, CHUNK)], wd_v.at[i], wd_sems.at[i]).wait()
+
+            def up_wait(i):
+                pltpu.make_async_copy(
+                    wuo.at[:, pl.ds(0, CHUNK)], wu_v.at[i], wu_sems.at[i]
+                ).wait()
+
+            def slope_wait(i):
+                pltpu.make_async_copy(
+                    slope.at[slot, :, pl.ds(0, CHUNK)], slope_v.at[i], slope_sems.at[i]
+                ).wait()
+
+            def copy_out(i, side):
+                part = pl.ds(pl.multiple_of(i * CHUNK, CHUNK), CHUNK)
+                return pltpu.make_async_copy(
+                    before_v.at[side], before_out.at[slot, :, part], before_sems.at[side]
+                )
+
+            def differentiate(i, source, side):
+                total = jnp.zeros((8, CHUNK), F32)
+                for t in tiles(rows):
+                    grad_before = (source[t] * slope_v[i, t].astype(F32)).astype(BF16)
+                    before_v[side, t] = grad_before
+                    total = total + eights(grad_before.astype(F32))
+                shift_out[pl.ds(i, 1), :] = col_sum(total)
+
+            def pair(j, carry):
+                i = 2 * j
+                slope_wait(i)
+                down_wait(i + 1)
+
+                @pl.when(j > 0)
+                def _():
+                    copy_out(i - 2, 0).wait()
+                    copy_out(i - 1, 1).wait()
+
+                down_product(i + 1, d_two)
+                differentiate(i, d_one, 0)
+                copy_out(i, 0).start()
+                slope_wait(i + 1)
+                up_wait(i)
+
+                @pl.when(i + 2 < steps)
+                def _():
+                    down_wait(i + 2)
+
+                down_product(jnp.minimum(i + 2, steps - 1), d_one)
+                acc[...] += dot_nt(before_v[0], wu_v[i])
+                differentiate(i + 1, d_two, 1)
+                copy_out(i + 1, 1).start()
+                up_wait(i + 1)
+                acc[...] += dot_nt(before_v[1], wu_v[i + 1])
+                return carry
+
+            acc[...] = jnp.zeros_like(acc)
+            down_wait(0)
+            down_product(0, d_one)
             branch_in.wait()
             sums[...] = jnp.zeros_like(sums)
-            for t in tiles(rows):
+
+            def branch_sums(t):
                 sums[0] += eights(g_v[t].astype(F32) * branch_v[t].astype(F32))
                 sums[1] += eights(gb_v[t].astype(F32))
 
-            def up_product(i):
-                ups[i].wait()
-                part = pl.ds(i * CHUNK, CHUNK)
-                outs.append(begin(before_v.at[i], before_out.at[slot, :, part], before_sems.at[i]))
-                product = dot_nt(before_v[i], wu_v[i])
-                acc[...] = product if i == 0 else acc[...] + product
-
-            for i in range(steps):
-                prefetch(i + 2)
-                if i == steps - 2:
-                    last = [
-                        begin(res.at[slot], res_v, in_sems.at[1]),
-                        begin(att.at[slot], att_v, in_sems.at[2]),
-                        begin(woo, wo_v.at[0], in_sems.at[3]),
-                        begin(wot, wo_v.at[1], in_sems.at[4]),
-                    ]
-                slopes[i].wait()
-                if i > 0:
-                    up_product(i - 1)
-                if i + 1 < steps:
-                    down_product(i + 1)
-                total = jnp.zeros((8, CHUNK), F32)
-                for t in tiles(rows):
-                    grad_before = (d_v[i % 2, t] * slope_v[i, t].astype(F32)).astype(BF16)
-                    before_v[i, t] = grad_before
-                    total = total + eights(grad_before.astype(F32))
-                shift_out[i : i + 1] = col_sum(total)
-            up_product(steps - 1)
+            each_tile(rows, branch_sums)
+            lax.fori_loop(0, steps // 2, pair, 0)
+            outs += [copy_out(steps - 2, 0), copy_out(steps - 1, 1)]
             for copy in last:
                 copy.wait()
-            for t in tiles(rows):
+
+            def last_norm(t):
                 hat, scale = norm_stats(res_v[t])
                 error = acc[t]
                 sums[2] += eights(error * hat)
@@ -667,6 +755,8 @@
                 ga = (v[SATT : SATT + 1] * grad).astype(BF16)
                 ga_v[t] = ga
                 sums[5] += eights(ga.astype(F32))
+
+            each_tile(rows, last_norm)
             outs.append(begin(ga_v, ga_out.at[slot], out_sems.at[1]))
             outs.append(begin(gr_v, gr_out, out_sems.at[3]))
             gm_v[:, :half] = dot_nt(ga_v[...], wo_v[0]).astype(BF16)
@@ -718,8 +808,9 @@
             pltpu.VMEM((steps, width, CHUNK), BF16),
             pltpu.VMEM((steps, CHUNK, width), BF16),
             plain,
-            pltpu.VMEM((2, rows, CHUNK), F32),
-            chunks,
+            pltpu.VMEM((rows, CHUNK), F32),
+            pltpu.VMEM((rows, CHUNK), F32),
+            pltpu.VMEM((2, rows, CHUNK), BF16),
             plain,
             plain,
             full,
@@ -731,7 +822,7 @@
             dma_sems(steps),
             dma_sems(steps),
             dma_sems(4),
-            dma_sems(steps),
+            dma_sems(2),
         ],
         flops=4 * rows * width * hidden + 2 * rows * width * width,
         moved=4 * width * hidden + 2 * width * width + 8 * rows * hidden,
@@ -849,56 +940,65 @@
         @pl.when(s[ACTIVE + owner] == 1)
         def _():
             slot = number
-            loads = []
             for part in range(6):
                 kind, side = part % 3, part // 3
                 columns = pl.ds(side * half, half)
                 if kind == 0:
-                    copies = [begin(dq_ref.at[:, columns], a_v.at[part], a_sems.at[part])]
+                    begin(dq_ref.at[:, columns], a_v.at[part], a_sems.at[part])
                 else:
                     turned = pl.ds((1 - side) * half, half)
-                    copies = [
-                        begin(here.at[kind - 1, :, columns], a_v.at[part], a_sems.at[part]),
-                        begin(there.at[kind - 1, :, turned], b_v.at[part], b_sems.at[part]),
-                    ]
+                    begin(here.at[kind - 1, :, columns], a_v.at[part], a_sems.at[part])
+                    begin(there.at[kind - 1, :, turned], b_v.at[part], b_sems.at[part])
                 weight = own if side == 0 else oth
-                copies.append(begin(weight.at[kind], w_v.at[part], w_sems.at[part]))
-                loads.append(copies)
+                begin(weight.at[kind], w_v.at[part], w_sems.at[part])
             last = [
                 begin(x_ref.at[slot], x_v, in_sems.at[0]),
                 begin(gr, gr_v, in_sems.at[1]),
             ]
-            outs = []
-            for part in range(6):
-                for copy in loads[part]:
-                    copy.wait()
+
+            def out_copy(part):
+                columns = pl.ds(pl.multiple_of(part * half, half), half)
+                return pltpu.make_async_copy(
+                    p_v.at[part], packed_out.at[slot, :, columns], packed_sems.at[part]
+                )
+
+            def project(part, carry):
+                first = dq_ref.at[:, pl.ds(0, half)]
+                pltpu.make_async_copy(first, a_v.at[part], a_sems.at[part]).wait()
+
+                @pl.when(part % 3 > 0)
+                def _():
+                    pltpu.make_async_copy(first, b_v.at[part], b_sems.at[part]).wait()
+
                 total = jnp.zeros((8, half), F32)
+                both = part % 3 > 0
                 for t in tiles(rows):
-                    packed = a_v[part, t]
-                    if part % 3 > 0:
-                        packed = (packed.astype(F32) + b_v[part, t].astype(F32)).astype(BF16)
+                    added = jnp.where(both, b_v[part, t].astype(F32), 0.0)
+                    packed = (a_v[part, t].astype(F32) + added).astype(BF16)
                     p_v[part, t] = packed
                     total = total + eights(packed.astype(F32))
-                shift_out[part : part + 1] = col_sum(total)
-                outs.append(
-                    begin(
-                        p_v.at[part],
-                        packed_out.at[slot, :, pl.ds(part * half, half)],
-                        packed_sems.at[part],
-                    )
-                )
-                product = dot_nt(p_v[part], w_v[part])
-                acc[...] = product if part == 0 else acc[...] + product
+                shift_out[pl.ds(part, 1), :] = col_sum(total)
+                out_copy(part).start()
+                pltpu.make_async_copy(own.at[0], w_v.at[part], w_sems.at[part]).wait()
+                acc[...] += dot_nt(p_v[part], w_v[part])
+                return carry
+
+            acc[...] = jnp.zeros_like(acc)
+            lax.fori_loop(0, 6, project, 0)
+            outs = [out_copy(part) for part in range(6)]
             for copy in last:
                 copy.wait()
             sums[...] = jnp.zeros_like(sums)
-            for t in tiles(rows):
+
+            def norm(t):
                 hat, scale = norm_stats(x_v[t].astype(F32))
                 error = acc[t]
                 grad = gr_v[t] + norm_backward(hat, scale, v[LN1G : LN1G + 1], error)
                 gx_v[t] = grad.astype(BF16)
                 sums[0] += eights(error * hat)
                 sums[1] += eights(error)
+
+            each_tile(rows, norm)
             outs.append(begin(gx_v, relay_out, out_sems.at[0]))
             outs.append(begin(gx_v, gx_out.at[slot], out_sems.at[1]))
             small_out[...] = jnp.zeros_like(small_out)
@@ -976,6 +1076,7 @@
         self.routes = [[(order[i], order[(i + s) % n]) for i in range(n)] for s in self.signs]
         self.step = 0
         self.steps = 2 * (n - 1)
+        self.vmem = RING_MIB
         self.totals = [None] * len(shapes)
         self.moving = self.add([0, 0], None)
 
@@ -1030,7 +1131,7 @@
             [((chunk, width), BF16, True, None)] * 2,
             [pltpu.VMEM((2, terms, chunk, width), BF16), pltpu.SemaphoreType.DMA((2, 3, parts))],
             moved=2 * (terms + 1) * 2 * chunk * width,
-            vmem=RING_MIB,
+            vmem=self.vmem,
             after=after,
         )
 
@@ -1082,7 +1183,7 @@
                 pltpu.SemaphoreType.DMA((size, pieces)),
             ],
             moved=2 * 6 * chunk * width,
-            vmem=RING_MIB,
+            vmem=self.vmem,
             after=after,
             same={size - 2: count, size - 1: count + 1},
         )
@@ -1457,9 +1558,9 @@
         sums.append((small, shift, small_one, shift_qkv))
         return relayed
 
-    def backward(owner, number, source, tokens, after):
+    def backward(owner, number, source, tokens, after, late=()):
         grad_mixed, grad_res, small, shift = backward_mlp(owner, number, source, tokens, after)
-        flows = backward_attention(owner, number, grad_mixed)
+        flows = backward_attention(owner, number, grad_mixed, late)
         return backward_qkv(owner, number, *flows, grad_res, small, shift)
 
     relayed = forward(0, 0, "argument", (inputs, first_oth))
@@ -1467,7 +1568,7 @@
     relayed = forward(0, 1, "argument", (inputs, second_oth), [relayed])
     second = lax.ppermute(relayed, "section", [(0, 1)])
     relayed = forward(1, 0, "relay", (first,), [relayed])
-    relayed = backward(1, 0, "argument", (cotangent, cot_oth[0]), [relayed, second])
+    relayed = backward(1, 0, "argument", (cotangent, cot_oth[0]), [relayed], [second])
     first = lax.ppermute(relayed, "section", [(1, 0)])
     relayed = forward(1, 1, "relay", (second,), [relayed], [first])
     relayed = backward(1, 1, "argument", (cotangent, cot_oth[1]), [relayed])
@@ -1533,6 +1634,8 @@
         TailPlaces(half, LANES),
     )
     rings = [ring_down, ring_up, ring_tail]
+    for ring in rings:
+        ring.vmem = 16
     before_it = ring_tail
     while not all(ring.done() for ring in rings):
         for ring in rings:

time: 779 us -> 798 us (1.024)
  waiting for transfers between devices: 206 us -> 264 us
  local copies, waits for them, and re-layouts: 37.1 us -> 18.6 us
  Pallas kernels: 376 us -> 358 us
    ppermute x84, waiting for transfers between devices: 91.9 us -> 121 us  [advance(): lax.ppermute(self.moving[w], 'dp', self.routes[w])]
    ppermute x1, waiting for transfers between devices: 51.5 us -> 76.3 us  [shards(): first = lax.ppermute(relayed, 'section', [(1, 0)])]
    unnamed x234 -> x114, local copies, waits for them, and re-layouts: 35.5 us -> 17 us
    pallas_call x73, Pallas kernels: 297 us -> 279 us  [manual(): pl.pallas_call(body, out_shape=[jax.ShapeDtypeStruct(s, d) for s, d, _, _...]
  transfers between devices with their start and end apart: 111 -> 111, of which waited for: 41 -> 54; matrix products, arithmetic and copies ran while one was open for 4% -> 4% of each run, Pallas kernels for 32% -> 31%
where the time goes in v4:
time: 798 us; the launch traced here: 787 us
  Pallas kernels  358 us (45%)
  waiting for transfers between devices  264 us (33%)
  starting transfers between devices  97.2 us (12%)
  matrix products  43.9 us (6%)
  local copies, waits for them, and re-layouts  18.6 us (2%)
    pallas_call x73, Pallas kernels, manual(): pl.pallas_call(body, out_shape=[jax.ShapeDtypeStruct(s, d) for s, d, _, _...  279 us
    ppermute x84, waiting for transfers between devices, advance(): lax.ppermute(self.moving[w], 'dp', self.routes[w])  121 us
    ppermute x84, starting transfers between devices, advance(): lax.ppermute(self.moving[w], 'dp', self.routes[w])  86.5 us
    ppermute x1, waiting for transfers between devices, shards(): first = lax.ppermute(relayed, 'section', [(1, 0)])  76.3 us
    pallas_call x8, Pallas kernels, call(): pl.pallas_call(body, out_shape=[jax.ShapeDtypeStruct(s, d) for s, d, _, _...  71.9 us
    dot_general x10, matrix products, weight_grad(): lax.dot_general(left, right, (((0, 1), (0, 1)), ((), ())), preferred_elem...  43.9 us
    ppermute x1, waiting for transfers between devices, shards(): second = lax.ppermute(relayed, 'section', [(1, 0)])  40.1 us
    unnamed x114, local copies, waits for them, and re-layouts  17 us
  transfers between devices with their start and end apart: 111, of which 54 were waited for; matrix products, arithmetic and copies ran while one was open for 4% of the time, Pallas kernels for 31%

profile of v4, /device:TPU:0, one launch (start us, length us, event | category | flops | bytes accessed | tf_op | source)
XLA Modules:
  0.0 787.2 jit_solution(8359040039153360378)
XLA Ops:
  10.4 8.4 %shard_map.292 = (bf16[2,384,1024]{2,1,0:T(8,128)(2,1)}, bf16[2,384,1024]{2,1,0:T(8,128)(2,1)}, bf16[2,384,1024]{2,1,0:T(8,128)(2,1)}) custom-call(s32[19]{0:T(128)} %copy-done.15, bf16[2,1,768,512]{3,2,1,0:T(8,128)(2,1)} %refs_1_.10, bf16[384,512]{1,0:T(8,128)(2,1)} %copy-done.36, f32[8,1024]{1,0:T(8,128)} %get-tuple-element.376.refs_3_.refs_2_.refs_7_.refs_8_.refs_6_, ...), custom_call_target="tpu_custom_call" | custom-call | flops 1610612736 | bytes 8126464 | tf_op jit(solution)/shard_map/pallas_call | solution.py:131
  24.9 12.2 %shard_map.294 = (bf16[3,16,384,768]{3,2,1,0:T(8,128)(2,1)}, f32[3,384,1024]{2,1,0:T(8,128)}, bf16[384,1024]{1,0:T(8,128)(2,1)}, f32[3,384,1024]{2,1,0:T(8,128)}, bf16[3,2,768,1024]{3,2,1,0:T(8,128)(2,1)}) custom-call(s32[19]{0:T(128)} %copy-done.15, bf16[2,384,1024]{2,1,0:T(8,128)(2,1)} %shard_map.293.refs_1_.refs_5_, ...), custom_call_target="tpu_custom_call" | custom-call | flops 1207959552 | bytes 21233664 | tf_op jit(solution)/shard_map/pallas_call | solution.py:91
  37.1 28.1 %shard_map.295 = (bf16[2,384,1024]{2,1,0:T(8,128)(2,1)}, f32[2,384,1024]{2,1,0:T(8,128)}, bf16[2,384,1024]{2,1,0:T(8,128)(2,1)}, bf16[2,384,4096]{2,1,0:T(8,128)...) custom-call(s32[19]{0:T(128)} %copy-done.15, ...), custom_call_target="tpu_custom_call" | custom-call | flops 7247757312 | bytes 31457280 | tf_op jit(solution)/shard_map/pallas_call | solution.py:131
  66.0 8.4 %shard_map.296 = (bf16[2,384,1024]{2,1,0:T(8,128)(2,1)}, bf16[2,384,1024]{2,1,0:T(8,128)(2,1)}, bf16[2,384,1024]{2,1,0:T(8,128)(2,1)}) custom-call(s32[19]{0:T(128)} %copy-done.15, bf16[2,1,768,512]{3,2,1,0:T(8,128)(2,1)} %refs_1_.10, bf16[384,512]{1,0:T(8,128)(2,1)} %copy-done.35, ...), custom_call_target="tpu_custom_call", output_to_operand_aliasing={{0}: (7, {}), {1}: (8, {})} | custom-call | flops 1610612736 | bytes 8126464 | tf_op jit(solution)/shard_map/pallas_call | solution.py:131
  82.1 12.2 %shard_map.298 = (bf16[3,16,384,768]{3,2,1,0:T(8,128)(2,1)}, f32[3,384,1024]{2,1,0:T(8,128)}, bf16[384,1024]{1,0:T(8,128)(2,1)}, f32[3,384,1024]{2,1,0:T(8,128)}, bf16[3,2,768,1024]{3,2,1,0:T(8,128)(2,1)}) custom-call(s32[19]{0:T(128)} %copy-done.15, ...), custom_call_target="tpu_custom_call", output_to_operand_aliasing={{0}: (4, {}), {1}: (5, {}), {3}: (6, {}), {4}: (7, {})} | custom-call | flops 1207959552 | bytes 21233664 | tf_op jit(solution)/shard_map/pallas_call | solution.py:91
  94.3 27.9 %shard_map.299 = (bf16[2,384,1024]{2,1,0:T(8,128)(2,1)}, f32[2,384,1024]{2,1,0:T(8,128)}, bf16[2,384,1024]{2,1,0:T(8,128)(2,1)}, bf16[2,384,4096]{2,1,0:T(8,128)...) custom-call(s32[19]{0:T(128)} %copy-done.15, ...), custom_call_target="tpu_custom_call", output_to_operand_aliasing={{0}: (11, {}), {1}: (12, {}), {2}: (13, {}), {3}: (14, {}),... | custom-call | flops 7247757312 | bytes 31457280 | tf_op jit(solution)/shard_map/pallas_call | solution.py:131
  138.2 9.9 %collective-permute-done.9.refs_7_.refs_1_ = bf16[384,1024]{1,0:T(8,128)(2,1)S(1)} collective-permute-done((bf16[384,1024]{1,0:T(8,128)(2,1)}, bf16[384,1024]{1,0:T(8,128)(2,1)S(1)}, u32[]{:S(2)}, u32[]{:S(2)}) %collective-permute-start.9) | collective-permute-done | bytes 786464 | tf_op jit(solution)/shard_map/ppermute | solution.py:1569
  168.2 76.3 %collective-permute-done.15.refs_19_.refs_1_ = bf16[384,1024]{1,0:T(8,128)(2,1)S(1)} collective-permute-done((bf16[384,1024]{1,0:T(8,128)(2,1)S(1)}, bf16[384,1024]{1,0:T(8,128)(2,1)S(1)}, u32[]{:S(2)}, u32[]{:S(2)}) %collective-permute-start.15) | collective-permute-done | bytes 786464 | tf_op jit(solution)/shard_map/ppermute | solution.py:1572
  258.8 26.2 %shard_map.317 = (bf16[2,384,1024]{2,1,0:T(8,128)(2,1)}, bf16[2,384,4096]{2,1,0:T(8,128)(2,1)}, bf16[2,384,1024]{2,1,0:T(8,128)(2,1)}, bf16[384,1024]{1,0:T(8,12...) custom-call(s32[19]{0:T(128)} %copy-done.15, ...), custom_call_target="tpu_custom_call", output_to_operand_aliasing={{0}: (13, {}), {1}: (14, {}), {2}: (15, {})} | custom-call | flops 7247757312 | bytes 31457280 | tf_op jit(solution)/shard_map/pallas_call | solution.py:131
  285.0 15.8 %shard_map.318 = (bf16[384,1024]{1,0:T(8,128)(2,1)}, bf16[2,384,1024]{2,1,0:T(8,128)(2,1)}, bf16[2,384,1024]{2,1,0:T(8,128)(2,1)}) custom-call(s32[19]{0:T(128)} %copy-done.15, bf16[384,1024]{1,0:T(8,128)(2,1)} %get-tuple-element.471.refs_1_, bf16[2,384,1024]{2,1,0:T(8,128)(2,1)} %shard_map.309.refs_1_.refs_2_, ...), custom_call_target="tpu_custom_call" | custom-call | flops 2415919104 | bytes 21233664 | tf_op jit(solution)/shard_map/pallas_call | solution.py:91
  304.6 12.3 %shard_map.319 = (bf16[2,384,3072]{2,1,0:T(8,128)(2,1)}, bf16[2,384,1024]{2,1,0:T(8,128)(2,1)}, bf16[384,1024]{1,0:T(8,128)(2,1)}, f32[8,1024]{1,0:T(8,128)}, f32[8,512]{1,0:T(8,128)}) custom-call(s32[19]{0:T(128)} %copy-done.15, bf16[384,1024]{1,0:T(8,128)(2,1)} %get-tuple-element.472.refs_1_, ...), custom_call_target="tpu_custom_call", output_to_operand_aliasing={{0}: (9, {}), {1}: (10, {})} | custom-call | flops 2415919104 | bytes 12582912 | tf_op jit(solution)/shard_map/pallas_call | solution.py:131
  316.9 40.1 %collective-permute-done.18.refs_1_ = bf16[384,1024]{1,0:T(8,128)(2,1)S(1)} collective-permute-done((bf16[384,1024]{1,0:T(8,128)(2,1)S(1)}, bf16[384,1024]{1,0:T(8,128)(2,1)S(1)}, u32[]{:S(2)}, u32[]{:S(2)}) %collective-permute-start.18) | collective-permute-done | bytes 786464 | tf_op jit(solution)/shard_map/ppermute | solution.py:1575
  361.2 5.9 bitcast_convert_fusion.2
  367.2 7.1 bitcast_convert_fusion.3.refs_1_
  380.0 25.8 %shard_map.322 = (bf16[2,384,1024]{2,1,0:T(8,128)(2,1)}, bf16[2,384,4096]{2,1,0:T(8,128)(2,1)}, bf16[2,384,1024]{2,1,0:T(8,128)(2,1)}, bf16[384,1024]{1,0:T(8,12...) custom-call(s32[19]{0:T(128)} %copy-done.15, ...), custom_call_target="tpu_custom_call", output_to_operand_aliasing={{1}: (13, {}), {2}: (14, {})} | custom-call | flops 7247757312 | bytes 31457280 | tf_op jit(solution)/shard_map/pallas_call | solution.py:131
  409.7 7.0 bitcast_convert_fusion.1
  418.8 6.9 collective-permute-done.23.refs_3_
  433.1 6.9 bitcast_convert_fusion.refs_1_
  447.2 15.8 %shard_map.327 = (bf16[384,1024]{1,0:T(8,128)(2,1)}, bf16[2,384,1024]{2,1,0:T(8,128)(2,1)}, bf16[2,384,1024]{2,1,0:T(8,128)(2,1)}) custom-call(s32[19]{0:T(128)} %copy-done.15, bf16[384,1024]{1,0:T(8,128)(2,1)} %get-tuple-element.503.refs_1_, bf16[2,384,1024]{2,1,0:T(8,128)(2,1)} %shard_map.309.refs_1_.refs_2_, ...), custom_call_target="tpu_custom_call" | custom-call | flops 2415919104 | bytes 21233664 | tf_op jit(solution)/shard_map/pallas_call | solution.py:91
  467.1 5.3 collective-permute-done.29.refs_3_
  490.6 12.3 %shard_map.330 = (bf16[2,384,3072]{2,1,0:T(8,128)(2,1)}, bf16[2,384,1024]{2,1,0:T(8,128)(2,1)}, bf16[384,1024]{1,0:T(8,128)(2,1)}, f32[8,1024]{1,0:T(8,128)}, f32[8,512]{1,0:T(8,128)}) custom-call(s32[19]{0:T(128)} %copy-done.15, bf16[384,1024]{1,0:T(8,128)(2,1)} %get-tuple-element.504.refs_1_, ...), custom_call_target="tpu_custom_call", output_to_operand_aliasing={{0}: (9, {}), {1}: (10, {})} | custom-call | flops 2415919104 | bytes 12582912 | tf_op jit(solution)/shard_map/pallas_call | solution.py:131
  509.7 5.9 bitcast_convert_fusion.5
  529.5 5.9 collective-permute-done.41.refs_4_
  544.9 5.7 bitcast_convert_fusion.4.refs_1_
  627.1 6.8 collective-permute-done.70.refs_4_
  644.7 6.9 collective-permute-done.75.refs_1_
  660.1 5.3 collective-permute-done.84.refs_2_
  678.5 8.5 %collective-permute-done.87.refs_1_ = bf16[64,2048]{1,0:T(8,128)(2,1)S(1)} collective-permute-done((bf16[64,2048]{1,0:T(8,128)(2,1)S(1)}, bf16[64,2048]{1,0:T(8,128)(2,1)S(1)}, u32[]{:S(2)}, u32[]{:S(2)}) %collective-permute-start.87) | collective-permute-done | bytes 262176 | tf_op jit(solution)/shard_map/ppermute | solution.py:1194
  697.5 10.4 %collective-permute-done.91.refs_1_ = bf16[64,2048]{1,0:T(8,128)(2,1)S(1)} collective-permute-done((bf16[64,2048]{1,0:T(8,128)(2,1)S(1)}, bf16[64,2048]{1,0:T(8,128)(2,1)S(1)}, u32[]{:S(2)}, u32[]{:S(2)}) %collective-permute-start.91) | collective-permute-done | bytes 262176 | tf_op jit(solution)/shard_map/ppermute | solution.py:1194
  716.7 7.0 collective-permute-done.95.refs_1_
  729.3 4.5 collective-permute-done.97.refs_1_
  747.0 4.5 collective-permute-done.101.refs_1_
  (403 shorter events, 342.5 us)
Async XLA Ops:
  8.8 28.3 %collective-permute-start.7 = (bf16[1024,2048]{1,0:T(8,128)(2,1)}, bf16[1024,2048]{1,0:T(8,128)(2,1)}, u32[]{:S(2)}, u32[]{:S(2)}) collective-permute-start(bf16[1024,2048]{1,0:T(8,128)(2,1)} %bitcast.74), channel_id=1, source_target_pairs={{0,8},{8,0},{1,9},{9,1},{2,10},{10,2},{3,11},{11,3},{4,12},{12,4},... | collective-permute-start | bytes 12582920 | tf_op jit(solution)/shard_map/ppermute | solution.py:1056
  19.2 17.9 %collective-permute-start.6 = (bf16[512,1024]{1,0:T(8,128)(2,1)}, bf16[512,1024]{1,0:T(8,128)(2,1)}, u32[]{:S(2)}, u32[]{:S(2)}) collective-permute-start(bf16[512,1024]{1,0:T(8,128)(2,1)} %bitcast.8.refs_4_.refs_8_.refs_7_), channel_id=1, source_target_pairs={{0,8},{8,0},{1,9},{9,1},{2,10},{10,2},{3,11},{11,3},{4,12},{12,4},... | collective-permute-start | bytes 3145736 | tf_op jit(solution)/shard_map/ppermute | solution.py:1056
  24.5 40.8 %collective-permute-start.3 = (bf16[384,512]{1,0:T(8,128)(2,1)S(1)}, bf16[384,512]{1,0:T(8,128)(2,1)S(1)}, u32[]{:S(2)}, u32[]{:S(2)}) collective-permute-start(bf16[384,512]{1,0:T(8,128)(2,1)S(1)} %bitcast.56), channel_id=1, source_target_pairs={{0,8},{8,0},{1,9},{9,1},{2,10},{10,2},{3,11},{11,3},{4,12},{12,4},... | collective-permute-start | bytes 1179656 | tf_op jit(solution)/shard_map/ppermute | solution.py:1056
  74.6 47.7 %collective-permute-start.10 = (bf16[384,1024]{1,0:T(8,128)(2,1)}, bf16[384,1024]{1,0:T(8,128)(2,1)}, u32[]{:S(2)}, u32[]{:S(2)}) collective-permute-start(bf16[384,1024]{1,0:T(8,128)(2,1)} %get-tuple-element.387.refs_9_), channel_id=1, source_target_pairs={{0,16},{1,17},{2,18},{3,19},{4,20},{5,21},{6,22},{7,23},{8,24},{9,... | collective-permute-start | bytes 2359304 | tf_op jit(solution)/shard_map/ppermute | solution.py:1567
  128.8 19.2 %collective-permute-start.9 = (bf16[384,1024]{1,0:T(8,128)(2,1)}, bf16[384,1024]{1,0:T(8,128)(2,1)S(1)}, u32[]{:S(2)}, u32[]{:S(2)}) collective-permute-start(bf16[384,1024]{1,0:T(8,128)(2,1)} %get-tuple-element.404.refs_8_), channel_id=1, source_target_pairs={{0,16},{1,17},{2,18},{3,19},{4,20},{5,21},{6,22},{7,23},{8,24},{9,... | collective-permute-start | bytes 2359304 | tf_op jit(solution)/shard_map/ppermute | solution.py:1569
  160.6 83.9 %collective-permute-start.15 = (bf16[384,1024]{1,0:T(8,128)(2,1)S(1)}, bf16[384,1024]{1,0:T(8,128)(2,1)S(1)}, u32[]{:S(2)}, u32[]{:S(2)}) collective-permute-start(bf16[384,1024]{1,0:T(8,128)(2,1)S(1)} %copy-done.33), channel_id=1, source_target_pairs={{16,0},{17,1},{18,2},{19,3},{20,4},{21,5},{22,6},{23,7},{24,8},{25... | collective-permute-start | bytes 2359304 | tf_op jit(solution)/shard_map/ppermute | solution.py:1572
  300.9 56.0 %collective-permute-start.18 = (bf16[384,1024]{1,0:T(8,128)(2,1)S(1)}, bf16[384,1024]{1,0:T(8,128)(2,1)S(1)}, u32[]{:S(2)}, u32[]{:S(2)}) collective-permute-start(bf16[384,1024]{1,0:T(8,128)(2,1)S(1)} %copy-done.34), channel_id=1, source_target_pairs={{16,0},{17,1},{18,2},{19,3},{20,4},{21,5},{22,6},{23,7},{24,8},{25... | collective-permute-start | bytes 2359304 | tf_op jit(solution)/shard_map/ppermute | solution.py:1575
  377.2 28.6 %collective-permute-start.21 = (bf16[128,1024]{1,0:T(8,128)(2,1)}, bf16[128,1024]{1,0:T(8,128)(2,1)S(1)}, u32[]{:S(2)}, u32[]{:S(2)}) collective-permute-start(bf16[128,1024]{1,0:T(8,128)(2,1)} %get-tuple-element.479.refs_15_), channel_id=1, source_target_pairs={{0,2},{2,4},{4,6},{6,7},{7,5},{5,3},{3,1},{1,0},{8,10},{10,12},{12... | collective-permute-start | bytes 786440 | tf_op jit(solution)/shard_map/ppermute | solution.py:1194
  380.0 25.9 %collective-permute-start.22 = (bf16[128,1024]{1,0:T(8,128)(2,1)}, bf16[128,1024]{1,0:T(8,128)(2,1)S(1)}, u32[]{:S(2)}, u32[]{:S(2)}) collective-permute-start(bf16[128,1024]{1,0:T(8,128)(2,1)} %get-tuple-element.480.refs_16_), channel_id=1, source_target_pairs={{0,1},{2,0},{4,2},{6,4},{7,6},{5,7},{3,5},{1,3},{8,9},{10,8},{12,1... | collective-permute-start | bytes 786440 | tf_op jit(solution)/shard_map/ppermute | solution.py:1194
  416.7 27.7 %collective-permute-start.27 = (bf16[1024,2048]{1,0:T(8,128)(2,1)}, bf16[1024,2048]{1,0:T(8,128)(2,1)}, u32[]{:S(2)}, u32[]{:S(2)}) collective-permute-start(bf16[1024,2048]{1,0:T(8,128)(2,1)} %bitcast_convert_fusion.1), channel_id=1, source_target_pairs={{0,8},{8,0},{1,9},{9,1},{2,10},{10,2},{3,11},{11,3},{4,12},{12,4},... | collective-permute-start | bytes 12582920 | tf_op jit(solution)/shard_map/ppermute | solution.py:1056
  462.9 26.5 %collective-permute-start.28 = (bf16[2,384,1024]{2,1,0:T(8,128)(2,1)}, bf16[2,384,1024]{2,1,0:T(8,128)(2,1)S(1)}, u32[]{:S(2)}, u32[]{:S(2)}) collective-permute-start(bf16[2,384,1024]{2,1,0:T(8,128)(2,1)} %get-tuple-element.506), channel_id=1, source_target_pairs={{0,8},{8,0},{1,9},{9,1},{2,10},{10,2},{3,11},{11,3},{4,12},{12,4},... | collective-permute-start | bytes 4718600 | tf_op jit(solution)/shard_map/ppermute | solution.py:1056
  482.3 20.6 %collective-permute-start.36 = (bf16[64,2048]{1,0:T(8,128)(2,1)}, bf16[64,2048]{1,0:T(8,128)(2,1)S(1)}, u32[]{:S(2)}, u32[]{:S(2)}) collective-permute-start(bf16[64,2048]{1,0:T(8,128)(2,1)} %get-tuple-element.514), channel_id=1, source_target_pairs={{0,2},{2,4},{4,6},{6,7},{7,5},{5,3},{3,1},{1,0},{8,10},{10,12},{12... | collective-permute-start | bytes 786440 | tf_op jit(solution)/shard_map/ppermute | solution.py:1194
  483.9 19.0 %collective-permute-start.37 = (bf16[64,2048]{1,0:T(8,128)(2,1)}, bf16[64,2048]{1,0:T(8,128)(2,1)}, u32[]{:S(2)}, u32[]{:S(2)}) collective-permute-start(bf16[64,2048]{1,0:T(8,128)(2,1)} %get-tuple-element.515), channel_id=1, source_target_pairs={{0,1},{2,0},{4,2},{6,4},{7,6},{5,7},{3,5},{1,3},{8,9},{10,8},{12,1... | collective-permute-start | bytes 786440 | tf_op jit(solution)/shard_map/ppermute | solution.py:1194
  487.3 15.6 %collective-permute-start.34 = (bf16[128,1024]{1,0:T(8,128)(2,1)}, bf16[128,1024]{1,0:T(8,128)(2,1)}, u32[]{:S(2)}, u32[]{:S(2)}) collective-permute-start(bf16[128,1024]{1,0:T(8,128)(2,1)} %get-tuple-element.510), channel_id=1, source_target_pairs={{0,2},{2,4},{4,6},{6,7},{7,5},{5,3},{3,1},{1,0},{8,10},{10,12},{12... | collective-permute-start | bytes 786440 | tf_op jit(solution)/shard_map/ppermute | solution.py:1194
  515.6 52.2 %collective-permute-start.42 = (bf16[1024,1536]{1,0:T(8,128)(2,1)}, bf16[1024,1536]{1,0:T(8,128)(2,1)}, u32[]{:S(2)}, u32[]{:S(2)}) collective-permute-start(bf16[1024,1536]{1,0:T(8,128)(2,1)} %bitcast_convert_fusion.5), channel_id=1, source_target_pairs={{0,8},{8,0},{1,9},{9,1},{2,10},{10,2},{3,11},{11,3},{4,12},{12,4},... | collective-permute-start | bytes 9437192 | tf_op jit(solution)/shard_map/ppermute | solution.py:1056
  519.8 43.6 %collective-permute-start.43 = (bf16[1024,512]{1,0:T(8,128)(2,1)}, bf16[1024,512]{1,0:T(8,128)(2,1)S(1)}, u32[]{:S(2)}, u32[]{:S(2)}) collective-permute-start(bf16[1024,512]{1,0:T(8,128)(2,1)} %pad_maximum_fusion.1), channel_id=1, source_target_pairs={{0,8},{8,0},{1,9},{9,1},{2,10},{10,2},{3,11},{11,3},{4,12},{12,4},... | collective-permute-start | bytes 3145736 | tf_op jit(solution)/shard_map/ppermute | solution.py:1056
  519.8 15.7 %collective-permute-start.38 = (bf16[128,1024]{1,0:T(8,128)(2,1)}, bf16[128,1024]{1,0:T(8,128)(2,1)}, u32[]{:S(2)}, u32[]{:S(2)}) collective-permute-start(bf16[128,1024]{1,0:T(8,128)(2,1)} %get-tuple-element.523), channel_id=1, source_target_pairs={{0,2},{2,4},{4,6},{6,7},{7,5},{5,3},{3,1},{1,0},{8,10},{10,12},{12... | collective-permute-start | bytes 786440 | tf_op jit(solution)/shard_map/ppermute | solution.py:1194
  554.6 17.6 %collective-permute-start.53 = (bf16[128,1024]{1,0:T(8,128)(2,1)}, bf16[128,1024]{1,0:T(8,128)(2,1)S(1)}, u32[]{:S(2)}, u32[]{:S(2)}) collective-permute-start(bf16[128,1024]{1,0:T(8,128)(2,1)} %get-tuple-element.567.refs_1_), channel_id=1, source_target_pairs={{0,2},{2,4},{4,6},{6,7},{7,5},{5,3},{3,1},{1,0},{8,10},{10,12},{12... | collective-permute-start | bytes 786440 | tf_op jit(solution)/shard_map/ppermute | solution.py:1194
  618.2 17.8 %collective-permute-start.67 = (bf16[64,2176]{1,0:T(8,128)(2,1)S(1)}, bf16[64,2176]{1,0:T(8,128)(2,1)S(1)}, u32[]{:S(2)}, u32[]{:S(2)}) collective-permute-start(bf16[64,2176]{1,0:T(8,128)(2,1)S(1)} %get-tuple-element.605), channel_id=1, source_target_pairs={{0,2},{2,4},{4,6},{6,7},{7,5},{5,3},{3,1},{1,0},{8,10},{10,12},{12... | collective-permute-start | bytes 835592 | tf_op jit(solution)/shard_map/ppermute | solution.py:1194
  619.2 16.7 %collective-permute-start.68 = (bf16[64,2176]{1,0:T(8,128)(2,1)S(1)}, bf16[64,2176]{1,0:T(8,128)(2,1)S(1)}, u32[]{:S(2)}, u32[]{:S(2)}) collective-permute-start(bf16[64,2176]{1,0:T(8,128)(2,1)S(1)} %get-tuple-element.606), channel_id=1, source_target_pairs={{0,1},{2,0},{4,2},{6,4},{7,6},{5,7},{3,5},{1,3},{8,9},{10,8},{12,1... | collective-permute-start | bytes 835592 | tf_op jit(solution)/shard_map/ppermute | solution.py:1194
  623.4 17.6 %collective-permute-start.77 = (bf16[128,1024]{1,0:T(8,128)(2,1)S(1)}, bf16[128,1024]{1,0:T(8,128)(2,1)S(1)}, u32[]{:S(2)}, u32[]{:S(2)}) collective-permute-start(bf16[128,1024]{1,0:T(8,128)(2,1)S(1)} %get-tuple-element.610), channel_id=1, source_target_pairs={{0,2},{2,4},{4,6},{6,7},{7,5},{5,3},{3,1},{1,0},{8,10},{10,12},{12... | collective-permute-start | bytes 786440 | tf_op jit(solution)/shard_map/ppermute | solution.py:1194
  626.4 15.7 %collective-permute-start.78 = (bf16[128,1024]{1,0:T(8,128)(2,1)S(1)}, bf16[128,1024]{1,0:T(8,128)(2,1)S(1)}, u32[]{:S(2)}, u32[]{:S(2)}) collective-permute-start(bf16[128,1024]{1,0:T(8,128)(2,1)S(1)} %get-tuple-element.611), channel_id=1, source_target_pairs={{0,1},{2,0},{4,2},{6,4},{7,6},{5,7},{3,5},{1,3},{8,9},{10,8},{12,1... | collective-permute-start | bytes 786440 | tf_op jit(solution)/shard_map/ppermute | solution.py:1194
  638.0 15.3 %collective-permute-start.73 = (bf16[64,2176]{1,0:T(8,128)(2,1)S(1)}, bf16[64,2176]{1,0:T(8,128)(2,1)S(1)}, u32[]{:S(2)}, u32[]{:S(2)}) collective-permute-start(bf16[64,2176]{1,0:T(8,128)(2,1)S(1)} %get-tuple-element.618), channel_id=1, source_target_pairs={{0,2},{2,4},{4,6},{6,7},{7,5},{5,3},{3,1},{1,0},{8,10},{10,12},{12... | collective-permute-start | bytes 835592 | tf_op jit(solution)/shard_map/ppermute | solution.py:1194
  643.7 15.7 %collective-permute-start.83 = (bf16[128,1024]{1,0:T(8,128)(2,1)S(1)}, bf16[128,1024]{1,0:T(8,128)(2,1)S(1)}, u32[]{:S(2)}, u32[]{:S(2)}) collective-permute-start(bf16[128,1024]{1,0:T(8,128)(2,1)S(1)} %get-tuple-element.623), channel_id=1, source_target_pairs={{0,2},{2,4},{4,6},{6,7},{7,5},{5,3},{3,1},{1,0},{8,10},{10,12},{12... | collective-permute-start | bytes 786440 | tf_op jit(solution)/shard_map/ppermute | solution.py:1194
  655.3 16.4 %collective-permute-start.79 = (bf16[64,2176]{1,0:T(8,128)(2,1)S(1)}, bf16[64,2176]{1,0:T(8,128)(2,1)S(1)}, u32[]{:S(2)}, u32[]{:S(2)}) collective-permute-start(bf16[64,2176]{1,0:T(8,128)(2,1)S(1)} %get-tuple-element.632), channel_id=1, source_target_pairs={{0,2},{2,4},{4,6},{6,7},{7,5},{5,3},{3,1},{1,0},{8,10},{10,12},{12... | collective-permute-start | bytes 835592 | tf_op jit(solution)/shard_map/ppermute | solution.py:1194
  656.1 15.7 %collective-permute-start.80 = (bf16[64,2176]{1,0:T(8,128)(2,1)S(1)}, bf16[64,2176]{1,0:T(8,128)(2,1)S(1)}, u32[]{:S(2)}, u32[]{:S(2)}) collective-permute-start(bf16[64,2176]{1,0:T(8,128)(2,1)S(1)} %get-tuple-element.633), channel_id=1, source_target_pairs={{0,1},{2,0},{4,2},{6,4},{7,6},{5,7},{3,5},{1,3},{8,9},{10,8},{12,1... | collective-permute-start | bytes 835592 | tf_op jit(solution)/shard_map/ppermute | solution.py:1194
  673.8 17.6 %collective-permute-start.85 = (bf16[64,2176]{1,0:T(8,128)(2,1)S(1)}, bf16[64,2176]{1,0:T(8,128)(2,1)S(1)}, u32[]{:S(2)}, u32[]{:S(2)}) collective-permute-start(bf16[64,2176]{1,0:T(8,128)(2,1)S(1)} %get-tuple-element.646), channel_id=1, source_target_pairs={{0,2},{2,4},{4,6},{6,7},{7,5},{5,3},{3,1},{1,0},{8,10},{10,12},{12... | collective-permute-start | bytes 835592 | tf_op jit(solution)/shard_map/ppermute | solution.py:1194
  693.4 16.9 %collective-permute-start.89 = (bf16[64,2176]{1,0:T(8,128)(2,1)S(1)}, bf16[64,2176]{1,0:T(8,128)(2,1)S(1)}, u32[]{:S(2)}, u32[]{:S(2)}) collective-permute-start(bf16[64,2176]{1,0:T(8,128)(2,1)S(1)} %get-tuple-element.655.refs_1_), channel_id=1, source_target_pairs={{0,2},{2,4},{4,6},{6,7},{7,5},{5,3},{3,1},{1,0},{8,10},{10,12},{12... | collective-permute-start | bytes 835592 | tf_op jit(solution)/shard_map/ppermute | solution.py:1194
  693.9 16.4 %collective-permute-start.90 = (bf16[64,2176]{1,0:T(8,128)(2,1)S(1)}, bf16[64,2176]{1,0:T(8,128)(2,1)S(1)}, u32[]{:S(2)}, u32[]{:S(2)}) collective-permute-start(bf16[64,2176]{1,0:T(8,128)(2,1)S(1)} %get-tuple-element.656.refs_2_), channel_id=1, source_target_pairs={{0,1},{2,0},{4,2},{6,4},{7,6},{5,7},{3,5},{1,3},{8,9},{10,8},{12,1... | collective-permute-start | bytes 835592 | tf_op jit(solution)/shard_map/ppermute | solution.py:1194
  738.6 30.1 %collective-permute-start.16 = (bf16[2,384,512]{2,1,0:T(8,128)(2,1)S(1)}, bf16[2,384,512]{2,1,0:T(8,128)(2,1)S(1)}, u32[]{:S(2)}, u32[]{:S(2)}) collective-permute-start(bf16[2,384,512]{2,1,0:T(8,128)(2,1)S(1)} %shard_map.312), channel_id=1, source_target_pairs={{0,8},{8,0},{1,9},{9,1},{2,10},{10,2},{3,11},{11,3},{4,12},{12,4},... | collective-permute-start | bytes 2359304 | tf_op jit(solution)/shard_map/ppermute | solution.py:1056
  739.4 29.7 %collective-permute-start.33 = (bf16[2,384,512]{2,1,0:T(8,128)(2,1)S(1)}, bf16[2,384,512]{2,1,0:T(8,128)(2,1)S(1)}, u32[]{:S(2)}, u32[]{:S(2)}) collective-permute-start(bf16[2,384,512]{2,1,0:T(8,128)(2,1)S(1)} %shard_map.331), channel_id=1, source_target_pairs={{0,8},{8,0},{1,9},{9,1},{2,10},{10,2},{3,11},{11,3},{4,12},{12,4},... | collective-permute-start | bytes 2359304 | tf_op jit(solution)/shard_map/ppermute | solution.py:1056
  766.6 15.8 %collective-permute-start.105 = (bf16[64,2176]{1,0:T(8,128)(2,1)S(1)}, bf16[64,2176]{1,0:T(8,128)(2,1)S(1)}, u32[]{:S(2)}, u32[]{:S(2)}) collective-permute-start(bf16[64,2176]{1,0:T(8,128)(2,1)S(1)} %get-tuple-element.704), channel_id=1, source_target_pairs={{0,2},{2,4},{4,6},{6,7},{7,5},{5,3},{3,1},{1,0},{8,10},{10,12},{12... | collective-permute-start | bytes 835592 | tf_op jit(solution)/shard_map/ppermute | solution.py:1194
  (136 other events, 1018.0 us)

commit v5 on v3

--- a/solution.py
+++ b/solution.py
@@ -977,7 +977,9 @@
         self.step = 0
         self.steps = 2 * (n - 1)
         self.totals = [None] * len(shapes)
+        self.vmem = RING_MIB
         self.moving = self.add([0, 0], None)
+        self.vmem = 16
 
     def unit(self, way, ahead):
         return UNITS + way * self.count + ahead % self.count
@@ -1030,7 +1032,7 @@
             [((chunk, width), BF16, True, None)] * 2,
             [pltpu.VMEM((2, terms, chunk, width), BF16), pltpu.SemaphoreType.DMA((2, 3, parts))],
             moved=2 * (terms + 1) * 2 * chunk * width,
-            vmem=RING_MIB,
+            vmem=self.vmem,
             after=after,
         )
 
@@ -1082,7 +1084,7 @@
                 pltpu.SemaphoreType.DMA((size, pieces)),
             ],
             moved=2 * 6 * chunk * width,
-            vmem=RING_MIB,
+            vmem=self.vmem,
             after=after,
             same={size - 2: count, size - 1: count + 1},
         )
@@ -1114,15 +1116,18 @@
         return self.totals
 
 
-class WholeRows:
-    def __init__(self, width):
-        self.width = width
+class MlpPlaces:
+    def __init__(self, width, second, rows):
+        self.width, self.second, self.rows = width, second, rows
 
     def columns(self, target):
-        return [(0, self.width)]
+        if target == 0:
+            return [(0, self.width)]
+        return [(self.width, self.second), (self.width + self.second, self.second)]
 
     def ref(self, out, target, first, columns, unit, chunk):
-        return out.at[pl.ds(pl.multiple_of(unit * chunk, chunk), chunk)]
+        base = self.rows if first > self.width else 0
+        return out.at[pl.ds(pl.multiple_of(base + unit * chunk, chunk), chunk)]
 
 
 class TailPlaces:
@@ -1481,34 +1486,35 @@
 
     grads["branch"] = scale_branch(info, 0, 1, second, vec, grads["branch"], [relayed])
     active, g_branch = kept["active"], grads["branch"]
-    down_oth = weight_grad(active[:, :, hidden_half:], g_branch)
-    down_sent = swap(down_oth)
-    down_own = weight_grad(active[:, :, :hidden_half], g_branch)
-    ring_down = Ring(info, [(down_own, down_sent)], [down_own.shape], WholeRows(width))
-    second = tied(second, *ring_down.moving)
+    split = hidden_half // 2
+    assert split == width
+
+    def down_grad(start):
+        return weight_grad(active[:, :, start : start + split], g_branch)
+
+    down = []
+    for start in (0, split):
+        sent = swap(down_grad(hidden_half + start))
+        down.append((down_grad(start), sent))
     grad_mixed, grad_res, small, shift = backward_mlp(
-        0, 1, "relay", (second,), list(ring_down.moving), scaled=True
+        0, 1, "relay", (second,), [pair[0] for pair in down], scaled=True
     )
-    ring_down.advance(grad_mixed)
-    normed2 = tied(kept["normed2"], *ring_down.moving)
-    before = grads["before"]
-    up_oth = weight_grad(normed2, before[:, :, hidden_half:])
-    up_sent = swap(up_oth)
-    ring_down.advance(up_oth)
-    normed2 = tied(normed2, *ring_down.moving)
+    normed2, before = kept["normed2"], grads["before"]
+    up_sent = swap(weight_grad(normed2, before[:, :, hidden_half:]))
     up_own = weight_grad(normed2, before[:, :, :hidden_half])
-    ring_down.advance(up_own)
-    ring_up = Ring(info, [(up_own, up_sent)], [up_own.shape], WholeRows(hidden_half))
-    grad_mixed = tied(grad_mixed, *ring_down.moving, *ring_up.moving)
-    flows = backward_attention(0, 1, grad_mixed)
-    ring_down.advance(flows[0])
-    ring_up.advance(flows[0])
-    grad_res = tied(grad_res, *ring_down.moving, *ring_up.moving)
+    ring_mlp = Ring(
+        info,
+        [(up_own, up_sent), *down],
+        [up_own.shape, (hidden_half, width)],
+        MlpPlaces(hidden_half, width, split),
+    )
+    flows = backward_attention(0, 1, grad_mixed, list(ring_mlp.moving))
+    ring_mlp.advance(flows[0])
+    grad_res = tied(grad_res, *ring_mlp.moving)
     backward_qkv(0, 1, *flows, grad_res, small, shift)
     packed = grads["packed"]
-    ring_down.advance(packed)
-    ring_up.advance(packed)
-    normed1 = tied(kept["normed1"], *ring_down.moving, *ring_up.moving)
+    ring_mlp.advance(packed)
+    normed1 = tied(kept["normed1"], *ring_mlp.moving)
     vectors = gather_vectors(info, sums, width)
 
     def tail(index):
@@ -1520,27 +1526,22 @@
 
     tail_oth = tail(1)
     tail_sent = [swap(block) for block in tail_oth]
-    ring_down.advance(tail_oth[0])
-    ring_up.advance(tail_oth[0])
-    normed1 = tied(normed1, *ring_down.moving, *ring_up.moving)
     tail_own = tail(0)
-    ring_down.advance(tail_own[0])
-    ring_up.advance(tail_own[0])
+    ring_mlp.advance(tail_own[0])
     ring_tail = Ring(
         info,
         list(zip(tail_own, tail_sent)),
         [(3, width, half), (half, width), (width, LANES)],
         TailPlaces(half, LANES),
     )
-    rings = [ring_down, ring_up, ring_tail]
+    rings = [ring_mlp, ring_tail]
     before_it = ring_tail
     while not all(ring.done() for ring in rings):
         for ring in rings:
             if not ring.done():
                 ring.advance(*before_it.moving)
                 before_it = ring
-    (total_down,) = ring_down.finish()
-    (total_up,) = ring_up.finish()
+    total_up, total_down = ring_mlp.finish()
     total_qkv, total_out, total_vectors = ring_tail.finish()
     block_outputs = join_tokens(info, kept["output"], swap(partner_features(info, kept["output"])))
     input_grads = join_tokens(info, grads["input"], swap(partner_features(info, grads["input"])))

time: 779 us -> 736 us (0.945)
  Pallas kernels: 376 us -> 309 us
  waiting for transfers between devices: 206 us -> 272 us
  starting transfers between devices: 99 us -> 70.5 us
    pallas_call x73 -> x58, Pallas kernels: 297 us -> 231 us  [manual(): pl.pallas_call(body, out_shape=[jax.ShapeDtypeStruct(s, d) for s, d, _, _...]
    ppermute x84 -> x56, waiting for transfers between devices: 91.9 us -> 158 us  [advance(): lax.ppermute(self.moving[w], 'dp', self.routes[w])]
    ppermute x84 -> x56, starting transfers between devices: 88.3 us -> 58.7 us  [advance(): lax.ppermute(self.moving[w], 'dp', self.routes[w])]
    unnamed x234 -> x124, local copies, waits for them, and re-layouts: 35.5 us -> 31.5 us
    dot_general x10 -> x12, matrix products: 43.5 us -> 40.2 us  [weight_grad(): lax.dot_general(left, right, (((0, 1), (0, 1)), ((), ())), preferred_elem...]
    ppermute x23 -> x24, waiting for transfers between devices: 18.1 us -> 19.6 us  [swap(): return lax.ppermute(block, 'tensor', [(0, 1), (1, 0)])]
  transfers between devices with their start and end apart: 111 -> 84, of which waited for: 41 -> 50; matrix products, arithmetic and copies ran while one was open for 4% -> 3% of each run, Pallas kernels for 32% -> 22%
where the time goes in v5:
time: 736 us; the launch traced here: 729 us
  Pallas kernels  309 us (42%)
  waiting for transfers between devices  272 us (37%)
  starting transfers between devices  70.5 us (10%)
  matrix products  40.2 us (5%)
  local copies, waits for them, and re-layouts  33.1 us (4%)
    pallas_call x58, Pallas kernels, manual(): pl.pallas_call(body, out_shape=[jax.ShapeDtypeStruct(s, d) for s, d, _, _...  231 us
    ppermute x56, waiting for transfers between devices, advance(): lax.ppermute(self.moving[w], 'dp', self.routes[w])  158 us
    pallas_call x8, Pallas kernels, call(): pl.pallas_call(body, out_shape=[jax.ShapeDtypeStruct(s, d) for s, d, _, _...  72 us
    ppermute x56, starting transfers between devices, advance(): lax.ppermute(self.moving[w], 'dp', self.routes[w])  58.7 us
    ppermute x1, waiting for transfers between devices, shards(): first = lax.ppermute(relayed, 'section', [(1, 0)])  51.6 us
    dot_general x12, matrix products, weight_grad(): lax.dot_general(left, right, (((0, 1), (0, 1)), ((), ())), preferred_elem...  40.2 us
    unnamed x124, local copies, waits for them, and re-layouts  31.5 us
    ppermute x1, waiting for transfers between devices, shards(): second = lax.ppermute(relayed, 'section', [(1, 0)])  31.1 us
  transfers between devices with their start and end apart: 84, of which 50 were waited for; matrix products, arithmetic and copies ran while one was open for 3% of the time, Pallas kernels for 22%

profile of v5, /device:TPU:0, one launch (start us, length us, event | category | flops | bytes accessed | tf_op | source)
XLA Modules:
  0.0 728.8 jit_solution(4603114271655933105)
XLA Ops:
  10.4 6.5 shard_map.292
  24.2 12.2 %shard_map.294 = (bf16[3,16,384,768]{3,2,1,0:T(8,128)(2,1)}, f32[3,384,1024]{2,1,0:T(8,128)}, bf16[384,1024]{1,0:T(8,128)(2,1)}, f32[3,384,1024]{2,1,0:T(8,128)}, bf16[3,2,768,1024]{3,2,1,0:T(8,128)(2,1)}) custom-call(s32[19]{0:T(128)} %copy-done.29, bf16[2,384,1024]{2,1,0:T(8,128)(2,1)} %shard_map.293.refs_1_.refs_5_, ...), custom_call_target="tpu_custom_call" | custom-call | flops 1207959552 | bytes 21233664 | tf_op jit(solution)/shard_map/pallas_call | solution.py:83
  36.5 22.3 %shard_map.295 = (bf16[2,384,1024]{2,1,0:T(8,128)(2,1)}, f32[2,384,1024]{2,1,0:T(8,128)}, bf16[2,384,1024]{2,1,0:T(8,128)(2,1)}, bf16[2,384,4096]{2,1,0:T(8,128)...) custom-call(s32[19]{0:T(128)} %copy-done.29, ...), custom_call_target="tpu_custom_call" | custom-call | flops 7247757312 | bytes 31457280 | tf_op jit(solution)/shard_map/pallas_call | solution.py:123
  59.6 7.0 shard_map.296
  74.5 12.2 %shard_map.298 = (bf16[3,16,384,768]{3,2,1,0:T(8,128)(2,1)}, f32[3,384,1024]{2,1,0:T(8,128)}, bf16[384,1024]{1,0:T(8,128)(2,1)}, f32[3,384,1024]{2,1,0:T(8,128)}, bf16[3,2,768,1024]{3,2,1,0:T(8,128)(2,1)}) custom-call(s32[19]{0:T(128)} %copy-done.29, ...), custom_call_target="tpu_custom_call", output_to_operand_aliasing={{0}: (4, {}), {1}: (5, {}), {3}: (6, {}), {4}: (7, {})} | custom-call | flops 1207959552 | bytes 21233664 | tf_op jit(solution)/shard_map/pallas_call | solution.py:83
  86.7 21.0 %shard_map.299 = (bf16[2,384,1024]{2,1,0:T(8,128)(2,1)}, f32[2,384,1024]{2,1,0:T(8,128)}, bf16[2,384,1024]{2,1,0:T(8,128)(2,1)}, bf16[2,384,4096]{2,1,0:T(8,128)...) custom-call(s32[19]{0:T(128)} %copy-done.29, ...), custom_call_target="tpu_custom_call", output_to_operand_aliasing={{0}: (11, {}), {1}: (12, {}), {2}: (13, {}), {3}: (14, {}),... | custom-call | flops 7247757312 | bytes 31457280 | tf_op jit(solution)/shard_map/pallas_call | solution.py:123
  121.8 11.7 %collective-permute-done.9.refs_15_.refs_1_ = bf16[384,1024]{1,0:T(8,128)(2,1)S(1)} collective-permute-done((bf16[384,1024]{1,0:T(8,128)(2,1)}, bf16[384,1024]{1,0:T(8,128)(2,1)S(1)}, u32[]{:S(2)}, u32[]{:S(2)}) %collective-permute-start.9) | collective-permute-done | bytes 786464 | tf_op jit(solution)/shard_map/ppermute | solution.py:1473
  134.4 10.3 %shard_map.305 = (bf16[2,384,1024]{2,1,0:T(8,128)(2,1)}, bf16[2,384,4096]{2,1,0:T(8,128)(2,1)}, bf16[2,384,1024]{2,1,0:T(8,128)(2,1)}, bf16[384,1024]{1,0:T(8,12...) custom-call(s32[19]{0:T(128)} %copy-done.29, bf16[2,1,768,512]{3,2,1,0:T(8,128)(2,1)} %refs_1_.13, ...), custom_call_target="tpu_custom_call" | custom-call | flops 7247757312 | bytes 31457280 | tf_op jit(solution)/shard_map/pallas_call | solution.py:123
  163.8 51.6 %collective-permute-done.15.refs_19_.refs_1_ = bf16[384,1024]{1,0:T(8,128)(2,1)S(1)} collective-permute-done((bf16[384,1024]{1,0:T(8,128)(2,1)S(1)}, bf16[384,1024]{1,0:T(8,128)(2,1)S(1)}, u32[]{:S(2)}, u32[]{:S(2)}) %collective-permute-start.15) | collective-permute-done | bytes 786464 | tf_op jit(solution)/shard_map/ppermute | solution.py:1476
  217.7 12.6 %shard_map.314 = (bf16[2,384,1024]{2,1,0:T(8,128)(2,1)}, bf16[2,384,4096]{2,1,0:T(8,128)(2,1)}, bf16[2,384,1024]{2,1,0:T(8,128)(2,1)}, bf16[384,1024]{1,0:T(8,12...) custom-call(s32[19]{0:T(128)} %copy-done.29, ...), custom_call_target="tpu_custom_call", output_to_operand_aliasing={{0}: (14, {}), {1}: (15, {}), {2}: (16, {})} | custom-call | flops 7247757312 | bytes 31457280 | tf_op jit(solution)/shard_map/pallas_call | solution.py:123
  240.7 17.8 %shard_map.317 = (bf16[2,384,1024]{2,1,0:T(8,128)(2,1)}, bf16[2,384,4096]{2,1,0:T(8,128)(2,1)}, bf16[2,384,1024]{2,1,0:T(8,128)(2,1)}, bf16[384,1024]{1,0:T(8,12...) custom-call(s32[19]{0:T(128)} %copy-done.29, ...), custom_call_target="tpu_custom_call", output_to_operand_aliasing={{0}: (13, {}), {1}: (14, {}), {2}: (15, {})} | custom-call | flops 7247757312 | bytes 31457280 | tf_op jit(solution)/shard_map/pallas_call | solution.py:123
  258.5 15.8 %shard_map.318 = (bf16[384,1024]{1,0:T(8,128)(2,1)}, bf16[2,384,1024]{2,1,0:T(8,128)(2,1)}, bf16[2,384,1024]{2,1,0:T(8,128)(2,1)}) custom-call(s32[19]{0:T(128)} %copy-done.29, bf16[384,1024]{1,0:T(8,128)(2,1)} %get-tuple-element.412.refs_1_, bf16[2,384,1024]{2,1,0:T(8,128)(2,1)} %shard_map.309.refs_1_.refs_2_, ...), custom_call_target="tpu_custom_call" | custom-call | flops 2415919104 | bytes 21233664 | tf_op jit(solution)/shard_map/pallas_call | solution.py:83
  278.1 9.3 %shard_map.319 = (bf16[2,384,3072]{2,1,0:T(8,128)(2,1)}, bf16[2,384,1024]{2,1,0:T(8,128)(2,1)}, bf16[384,1024]{1,0:T(8,128)(2,1)}, f32[8,1024]{1,0:T(8,128)}, f32[8,512]{1,0:T(8,128)}) custom-call(s32[19]{0:T(128)} %copy-done.29, bf16[384,1024]{1,0:T(8,128)(2,1)} %get-tuple-element.413.refs_1_, ...), custom_call_target="tpu_custom_call", output_to_operand_aliasing={{0}: (9, {}), {1}: (10, {})} | custom-call | flops 2415919104 | bytes 12582912 | tf_op jit(solution)/shard_map/pallas_call | solution.py:123
  287.4 31.1 %collective-permute-done.18.refs_1_ = bf16[384,1024]{1,0:T(8,128)(2,1)S(1)} collective-permute-done((bf16[384,1024]{1,0:T(8,128)(2,1)S(1)}, bf16[384,1024]{1,0:T(8,128)(2,1)S(1)}, u32[]{:S(2)}, u32[]{:S(2)}) %collective-permute-start.18) | collective-permute-done | bytes 786464 | tf_op jit(solution)/shard_map/ppermute | solution.py:1479
  322.4 5.2 bitcast_convert_fusion.6.refs_16_.refs_5_
  327.6 4.6 bitcast_convert_fusion.7.refs_15_.refs_3_
  332.2 18.4 %shard_map.321 = (bf16[2,384,1024]{2,1,0:T(8,128)(2,1)}, bf16[2,384,4096]{2,1,0:T(8,128)(2,1)}, bf16[2,384,1024]{2,1,0:T(8,128)(2,1)}, bf16[384,1024]{1,0:T(8,12...) custom-call(s32[19]{0:T(128)} %copy-done.29, ...), custom_call_target="tpu_custom_call", output_to_operand_aliasing={{1}: (13, {}), {2}: (14, {})} | custom-call | flops 7247757312 | bytes 31457280 | tf_op jit(solution)/shard_map/pallas_call | solution.py:123
  350.7 5.7 bitcast_convert_fusion
  364.0 5.1 bitcast_convert_fusion.1.refs_1_
  374.8 15.8 %shard_map.323 = (bf16[384,1024]{1,0:T(8,128)(2,1)}, bf16[2,384,1024]{2,1,0:T(8,128)(2,1)}, bf16[2,384,1024]{2,1,0:T(8,128)(2,1)}) custom-call(s32[19]{0:T(128)} %copy-done.29, bf16[384,1024]{1,0:T(8,128)(2,1)} %get-tuple-element.420.refs_1_, bf16[2,384,1024]{2,1,0:T(8,128)(2,1)} %shard_map.309.refs_1_.refs_2_, ...), custom_call_target="tpu_custom_call" | custom-call | flops 2415919104 | bytes 21233664 | tf_op jit(solution)/shard_map/pallas_call | solution.py:83
  393.9 12.1 %collective-permute-done.24.refs_7_ = bf16[64,4096]{1,0:T(8,128)(2,1)S(1)} collective-permute-done((bf16[64,4096]{1,0:T(8,128)(2,1)S(1)}, bf16[64,4096]{1,0:T(8,128)(2,1)S(1)}, u32[]{:S(2)}, u32[]{:S(2)}) %collective-permute-start.24) | collective-permute-done | bytes 524320 | tf_op jit(solution)/shard_map/ppermute | solution.py:1095
  420.6 9.5 %shard_map.325 = (bf16[2,384,3072]{2,1,0:T(8,128)(2,1)}, bf16[2,384,1024]{2,1,0:T(8,128)(2,1)}, bf16[384,1024]{1,0:T(8,128)(2,1)}, f32[8,1024]{1,0:T(8,128)}, f32[8,512]{1,0:T(8,128)}) custom-call(s32[19]{0:T(128)} %copy-done.29, bf16[384,1024]{1,0:T(8,128)(2,1)} %get-tuple-element.425.refs_1_, ...), custom_call_target="tpu_custom_call", output_to_operand_aliasing={{0}: (9, {}), {1}: (10, {})} | custom-call | flops 2415919104 | bytes 12582912 | tf_op jit(solution)/shard_map/pallas_call | solution.py:123
  454.5 7.8 %collective-permute-done.34.refs_7_ = bf16[64,4096]{1,0:T(8,128)(2,1)S(1)} collective-permute-done((bf16[64,4096]{1,0:T(8,128)(2,1)S(1)}, bf16[64,4096]{1,0:T(8,128)(2,1)S(1)}, u32[]{:S(2)}, u32[]{:S(2)}) %collective-permute-start.34) | collective-permute-done | bytes 524320 | tf_op jit(solution)/shard_map/ppermute | solution.py:1095
  493.7 14.0 %collective-permute-done.32.refs_7_ = bf16[64,2176]{1,0:T(8,128)(2,1)S(1)} collective-permute-done((bf16[64,2176]{1,0:T(8,128)(2,1)S(1)}, bf16[64,2176]{1,0:T(8,128)(2,1)S(1)}, u32[]{:S(2)}, u32[]{:S(2)}) %collective-permute-start.32) | collective-permute-done | bytes 278560 | tf_op jit(solution)/shard_map/ppermute | solution.py:1095
  517.7 14.0 %collective-permute-done.38.refs_7_ = bf16[64,2176]{1,0:T(8,128)(2,1)S(1)} collective-permute-done((bf16[64,2176]{1,0:T(8,128)(2,1)S(1)}, bf16[64,2176]{1,0:T(8,128)(2,1)S(1)}, u32[]{:S(2)}, u32[]{:S(2)}) %collective-permute-start.38) | collective-permute-done | bytes 278560 | tf_op jit(solution)/shard_map/ppermute | solution.py:1095
  540.5 12.8 %collective-permute-done.42.refs_7_ = bf16[64,2176]{1,0:T(8,128)(2,1)S(1)} collective-permute-done((bf16[64,2176]{1,0:T(8,128)(2,1)S(1)}, bf16[64,2176]{1,0:T(8,128)(2,1)S(1)}, u32[]{:S(2)}, u32[]{:S(2)}) %collective-permute-start.42) | collective-permute-done | bytes 278560 | tf_op jit(solution)/shard_map/ppermute | solution.py:1095
  562.2 11.7 %collective-permute-done.46.refs_7_ = bf16[64,2176]{1,0:T(8,128)(2,1)S(1)} collective-permute-done((bf16[64,2176]{1,0:T(8,128)(2,1)S(1)}, bf16[64,2176]{1,0:T(8,128)(2,1)S(1)}, u32[]{:S(2)}, u32[]{:S(2)}) %collective-permute-start.46) | collective-permute-done | bytes 278560 | tf_op jit(solution)/shard_map/ppermute | solution.py:1095
  583.3 10.6 %collective-permute-done.50.refs_7_ = bf16[64,2176]{1,0:T(8,128)(2,1)S(1)} collective-permute-done((bf16[64,2176]{1,0:T(8,128)(2,1)S(1)}, bf16[64,2176]{1,0:T(8,128)(2,1)S(1)}, u32[]{:S(2)}, u32[]{:S(2)}) %collective-permute-start.50) | collective-permute-done | bytes 278560 | tf_op jit(solution)/shard_map/ppermute | solution.py:1095
  602.6 9.5 %collective-permute-done.54.refs_7_ = bf16[64,2176]{1,0:T(8,128)(2,1)S(1)} collective-permute-done((bf16[64,2176]{1,0:T(8,128)(2,1)S(1)}, bf16[64,2176]{1,0:T(8,128)(2,1)S(1)}, u32[]{:S(2)}, u32[]{:S(2)}) %collective-permute-start.54) | collective-permute-done | bytes 278560 | tf_op jit(solution)/shard_map/ppermute | solution.py:1095
  620.9 9.4 %collective-permute-done.58.refs_7_ = bf16[64,2176]{1,0:T(8,128)(2,1)S(1)} collective-permute-done((bf16[64,2176]{1,0:T(8,128)(2,1)S(1)}, bf16[64,2176]{1,0:T(8,128)(2,1)S(1)}, u32[]{:S(2)}, u32[]{:S(2)}) %collective-permute-start.58) | collective-permute-done | bytes 278560 | tf_op jit(solution)/shard_map/ppermute | solution.py:1095
  639.4 12.1 %collective-permute-done.62.refs_3_ = bf16[64,2176]{1,0:T(8,128)(2,1)S(1)} collective-permute-done((bf16[64,2176]{1,0:T(8,128)(2,1)S(1)}, bf16[64,2176]{1,0:T(8,128)(2,1)S(1)}, u32[]{:S(2)}, u32[]{:S(2)}) %collective-permute-start.62) | collective-permute-done | bytes 278560 | tf_op jit(solution)/shard_map/ppermute | solution.py:1095
  681.6 4.5 collective-permute-done.74.refs_1_
  (347 shorter events, 302.5 us)
Async XLA Ops:
  8.8 27.6 %collective-permute-start.7 = (bf16[1024,2048]{1,0:T(8,128)(2,1)}, bf16[1024,2048]{1,0:T(8,128)(2,1)}, u32[]{:S(2)}, u32[]{:S(2)}) collective-permute-start(bf16[1024,2048]{1,0:T(8,128)(2,1)} %bitcast.80), channel_id=1, source_target_pairs={{0,8},{8,0},{1,9},{9,1},{2,10},{10,2},{3,11},{11,3},{4,12},{12,4},... | collective-permute-start | bytes 12582920 | tf_op jit(solution)/shard_map/ppermute | solution.py:956
  17.4 19.1 %collective-permute-start.6 = (bf16[512,1024]{1,0:T(8,128)(2,1)}, bf16[512,1024]{1,0:T(8,128)(2,1)}, u32[]{:S(2)}, u32[]{:S(2)}) collective-permute-start(bf16[512,1024]{1,0:T(8,128)(2,1)} %bitcast.8.refs_4_.refs_8_.refs_7_), channel_id=1, source_target_pairs={{0,8},{8,0},{1,9},{9,1},{2,10},{10,2},{3,11},{11,3},{4,12},{12,4},... | collective-permute-start | bytes 3145736 | tf_op jit(solution)/shard_map/ppermute | solution.py:956
  22.5 36.3 %collective-permute-start.3 = (bf16[384,512]{1,0:T(8,128)(2,1)S(1)}, bf16[384,512]{1,0:T(8,128)(2,1)S(1)}, u32[]{:S(2)}, u32[]{:S(2)}) collective-permute-start(bf16[384,512]{1,0:T(8,128)(2,1)S(1)} %bitcast.62), channel_id=1, source_target_pairs={{0,8},{8,0},{1,9},{9,1},{2,10},{10,2},{3,11},{11,3},{4,12},{12,4},... | collective-permute-start | bytes 1179656 | tf_op jit(solution)/shard_map/ppermute | solution.py:956
  67.0 40.7 %collective-permute-start.10 = (bf16[384,1024]{1,0:T(8,128)(2,1)}, bf16[384,1024]{1,0:T(8,128)(2,1)}, u32[]{:S(2)}, u32[]{:S(2)}) collective-permute-start(bf16[384,1024]{1,0:T(8,128)(2,1)} %get-tuple-element.326.refs_9_), channel_id=1, source_target_pairs={{0,16},{1,17},{2,18},{3,19},{4,20},{5,21},{6,22},{7,23},{8,24},{9,... | collective-permute-start | bytes 2359304 | tf_op jit(solution)/shard_map/ppermute | solution.py:1471
  114.5 19.0 %collective-permute-start.9 = (bf16[384,1024]{1,0:T(8,128)(2,1)}, bf16[384,1024]{1,0:T(8,128)(2,1)S(1)}, u32[]{:S(2)}, u32[]{:S(2)}) collective-permute-start(bf16[384,1024]{1,0:T(8,128)(2,1)} %get-tuple-element.343.refs_8_), channel_id=1, source_target_pairs={{0,16},{1,17},{2,18},{3,19},{4,20},{5,21},{6,22},{7,23},{8,24},{9,... | collective-permute-start | bytes 2359304 | tf_op jit(solution)/shard_map/ppermute | solution.py:1473
  156.2 59.2 %collective-permute-start.15 = (bf16[384,1024]{1,0:T(8,128)(2,1)S(1)}, bf16[384,1024]{1,0:T(8,128)(2,1)S(1)}, u32[]{:S(2)}, u32[]{:S(2)}) collective-permute-start(bf16[384,1024]{1,0:T(8,128)(2,1)S(1)} %copy-done.50), channel_id=1, source_target_pairs={{16,0},{17,1},{18,2},{19,3},{20,4},{21,5},{22,6},{23,7},{24,8},{25... | collective-permute-start | bytes 2359304 | tf_op jit(solution)/shard_map/ppermute | solution.py:1476
  274.5 44.1 %collective-permute-start.18 = (bf16[384,1024]{1,0:T(8,128)(2,1)S(1)}, bf16[384,1024]{1,0:T(8,128)(2,1)S(1)}, u32[]{:S(2)}, u32[]{:S(2)}) collective-permute-start(bf16[384,1024]{1,0:T(8,128)(2,1)S(1)} %copy-done.51), channel_id=1, source_target_pairs={{16,0},{17,1},{18,2},{19,3},{20,4},{21,5},{22,6},{23,7},{24,8},{25... | collective-permute-start | bytes 2359304 | tf_op jit(solution)/shard_map/ppermute | solution.py:1479
  390.5 29.0 %collective-permute-start.23 = (bf16[2,384,1024]{2,1,0:T(8,128)(2,1)}, bf16[2,384,1024]{2,1,0:T(8,128)(2,1)S(1)}, u32[]{:S(2)}, u32[]{:S(2)}) collective-permute-start(bf16[2,384,1024]{2,1,0:T(8,128)(2,1)} %get-tuple-element.427), channel_id=1, source_target_pairs={{0,8},{8,0},{1,9},{9,1},{2,10},{10,2},{3,11},{11,3},{4,12},{12,4},... | collective-permute-start | bytes 4718600 | tf_op jit(solution)/shard_map/ppermute | solution.py:956
  445.7 29.6 %collective-permute-start.29 = (bf16[1024,1536]{1,0:T(8,128)(2,1)}, bf16[1024,1536]{1,0:T(8,128)(2,1)}, u32[]{:S(2)}, u32[]{:S(2)}) collective-permute-start(bf16[1024,1536]{1,0:T(8,128)(2,1)} %bitcast_convert_fusion.2), channel_id=1, source_target_pairs={{0,8},{8,0},{1,9},{9,1},{2,10},{10,2},{3,11},{11,3},{4,12},{12,4},... | collective-permute-start | bytes 9437192 | tf_op jit(solution)/shard_map/ppermute | solution.py:956
  448.0 27.3 %collective-permute-start.30 = (bf16[1024,512]{1,0:T(8,128)(2,1)}, bf16[1024,512]{1,0:T(8,128)(2,1)}, u32[]{:S(2)}, u32[]{:S(2)}) collective-permute-start(bf16[1024,512]{1,0:T(8,128)(2,1)} %pad_maximum_fusion.1), channel_id=1, source_target_pairs={{0,8},{8,0},{1,9},{9,1},{2,10},{10,2},{3,11},{11,3},{4,12},{12,4},... | collective-permute-start | bytes 3145736 | tf_op jit(solution)/shard_map/ppermute | solution.py:956
  489.2 22.0 %collective-permute-start.40 = (bf16[64,4096]{1,0:T(8,128)(2,1)S(1)}, bf16[64,4096]{1,0:T(8,128)(2,1)S(1)}, u32[]{:S(2)}, u32[]{:S(2)}) collective-permute-start(bf16[64,4096]{1,0:T(8,128)(2,1)S(1)} %get-tuple-element.471), channel_id=1, source_target_pairs={{0,2},{2,4},{4,6},{6,7},{7,5},{5,3},{3,1},{1,0},{8,10},{10,12},{12... | collective-permute-start | bytes 1572872 | tf_op jit(solution)/shard_map/ppermute | solution.py:1095
  489.9 21.4 %collective-permute-start.41 = (bf16[64,4096]{1,0:T(8,128)(2,1)S(1)}, bf16[64,4096]{1,0:T(8,128)(2,1)S(1)}, u32[]{:S(2)}, u32[]{:S(2)}) collective-permute-start(bf16[64,4096]{1,0:T(8,128)(2,1)S(1)} %get-tuple-element.472), channel_id=1, source_target_pairs={{0,1},{2,0},{4,2},{6,4},{7,6},{5,7},{3,5},{1,3},{8,9},{10,8},{12,1... | collective-permute-start | bytes 1572872 | tf_op jit(solution)/shard_map/ppermute | solution.py:1095
  491.3 16.4 %collective-permute-start.32 = (bf16[64,2176]{1,0:T(8,128)(2,1)S(1)}, bf16[64,2176]{1,0:T(8,128)(2,1)S(1)}, u32[]{:S(2)}, u32[]{:S(2)}) collective-permute-start(bf16[64,2176]{1,0:T(8,128)(2,1)S(1)} %copy-done.59), channel_id=1, source_target_pairs={{0,2},{2,4},{4,6},{6,7},{7,5},{5,3},{3,1},{1,0},{8,10},{10,12},{12... | collective-permute-start | bytes 835592 | tf_op jit(solution)/shard_map/ppermute | solution.py:1095
  491.9 17.0 %collective-permute-start.33 = (bf16[64,2176]{1,0:T(8,128)(2,1)S(1)}, bf16[64,2176]{1,0:T(8,128)(2,1)S(1)}, u32[]{:S(2)}, u32[]{:S(2)}) collective-permute-start(bf16[64,2176]{1,0:T(8,128)(2,1)S(1)} %copy-done.58), channel_id=1, source_target_pairs={{0,1},{2,0},{4,2},{6,4},{7,6},{5,7},{3,5},{1,3},{8,9},{10,8},{12,1... | collective-permute-start | bytes 835592 | tf_op jit(solution)/shard_map/ppermute | solution.py:1095
  513.6 20.5 %collective-permute-start.44 = (bf16[64,4096]{1,0:T(8,128)(2,1)S(1)}, bf16[64,4096]{1,0:T(8,128)(2,1)S(1)}, u32[]{:S(2)}, u32[]{:S(2)}) collective-permute-start(bf16[64,4096]{1,0:T(8,128)(2,1)S(1)} %get-tuple-element.479), channel_id=1, source_target_pairs={{0,2},{2,4},{4,6},{6,7},{7,5},{5,3},{3,1},{1,0},{8,10},{10,12},{12... | collective-permute-start | bytes 1572872 | tf_op jit(solution)/shard_map/ppermute | solution.py:1095
  514.3 19.9 %collective-permute-start.45 = (bf16[64,4096]{1,0:T(8,128)(2,1)S(1)}, bf16[64,4096]{1,0:T(8,128)(2,1)S(1)}, u32[]{:S(2)}, u32[]{:S(2)}) collective-permute-start(bf16[64,4096]{1,0:T(8,128)(2,1)S(1)} %get-tuple-element.480), channel_id=1, source_target_pairs={{0,1},{2,0},{4,2},{6,4},{7,6},{5,7},{3,5},{1,3},{8,9},{10,8},{12,1... | collective-permute-start | bytes 1572872 | tf_op jit(solution)/shard_map/ppermute | solution.py:1095
  515.7 16.1 %collective-permute-start.38 = (bf16[64,2176]{1,0:T(8,128)(2,1)S(1)}, bf16[64,2176]{1,0:T(8,128)(2,1)S(1)}, u32[]{:S(2)}, u32[]{:S(2)}) collective-permute-start(bf16[64,2176]{1,0:T(8,128)(2,1)S(1)} %get-tuple-element.475), channel_id=1, source_target_pairs={{0,2},{2,4},{4,6},{6,7},{7,5},{5,3},{3,1},{1,0},{8,10},{10,12},{12... | collective-permute-start | bytes 835592 | tf_op jit(solution)/shard_map/ppermute | solution.py:1095
  516.3 15.8 %collective-permute-start.39 = (bf16[64,2176]{1,0:T(8,128)(2,1)S(1)}, bf16[64,2176]{1,0:T(8,128)(2,1)S(1)}, u32[]{:S(2)}, u32[]{:S(2)}) collective-permute-start(bf16[64,2176]{1,0:T(8,128)(2,1)S(1)} %get-tuple-element.476), channel_id=1, source_target_pairs={{0,1},{2,0},{4,2},{6,4},{7,6},{5,7},{3,5},{1,3},{8,9},{10,8},{12,1... | collective-permute-start | bytes 835592 | tf_op jit(solution)/shard_map/ppermute | solution.py:1095
  536.4 19.4 %collective-permute-start.48 = (bf16[64,4096]{1,0:T(8,128)(2,1)S(1)}, bf16[64,4096]{1,0:T(8,128)(2,1)S(1)}, u32[]{:S(2)}, u32[]{:S(2)}) collective-permute-start(bf16[64,4096]{1,0:T(8,128)(2,1)S(1)} %get-tuple-element.487), channel_id=1, source_target_pairs={{0,2},{2,4},{4,6},{6,7},{7,5},{5,3},{3,1},{1,0},{8,10},{10,12},{12... | collective-permute-start | bytes 1572872 | tf_op jit(solution)/shard_map/ppermute | solution.py:1095
  537.0 18.7 %collective-permute-start.49 = (bf16[64,4096]{1,0:T(8,128)(2,1)S(1)}, bf16[64,4096]{1,0:T(8,128)(2,1)S(1)}, u32[]{:S(2)}, u32[]{:S(2)}) collective-permute-start(bf16[64,4096]{1,0:T(8,128)(2,1)S(1)} %get-tuple-element.488), channel_id=1, source_target_pairs={{0,1},{2,0},{4,2},{6,4},{7,6},{5,7},{3,5},{1,3},{8,9},{10,8},{12,1... | collective-permute-start | bytes 1572872 | tf_op jit(solution)/shard_map/ppermute | solution.py:1095
  558.1 18.2 %collective-permute-start.52 = (bf16[64,4096]{1,0:T(8,128)(2,1)S(1)}, bf16[64,4096]{1,0:T(8,128)(2,1)S(1)}, u32[]{:S(2)}, u32[]{:S(2)}) collective-permute-start(bf16[64,4096]{1,0:T(8,128)(2,1)S(1)} %get-tuple-element.495.refs_1_), channel_id=1, source_target_pairs={{0,2},{2,4},{4,6},{6,7},{7,5},{5,3},{3,1},{1,0},{8,10},{10,12},{12... | collective-permute-start | bytes 1572872 | tf_op jit(solution)/shard_map/ppermute | solution.py:1095
  558.7 17.6 %collective-permute-start.53 = (bf16[64,4096]{1,0:T(8,128)(2,1)S(1)}, bf16[64,4096]{1,0:T(8,128)(2,1)S(1)}, u32[]{:S(2)}, u32[]{:S(2)}) collective-permute-start(bf16[64,4096]{1,0:T(8,128)(2,1)S(1)} %get-tuple-element.496.refs_2_), channel_id=1, source_target_pairs={{0,1},{2,0},{4,2},{6,4},{7,6},{5,7},{3,5},{1,3},{8,9},{10,8},{12,1... | collective-permute-start | bytes 1572872 | tf_op jit(solution)/shard_map/ppermute | solution.py:1095
  579.2 17.2 %collective-permute-start.56 = (bf16[64,4096]{1,0:T(8,128)(2,1)S(1)}, bf16[64,4096]{1,0:T(8,128)(2,1)S(1)}, u32[]{:S(2)}, u32[]{:S(2)}) collective-permute-start(bf16[64,4096]{1,0:T(8,128)(2,1)S(1)} %get-tuple-element.503), channel_id=1, source_target_pairs={{0,2},{2,4},{4,6},{6,7},{7,5},{5,3},{3,1},{1,0},{8,10},{10,12},{12... | collective-permute-start | bytes 1572872 | tf_op jit(solution)/shard_map/ppermute | solution.py:1095
  579.9 16.5 %collective-permute-start.57 = (bf16[64,4096]{1,0:T(8,128)(2,1)S(1)}, bf16[64,4096]{1,0:T(8,128)(2,1)S(1)}, u32[]{:S(2)}, u32[]{:S(2)}) collective-permute-start(bf16[64,4096]{1,0:T(8,128)(2,1)S(1)} %get-tuple-element.504), channel_id=1, source_target_pairs={{0,1},{2,0},{4,2},{6,4},{7,6},{5,7},{3,5},{1,3},{8,9},{10,8},{12,1... | collective-permute-start | bytes 1572872 | tf_op jit(solution)/shard_map/ppermute | solution.py:1095
  598.5 16.2 %collective-permute-start.60 = (bf16[64,4096]{1,0:T(8,128)(2,1)S(1)}, bf16[64,4096]{1,0:T(8,128)(2,1)S(1)}, u32[]{:S(2)}, u32[]{:S(2)}) collective-permute-start(bf16[64,4096]{1,0:T(8,128)(2,1)S(1)} %get-tuple-element.513), channel_id=1, source_target_pairs={{0,2},{2,4},{4,6},{6,7},{7,5},{5,3},{3,1},{1,0},{8,10},{10,12},{12... | collective-permute-start | bytes 1572872 | tf_op jit(solution)/shard_map/ppermute | solution.py:1095
  599.2 15.5 %collective-permute-start.61 = (bf16[64,4096]{1,0:T(8,128)(2,1)S(1)}, bf16[64,4096]{1,0:T(8,128)(2,1)S(1)}, u32[]{:S(2)}, u32[]{:S(2)}) collective-permute-start(bf16[64,4096]{1,0:T(8,128)(2,1)S(1)} %get-tuple-element.514), channel_id=1, source_target_pairs={{0,1},{2,0},{4,2},{6,4},{7,6},{5,7},{3,5},{1,3},{8,9},{10,8},{12,1... | collective-permute-start | bytes 1572872 | tf_op jit(solution)/shard_map/ppermute | solution.py:1095
  616.8 16.4 %collective-permute-start.64 = (bf16[64,4096]{1,0:T(8,128)(2,1)S(1)}, bf16[64,4096]{1,0:T(8,128)(2,1)S(1)}, u32[]{:S(2)}, u32[]{:S(2)}) collective-permute-start(bf16[64,4096]{1,0:T(8,128)(2,1)S(1)} %get-tuple-element.523), channel_id=1, source_target_pairs={{0,2},{2,4},{4,6},{6,7},{7,5},{5,3},{3,1},{1,0},{8,10},{10,12},{12... | collective-permute-start | bytes 1572872 | tf_op jit(solution)/shard_map/ppermute | solution.py:1095
  635.3 23.2 %collective-permute-start.68 = (bf16[64,4096]{1,0:T(8,128)(2,1)S(1)}, bf16[64,4096]{1,0:T(8,128)(2,1)S(1)}, u32[]{:S(2)}, u32[]{:S(2)}) collective-permute-start(bf16[64,4096]{1,0:T(8,128)(2,1)S(1)} %get-tuple-element.533), channel_id=1, source_target_pairs={{0,2},{2,4},{4,6},{6,7},{7,5},{5,3},{3,1},{1,0},{8,10},{10,12},{12... | collective-permute-start | bytes 1572872 | tf_op jit(solution)/shard_map/ppermute | solution.py:1095
  636.4 22.1 %collective-permute-start.69 = (bf16[64,4096]{1,0:T(8,128)(2,1)S(1)}, bf16[64,4096]{1,0:T(8,128)(2,1)S(1)}, u32[]{:S(2)}, u32[]{:S(2)}) collective-permute-start(bf16[64,4096]{1,0:T(8,128)(2,1)S(1)} %get-tuple-element.534), channel_id=1, source_target_pairs={{0,1},{2,0},{4,2},{6,4},{7,6},{5,7},{3,5},{1,3},{8,9},{10,8},{12,1... | collective-permute-start | bytes 1572872 | tf_op jit(solution)/shard_map/ppermute | solution.py:1095
  690.6 19.4 %collective-permute-start.16 = (bf16[2,384,512]{2,1,0:T(8,128)(2,1)S(1)}, bf16[2,384,512]{2,1,0:T(8,128)(2,1)S(1)}, u32[]{:S(2)}, u32[]{:S(2)}) collective-permute-start(bf16[2,384,512]{2,1,0:T(8,128)(2,1)S(1)} %shard_map.312), channel_id=1, source_target_pairs={{0,8},{8,0},{1,9},{9,1},{2,10},{10,2},{3,11},{11,3},{4,12},{12,4},... | collective-permute-start | bytes 2359304 | tf_op jit(solution)/shard_map/ppermute | solution.py:956
  698.1 15.6 %collective-permute-start.26 = (bf16[2,384,512]{2,1,0:T(8,128)(2,1)S(1)}, bf16[2,384,512]{2,1,0:T(8,128)(2,1)S(1)}, u32[]{:S(2)}, u32[]{:S(2)}) collective-permute-start(bf16[2,384,512]{2,1,0:T(8,128)(2,1)S(1)} %shard_map.326), channel_id=1, source_target_pairs={{0,8},{8,0},{1,9},{9,1},{2,10},{10,2},{3,11},{11,3},{4,12},{12,4},... | collective-permute-start | bytes 2359304 | tf_op jit(solution)/shard_map/ppermute | solution.py:956
  699.8 16.0 %collective-permute-start.82 = (bf16[64,4096]{1,0:T(8,128)(2,1)S(1)}, bf16[64,4096]{1,0:T(8,128)(2,1)S(1)}, u32[]{:S(2)}, u32[]{:S(2)}) collective-permute-start(bf16[64,4096]{1,0:T(8,128)(2,1)S(1)} %get-tuple-element.556), channel_id=1, source_target_pairs={{0,2},{2,4},{4,6},{6,7},{7,5},{5,3},{3,1},{1,0},{8,10},{10,12},{12... | collective-permute-start | bytes 1572872 | tf_op jit(solution)/shard_map/ppermute | solution.py:1095
  (114 other events, 927.8 us)

commit v6 on v5

--- a/solution.py
+++ b/solution.py
@@ -43,6 +43,14 @@
 
 def tiles(rows):
     return [slice(r, r + TILE) for r in range(0, rows, TILE)]
+
+
+def each_tile(rows, body):
+    def step(i, carry):
+        body(pl.ds(pl.multiple_of(i * TILE, TILE), TILE))
+        return carry
+
+    lax.fori_loop(0, rows // TILE, step, 0, unroll=8)
 
 
 def eights(values):
@@ -411,7 +419,8 @@
     def kernel(
         s, m, x_ref, v, woo, wot, wuo, wut, wdo, wdt, bu,
         att_out, res_out, n_out, act_out, slope_out, branch_out, y_out, relay_out, m_out,
-        m_v, x_v, wo_v, wu_v, wd_v, att_v, res_v, n_v, h_v, act_v, slope_v, branch_v, y_v, acc,
+        m_v, x_v, wo_v, wu_v, wd_v, att_v, res_v, n_v, h_one, h_two, a_one, a_two, d_one, d_two,
+        branch_v, y_v, acc,
         in_sems, wu_sems, wd_sems, out_sems, act_sems, slope_sems,
     ):
         @pl.when(s[ACTIVE + owner] == 1)
@@ -423,27 +432,24 @@
                 begin(wot, wo_v.at[1], in_sems.at[2]),
                 begin(x_ref.at[slot], x_v, in_sems.at[3]),
             ]
-            ups, downs = [], []
-
-            def prefetch(i):
-                if i < steps:
-                    part = pl.ds((i % split) * CHUNK, CHUNK)
-                    up, down = (wuo, wdo) if i < split else (wut, wdt)
-                    ups.append(begin(up.at[:, part], wu_v.at[i], wu_sems.at[i]))
-                    downs.append(begin(down.at[part], wd_v.at[i], wd_sems.at[i]))
-
-            prefetch(0)
-            prefetch(1)
+            for i in range(steps):
+                part = pl.ds((i % split) * CHUNK, CHUNK)
+                up, down = (wuo, wdo) if i < split else (wut, wdt)
+                begin(up.at[:, part], wu_v.at[i], wu_sems.at[i])
+                begin(down.at[part], wd_v.at[i], wd_sems.at[i])
             for copy in first:
                 copy.wait()
             acc[...] = dot(m_v[:, :half], wo_v[0]) + dot(m_v[:, half:], wo_v[1])
-            for t in tiles(rows):
+
+            def first_norm(t):
                 attended = acc[t] + v[OUTB : OUTB + 1]
                 att_v[t] = attended.astype(BF16)
                 residual = x_v[t].astype(F32) + v[SATT : SATT + 1] * attended
                 res_v[t] = residual
                 hat, _ = norm_stats(residual)
                 n_v[t] = (hat * v[LN2G : LN2G + 1] + v[LN2B : LN2B + 1]).astype(BF16)
+
+            each_tile(rows, first_norm)
             outs = [
                 begin(att_v, att_out.at[slot], out_sems.at[0]),
                 begin(res_v, res_out.at[slot], out_sems.at[1]),
@@ -451,34 +457,83 @@
                 begin(m_v, m_out.at[slot], out_sems.at[6]),
             ]
 
-            def up_product(i):
-                ups[i].wait()
-                h_v[i % 2] = dot(n_v[...], wu_v[i])
-
-            def down_product(i):
-                downs[i].wait()
-                part = pl.ds(i * CHUNK, CHUNK)
-                outs.append(begin(act_v.at[i], act_out.at[slot, :, part], act_sems.at[i]))
-                outs.append(begin(slope_v.at[i], slope_out.at[slot, :, part], slope_sems.at[i]))
-                product = dot(act_v[i], wd_v[i])
-                acc[...] = product if i == 0 else acc[...] + product
-
-            up_product(0)
-            for i in range(steps):
-                prefetch(i + 2)
-                if i > 0:
-                    down_product(i - 1)
-                if i + 1 < steps:
-                    up_product(i + 1)
+            def up_product(i, target):
+                target[...] = dot(n_v[...], wu_v[i])
+
+            def up_wait(i):
+                pltpu.make_async_copy(
+                    wuo.at[:, pl.ds(0, CHUNK)], wu_v.at[i], wu_sems.at[i]
+                ).wait()
+
+            def down_wait(i):
+                pltpu.make_async_copy(wdo.at[pl.ds(0, CHUNK)], wd_v.at[i], wd_sems.at[i]).wait()
+
+            def copies(i, active, slope, side):
+                part = pl.ds(pl.multiple_of(i * CHUNK, CHUNK), CHUNK)
+                return [
+                    pltpu.make_async_copy(active, act_out.at[slot, :, part], act_sems.at[side]),
+                    pltpu.make_async_copy(
+                        slope, slope_out.at[slot, :, part], slope_sems.at[side]
+                    ),
+                ]
+
+            def activate(i, source, active_to, slope_to):
+                shift = bu[pl.ds(i, 1), :]
                 for t in tiles(rows):
-                    active, slope = gelu_parts(h_v[i % 2, t] + bu[i : i + 1])
-                    act_v[i, t] = active.astype(BF16)
-                    slope_v[i, t] = slope.astype(BF16)
-            down_product(steps - 1)
-            for t in tiles(rows):
+                    active, slope = gelu_parts(source[t] + shift)
+                    active_to[t] = active.astype(BF16)
+                    slope_to[t] = slope.astype(BF16)
+
+            def pair(j, carry):
+                i = 2 * j
+                before = jnp.maximum(i - 1, 0)
+                up_wait(i + 1)
+
+                @pl.when(j > 0)
+                def _():
+                    for copy in copies(i - 2, a_one, d_one, 0):
+                        copy.wait()
+                    down_wait(i - 1)
+
+                acc[...] += dot(a_two[...], wd_v[before])
+                up_product(i + 1, h_two)
+                activate(i, h_one, a_one, d_one)
+                for copy in copies(i, a_one, d_one, 0):
+                    copy.start()
+
+                @pl.when(j > 0)
+                def _():
+                    down_wait(i)
+                    for copy in copies(i - 1, a_two, d_two, 1):
+                        copy.wait()
+
+                @pl.when(i + 2 < steps)
+                def _():
+                    up_wait(i + 2)
+
+                acc[...] += dot(a_one[...], wd_v[i])
+                up_product(jnp.minimum(i + 2, steps - 1), h_one)
+                activate(i + 1, h_two, a_two, d_two)
+                for copy in copies(i + 1, a_two, d_two, 1):
+                    copy.start()
+                return carry
+
+            acc[...] = jnp.zeros_like(acc)
+            a_two[...] = jnp.zeros_like(a_two)
+            up_wait(0)
+            down_wait(0)
+            up_product(0, h_one)
+            lax.fori_loop(0, steps // 2, pair, 0)
+            down_wait(steps - 1)
+            acc[...] += dot(a_two[...], wd_v[steps - 1])
+
+            def finish(t):
                 branch = acc[t] + v[FC2B : FC2B + 1]
                 y_v[t] = (res_v[t] + v[SMLP : SMLP + 1] * branch).astype(BF16)
                 branch_v[t] = branch.astype(BF16)
+
+            each_tile(rows, finish)
+            outs += copies(steps - 2, a_one, d_one, 0) + copies(steps - 1, a_two, d_two, 1)
             outs.append(begin(y_v, relay_out, out_sems.at[3]))
             outs.append(begin(y_v, y_out.at[slot], out_sems.at[4]))
             outs.append(begin(branch_v, branch_out.at[slot], out_sems.at[5]))
@@ -489,7 +544,8 @@
     tall = (MICRO, rows, hidden)
     plain = pltpu.VMEM((rows, width), BF16)
     full = pltpu.VMEM((rows, width), F32)
-    chunks = pltpu.VMEM((steps, rows, CHUNK), BF16)
+    chunk = pltpu.VMEM((rows, CHUNK), BF16)
+    wide = pltpu.VMEM((rows, CHUNK), F32)
     return manual(
         kernel,
         info,
@@ -525,9 +581,12 @@
             plain,
             full,
             plain,
-            pltpu.VMEM((2, rows, CHUNK), F32),
-            chunks,
-            chunks,
+            wide,
+            wide,
+            chunk,
+            chunk,
+            chunk,
+            chunk,
             plain,
             plain,
             full,
@@ -535,8 +594,8 @@
             dma_sems(steps),
             dma_sems(steps),
             dma_sems(7),
-            dma_sems(steps),
-            dma_sems(steps),
+            dma_sems(2),
+            dma_sems(2),
         ],
         flops=4 * rows * width * hidden + 2 * rows * width * width,
         moved=4 * width * hidden + 2 * width * width + 8 * rows * hidden,
@@ -580,7 +639,7 @@
     def work(
         s, token_refs, branch, slope, res, att, v, woo, wot, wuo, wut, wdo, wdt,
         gb_out, before_out, ga_out, gm_out, gr_out, small_out, shift_out,
-        g_v, branch_v, slope_v, res_v, att_v, wo_v, wu_v, wd_v, gb_v, d_v, before_v, ga_v, gm_v,
+        g_v, branch_v, slope_v, res_v, att_v, wo_v, wu_v, wd_v, gb_v, d_one, d_two, b_one, b_two, ga_v, gm_v,
         gr_v, acc, sums, tok_sems, in_sems, slope_sems, wu_sems, wd_sems, out_sems, before_sems,
     ):
         @pl.when(s[ACTIVE + owner] == 0)
@@ -592,71 +651,114 @@
         def _():
             slot = number
             arriving = token_copies(s, source, number, token_refs, g_v, tok_sems)
-            ups, downs, slopes = [], [], []
-
-            def prefetch(i):
-                if i < steps:
-                    part = pl.ds((i % split) * CHUNK, CHUNK)
-                    up, down = (wuo, wdo) if i < split else (wut, wdt)
-                    here = pl.ds(i * CHUNK, CHUNK)
-                    downs.append(begin(down.at[part], wd_v.at[i], wd_sems.at[i]))
-                    slopes.append(begin(slope.at[slot, :, here], slope_v.at[i], slope_sems.at[i]))
-                    ups.append(begin(up.at[:, part], wu_v.at[i], wu_sems.at[i]))
-
-            prefetch(0)
             branch_in = begin(branch.at[slot], branch_v, in_sems.at[0])
-            prefetch(1)
-            last = []
+            for i in range(steps):
+                part = pl.ds((i % split) * CHUNK, CHUNK)
+                up, down = (wuo, wdo) if i < split else (wut, wdt)
+                here = pl.ds(i * CHUNK, CHUNK)
+                begin(down.at[part], wd_v.at[i], wd_sems.at[i])
+                begin(slope.at[slot, :, here], slope_v.at[i], slope_sems.at[i])
+                begin(up.at[:, part], wu_v.at[i], wu_sems.at[i])
+            last = [
+                begin(res.at[slot], res_v, in_sems.at[1]),
+                begin(att.at[slot], att_v, in_sems.at[2]),
+                begin(woo, wo_v.at[0], in_sems.at[3]),
+                begin(wot, wo_v.at[1], in_sems.at[4]),
+            ]
             for copy in arriving:
                 copy.wait()
-            for t in tiles(rows):
+
+            def scale(t):
                 gb_v[t] = (v[SMLP : SMLP + 1] * g_v[t].astype(F32)).astype(BF16)
+
+            each_tile(rows, scale)
             outs = []
             if not scaled:
                 outs.append(begin(gb_v, gb_out.at[slot], out_sems.at[0]))
 
-            def down_product(i):
-                downs[i].wait()
-                d_v[i % 2] = dot_nt(gb_v[...], wd_v[i])
-
-            down_product(0)
+            def down_product(i, target):
+                target[...] = dot_nt(gb_v[...], wd_v[i])
+
+            def down_wait(i):
+                pltpu.make_async_copy(wdo.at[pl.ds(0, CHUNK)], wd_v.at[i], wd_sems.at[i]).wait()
+
+            def up_wait(i):
+                pltpu.make_async_copy(
+                    wuo.at[:, pl.ds(0, CHUNK)], wu_v.at[i], wu_sems.at[i]
+                ).wait()
+
+            def slope_wait(i):
+                pltpu.make_async_copy(
+                    slope.at[slot, :, pl.ds(0, CHUNK)], slope_v.at[i], slope_sems.at[i]
+                ).wait()
+
+            def copy_out(i, held, side):
+                part = pl.ds(pl.multiple_of(i * CHUNK, CHUNK), CHUNK)
+                return pltpu.make_async_copy(
+                    held, before_out.at[slot, :, part], before_sems.at[side]
+                )
+
+            def differentiate(i, source, target):
+                total = jnp.zeros((8, CHUNK), F32)
+                for t in tiles(rows):
+                    grad_before = (source[t] * slope_v[i, t].astype(F32)).astype(BF16)
+                    target[t] = grad_before
+                    total = total + eights(grad_before.astype(F32))
+                shift_out[pl.ds(i, 1), :] = col_sum(total)
+
+            def pair(j, carry):
+                i = 2 * j
+                before = jnp.maximum(i - 1, 0)
+                slope_wait(i)
+                down_wait(i + 1)
+
+                @pl.when(j > 0)
+                def _():
+                    copy_out(i - 2, b_one, 0).wait()
+                    up_wait(i - 1)
+
+                acc[...] += dot_nt(b_two[...], wu_v[before])
+                down_product(i + 1, d_two)
+                differentiate(i, d_one, b_one)
+                copy_out(i, b_one, 0).start()
+                slope_wait(i + 1)
+
+                @pl.when(j > 0)
+                def _():
+                    up_wait(i)
+                    copy_out(i - 1, b_two, 1).wait()
+
+                @pl.when(i + 2 < steps)
+                def _():
+                    down_wait(i + 2)
+
+                acc[...] += dot_nt(b_one[...], wu_v[i])
+                down_product(jnp.minimum(i + 2, steps - 1), d_one)
+                differentiate(i + 1, d_two, b_two)
+                copy_out(i + 1, b_two, 1).start()
+                return carry
+
+            acc[...] = jnp.zeros_like(acc)
+            b_two[...] = jnp.zeros_like(b_two)
+            down_wait(0)
+            down_product(0, d_one)
             branch_in.wait()
             sums[...] = jnp.zeros_like(sums)
-            for t in tiles(rows):
+
+            def branch_sums(t):
                 sums[0] += eights(g_v[t].astype(F32) * branch_v[t].astype(F32))
                 sums[1] += eights(gb_v[t].astype(F32))
 
-            def up_product(i):
-                ups[i].wait()
-                part = pl.ds(i * CHUNK, CHUNK)
-                outs.append(begin(before_v.at[i], before_out.at[slot, :, part], before_sems.at[i]))
-                product = dot_nt(before_v[i], wu_v[i])
-                acc[...] = product if i == 0 else acc[...] + product
-
-            for i in range(steps):
-                prefetch(i + 2)
-                if i == steps - 2:
-                    last = [
-                        begin(res.at[slot], res_v, in_sems.at[1]),
-                        begin(att.at[slot], att_v, in_sems.at[2]),
-                        begin(woo, wo_v.at[0], in_sems.at[3]),
-                        begin(wot, wo_v.at[1], in_sems.at[4]),
-                    ]
-                slopes[i].wait()
-                if i > 0:
-                    up_product(i - 1)
-                if i + 1 < steps:
-                    down_product(i + 1)
-                total = jnp.zeros((8, CHUNK), F32)
-                for t in tiles(rows):
-                    grad_before = (d_v[i % 2, t] * slope_v[i, t].astype(F32)).astype(BF16)
-                    before_v[i, t] = grad_before
-                    total = total + eights(grad_before.astype(F32))
-                shift_out[i : i + 1] = col_sum(total)
-            up_product(steps - 1)
+            each_tile(rows, branch_sums)
+            up_wait(0)
+            lax.fori_loop(0, steps // 2, pair, 0)
+            up_wait(steps - 1)
+            acc[...] += dot_nt(b_two[...], wu_v[steps - 1])
+            outs += [copy_out(steps - 2, b_one, 0), copy_out(steps - 1, b_two, 1)]
             for copy in last:
                 copy.wait()
-            for t in tiles(rows):
+
+            def last_norm(t):
                 hat, scale = norm_stats(res_v[t])
                 error = acc[t]
                 sums[2] += eights(error * hat)
@@ -667,6 +769,8 @@
                 ga = (v[SATT : SATT + 1] * grad).astype(BF16)
                 ga_v[t] = ga
                 sums[5] += eights(ga.astype(F32))
+
+            each_tile(rows, last_norm)
             outs.append(begin(ga_v, ga_out.at[slot], out_sems.at[1]))
             outs.append(begin(gr_v, gr_out, out_sems.at[3]))
             gm_v[:, :half] = dot_nt(ga_v[...], wo_v[0]).astype(BF16)
@@ -718,8 +822,10 @@
             pltpu.VMEM((steps, width, CHUNK), BF16),
             pltpu.VMEM((steps, CHUNK, width), BF16),
             plain,
-            pltpu.VMEM((2, rows, CHUNK), F32),
-            chunks,
+            pltpu.VMEM((rows, CHUNK), F32),
+            pltpu.VMEM((rows, CHUNK), F32),
+            pltpu.VMEM((rows, CHUNK), BF16),
+            pltpu.VMEM((rows, CHUNK), BF16),
             plain,
             plain,
             full,
@@ -731,7 +837,7 @@
             dma_sems(steps),
             dma_sems(steps),
             dma_sems(4),
-            dma_sems(steps),
+            dma_sems(2),
         ],
         flops=4 * rows * width * hidden + 2 * rows * width * width,
         moved=4 * width * hidden + 2 * width * width + 8 * rows * hidden,
@@ -979,7 +1085,6 @@
         self.totals = [None] * len(shapes)
         self.vmem = RING_MIB
         self.moving = self.add([0, 0], None)
-        self.vmem = 16
 
     def unit(self, way, ahead):
         return UNITS + way * self.count + ahead % self.count
@@ -1535,6 +1640,8 @@
         TailPlaces(half, LANES),
     )
     rings = [ring_mlp, ring_tail]
+    for ring in rings:
+        ring.vmem = 16
     before_it = ring_tail
     while not all(ring.done() for ring in rings):
         for ring in rings:

time: 736 us -> 759 us (1.031)
  waiting for transfers between devices: 272 us -> 299 us
  local copies, waits for them, and re-layouts: 33.1 us -> 19.8 us
    ppermute x1, waiting for transfers between devices: 51.6 us -> 65.3 us  [shards(): first = lax.ppermute(relayed, 'section', [(1, 0)])]
    unnamed x124 -> x106, local copies, waits for them, and re-layouts: 31.5 us -> 18.2 us
  transfers between devices with their start and end apart: 84 -> 84, of which waited for: 50 -> 50; matrix products, arithmetic and copies ran while one was open for 3% -> 3% of each run, Pallas kernels for 22% -> 23%
where the time goes in v6:
time: 759 us; the launch traced here: 748 us
  Pallas kernels  313 us (41%)
  waiting for transfers between devices  299 us (39%)
  starting transfers between devices  69.5 us (9%)
  matrix products  42.5 us (6%)
  local copies, waits for them, and re-layouts  19.8 us (3%)
    pallas_call x58, Pallas kernels, manual(): pl.pallas_call(body, out_shape=[jax.ShapeDtypeStruct(s, d) for s, d, _, _...  235 us
    ppermute x56, waiting for transfers between devices, advance(): lax.ppermute(self.moving[w], 'dp', self.routes[w])  164 us
    pallas_call x8, Pallas kernels, call(): pl.pallas_call(body, out_shape=[jax.ShapeDtypeStruct(s, d) for s, d, _, _...  71.8 us
    ppermute x1, waiting for transfers between devices, shards(): first = lax.ppermute(relayed, 'section', [(1, 0)])  65.3 us
    ppermute x56, starting transfers between devices, advance(): lax.ppermute(self.moving[w], 'dp', self.routes[w])  58 us
    dot_general x12, matrix products, weight_grad(): lax.dot_general(left, right, (((0, 1), (0, 1)), ((), ())), preferred_elem...  42.5 us
    ppermute x1, waiting for transfers between devices, shards(): second = lax.ppermute(relayed, 'section', [(1, 0)])  38.5 us
    ppermute x24, waiting for transfers between devices, swap(): return lax.ppermute(block, 'tensor', [(0, 1), (1, 0)])  19.6 us
  transfers between devices with their start and end apart: 84, of which 50 were waited for; matrix products, arithmetic and copies ran while one was open for 3% of the time, Pallas kernels for 23%

profile of v6, /device:TPU:0, one launch (start us, length us, event | category | flops | bytes accessed | tf_op | source)
XLA Modules:
  0.0 747.8 jit_solution(7414220743498437999)
XLA Ops:
  10.4 6.5 shard_map.292
  24.2 12.3 %shard_map.294 = (bf16[3,16,384,768]{3,2,1,0:T(8,128)(2,1)}, f32[3,384,1024]{2,1,0:T(8,128)}, bf16[384,1024]{1,0:T(8,128)(2,1)}, f32[3,384,1024]{2,1,0:T(8,128)}, bf16[3,2,768,1024]{3,2,1,0:T(8,128)(2,1)}) custom-call(s32[19]{0:T(128)} %copy-done.21, bf16[2,384,1024]{2,1,0:T(8,128)(2,1)} %shard_map.293.refs_1_.refs_5_, ...), custom_call_target="tpu_custom_call" | custom-call | flops 1207959552 | bytes 21233664 | tf_op jit(solution)/shard_map/pallas_call | solution.py:91
  36.5 26.4 %shard_map.295 = (bf16[2,384,1024]{2,1,0:T(8,128)(2,1)}, f32[2,384,1024]{2,1,0:T(8,128)}, bf16[2,384,1024]{2,1,0:T(8,128)(2,1)}, bf16[2,384,4096]{2,1,0:T(8,128)...) custom-call(s32[19]{0:T(128)} %copy-done.21, ...), custom_call_target="tpu_custom_call" | custom-call | flops 7247757312 | bytes 31457280 | tf_op jit(solution)/shard_map/pallas_call | solution.py:131
  63.6 6.5 shard_map.296
  72.8 4.3 shard_map.297.refs_1_.refs_5_
  78.2 12.2 %shard_map.298 = (bf16[3,16,384,768]{3,2,1,0:T(8,128)(2,1)}, f32[3,384,1024]{2,1,0:T(8,128)}, bf16[384,1024]{1,0:T(8,128)(2,1)}, f32[3,384,1024]{2,1,0:T(8,128)}, bf16[3,2,768,1024]{3,2,1,0:T(8,128)(2,1)}) custom-call(s32[19]{0:T(128)} %copy-done.21, ...), custom_call_target="tpu_custom_call", output_to_operand_aliasing={{0}: (4, {}), {1}: (5, {}), {3}: (6, {}), {4}: (7, {})} | custom-call | flops 1207959552 | bytes 21233664 | tf_op jit(solution)/shard_map/pallas_call | solution.py:91
  90.4 26.0 %shard_map.299 = (bf16[2,384,1024]{2,1,0:T(8,128)(2,1)}, f32[2,384,1024]{2,1,0:T(8,128)}, bf16[2,384,1024]{2,1,0:T(8,128)(2,1)}, bf16[2,384,4096]{2,1,0:T(8,128)...) custom-call(s32[19]{0:T(128)} %copy-done.21, ...), custom_call_target="tpu_custom_call", output_to_operand_aliasing={{0}: (11, {}), {1}: (12, {}), {2}: (13, {}), {3}: (14, {}),... | custom-call | flops 7247757312 | bytes 31457280 | tf_op jit(solution)/shard_map/pallas_call | solution.py:131
  130.6 11.4 %collective-permute-done.9.refs_15_.refs_1_ = bf16[384,1024]{1,0:T(8,128)(2,1)S(1)} collective-permute-done((bf16[384,1024]{1,0:T(8,128)(2,1)}, bf16[384,1024]{1,0:T(8,128)(2,1)S(1)}, u32[]{:S(2)}, u32[]{:S(2)}) %collective-permute-start.9) | collective-permute-done | bytes 786464 | tf_op jit(solution)/shard_map/ppermute | solution.py:1578
  164.1 65.3 %collective-permute-done.15.refs_19_.refs_1_ = bf16[384,1024]{1,0:T(8,128)(2,1)S(1)} collective-permute-done((bf16[384,1024]{1,0:T(8,128)(2,1)S(1)}, bf16[384,1024]{1,0:T(8,128)(2,1)S(1)}, u32[]{:S(2)}, u32[]{:S(2)}) %collective-permute-start.15) | collective-permute-done | bytes 786464 | tf_op jit(solution)/shard_map/ppermute | solution.py:1581
  244.1 23.5 %shard_map.317 = (bf16[2,384,1024]{2,1,0:T(8,128)(2,1)}, bf16[2,384,4096]{2,1,0:T(8,128)(2,1)}, bf16[2,384,1024]{2,1,0:T(8,128)(2,1)}, bf16[384,1024]{1,0:T(8,12...) custom-call(s32[19]{0:T(128)} %copy-done.21, ...), custom_call_target="tpu_custom_call", output_to_operand_aliasing={{0}: (13, {}), {1}: (14, {}), {2}: (15, {})} | custom-call | flops 7247757312 | bytes 31457280 | tf_op jit(solution)/shard_map/pallas_call | solution.py:131
  267.6 15.8 %shard_map.318 = (bf16[384,1024]{1,0:T(8,128)(2,1)}, bf16[2,384,1024]{2,1,0:T(8,128)(2,1)}, bf16[2,384,1024]{2,1,0:T(8,128)(2,1)}) custom-call(s32[19]{0:T(128)} %copy-done.21, bf16[384,1024]{1,0:T(8,128)(2,1)} %get-tuple-element.412.refs_1_, bf16[2,384,1024]{2,1,0:T(8,128)(2,1)} %shard_map.309.refs_1_.refs_2_, ...), custom_call_target="tpu_custom_call" | custom-call | flops 2415919104 | bytes 21233664 | tf_op jit(solution)/shard_map/pallas_call | solution.py:91
  287.2 9.5 %shard_map.319 = (bf16[2,384,3072]{2,1,0:T(8,128)(2,1)}, bf16[2,384,1024]{2,1,0:T(8,128)(2,1)}, bf16[384,1024]{1,0:T(8,128)(2,1)}, f32[8,1024]{1,0:T(8,128)}, f32[8,512]{1,0:T(8,128)}) custom-call(s32[19]{0:T(128)} %copy-done.21, bf16[384,1024]{1,0:T(8,128)(2,1)} %get-tuple-element.413.refs_1_, ...), custom_call_target="tpu_custom_call", output_to_operand_aliasing={{0}: (9, {}), {1}: (10, {})} | custom-call | flops 2415919104 | bytes 12582912 | tf_op jit(solution)/shard_map/pallas_call | solution.py:131
  296.7 38.5 %collective-permute-done.18.refs_1_ = bf16[384,1024]{1,0:T(8,128)(2,1)S(1)} collective-permute-done((bf16[384,1024]{1,0:T(8,128)(2,1)S(1)}, bf16[384,1024]{1,0:T(8,128)(2,1)S(1)}, u32[]{:S(2)}, u32[]{:S(2)}) %collective-permute-start.18) | collective-permute-done | bytes 786464 | tf_op jit(solution)/shard_map/ppermute | solution.py:1584
  339.0 5.2 bitcast_convert_fusion.6.refs_16_.refs_5_
  344.2 4.6 bitcast_convert_fusion.7.refs_15_.refs_3_
  348.8 23.9 %shard_map.321 = (bf16[2,384,1024]{2,1,0:T(8,128)(2,1)}, bf16[2,384,4096]{2,1,0:T(8,128)(2,1)}, bf16[2,384,1024]{2,1,0:T(8,128)(2,1)}, bf16[384,1024]{1,0:T(8,12...) custom-call(s32[19]{0:T(128)} %copy-done.21, ...), custom_call_target="tpu_custom_call", output_to_operand_aliasing={{1}: (13, {}), {2}: (14, {})} | custom-call | flops 7247757312 | bytes 31457280 | tf_op jit(solution)/shard_map/pallas_call | solution.py:131
  372.7 5.7 bitcast_convert_fusion
  386.1 5.1 bitcast_convert_fusion.1.refs_1_
  396.8 15.6 %shard_map.323 = (bf16[384,1024]{1,0:T(8,128)(2,1)}, bf16[2,384,1024]{2,1,0:T(8,128)(2,1)}, bf16[2,384,1024]{2,1,0:T(8,128)(2,1)}) custom-call(s32[19]{0:T(128)} %copy-done.21, bf16[384,1024]{1,0:T(8,128)(2,1)} %get-tuple-element.420.refs_1_, bf16[2,384,1024]{2,1,0:T(8,128)(2,1)} %shard_map.309.refs_1_.refs_2_, ...), custom_call_target="tpu_custom_call" | custom-call | flops 2415919104 | bytes 21233664 | tf_op jit(solution)/shard_map/pallas_call | solution.py:91
  415.8 12.3 %collective-permute-done.24.refs_7_ = bf16[64,4096]{1,0:T(8,128)(2,1)S(1)} collective-permute-done((bf16[64,4096]{1,0:T(8,128)(2,1)}, bf16[64,4096]{1,0:T(8,128)(2,1)S(1)}, u32[]{:S(2)}, u32[]{:S(2)}) %collective-permute-start.24) | collective-permute-done | bytes 524320 | tf_op jit(solution)/shard_map/ppermute | solution.py:1200
  437.5 9.7 %shard_map.325 = (bf16[2,384,3072]{2,1,0:T(8,128)(2,1)}, bf16[2,384,1024]{2,1,0:T(8,128)(2,1)}, bf16[384,1024]{1,0:T(8,128)(2,1)}, f32[8,1024]{1,0:T(8,128)}, f32[8,512]{1,0:T(8,128)}) custom-call(s32[19]{0:T(128)} %copy-done.21, bf16[384,1024]{1,0:T(8,128)(2,1)} %get-tuple-element.425.refs_1_, ...), custom_call_target="tpu_custom_call", output_to_operand_aliasing={{0}: (9, {}), {1}: (10, {})} | custom-call | flops 2415919104 | bytes 12582912 | tf_op jit(solution)/shard_map/pallas_call | solution.py:131
  452.8 5.8 bitcast_convert_fusion.2
  467.5 7.9 %collective-permute-done.34.refs_7_ = bf16[64,4096]{1,0:T(8,128)(2,1)} collective-permute-done((bf16[64,4096]{1,0:T(8,128)(2,1)S(1)}, bf16[64,4096]{1,0:T(8,128)(2,1)}, u32[]{:S(2)}, u32[]{:S(2)}) %collective-permute-start.34) | collective-permute-done | bytes 524320 | tf_op jit(solution)/shard_map/ppermute | solution.py:1200
  507.3 15.1 %collective-permute-done.32.refs_7_ = bf16[64,2176]{1,0:T(8,128)(2,1)S(1)} collective-permute-done((bf16[64,2176]{1,0:T(8,128)(2,1)S(1)}, bf16[64,2176]{1,0:T(8,128)(2,1)S(1)}, u32[]{:S(2)}, u32[]{:S(2)}) %collective-permute-start.32) | collective-permute-done | bytes 278560 | tf_op jit(solution)/shard_map/ppermute | solution.py:1200
  532.3 14.8 %collective-permute-done.38.refs_7_ = bf16[64,2176]{1,0:T(8,128)(2,1)S(1)} collective-permute-done((bf16[64,2176]{1,0:T(8,128)(2,1)S(1)}, bf16[64,2176]{1,0:T(8,128)(2,1)S(1)}, u32[]{:S(2)}, u32[]{:S(2)}) %collective-permute-start.38) | collective-permute-done | bytes 278560 | tf_op jit(solution)/shard_map/ppermute | solution.py:1200
  556.2 13.8 %collective-permute-done.42.refs_7_ = bf16[64,2176]{1,0:T(8,128)(2,1)S(1)} collective-permute-done((bf16[64,2176]{1,0:T(8,128)(2,1)S(1)}, bf16[64,2176]{1,0:T(8,128)(2,1)S(1)}, u32[]{:S(2)}, u32[]{:S(2)}) %collective-permute-start.42) | collective-permute-done | bytes 278560 | tf_op jit(solution)/shard_map/ppermute | solution.py:1200
  578.9 12.7 %collective-permute-done.46.refs_7_ = bf16[64,2176]{1,0:T(8,128)(2,1)S(1)} collective-permute-done((bf16[64,2176]{1,0:T(8,128)(2,1)S(1)}, bf16[64,2176]{1,0:T(8,128)(2,1)S(1)}, u32[]{:S(2)}, u32[]{:S(2)}) %collective-permute-start.46) | collective-permute-done | bytes 278560 | tf_op jit(solution)/shard_map/ppermute | solution.py:1200
  601.1 11.7 %collective-permute-done.50.refs_7_ = bf16[64,2176]{1,0:T(8,128)(2,1)S(1)} collective-permute-done((bf16[64,2176]{1,0:T(8,128)(2,1)S(1)}, bf16[64,2176]{1,0:T(8,128)(2,1)S(1)}, u32[]{:S(2)}, u32[]{:S(2)}) %collective-permute-start.50) | collective-permute-done | bytes 278560 | tf_op jit(solution)/shard_map/ppermute | solution.py:1200
  621.4 10.6 %collective-permute-done.54.refs_7_ = bf16[64,2176]{1,0:T(8,128)(2,1)S(1)} collective-permute-done((bf16[64,2176]{1,0:T(8,128)(2,1)S(1)}, bf16[64,2176]{1,0:T(8,128)(2,1)S(1)}, u32[]{:S(2)}, u32[]{:S(2)}) %collective-permute-start.54) | collective-permute-done | bytes 278560 | tf_op jit(solution)/shard_map/ppermute | solution.py:1200
  640.7 9.6 %collective-permute-done.58.refs_7_ = bf16[64,2176]{1,0:T(8,128)(2,1)S(1)} collective-permute-done((bf16[64,2176]{1,0:T(8,128)(2,1)S(1)}, bf16[64,2176]{1,0:T(8,128)(2,1)S(1)}, u32[]{:S(2)}, u32[]{:S(2)}) %collective-permute-start.58) | collective-permute-done | bytes 278560 | tf_op jit(solution)/shard_map/ppermute | solution.py:1200
  659.0 11.3 %collective-permute-done.62.refs_3_ = bf16[64,2176]{1,0:T(8,128)(2,1)S(1)} collective-permute-done((bf16[64,2176]{1,0:T(8,128)(2,1)S(1)}, bf16[64,2176]{1,0:T(8,128)(2,1)S(1)}, u32[]{:S(2)}, u32[]{:S(2)}) %collective-permute-start.62) | collective-permute-done | bytes 278560 | tf_op jit(solution)/shard_map/ppermute | solution.py:1200
  698.1 5.0 collective-permute-done.74.refs_1_
  (329 shorter events, 287.2 us)
Async XLA Ops:
  8.8 27.6 %collective-permute-start.7 = (bf16[1024,2048]{1,0:T(8,128)(2,1)}, bf16[1024,2048]{1,0:T(8,128)(2,1)}, u32[]{:S(2)}, u32[]{:S(2)}) collective-permute-start(bf16[1024,2048]{1,0:T(8,128)(2,1)} %bitcast.80), channel_id=1, source_target_pairs={{0,8},{8,0},{1,9},{9,1},{2,10},{10,2},{3,11},{11,3},{4,12},{12,4},... | collective-permute-start | bytes 12582920 | tf_op jit(solution)/shard_map/ppermute | solution.py:1062
  17.4 19.1 %collective-permute-start.6 = (bf16[512,1024]{1,0:T(8,128)(2,1)}, bf16[512,1024]{1,0:T(8,128)(2,1)}, u32[]{:S(2)}, u32[]{:S(2)}) collective-permute-start(bf16[512,1024]{1,0:T(8,128)(2,1)} %bitcast.8.refs_4_.refs_8_.refs_7_), channel_id=1, source_target_pairs={{0,8},{8,0},{1,9},{9,1},{2,10},{10,2},{3,11},{11,3},{4,12},{12,4},... | collective-permute-start | bytes 3145736 | tf_op jit(solution)/shard_map/ppermute | solution.py:1062
  22.5 40.3 %collective-permute-start.3 = (bf16[384,512]{1,0:T(8,128)(2,1)S(1)}, bf16[384,512]{1,0:T(8,128)(2,1)S(1)}, u32[]{:S(2)}, u32[]{:S(2)}) collective-permute-start(bf16[384,512]{1,0:T(8,128)(2,1)S(1)} %bitcast.62), channel_id=1, source_target_pairs={{0,8},{8,0},{1,9},{9,1},{2,10},{10,2},{3,11},{11,3},{4,12},{12,4},... | collective-permute-start | bytes 1179656 | tf_op jit(solution)/shard_map/ppermute | solution.py:1062
  70.6 45.9 %collective-permute-start.10 = (bf16[384,1024]{1,0:T(8,128)(2,1)}, bf16[384,1024]{1,0:T(8,128)(2,1)}, u32[]{:S(2)}, u32[]{:S(2)}) collective-permute-start(bf16[384,1024]{1,0:T(8,128)(2,1)} %get-tuple-element.326.refs_9_), channel_id=1, source_target_pairs={{0,16},{1,17},{2,18},{3,19},{4,20},{5,21},{6,22},{7,23},{8,24},{9,... | collective-permute-start | bytes 2359304 | tf_op jit(solution)/shard_map/ppermute | solution.py:1576
  123.1 19.0 %collective-permute-start.9 = (bf16[384,1024]{1,0:T(8,128)(2,1)}, bf16[384,1024]{1,0:T(8,128)(2,1)S(1)}, u32[]{:S(2)}, u32[]{:S(2)}) collective-permute-start(bf16[384,1024]{1,0:T(8,128)(2,1)} %get-tuple-element.343.refs_8_), channel_id=1, source_target_pairs={{0,16},{1,17},{2,18},{3,19},{4,20},{5,21},{6,22},{7,23},{8,24},{9,... | collective-permute-start | bytes 2359304 | tf_op jit(solution)/shard_map/ppermute | solution.py:1578
  156.5 72.9 %collective-permute-start.15 = (bf16[384,1024]{1,0:T(8,128)(2,1)S(1)}, bf16[384,1024]{1,0:T(8,128)(2,1)S(1)}, u32[]{:S(2)}, u32[]{:S(2)}) collective-permute-start(bf16[384,1024]{1,0:T(8,128)(2,1)S(1)} %copy-done.40), channel_id=1, source_target_pairs={{16,0},{17,1},{18,2},{19,3},{20,4},{21,5},{22,6},{23,7},{24,8},{25... | collective-permute-start | bytes 2359304 | tf_op jit(solution)/shard_map/ppermute | solution.py:1581
  283.5 51.7 %collective-permute-start.18 = (bf16[384,1024]{1,0:T(8,128)(2,1)S(1)}, bf16[384,1024]{1,0:T(8,128)(2,1)S(1)}, u32[]{:S(2)}, u32[]{:S(2)}) collective-permute-start(bf16[384,1024]{1,0:T(8,128)(2,1)S(1)} %copy-done.41), channel_id=1, source_target_pairs={{16,0},{17,1},{18,2},{19,3},{20,4},{21,5},{22,6},{23,7},{24,8},{25... | collective-permute-start | bytes 2359304 | tf_op jit(solution)/shard_map/ppermute | solution.py:1584
  412.4 23.9 %collective-permute-start.23 = (bf16[2,384,1024]{2,1,0:T(8,128)(2,1)}, bf16[2,384,1024]{2,1,0:T(8,128)(2,1)S(1)}, u32[]{:S(2)}, u32[]{:S(2)}) collective-permute-start(bf16[2,384,1024]{2,1,0:T(8,128)(2,1)} %get-tuple-element.427), channel_id=1, source_target_pairs={{0,8},{8,0},{1,9},{9,1},{2,10},{10,2},{3,11},{11,3},{4,12},{12,4},... | collective-permute-start | bytes 4718600 | tf_op jit(solution)/shard_map/ppermute | solution.py:1062
  458.6 30.9 %collective-permute-start.29 = (bf16[1024,1536]{1,0:T(8,128)(2,1)}, bf16[1024,1536]{1,0:T(8,128)(2,1)}, u32[]{:S(2)}, u32[]{:S(2)}) collective-permute-start(bf16[1024,1536]{1,0:T(8,128)(2,1)} %bitcast_convert_fusion.2), channel_id=1, source_target_pairs={{0,8},{8,0},{1,9},{9,1},{2,10},{10,2},{3,11},{11,3},{4,12},{12,4},... | collective-permute-start | bytes 9437192 | tf_op jit(solution)/shard_map/ppermute | solution.py:1062
  460.9 28.6 %collective-permute-start.30 = (bf16[1024,512]{1,0:T(8,128)(2,1)}, bf16[1024,512]{1,0:T(8,128)(2,1)S(1)}, u32[]{:S(2)}, u32[]{:S(2)}) collective-permute-start(bf16[1024,512]{1,0:T(8,128)(2,1)} %pad_maximum_fusion.1), channel_id=1, source_target_pairs={{0,8},{8,0},{1,9},{9,1},{2,10},{10,2},{3,11},{11,3},{4,12},{12,4},... | collective-permute-start | bytes 3145736 | tf_op jit(solution)/shard_map/ppermute | solution.py:1062
  503.0 22.9 %collective-permute-start.40 = (bf16[64,4096]{1,0:T(8,128)(2,1)S(1)}, bf16[64,4096]{1,0:T(8,128)(2,1)S(1)}, u32[]{:S(2)}, u32[]{:S(2)}) collective-permute-start(bf16[64,4096]{1,0:T(8,128)(2,1)S(1)} %get-tuple-element.471), channel_id=1, source_target_pairs={{0,2},{2,4},{4,6},{6,7},{7,5},{5,3},{3,1},{1,0},{8,10},{10,12},{12... | collective-permute-start | bytes 1572872 | tf_op jit(solution)/shard_map/ppermute | solution.py:1200
  503.8 22.1 %collective-permute-start.41 = (bf16[64,4096]{1,0:T(8,128)(2,1)S(1)}, bf16[64,4096]{1,0:T(8,128)(2,1)S(1)}, u32[]{:S(2)}, u32[]{:S(2)}) collective-permute-start(bf16[64,4096]{1,0:T(8,128)(2,1)S(1)} %get-tuple-element.472), channel_id=1, source_target_pairs={{0,1},{2,0},{4,2},{6,4},{7,6},{5,7},{3,5},{1,3},{8,9},{10,8},{12,1... | collective-permute-start | bytes 1572872 | tf_op jit(solution)/shard_map/ppermute | solution.py:1200
  505.1 17.3 %collective-permute-start.32 = (bf16[64,2176]{1,0:T(8,128)(2,1)S(1)}, bf16[64,2176]{1,0:T(8,128)(2,1)S(1)}, u32[]{:S(2)}, u32[]{:S(2)}) collective-permute-start(bf16[64,2176]{1,0:T(8,128)(2,1)S(1)} %copy-done.50), channel_id=1, source_target_pairs={{0,2},{2,4},{4,6},{6,7},{7,5},{5,3},{3,1},{1,0},{8,10},{10,12},{12... | collective-permute-start | bytes 835592 | tf_op jit(solution)/shard_map/ppermute | solution.py:1200
  505.9 17.7 %collective-permute-start.33 = (bf16[64,2176]{1,0:T(8,128)(2,1)S(1)}, bf16[64,2176]{1,0:T(8,128)(2,1)S(1)}, u32[]{:S(2)}, u32[]{:S(2)}) collective-permute-start(bf16[64,2176]{1,0:T(8,128)(2,1)S(1)} %copy-done.49), channel_id=1, source_target_pairs={{0,1},{2,0},{4,2},{6,4},{7,6},{5,7},{3,5},{1,3},{8,9},{10,8},{12,1... | collective-permute-start | bytes 835592 | tf_op jit(solution)/shard_map/ppermute | solution.py:1200
  528.2 21.6 %collective-permute-start.44 = (bf16[64,4096]{1,0:T(8,128)(2,1)S(1)}, bf16[64,4096]{1,0:T(8,128)(2,1)S(1)}, u32[]{:S(2)}, u32[]{:S(2)}) collective-permute-start(bf16[64,4096]{1,0:T(8,128)(2,1)S(1)} %get-tuple-element.479), channel_id=1, source_target_pairs={{0,2},{2,4},{4,6},{6,7},{7,5},{5,3},{3,1},{1,0},{8,10},{10,12},{12... | collective-permute-start | bytes 1572872 | tf_op jit(solution)/shard_map/ppermute | solution.py:1200
  529.1 20.8 %collective-permute-start.45 = (bf16[64,4096]{1,0:T(8,128)(2,1)S(1)}, bf16[64,4096]{1,0:T(8,128)(2,1)S(1)}, u32[]{:S(2)}, u32[]{:S(2)}) collective-permute-start(bf16[64,4096]{1,0:T(8,128)(2,1)S(1)} %get-tuple-element.480), channel_id=1, source_target_pairs={{0,1},{2,0},{4,2},{6,4},{7,6},{5,7},{3,5},{1,3},{8,9},{10,8},{12,1... | collective-permute-start | bytes 1572872 | tf_op jit(solution)/shard_map/ppermute | solution.py:1200
  530.3 16.8 %collective-permute-start.38 = (bf16[64,2176]{1,0:T(8,128)(2,1)S(1)}, bf16[64,2176]{1,0:T(8,128)(2,1)S(1)}, u32[]{:S(2)}, u32[]{:S(2)}) collective-permute-start(bf16[64,2176]{1,0:T(8,128)(2,1)S(1)} %get-tuple-element.475), channel_id=1, source_target_pairs={{0,2},{2,4},{4,6},{6,7},{7,5},{5,3},{3,1},{1,0},{8,10},{10,12},{12... | collective-permute-start | bytes 835592 | tf_op jit(solution)/shard_map/ppermute | solution.py:1200
  531.1 16.7 %collective-permute-start.39 = (bf16[64,2176]{1,0:T(8,128)(2,1)S(1)}, bf16[64,2176]{1,0:T(8,128)(2,1)S(1)}, u32[]{:S(2)}, u32[]{:S(2)}) collective-permute-start(bf16[64,2176]{1,0:T(8,128)(2,1)S(1)} %get-tuple-element.476), channel_id=1, source_target_pairs={{0,1},{2,0},{4,2},{6,4},{7,6},{5,7},{3,5},{1,3},{8,9},{10,8},{12,1... | collective-permute-start | bytes 835592 | tf_op jit(solution)/shard_map/ppermute | solution.py:1200
  552.1 20.4 %collective-permute-start.48 = (bf16[64,4096]{1,0:T(8,128)(2,1)S(1)}, bf16[64,4096]{1,0:T(8,128)(2,1)S(1)}, u32[]{:S(2)}, u32[]{:S(2)}) collective-permute-start(bf16[64,4096]{1,0:T(8,128)(2,1)S(1)} %get-tuple-element.487), channel_id=1, source_target_pairs={{0,2},{2,4},{4,6},{6,7},{7,5},{5,3},{3,1},{1,0},{8,10},{10,12},{12... | collective-permute-start | bytes 1572872 | tf_op jit(solution)/shard_map/ppermute | solution.py:1200
  552.8 19.8 %collective-permute-start.49 = (bf16[64,4096]{1,0:T(8,128)(2,1)S(1)}, bf16[64,4096]{1,0:T(8,128)(2,1)S(1)}, u32[]{:S(2)}, u32[]{:S(2)}) collective-permute-start(bf16[64,4096]{1,0:T(8,128)(2,1)S(1)} %get-tuple-element.488), channel_id=1, source_target_pairs={{0,1},{2,0},{4,2},{6,4},{7,6},{5,7},{3,5},{1,3},{8,9},{10,8},{12,1... | collective-permute-start | bytes 1572872 | tf_op jit(solution)/shard_map/ppermute | solution.py:1200
  554.2 15.8 %collective-permute-start.42 = (bf16[64,2176]{1,0:T(8,128)(2,1)S(1)}, bf16[64,2176]{1,0:T(8,128)(2,1)S(1)}, u32[]{:S(2)}, u32[]{:S(2)}) collective-permute-start(bf16[64,2176]{1,0:T(8,128)(2,1)S(1)} %get-tuple-element.483), channel_id=1, source_target_pairs={{0,2},{2,4},{4,6},{6,7},{7,5},{5,3},{3,1},{1,0},{8,10},{10,12},{12... | collective-permute-start | bytes 835592 | tf_op jit(solution)/shard_map/ppermute | solution.py:1200
  574.8 19.3 %collective-permute-start.52 = (bf16[64,4096]{1,0:T(8,128)(2,1)S(1)}, bf16[64,4096]{1,0:T(8,128)(2,1)S(1)}, u32[]{:S(2)}, u32[]{:S(2)}) collective-permute-start(bf16[64,4096]{1,0:T(8,128)(2,1)S(1)} %get-tuple-element.495.refs_1_), channel_id=1, source_target_pairs={{0,2},{2,4},{4,6},{6,7},{7,5},{5,3},{3,1},{1,0},{8,10},{10,12},{12... | collective-permute-start | bytes 1572872 | tf_op jit(solution)/shard_map/ppermute | solution.py:1200
  575.4 18.7 %collective-permute-start.53 = (bf16[64,4096]{1,0:T(8,128)(2,1)S(1)}, bf16[64,4096]{1,0:T(8,128)(2,1)S(1)}, u32[]{:S(2)}, u32[]{:S(2)}) collective-permute-start(bf16[64,4096]{1,0:T(8,128)(2,1)S(1)} %get-tuple-element.496.refs_2_), channel_id=1, source_target_pairs={{0,1},{2,0},{4,2},{6,4},{7,6},{5,7},{3,5},{1,3},{8,9},{10,8},{12,1... | collective-permute-start | bytes 1572872 | tf_op jit(solution)/shard_map/ppermute | solution.py:1200
  597.0 18.2 %collective-permute-start.56 = (bf16[64,4096]{1,0:T(8,128)(2,1)S(1)}, bf16[64,4096]{1,0:T(8,128)(2,1)S(1)}, u32[]{:S(2)}, u32[]{:S(2)}) collective-permute-start(bf16[64,4096]{1,0:T(8,128)(2,1)S(1)} %get-tuple-element.503), channel_id=1, source_target_pairs={{0,2},{2,4},{4,6},{6,7},{7,5},{5,3},{3,1},{1,0},{8,10},{10,12},{12... | collective-permute-start | bytes 1572872 | tf_op jit(solution)/shard_map/ppermute | solution.py:1200
  597.6 17.6 %collective-permute-start.57 = (bf16[64,4096]{1,0:T(8,128)(2,1)S(1)}, bf16[64,4096]{1,0:T(8,128)(2,1)S(1)}, u32[]{:S(2)}, u32[]{:S(2)}) collective-permute-start(bf16[64,4096]{1,0:T(8,128)(2,1)S(1)} %get-tuple-element.504), channel_id=1, source_target_pairs={{0,1},{2,0},{4,2},{6,4},{7,6},{5,7},{3,5},{1,3},{8,9},{10,8},{12,1... | collective-permute-start | bytes 1572872 | tf_op jit(solution)/shard_map/ppermute | solution.py:1200
  617.3 17.2 %collective-permute-start.60 = (bf16[64,4096]{1,0:T(8,128)(2,1)S(1)}, bf16[64,4096]{1,0:T(8,128)(2,1)S(1)}, u32[]{:S(2)}, u32[]{:S(2)}) collective-permute-start(bf16[64,4096]{1,0:T(8,128)(2,1)S(1)} %get-tuple-element.513), channel_id=1, source_target_pairs={{0,2},{2,4},{4,6},{6,7},{7,5},{5,3},{3,1},{1,0},{8,10},{10,12},{12... | collective-permute-start | bytes 1572872 | tf_op jit(solution)/shard_map/ppermute | solution.py:1200
  618.0 16.6 %collective-permute-start.61 = (bf16[64,4096]{1,0:T(8,128)(2,1)S(1)}, bf16[64,4096]{1,0:T(8,128)(2,1)S(1)}, u32[]{:S(2)}, u32[]{:S(2)}) collective-permute-start(bf16[64,4096]{1,0:T(8,128)(2,1)S(1)} %get-tuple-element.514), channel_id=1, source_target_pairs={{0,1},{2,0},{4,2},{6,4},{7,6},{5,7},{3,5},{1,3},{8,9},{10,8},{12,1... | collective-permute-start | bytes 1572872 | tf_op jit(solution)/shard_map/ppermute | solution.py:1200
  636.6 16.2 %collective-permute-start.64 = (bf16[64,4096]{1,0:T(8,128)(2,1)S(1)}, bf16[64,4096]{1,0:T(8,128)(2,1)S(1)}, u32[]{:S(2)}, u32[]{:S(2)}) collective-permute-start(bf16[64,4096]{1,0:T(8,128)(2,1)S(1)} %get-tuple-element.523), channel_id=1, source_target_pairs={{0,2},{2,4},{4,6},{6,7},{7,5},{5,3},{3,1},{1,0},{8,10},{10,12},{12... | collective-permute-start | bytes 1572872 | tf_op jit(solution)/shard_map/ppermute | solution.py:1200
  654.9 20.4 %collective-permute-start.68 = (bf16[64,4096]{1,0:T(8,128)(2,1)S(1)}, bf16[64,4096]{1,0:T(8,128)(2,1)S(1)}, u32[]{:S(2)}, u32[]{:S(2)}) collective-permute-start(bf16[64,4096]{1,0:T(8,128)(2,1)S(1)} %get-tuple-element.533), channel_id=1, source_target_pairs={{0,2},{2,4},{4,6},{6,7},{7,5},{5,3},{3,1},{1,0},{8,10},{10,12},{12... | collective-permute-start | bytes 1572872 | tf_op jit(solution)/shard_map/ppermute | solution.py:1200
  655.5 19.8 %collective-permute-start.69 = (bf16[64,4096]{1,0:T(8,128)(2,1)S(1)}, bf16[64,4096]{1,0:T(8,128)(2,1)S(1)}, u32[]{:S(2)}, u32[]{:S(2)}) collective-permute-start(bf16[64,4096]{1,0:T(8,128)(2,1)S(1)} %get-tuple-element.534), channel_id=1, source_target_pairs={{0,1},{2,0},{4,2},{6,4},{7,6},{5,7},{3,5},{1,3},{8,9},{10,8},{12,1... | collective-permute-start | bytes 1572872 | tf_op jit(solution)/shard_map/ppermute | solution.py:1200
  708.0 21.7 %collective-permute-start.16 = (bf16[2,384,512]{2,1,0:T(8,128)(2,1)S(1)}, bf16[2,384,512]{2,1,0:T(8,128)(2,1)S(1)}, u32[]{:S(2)}, u32[]{:S(2)}) collective-permute-start(bf16[2,384,512]{2,1,0:T(8,128)(2,1)S(1)} %shard_map.312), channel_id=1, source_target_pairs={{0,8},{8,0},{1,9},{9,1},{2,10},{10,2},{3,11},{11,3},{4,12},{12,4},... | collective-permute-start | bytes 2359304 | tf_op jit(solution)/shard_map/ppermute | solution.py:1062
  718.2 16.6 %collective-permute-start.82 = (bf16[64,4096]{1,0:T(8,128)(2,1)S(1)}, bf16[64,4096]{1,0:T(8,128)(2,1)S(1)}, u32[]{:S(2)}, u32[]{:S(2)}) collective-permute-start(bf16[64,4096]{1,0:T(8,128)(2,1)S(1)} %get-tuple-element.556), channel_id=1, source_target_pairs={{0,2},{2,4},{4,6},{6,7},{7,5},{5,3},{3,1},{1,0},{8,10},{10,12},{12... | collective-permute-start | bytes 1572872 | tf_op jit(solution)/shard_map/ppermute | solution.py:1200
  (105 other events, 853.1 us)

commit v7 on v5

--- a/solution.py
+++ b/solution.py
@@ -979,7 +979,6 @@
         self.totals = [None] * len(shapes)
         self.vmem = RING_MIB
         self.moving = self.add([0, 0], None)
-        self.vmem = 16
 
     def unit(self, way, ahead):
         return UNITS + way * self.count + ahead % self.count
@@ -1405,10 +1404,13 @@
 
     kept = {}
 
-    def forward(owner, number, source, tokens, after=(), late=()):
+    def enter(owner, number, source, tokens, after=()):
         kept["x"], kept["normed1"], kv_here = norm_kv(
             info, owner, number, source, tokens, vec, wq_own, wq_oth, bias_v, kept, after
         )
+        return kv_here
+
+    def forward(owner, number, kv_here, late=()):
         kv_there = swap(kv_here)
         kept["q"] = project_q(info, owner, number, kept["normed1"], wq_own, wq_oth, bias_q, kept)
         kept["grown"], kept["mixed_full"], mixed, kept["inverse"], kept["kv"] = attend(
@@ -1467,14 +1469,16 @@
         flows = backward_attention(owner, number, grad_mixed)
         return backward_qkv(owner, number, *flows, grad_res, small, shift)
 
-    relayed = forward(0, 0, "argument", (inputs, first_oth))
+    kv_here = enter(0, 0, "argument", (inputs, first_oth))
+    kv_next = enter(0, 1, "argument", (inputs, second_oth), [kv_here])
+    relayed = forward(0, 0, kv_here, [kv_next])
     first = lax.ppermute(relayed, "section", [(0, 1)])
-    relayed = forward(0, 1, "argument", (inputs, second_oth), [relayed])
+    relayed = forward(0, 1, kv_next, [relayed])
     second = lax.ppermute(relayed, "section", [(0, 1)])
-    relayed = forward(1, 0, "relay", (first,), [relayed])
+    relayed = forward(1, 0, enter(1, 0, "relay", (first,), [relayed]))
     relayed = backward(1, 0, "argument", (cotangent, cot_oth[0]), [relayed, second])
     first = lax.ppermute(relayed, "section", [(1, 0)])
-    relayed = forward(1, 1, "relay", (second,), [relayed], [first])
+    relayed = forward(1, 1, enter(1, 1, "relay", (second,), [relayed]), [first])
     relayed = backward(1, 1, "argument", (cotangent, cot_oth[1]), [relayed])
     second = lax.ppermute(relayed, "section", [(1, 0)])
     relayed = backward(0, 0, "relay", (first,), [relayed])
@@ -1535,6 +1539,8 @@
         TailPlaces(half, LANES),
     )
     rings = [ring_mlp, ring_tail]
+    for ring in rings:
+        ring.vmem = 16
     before_it = ring_tail
     while not all(ring.done() for ring in rings):
         for ring in rings:

time: 736 us -> 751 us (1.020)
  waiting for transfers between devices: 272 us -> 293 us
  local copies, waits for them, and re-layouts: 33.1 us -> 22.5 us
    ppermute x24, waiting for transfers between devices: 19.6 us -> 33.9 us  [swap(): return lax.ppermute(block, 'tensor', [(0, 1), (1, 0)])]
    unnamed x124 -> x110, local copies, waits for them, and re-layouts: 31.5 us -> 20.9 us
  transfers between devices with their start and end apart: 84 -> 84, of which waited for: 50 -> 50; matrix products, arithmetic and copies ran while one was open for 3% -> 3% of each run, Pallas kernels for 22% -> 23%
where the time goes in v7:
time: 751 us; the launch traced here: 743 us
  Pallas kernels  312 us (42%)
  waiting for transfers between devices  293 us (39%)
  starting transfers between devices  68.2 us (9%)
  matrix products  42.5 us (6%)
  local copies, waits for them, and re-layouts  22.5 us (3%)
    pallas_call x58, Pallas kernels, manual(): pl.pallas_call(body, out_shape=[jax.ShapeDtypeStruct(s, d) for s, d, _, _...  233 us
    ppermute x56, waiting for transfers between devices, advance(): lax.ppermute(self.moving[w], 'dp', self.routes[w])  164 us
    pallas_call x8, Pallas kernels, call(): pl.pallas_call(body, out_shape=[jax.ShapeDtypeStruct(s, d) for s, d, _, _...  72 us
    ppermute x56, starting transfers between devices, advance(): lax.ppermute(self.moving[w], 'dp', self.routes[w])  58 us
    ppermute x1, waiting for transfers between devices, shards(): first = lax.ppermute(relayed, 'section', [(1, 0)])  52.9 us
    dot_general x12, matrix products, weight_grad(): lax.dot_general(left, right, (((0, 1), (0, 1)), ((), ())), preferred_elem...  42.5 us
    ppermute x24, waiting for transfers between devices, swap(): return lax.ppermute(block, 'tensor', [(0, 1), (1, 0)])  33.9 us
    ppermute x1, waiting for transfers between devices, shards(): second = lax.ppermute(relayed, 'section', [(1, 0)])  31.2 us
  transfers between devices with their start and end apart: 84, of which 50 were waited for; matrix products, arithmetic and copies ran while one was open for 3% of the time, Pallas kernels for 23%

profile of v7, /device:TPU:0, one launch (start us, length us, event | category | flops | bytes accessed | tf_op | source)
XLA Modules:
  0.0 742.6 jit_solution(5257610368381079507)
XLA Ops:
  9.5 13.6 %collective-permute-done.4.refs_5_.refs_3_.refs_4_ = bf16[3,1024,512]{2,1,0:T(8,128)(2,1)S(1)} collective-permute-done((bf16[3,1024,512]{2,1,0:T(8,128)(2,1)}, bf16[3,1024,512]{2,1,0:T(8,128)(2,1)S(1)}, u32[]{:S(2)}, u32[]{:S(2)}) %collective-permute-start.4) | collective-permute-done | bytes 3145760 | tf_op jit(solution)/shard_map/ppermute | solution.py:956
  24.7 6.8 shard_map.292
  36.9 6.5 shard_map.293
  47.8 12.2 %shard_map.296 = (bf16[3,16,384,768]{3,2,1,0:T(8,128)(2,1)}, f32[3,384,1024]{2,1,0:T(8,128)}, bf16[384,1024]{1,0:T(8,128)(2,1)}, f32[3,384,1024]{2,1,0:T(8,128)}, bf16[3,2,768,1024]{3,2,1,0:T(8,128)(2,1)}) custom-call(s32[19]{0:T(128)} %copy-done.21, bf16[2,384,1024]{2,1,0:T(8,128)(2,1)} %shard_map.294.refs_5_.refs_1_, ...), custom_call_target="tpu_custom_call" | custom-call | flops 1207959552 | bytes 21233664 | tf_op jit(solution)/shard_map/pallas_call | solution.py:83
  61.1 21.9 %shard_map.298 = (bf16[2,384,1024]{2,1,0:T(8,128)(2,1)}, f32[2,384,1024]{2,1,0:T(8,128)}, bf16[2,384,1024]{2,1,0:T(8,128)(2,1)}, bf16[2,384,4096]{2,1,0:T(8,128)...) custom-call(s32[19]{0:T(128)} %copy-done.21, ...), custom_call_target="tpu_custom_call" | custom-call | flops 7247757312 | bytes 31457280 | tf_op jit(solution)/shard_map/pallas_call | solution.py:123
  89.0 12.3 %shard_map.297 = (bf16[3,16,384,768]{3,2,1,0:T(8,128)(2,1)}, f32[3,384,1024]{2,1,0:T(8,128)}, bf16[384,1024]{1,0:T(8,128)(2,1)}, f32[3,384,1024]{2,1,0:T(8,128)}, bf16[3,2,768,1024]{3,2,1,0:T(8,128)(2,1)}) custom-call(s32[19]{0:T(128)} %copy-done.21, ...), custom_call_target="tpu_custom_call", output_to_operand_aliasing={{0}: (4, {}), {1}: (5, {}), {3}: (6, {}), {4}: (7, {})} | custom-call | flops 1207959552 | bytes 21233664 | tf_op jit(solution)/shard_map/pallas_call | solution.py:83
  101.2 21.0 %shard_map.299 = (bf16[2,384,1024]{2,1,0:T(8,128)(2,1)}, f32[2,384,1024]{2,1,0:T(8,128)}, bf16[2,384,1024]{2,1,0:T(8,128)(2,1)}, bf16[2,384,4096]{2,1,0:T(8,128)...) custom-call(s32[19]{0:T(128)} %copy-done.21, ...), custom_call_target="tpu_custom_call", output_to_operand_aliasing={{0}: (11, {}), {1}: (12, {}), {2}: (13, {}), {3}: (14, {}),... | custom-call | flops 7247757312 | bytes 31457280 | tf_op jit(solution)/shard_map/pallas_call | solution.py:123
  137.2 11.9 %collective-permute-done.9.refs_15_.refs_1_ = bf16[384,1024]{1,0:T(8,128)(2,1)S(1)} collective-permute-done((bf16[384,1024]{1,0:T(8,128)(2,1)}, bf16[384,1024]{1,0:T(8,128)(2,1)S(1)}, u32[]{:S(2)}, u32[]{:S(2)}) %collective-permute-start.9) | collective-permute-done | bytes 786464 | tf_op jit(solution)/shard_map/ppermute | solution.py:1477
  150.0 10.3 %shard_map.305 = (bf16[2,384,1024]{2,1,0:T(8,128)(2,1)}, bf16[2,384,4096]{2,1,0:T(8,128)(2,1)}, bf16[2,384,1024]{2,1,0:T(8,128)(2,1)}, bf16[384,1024]{1,0:T(8,12...) custom-call(s32[19]{0:T(128)} %copy-done.21, bf16[2,1,768,512]{3,2,1,0:T(8,128)(2,1)} %refs_1_.13, ...), custom_call_target="tpu_custom_call" | custom-call | flops 7247757312 | bytes 31457280 | tf_op jit(solution)/shard_map/pallas_call | solution.py:123
  179.5 52.9 %collective-permute-done.15.refs_19_.refs_1_ = bf16[384,1024]{1,0:T(8,128)(2,1)S(1)} collective-permute-done((bf16[384,1024]{1,0:T(8,128)(2,1)S(1)}, bf16[384,1024]{1,0:T(8,128)(2,1)S(1)}, u32[]{:S(2)}, u32[]{:S(2)}) %collective-permute-start.15) | collective-permute-done | bytes 786464 | tf_op jit(solution)/shard_map/ppermute | solution.py:1480
  234.7 12.6 %shard_map.314 = (bf16[2,384,1024]{2,1,0:T(8,128)(2,1)}, bf16[2,384,4096]{2,1,0:T(8,128)(2,1)}, bf16[2,384,1024]{2,1,0:T(8,128)(2,1)}, bf16[384,1024]{1,0:T(8,12...) custom-call(s32[19]{0:T(128)} %copy-done.21, ...), custom_call_target="tpu_custom_call", output_to_operand_aliasing={{0}: (14, {}), {1}: (15, {}), {2}: (16, {})} | custom-call | flops 7247757312 | bytes 31457280 | tf_op jit(solution)/shard_map/pallas_call | solution.py:123
  257.7 17.8 %shard_map.317 = (bf16[2,384,1024]{2,1,0:T(8,128)(2,1)}, bf16[2,384,4096]{2,1,0:T(8,128)(2,1)}, bf16[2,384,1024]{2,1,0:T(8,128)(2,1)}, bf16[384,1024]{1,0:T(8,12...) custom-call(s32[19]{0:T(128)} %copy-done.21, ...), custom_call_target="tpu_custom_call", output_to_operand_aliasing={{0}: (13, {}), {1}: (14, {}), {2}: (15, {})} | custom-call | flops 7247757312 | bytes 31457280 | tf_op jit(solution)/shard_map/pallas_call | solution.py:123
  275.5 15.8 %shard_map.318 = (bf16[384,1024]{1,0:T(8,128)(2,1)}, bf16[2,384,1024]{2,1,0:T(8,128)(2,1)}, bf16[2,384,1024]{2,1,0:T(8,128)(2,1)}) custom-call(s32[19]{0:T(128)} %copy-done.21, bf16[384,1024]{1,0:T(8,128)(2,1)} %get-tuple-element.412.refs_1_, bf16[2,384,1024]{2,1,0:T(8,128)(2,1)} %shard_map.309.refs_1_.refs_2_, ...), custom_call_target="tpu_custom_call" | custom-call | flops 2415919104 | bytes 21233664 | tf_op jit(solution)/shard_map/pallas_call | solution.py:83
  295.1 9.3 %shard_map.319 = (bf16[2,384,3072]{2,1,0:T(8,128)(2,1)}, bf16[2,384,1024]{2,1,0:T(8,128)(2,1)}, bf16[384,1024]{1,0:T(8,128)(2,1)}, f32[8,1024]{1,0:T(8,128)}, f32[8,512]{1,0:T(8,128)}) custom-call(s32[19]{0:T(128)} %copy-done.21, bf16[384,1024]{1,0:T(8,128)(2,1)} %get-tuple-element.413.refs_1_, ...), custom_call_target="tpu_custom_call", output_to_operand_aliasing={{0}: (9, {}), {1}: (10, {})} | custom-call | flops 2415919104 | bytes 12582912 | tf_op jit(solution)/shard_map/pallas_call | solution.py:123
  304.4 31.2 %collective-permute-done.18.refs_1_ = bf16[384,1024]{1,0:T(8,128)(2,1)S(1)} collective-permute-done((bf16[384,1024]{1,0:T(8,128)(2,1)S(1)}, bf16[384,1024]{1,0:T(8,128)(2,1)S(1)}, u32[]{:S(2)}, u32[]{:S(2)}) %collective-permute-start.18) | collective-permute-done | bytes 786464 | tf_op jit(solution)/shard_map/ppermute | solution.py:1483
  339.4 5.2 bitcast_convert_fusion.6.refs_16_.refs_5_
  349.2 18.4 %shard_map.321 = (bf16[2,384,1024]{2,1,0:T(8,128)(2,1)}, bf16[2,384,4096]{2,1,0:T(8,128)(2,1)}, bf16[2,384,1024]{2,1,0:T(8,128)(2,1)}, bf16[384,1024]{1,0:T(8,12...) custom-call(s32[19]{0:T(128)} %copy-done.21, ...), custom_call_target="tpu_custom_call", output_to_operand_aliasing={{1}: (13, {}), {2}: (14, {})} | custom-call | flops 7247757312 | bytes 31457280 | tf_op jit(solution)/shard_map/pallas_call | solution.py:123
  367.7 5.7 bitcast_convert_fusion
  381.0 5.1 bitcast_convert_fusion.1.refs_1_
  391.8 15.6 %shard_map.323 = (bf16[384,1024]{1,0:T(8,128)(2,1)}, bf16[2,384,1024]{2,1,0:T(8,128)(2,1)}, bf16[2,384,1024]{2,1,0:T(8,128)(2,1)}) custom-call(s32[19]{0:T(128)} %copy-done.21, bf16[384,1024]{1,0:T(8,128)(2,1)} %get-tuple-element.420.refs_1_, bf16[2,384,1024]{2,1,0:T(8,128)(2,1)} %shard_map.309.refs_1_.refs_2_, ...), custom_call_target="tpu_custom_call" | custom-call | flops 2415919104 | bytes 21233664 | tf_op jit(solution)/shard_map/pallas_call | solution.py:83
  410.7 12.4 %collective-permute-done.24.refs_7_ = bf16[64,4096]{1,0:T(8,128)(2,1)S(1)} collective-permute-done((bf16[64,4096]{1,0:T(8,128)(2,1)}, bf16[64,4096]{1,0:T(8,128)(2,1)S(1)}, u32[]{:S(2)}, u32[]{:S(2)}) %collective-permute-start.24) | collective-permute-done | bytes 524320 | tf_op jit(solution)/shard_map/ppermute | solution.py:1094
  432.5 9.5 %shard_map.325 = (bf16[2,384,3072]{2,1,0:T(8,128)(2,1)}, bf16[2,384,1024]{2,1,0:T(8,128)(2,1)}, bf16[384,1024]{1,0:T(8,128)(2,1)}, f32[8,1024]{1,0:T(8,128)}, f32[8,512]{1,0:T(8,128)}) custom-call(s32[19]{0:T(128)} %copy-done.21, bf16[384,1024]{1,0:T(8,128)(2,1)} %get-tuple-element.425.refs_1_, ...), custom_call_target="tpu_custom_call", output_to_operand_aliasing={{0}: (9, {}), {1}: (10, {})} | custom-call | flops 2415919104 | bytes 12582912 | tf_op jit(solution)/shard_map/pallas_call | solution.py:123
  447.7 5.8 bitcast_convert_fusion.2
  462.4 7.9 %collective-permute-done.34.refs_7_ = bf16[64,4096]{1,0:T(8,128)(2,1)} collective-permute-done((bf16[64,4096]{1,0:T(8,128)(2,1)S(1)}, bf16[64,4096]{1,0:T(8,128)(2,1)}, u32[]{:S(2)}, u32[]{:S(2)}) %collective-permute-start.34) | collective-permute-done | bytes 524320 | tf_op jit(solution)/shard_map/ppermute | solution.py:1094
  502.3 15.0 %collective-permute-done.32.refs_7_ = bf16[64,2176]{1,0:T(8,128)(2,1)S(1)} collective-permute-done((bf16[64,2176]{1,0:T(8,128)(2,1)S(1)}, bf16[64,2176]{1,0:T(8,128)(2,1)S(1)}, u32[]{:S(2)}, u32[]{:S(2)}) %collective-permute-start.32) | collective-permute-done | bytes 278560 | tf_op jit(solution)/shard_map/ppermute | solution.py:1094
  527.3 14.8 %collective-permute-done.38.refs_7_ = bf16[64,2176]{1,0:T(8,128)(2,1)S(1)} collective-permute-done((bf16[64,2176]{1,0:T(8,128)(2,1)S(1)}, bf16[64,2176]{1,0:T(8,128)(2,1)S(1)}, u32[]{:S(2)}, u32[]{:S(2)}) %collective-permute-start.38) | collective-permute-done | bytes 278560 | tf_op jit(solution)/shard_map/ppermute | solution.py:1094
  551.1 13.8 %collective-permute-done.42.refs_7_ = bf16[64,2176]{1,0:T(8,128)(2,1)S(1)} collective-permute-done((bf16[64,2176]{1,0:T(8,128)(2,1)S(1)}, bf16[64,2176]{1,0:T(8,128)(2,1)S(1)}, u32[]{:S(2)}, u32[]{:S(2)}) %collective-permute-start.42) | collective-permute-done | bytes 278560 | tf_op jit(solution)/shard_map/ppermute | solution.py:1094
  573.8 12.7 %collective-permute-done.46.refs_7_ = bf16[64,2176]{1,0:T(8,128)(2,1)S(1)} collective-permute-done((bf16[64,2176]{1,0:T(8,128)(2,1)S(1)}, bf16[64,2176]{1,0:T(8,128)(2,1)S(1)}, u32[]{:S(2)}, u32[]{:S(2)}) %collective-permute-start.46) | collective-permute-done | bytes 278560 | tf_op jit(solution)/shard_map/ppermute | solution.py:1094
  595.9 11.6 %collective-permute-done.50.refs_7_ = bf16[64,2176]{1,0:T(8,128)(2,1)S(1)} collective-permute-done((bf16[64,2176]{1,0:T(8,128)(2,1)S(1)}, bf16[64,2176]{1,0:T(8,128)(2,1)S(1)}, u32[]{:S(2)}, u32[]{:S(2)}) %collective-permute-start.50) | collective-permute-done | bytes 278560 | tf_op jit(solution)/shard_map/ppermute | solution.py:1094
  616.1 10.5 %collective-permute-done.54.refs_7_ = bf16[64,2176]{1,0:T(8,128)(2,1)S(1)} collective-permute-done((bf16[64,2176]{1,0:T(8,128)(2,1)S(1)}, bf16[64,2176]{1,0:T(8,128)(2,1)S(1)}, u32[]{:S(2)}, u32[]{:S(2)}) %collective-permute-start.54) | collective-permute-done | bytes 278560 | tf_op jit(solution)/shard_map/ppermute | solution.py:1094
  635.2 9.8 %collective-permute-done.58.refs_7_ = bf16[64,2176]{1,0:T(8,128)(2,1)S(1)} collective-permute-done((bf16[64,2176]{1,0:T(8,128)(2,1)S(1)}, bf16[64,2176]{1,0:T(8,128)(2,1)S(1)}, u32[]{:S(2)}, u32[]{:S(2)}) %collective-permute-start.58) | collective-permute-done | bytes 278560 | tf_op jit(solution)/shard_map/ppermute | solution.py:1094
  653.5 11.3 %collective-permute-done.62.refs_3_ = bf16[64,2176]{1,0:T(8,128)(2,1)S(1)} collective-permute-done((bf16[64,2176]{1,0:T(8,128)(2,1)S(1)}, bf16[64,2176]{1,0:T(8,128)(2,1)S(1)}, u32[]{:S(2)}, u32[]{:S(2)}) %collective-permute-start.62) | collective-permute-done | bytes 278560 | tf_op jit(solution)/shard_map/ppermute | solution.py:1094
  (333 shorter events, 299.2 us)
Async XLA Ops:
  6.9 24.9 %collective-permute-start.2 = (bf16[2048,1024]{1,0:T(8,128)(2,1)}, bf16[2048,1024]{1,0:T(8,128)(2,1)}, u32[]{:S(2)}, u32[]{:S(2)}) collective-permute-start(bf16[2048,1024]{1,0:T(8,128)(2,1)} %bitcast.89), channel_id=1, source_target_pairs={{0,8},{8,0},{1,9},{9,1},{2,10},{10,2},{3,11},{11,3},{4,12},{12,4},... | collective-permute-start | bytes 12582920 | tf_op jit(solution)/shard_map/ppermute | solution.py:956
  7.7 52.4 %collective-permute-start.8 = (bf16[1024,2048]{1,0:T(8,128)(2,1)}, bf16[1024,2048]{1,0:T(8,128)(2,1)}, u32[]{:S(2)}, u32[]{:S(2)}) collective-permute-start(bf16[1024,2048]{1,0:T(8,128)(2,1)} %bitcast.80), channel_id=1, source_target_pairs={{0,8},{8,0},{1,9},{9,1},{2,10},{10,2},{3,11},{11,3},{4,12},{12,4},... | collective-permute-start | bytes 12582920 | tf_op jit(solution)/shard_map/ppermute | solution.py:956
  31.5 16.3 %collective-permute-start.6 = (bf16[2,384,1024]{2,1,0:T(8,128)(2,1)}, bf16[2,384,1024]{2,1,0:T(8,128)(2,1)}, u32[]{:S(2)}, u32[]{:S(2)}) collective-permute-start(bf16[2,384,1024]{2,1,0:T(8,128)(2,1)} %get-tuple-element.320.refs_9_.refs_2_), channel_id=1, source_target_pairs={{0,8},{8,0},{1,9},{9,1},{2,10},{10,2},{3,11},{11,3},{4,12},{12,4},... | collective-permute-start | bytes 4718600 | tf_op jit(solution)/shard_map/ppermute | solution.py:956
  32.9 27.1 %collective-permute-start.7 = (bf16[512,1024]{1,0:T(8,128)(2,1)}, bf16[512,1024]{1,0:T(8,128)(2,1)S(1)}, u32[]{:S(2)}, u32[]{:S(2)}) collective-permute-start(bf16[512,1024]{1,0:T(8,128)(2,1)} %bitcast.101), channel_id=1, source_target_pairs={{0,8},{8,0},{1,9},{9,1},{2,10},{10,2},{3,11},{11,3},{4,12},{12,4},... | collective-permute-start | bytes 3145736 | tf_op jit(solution)/shard_map/ppermute | solution.py:956
  43.4 45.6 %collective-permute-start.5 = (bf16[2,384,1024]{2,1,0:T(8,128)(2,1)}, bf16[2,384,1024]{2,1,0:T(8,128)(2,1)}, u32[]{:S(2)}, u32[]{:S(2)}) collective-permute-start(bf16[2,384,1024]{2,1,0:T(8,128)(2,1)} %get-tuple-element.323.refs_2_.refs_11_), channel_id=1, source_target_pairs={{0,8},{8,0},{1,9},{9,1},{2,10},{10,2},{3,11},{11,3},{4,12},{12,4},... | collective-permute-start | bytes 4718600 | tf_op jit(solution)/shard_map/ppermute | solution.py:956
  83.0 39.2 %collective-permute-start.10 = (bf16[384,1024]{1,0:T(8,128)(2,1)}, bf16[384,1024]{1,0:T(8,128)(2,1)S(1)}, u32[]{:S(2)}, u32[]{:S(2)}) collective-permute-start(bf16[384,1024]{1,0:T(8,128)(2,1)} %get-tuple-element.342.refs_19_), channel_id=1, source_target_pairs={{0,16},{1,17},{2,18},{3,19},{4,20},{5,21},{6,22},{7,23},{8,24},{9,... | collective-permute-start | bytes 2359304 | tf_op jit(solution)/shard_map/ppermute | solution.py:1475
  129.9 19.2 %collective-permute-start.9 = (bf16[384,1024]{1,0:T(8,128)(2,1)}, bf16[384,1024]{1,0:T(8,128)(2,1)S(1)}, u32[]{:S(2)}, u32[]{:S(2)}) collective-permute-start(bf16[384,1024]{1,0:T(8,128)(2,1)} %get-tuple-element.343.refs_8_), channel_id=1, source_target_pairs={{0,16},{1,17},{2,18},{3,19},{4,20},{5,21},{6,22},{7,23},{8,24},{9,... | collective-permute-start | bytes 2359304 | tf_op jit(solution)/shard_map/ppermute | solution.py:1477
  171.8 60.5 %collective-permute-start.15 = (bf16[384,1024]{1,0:T(8,128)(2,1)S(1)}, bf16[384,1024]{1,0:T(8,128)(2,1)S(1)}, u32[]{:S(2)}, u32[]{:S(2)}) collective-permute-start(bf16[384,1024]{1,0:T(8,128)(2,1)S(1)} %copy-done.42), channel_id=1, source_target_pairs={{16,0},{17,1},{18,2},{19,3},{20,4},{21,5},{22,6},{23,7},{24,8},{25... | collective-permute-start | bytes 2359304 | tf_op jit(solution)/shard_map/ppermute | solution.py:1480
  291.5 44.1 %collective-permute-start.18 = (bf16[384,1024]{1,0:T(8,128)(2,1)S(1)}, bf16[384,1024]{1,0:T(8,128)(2,1)S(1)}, u32[]{:S(2)}, u32[]{:S(2)}) collective-permute-start(bf16[384,1024]{1,0:T(8,128)(2,1)S(1)} %copy-done.43), channel_id=1, source_target_pairs={{16,0},{17,1},{18,2},{19,3},{20,4},{21,5},{22,6},{23,7},{24,8},{25... | collective-permute-start | bytes 2359304 | tf_op jit(solution)/shard_map/ppermute | solution.py:1483
  407.4 23.9 %collective-permute-start.23 = (bf16[2,384,1024]{2,1,0:T(8,128)(2,1)}, bf16[2,384,1024]{2,1,0:T(8,128)(2,1)S(1)}, u32[]{:S(2)}, u32[]{:S(2)}) collective-permute-start(bf16[2,384,1024]{2,1,0:T(8,128)(2,1)} %get-tuple-element.427), channel_id=1, source_target_pairs={{0,8},{8,0},{1,9},{9,1},{2,10},{10,2},{3,11},{11,3},{4,12},{12,4},... | collective-permute-start | bytes 4718600 | tf_op jit(solution)/shard_map/ppermute | solution.py:956
  453.6 31.0 %collective-permute-start.29 = (bf16[1024,1536]{1,0:T(8,128)(2,1)}, bf16[1024,1536]{1,0:T(8,128)(2,1)}, u32[]{:S(2)}, u32[]{:S(2)}) collective-permute-start(bf16[1024,1536]{1,0:T(8,128)(2,1)} %bitcast_convert_fusion.2), channel_id=1, source_target_pairs={{0,8},{8,0},{1,9},{9,1},{2,10},{10,2},{3,11},{11,3},{4,12},{12,4},... | collective-permute-start | bytes 9437192 | tf_op jit(solution)/shard_map/ppermute | solution.py:956
  455.9 28.6 %collective-permute-start.30 = (bf16[1024,512]{1,0:T(8,128)(2,1)}, bf16[1024,512]{1,0:T(8,128)(2,1)S(1)}, u32[]{:S(2)}, u32[]{:S(2)}) collective-permute-start(bf16[1024,512]{1,0:T(8,128)(2,1)} %pad_maximum_fusion.1), channel_id=1, source_target_pairs={{0,8},{8,0},{1,9},{9,1},{2,10},{10,2},{3,11},{11,3},{4,12},{12,4},... | collective-permute-start | bytes 3145736 | tf_op jit(solution)/shard_map/ppermute | solution.py:956
  498.0 22.8 %collective-permute-start.40 = (bf16[64,4096]{1,0:T(8,128)(2,1)S(1)}, bf16[64,4096]{1,0:T(8,128)(2,1)S(1)}, u32[]{:S(2)}, u32[]{:S(2)}) collective-permute-start(bf16[64,4096]{1,0:T(8,128)(2,1)S(1)} %get-tuple-element.471), channel_id=1, source_target_pairs={{0,2},{2,4},{4,6},{6,7},{7,5},{5,3},{3,1},{1,0},{8,10},{10,12},{12... | collective-permute-start | bytes 1572872 | tf_op jit(solution)/shard_map/ppermute | solution.py:1094
  498.8 22.0 %collective-permute-start.41 = (bf16[64,4096]{1,0:T(8,128)(2,1)S(1)}, bf16[64,4096]{1,0:T(8,128)(2,1)S(1)}, u32[]{:S(2)}, u32[]{:S(2)}) collective-permute-start(bf16[64,4096]{1,0:T(8,128)(2,1)S(1)} %get-tuple-element.472), channel_id=1, source_target_pairs={{0,1},{2,0},{4,2},{6,4},{7,6},{5,7},{3,5},{1,3},{8,9},{10,8},{12,1... | collective-permute-start | bytes 1572872 | tf_op jit(solution)/shard_map/ppermute | solution.py:1094
  500.0 17.2 %collective-permute-start.32 = (bf16[64,2176]{1,0:T(8,128)(2,1)S(1)}, bf16[64,2176]{1,0:T(8,128)(2,1)S(1)}, u32[]{:S(2)}, u32[]{:S(2)}) collective-permute-start(bf16[64,2176]{1,0:T(8,128)(2,1)S(1)} %copy-done.52), channel_id=1, source_target_pairs={{0,2},{2,4},{4,6},{6,7},{7,5},{5,3},{3,1},{1,0},{8,10},{10,12},{12... | collective-permute-start | bytes 835592 | tf_op jit(solution)/shard_map/ppermute | solution.py:1094
  500.8 17.7 %collective-permute-start.33 = (bf16[64,2176]{1,0:T(8,128)(2,1)S(1)}, bf16[64,2176]{1,0:T(8,128)(2,1)S(1)}, u32[]{:S(2)}, u32[]{:S(2)}) collective-permute-start(bf16[64,2176]{1,0:T(8,128)(2,1)S(1)} %copy-done.51), channel_id=1, source_target_pairs={{0,1},{2,0},{4,2},{6,4},{7,6},{5,7},{3,5},{1,3},{8,9},{10,8},{12,1... | collective-permute-start | bytes 835592 | tf_op jit(solution)/shard_map/ppermute | solution.py:1094
  523.2 21.6 %collective-permute-start.44 = (bf16[64,4096]{1,0:T(8,128)(2,1)S(1)}, bf16[64,4096]{1,0:T(8,128)(2,1)S(1)}, u32[]{:S(2)}, u32[]{:S(2)}) collective-permute-start(bf16[64,4096]{1,0:T(8,128)(2,1)S(1)} %get-tuple-element.479), channel_id=1, source_target_pairs={{0,2},{2,4},{4,6},{6,7},{7,5},{5,3},{3,1},{1,0},{8,10},{10,12},{12... | collective-permute-start | bytes 1572872 | tf_op jit(solution)/shard_map/ppermute | solution.py:1094
  524.0 20.8 %collective-permute-start.45 = (bf16[64,4096]{1,0:T(8,128)(2,1)S(1)}, bf16[64,4096]{1,0:T(8,128)(2,1)S(1)}, u32[]{:S(2)}, u32[]{:S(2)}) collective-permute-start(bf16[64,4096]{1,0:T(8,128)(2,1)S(1)} %get-tuple-element.480), channel_id=1, source_target_pairs={{0,1},{2,0},{4,2},{6,4},{7,6},{5,7},{3,5},{1,3},{8,9},{10,8},{12,1... | collective-permute-start | bytes 1572872 | tf_op jit(solution)/shard_map/ppermute | solution.py:1094
  525.2 16.8 %collective-permute-start.38 = (bf16[64,2176]{1,0:T(8,128)(2,1)S(1)}, bf16[64,2176]{1,0:T(8,128)(2,1)S(1)}, u32[]{:S(2)}, u32[]{:S(2)}) collective-permute-start(bf16[64,2176]{1,0:T(8,128)(2,1)S(1)} %get-tuple-element.475), channel_id=1, source_target_pairs={{0,2},{2,4},{4,6},{6,7},{7,5},{5,3},{3,1},{1,0},{8,10},{10,12},{12... | collective-permute-start | bytes 835592 | tf_op jit(solution)/shard_map/ppermute | solution.py:1094
  526.0 16.7 %collective-permute-start.39 = (bf16[64,2176]{1,0:T(8,128)(2,1)S(1)}, bf16[64,2176]{1,0:T(8,128)(2,1)S(1)}, u32[]{:S(2)}, u32[]{:S(2)}) collective-permute-start(bf16[64,2176]{1,0:T(8,128)(2,1)S(1)} %get-tuple-element.476), channel_id=1, source_target_pairs={{0,1},{2,0},{4,2},{6,4},{7,6},{5,7},{3,5},{1,3},{8,9},{10,8},{12,1... | collective-permute-start | bytes 835592 | tf_op jit(solution)/shard_map/ppermute | solution.py:1094
  547.0 20.4 %collective-permute-start.48 = (bf16[64,4096]{1,0:T(8,128)(2,1)S(1)}, bf16[64,4096]{1,0:T(8,128)(2,1)S(1)}, u32[]{:S(2)}, u32[]{:S(2)}) collective-permute-start(bf16[64,4096]{1,0:T(8,128)(2,1)S(1)} %get-tuple-element.487), channel_id=1, source_target_pairs={{0,2},{2,4},{4,6},{6,7},{7,5},{5,3},{3,1},{1,0},{8,10},{10,12},{12... | collective-permute-start | bytes 1572872 | tf_op jit(solution)/shard_map/ppermute | solution.py:1094
  547.7 19.7 %collective-permute-start.49 = (bf16[64,4096]{1,0:T(8,128)(2,1)S(1)}, bf16[64,4096]{1,0:T(8,128)(2,1)S(1)}, u32[]{:S(2)}, u32[]{:S(2)}) collective-permute-start(bf16[64,4096]{1,0:T(8,128)(2,1)S(1)} %get-tuple-element.488), channel_id=1, source_target_pairs={{0,1},{2,0},{4,2},{6,4},{7,6},{5,7},{3,5},{1,3},{8,9},{10,8},{12,1... | collective-permute-start | bytes 1572872 | tf_op jit(solution)/shard_map/ppermute | solution.py:1094
  569.7 19.2 %collective-permute-start.52 = (bf16[64,4096]{1,0:T(8,128)(2,1)S(1)}, bf16[64,4096]{1,0:T(8,128)(2,1)S(1)}, u32[]{:S(2)}, u32[]{:S(2)}) collective-permute-start(bf16[64,4096]{1,0:T(8,128)(2,1)S(1)} %get-tuple-element.495.refs_1_), channel_id=1, source_target_pairs={{0,2},{2,4},{4,6},{6,7},{7,5},{5,3},{3,1},{1,0},{8,10},{10,12},{12... | collective-permute-start | bytes 1572872 | tf_op jit(solution)/shard_map/ppermute | solution.py:1094
  570.3 18.6 %collective-permute-start.53 = (bf16[64,4096]{1,0:T(8,128)(2,1)S(1)}, bf16[64,4096]{1,0:T(8,128)(2,1)S(1)}, u32[]{:S(2)}, u32[]{:S(2)}) collective-permute-start(bf16[64,4096]{1,0:T(8,128)(2,1)S(1)} %get-tuple-element.496.refs_2_), channel_id=1, source_target_pairs={{0,1},{2,0},{4,2},{6,4},{7,6},{5,7},{3,5},{1,3},{8,9},{10,8},{12,1... | collective-permute-start | bytes 1572872 | tf_op jit(solution)/shard_map/ppermute | solution.py:1094
  591.8 18.1 %collective-permute-start.56 = (bf16[64,4096]{1,0:T(8,128)(2,1)S(1)}, bf16[64,4096]{1,0:T(8,128)(2,1)S(1)}, u32[]{:S(2)}, u32[]{:S(2)}) collective-permute-start(bf16[64,4096]{1,0:T(8,128)(2,1)S(1)} %get-tuple-element.503), channel_id=1, source_target_pairs={{0,2},{2,4},{4,6},{6,7},{7,5},{5,3},{3,1},{1,0},{8,10},{10,12},{12... | collective-permute-start | bytes 1572872 | tf_op jit(solution)/shard_map/ppermute | solution.py:1094
  592.4 17.5 %collective-permute-start.57 = (bf16[64,4096]{1,0:T(8,128)(2,1)S(1)}, bf16[64,4096]{1,0:T(8,128)(2,1)S(1)}, u32[]{:S(2)}, u32[]{:S(2)}) collective-permute-start(bf16[64,4096]{1,0:T(8,128)(2,1)S(1)} %get-tuple-element.504), channel_id=1, source_target_pairs={{0,1},{2,0},{4,2},{6,4},{7,6},{5,7},{3,5},{1,3},{8,9},{10,8},{12,1... | collective-permute-start | bytes 1572872 | tf_op jit(solution)/shard_map/ppermute | solution.py:1094
  612.0 17.0 %collective-permute-start.60 = (bf16[64,4096]{1,0:T(8,128)(2,1)S(1)}, bf16[64,4096]{1,0:T(8,128)(2,1)S(1)}, u32[]{:S(2)}, u32[]{:S(2)}) collective-permute-start(bf16[64,4096]{1,0:T(8,128)(2,1)S(1)} %get-tuple-element.513), channel_id=1, source_target_pairs={{0,2},{2,4},{4,6},{6,7},{7,5},{5,3},{3,1},{1,0},{8,10},{10,12},{12... | collective-permute-start | bytes 1572872 | tf_op jit(solution)/shard_map/ppermute | solution.py:1094
  612.6 16.4 %collective-permute-start.61 = (bf16[64,4096]{1,0:T(8,128)(2,1)S(1)}, bf16[64,4096]{1,0:T(8,128)(2,1)S(1)}, u32[]{:S(2)}, u32[]{:S(2)}) collective-permute-start(bf16[64,4096]{1,0:T(8,128)(2,1)S(1)} %get-tuple-element.514), channel_id=1, source_target_pairs={{0,1},{2,0},{4,2},{6,4},{7,6},{5,7},{3,5},{1,3},{8,9},{10,8},{12,1... | collective-permute-start | bytes 1572872 | tf_op jit(solution)/shard_map/ppermute | solution.py:1094
  649.4 20.1 %collective-permute-start.68 = (bf16[64,4096]{1,0:T(8,128)(2,1)S(1)}, bf16[64,4096]{1,0:T(8,128)(2,1)S(1)}, u32[]{:S(2)}, u32[]{:S(2)}) collective-permute-start(bf16[64,4096]{1,0:T(8,128)(2,1)S(1)} %get-tuple-element.533), channel_id=1, source_target_pairs={{0,2},{2,4},{4,6},{6,7},{7,5},{5,3},{3,1},{1,0},{8,10},{10,12},{12... | collective-permute-start | bytes 1572872 | tf_op jit(solution)/shard_map/ppermute | solution.py:1094
  649.7 19.8 %collective-permute-start.69 = (bf16[64,4096]{1,0:T(8,128)(2,1)S(1)}, bf16[64,4096]{1,0:T(8,128)(2,1)S(1)}, u32[]{:S(2)}, u32[]{:S(2)}) collective-permute-start(bf16[64,4096]{1,0:T(8,128)(2,1)S(1)} %get-tuple-element.534), channel_id=1, source_target_pairs={{0,1},{2,0},{4,2},{6,4},{7,6},{5,7},{3,5},{1,3},{8,9},{10,8},{12,1... | collective-permute-start | bytes 1572872 | tf_op jit(solution)/shard_map/ppermute | solution.py:1094
  702.6 21.4 %collective-permute-start.16 = (bf16[2,384,512]{2,1,0:T(8,128)(2,1)S(1)}, bf16[2,384,512]{2,1,0:T(8,128)(2,1)S(1)}, u32[]{:S(2)}, u32[]{:S(2)}) collective-permute-start(bf16[2,384,512]{2,1,0:T(8,128)(2,1)S(1)} %shard_map.312), channel_id=1, source_target_pairs={{0,8},{8,0},{1,9},{9,1},{2,10},{10,2},{3,11},{11,3},{4,12},{12,4},... | collective-permute-start | bytes 2359304 | tf_op jit(solution)/shard_map/ppermute | solution.py:956
  712.8 16.5 %collective-permute-start.82 = (bf16[64,4096]{1,0:T(8,128)(2,1)S(1)}, bf16[64,4096]{1,0:T(8,128)(2,1)S(1)}, u32[]{:S(2)}, u32[]{:S(2)}) collective-permute-start(bf16[64,4096]{1,0:T(8,128)(2,1)S(1)} %get-tuple-element.556), channel_id=1, source_target_pairs={{0,2},{2,4},{4,6},{6,7},{7,5},{5,3},{3,1},{1,0},{8,10},{10,12},{12... | collective-permute-start | bytes 1572872 | tf_op jit(solution)/shard_map/ppermute | solution.py:1094
  (107 other events, 886.0 us)
